TPU v7x, 32 devices: a whole 2x2x4 slice. The times are simulated.
32 devices in a mesh: fluid: 8 (over y, x, core), wall: 4 (over z).
Axes of the slice: x: 2, y: 2, z: 4, core: 2. Of those that a mesh axis runs over, the one named last changes fastest.
Arguments:
- flow_state: float32 [4, 128, 32, 512], P(None, 'fluid', None, 'wall'), may hold values from -6 to 6
- regions: int32 [128, 32, 512], P('fluid', None, 'wall'), may hold values from 0 to 63
- obs_tiles: bfloat16 [8, 4, 32, 128, 128], P('fluid', 'wall'), may hold values from -0.5 to 0.5
- measured: bfloat16 [8, 4, 32, 3, 128], P('fluid', 'wall'), may hold values from -6 to 6
- tile_dest: int32 [8, 4, 32], P('fluid', 'wall'), may hold values from 0 to 7, as said below
- cell_list: int32 [8, 4, 8, 4], P('fluid', 'wall'), may hold values from 0 to 511
Outputs:
- velocity_next: float32 [3, 128, 32, 512], P(None, 'fluid', None, 'wall')
- adjoint: float32 [3, 128, 32, 512], P(None, 'fluid', None, 'wall')
- sensitivity: float32 [512], P(('fluid', 'wall'))
Inputs may be any that keep to these rules, and one draw needn't show every extreme that they name: `tile_dest`: each device's list names every fluid block at most 4 times. In each wall column one fluid block is named exactly 4 times by the list of every device of that column.
All inputs are finite; a program needn't handle non-finite values.
Results may differ from a plain program's by a relative error of at most 0.0032.
Values may be sent and summed in bfloat16 or wider, within the bound.
No kernel may reach another device: no remote copies, remote signals or barrier semaphores. Data moves between devices by JAX's collectives and lax.ppermute only.
A program may use at most 128 MiB of HBM per device.

v0:
```python
import jax
import jax.numpy as jnp
from jax import lax
from jax.sharding import PartitionSpec as P

REG_DEV = 16


time_step = 0.12
nu_floor = 0.1
nu_spread = 0.9
relax_sq = 4.0
sens_scale = 0.03


def with_halo(block, sides, width):
    for axis, dim in sides:
        count = lax.axis_size(axis)
        forward = [(i, i + 1) for i in range(count - 1)]
        backward = [(target, source) for source, target in forward]
        low = lax.ppermute(
            lax.slice_in_dim(block, block.shape[dim] - width, None, axis=dim), axis, forward
        )
        high = lax.ppermute(lax.slice_in_dim(block, 0, width, axis=dim), axis, backward)
        block = jnp.concatenate([low, block, high], axis=dim)
    return block


def face_differences(padded, spatial):
    extent = padded.shape[spatial]
    upper_cells = lax.slice_in_dim(padded, 1, extent, axis=spatial)
    lower_cells = lax.slice_in_dim(padded, 0, extent - 1, axis=spatial)
    face_jump = upper_cells - lower_cells
    for across in (1, 2, 3):
        if across != spatial:
            face_jump = lax.slice_in_dim(face_jump, 1, face_jump.shape[across] - 1, axis=across)
    return face_jump


def viscosity(face_jump):
    shear_sq = jnp.sum(face_jump * face_jump, axis=0)
    return nu_floor + nu_spread * jnp.power(1.0 + relax_sq * shear_sq, -0.25)


def divergence(face_nus, face_jumps):
    summed = 0.0
    for spatial, nu_face, face_jump in zip((1, 2, 3), face_nus, face_jumps):
        face_flux = nu_face[None] * face_jump
        extent = face_flux.shape[spatial]
        summed = (
            summed
            + lax.slice_in_dim(face_flux, 1, extent, axis=spatial)
            - lax.slice_in_dim(face_flux, 0, extent - 1, axis=spatial)
        )
    return summed


def forward(padded):
    velocity = padded[:3]
    pressure = padded[3:4]
    face_jumps = [face_differences(velocity, spatial) for spatial in (1, 2, 3)]
    face_nus = [viscosity(face_jump) for face_jump in face_jumps]
    halves = []
    for spatial in (1, 2, 3):
        pressure_jump = face_differences(pressure, spatial)
        extent = pressure_jump.shape[spatial]
        halves.append(
            0.5
            * (
                lax.slice_in_dim(pressure_jump, 1, extent, axis=spatial)
                + lax.slice_in_dim(pressure_jump, 0, extent - 1, axis=spatial)
            )
        )
    gradient = jnp.concatenate(halves, axis=0)
    interior = padded[:3, 1:-1, 1:-1, 1:-1]
    velocity_next = interior + time_step * (divergence(face_nus, face_jumps) - gradient)
    return (velocity_next, face_nus)


def adjoint_step(padded_forcing, face_nus):
    face_jumps = [face_differences(padded_forcing, spatial) for spatial in (1, 2, 3)]
    return padded_forcing[:, 1:-1, 1:-1, 1:-1] + time_step * divergence(face_nus, face_jumps)


def body(flow_state, regions, obs_tiles, measured, tile_dest, cell_list):
    rimmed = with_halo(flow_state, (("fluid", 1), ("wall", 3)), 1)
    padded = jnp.pad(rimmed, ((0, 0), (0, 0), (1, 1), (0, 0)))
    velocity_next, face_nus = forward(padded)
    obs_velocity = velocity_next.astype(jnp.bfloat16)
    block_groups = lax.axis_size("fluid")
    width_x = flow_state.shape[1]
    width_y = flow_state.shape[2]
    depth_width = flow_state.shape[3]
    slot_limit = cell_list.shape[3]
    count_tiles = obs_tiles.shape[2]
    total_slots = block_groups * slot_limit
    obs_cells = obs_velocity.reshape(3, width_x * width_y, depth_width)
    target = tile_dest[0, 0]
    same_target = target[:, None] == target[None, :]
    before = jnp.arange(count_tiles)[None, :] < jnp.arange(count_tiles)[:, None]
    slot_rank = jnp.sum((same_target & before).astype(jnp.int32), axis=1)
    index_of_slot = target * slot_limit + slot_rank
    cell_ids = cell_list[0, 0].reshape(total_slots)
    tile_rows = obs_tiles[0, 0]
    measurement_rows = measured[0, 0]
    send_tiles = (
        jnp.zeros((total_slots, depth_width, depth_width), jnp.bfloat16)
        .at[index_of_slot]
        .set(tile_rows)
    )
    outgoing_measurements = (
        jnp.zeros((total_slots, 3, depth_width), jnp.bfloat16)
        .at[index_of_slot]
        .set(measurement_rows)
    )
    received_tiles, received_measurements = (
        lax.all_to_all(
            send_tiles.reshape(block_groups, slot_limit, depth_width, depth_width),
            "fluid",
            split_axis=0,
            concat_axis=0,
            tiled=True,
        ),
        lax.all_to_all(
            outgoing_measurements.reshape(block_groups, slot_limit, 3, depth_width),
            "fluid",
            split_axis=0,
            concat_axis=0,
            tiled=True,
        ),
    )
    received_tiles = received_tiles.reshape(total_slots, depth_width, depth_width)
    received_measurements = received_measurements.reshape(total_slots, 3, depth_width)
    cell_values = jnp.take(obs_cells, cell_ids, axis=1)
    model_velocity = jnp.einsum(
        "mij,cmj->mci", received_tiles, cell_values, preferred_element_type=jnp.float32
    )
    data_residual = (model_velocity - received_measurements.astype(jnp.float32)).astype(
        jnp.bfloat16
    )
    contrib = jnp.einsum(
        "mij,mci->mcj", received_tiles, data_residual, preferred_element_type=jnp.float32
    )
    forcing = (
        jnp.zeros((3, width_x * width_y, depth_width), jnp.float32)
        .at[:, cell_ids]
        .add(jnp.transpose(contrib, (1, 0, 2)))
    )
    forcing = forcing.reshape(3, width_x, width_y, depth_width)
    rim_force = with_halo(forcing, (("fluid", 1), ("wall", 3)), 1)
    padded_forcing = jnp.pad(rim_force, ((0, 0), (0, 0), (1, 1), (0, 0)))
    adjoint = adjoint_step(padded_forcing, face_nus)
    product = jnp.sum(adjoint * velocity_next, axis=0)
    reg_count = REG_DEV * lax.axis_size("wall")
    labels = jnp.arange(reg_count, dtype=jnp.int32)

    def add_slab(running, slab_pair):
        values, slab_ids = slab_pair
        onehot = (slab_ids[:, None] == labels[None, :]).astype(jnp.float32)
        return (running + jnp.dot(values, onehot, precision=lax.Precision.HIGHEST), None)

    partial_sums, _ = lax.scan(
        add_slab,
        jnp.zeros((reg_count,), jnp.float32),
        (product.reshape(width_x, -1), regions.reshape(width_x, -1)),
    )
    owned = lax.psum_scatter(partial_sums, "wall", scatter_dimension=0, tiled=True)
    return (velocity_next, adjoint, sens_scale * owned)


def solution(mesh):
    in_specs = (
        P(None, "fluid", None, "wall"),
        P("fluid", None, "wall"),
        P("fluid", "wall", None, None, None),
        P("fluid", "wall", None, None, None),
        P("fluid", "wall", None),
        P("fluid", "wall", None, None),
    )
    out_specs = (
        P(None, "fluid", None, "wall"),
        P(None, "fluid", None, "wall"),
        P(("fluid", "wall")),
    )
    return jax.shard_map(body, mesh=mesh, in_specs=in_specs, out_specs=out_specs, check_vma=False)
```

profile of v0, /device:TPU:0, one launch (start us, length us, event | category | flops | bytes accessed | tf_op | source)
XLA Modules:
  0.0 118.7 jit_solution(15544320009929203803)
XLA Ops:
  1.6 2.4 %collective-permute-start = (f32[4,1,32,128]{3,2,1,0:T(8,128)S(1)}, f32[4,1,32,128]{3,2,1,0:T(8,128)S(1)}, u32[]{:S(2)}, u32[]{:S(2)}) collective-permute-start(f32[4,1,32,128]{3,2,1,0:T(8,128)S(1)} %get-tuple-element.80), channel_id=1, source_target_pairs={{0,4},{4,8},{8,12},{12,16},{16,20},{20,24},{24,28},{1,5},{5,9},{9,... | collective-permute-start | bytes 196616 | tf_op jit(solution)/shard_map/ppermute | solution.py:21
  4.0 1.3 %collective-permute-start.1 = (f32[4,1,32,128]{3,2,1,0:T(8,128)S(1)}, f32[4,1,32,128]{3,2,1,0:T(8,128)S(1)}, u32[]{:S(2)}, u32[]{:S(2)}) collective-permute-start(f32[4,1,32,128]{3,2,1,0:T(8,128)S(1)} %get-tuple-element.79), channel_id=1, source_target_pairs={{4,0},{8,4},{12,8},{16,12},{20,16},{24,20},{28,24},{5,1},{9,5},{13... | collective-permute-start | bytes 196616 | tf_op jit(solution)/shard_map/ppermute | solution.py:24
  7.6 1.5 %scatter_fusion.1 = bf16[32,3,128]{2,1,0:T(4,128)(2,1)S(1)} fusion(bf16[32,3,128]{2,1,0:T(4,128)(2,1)S(1)} %broadcast_in_dim.22, s32[32]{0:T(128)S(1)} %fusion.35, bf16[32,3,128]{2,1,0:T(4,128)(2,1)S(1)} %copy.127), kind=kCustom, calls=%fused_computation.2 | custom fusion | bytes 73856 | tf_op jit(solution)/shard_map/scatter | solution.py:114
  9.8 7.2 %all-to-all-start.1 = ((bf16[8,4,3,128]{3,1,2,0:T(4,128)(2,1)}), bf16[8,4,3,128]{3,1,2,0:T(4,128)(2,1)}, u32[]{:S(2)}, u32[]{:S(2)}) async-start(bf16[8,4,3,128]{3,1,2,0:T(4,128)(2,1)} %copy.128), calls=%async_computation.1 | async-start | bytes 49152 | tf_op jit(solution)/shard_map/all_to_all | solution.py:124
  19.6 4.6 %scatter_fusion = bf16[32,128,128]{2,1,0:T(8,128)(2,1)} fusion(bf16[32,128,128]{2,1,0:T(8,128)(2,1)} %broadcast_in_dim.21, s32[32]{0:T(128)S(1)} %fusion.35, bf16[32,128,128]{2,1,0:T(8,128)(2,1)S(1)} %bitcast.57), kind=kCustom, calls=%fused_computation.1 | custom fusion | bytes 3145856 | tf_op jit(solution)/shard_map/scatter | solution.py:109
  26.7 1.3 %collective-permute-start.3 = (f32[4,18,32,1]{2,1,3,0:T(8,128)}, f32[4,18,32,1]{2,1,3,0:T(8,128)S(1)}, u32[]{:S(2)}, u32[]{:S(2)}) collective-permute-start(f32[4,18,32,1]{2,1,3,0:T(8,128)} %copy.145), channel_id=1, source_target_pairs={{1,0},{2,1},{3,2},{5,4},{6,5},{7,6},{9,8},{10,9},{11,10},{13,12},{... | collective-permute-start | bytes 27656 | tf_op jit(solution)/shard_map/ppermute | solution.py:24
  28.6 4.5 %collective-permute-start.2 = (f32[4,18,32,1]{2,1,3,0:T(8,128)S(1)}, f32[4,18,32,1]{2,1,3,0:T(8,128)S(1)}, u32[]{:S(2)}, u32[]{:S(2)}) collective-permute-start(f32[4,18,32,1]{2,1,3,0:T(8,128)S(1)} %copy.144), channel_id=1, source_target_pairs={{0,1},{1,2},{2,3},{4,5},{5,6},{6,7},{8,9},{9,10},{10,11},{12,13},{... | collective-permute-start | bytes 27656 | tf_op jit(solution)/shard_map/ppermute | solution.py:21
  33.2 4.2 %all-to-all-start = ((bf16[8,4,128,128]{3,2,1,0:T(8,128)(2,1)}), bf16[8,4,128,128]{3,2,1,0:T(8,128)(2,1)S(1)}, u32[]{:S(2)}, u32[]{:S(2)}) async-start(bf16[8,4,128,128]{3,2,1,0:T(8,128)(2,1)} %bitcast.8), calls=%async_computation | async-start | bytes 2097152 | tf_op jit(solution)/shard_map/all_to_all | solution.py:117
  39.2 1.5 %copy.122 = f32[4,18,32,1]{3,2,1,0:T(8,128)} copy(f32[4,18,32,1]{2,1,3,0:T(8,128)S(1)} %collective-permute-done.2) | data formatting | bytes 18432 | tf_op jit(solution)/shard_map/ppermute | solution.py:21
  40.8 2.5 %select_maximum_fusion = f32[4,18,34,130]{3,2,1,0:T(8,128)S(1)} fusion(f32[4,18,32,1]{3,2,1,0:T(8,128)S(1)} %copy.123, f32[4,18,32,128]{3,2,1,0:T(8,128)S(1)} %constant_dynamic-update-slice_fusion, f32[4,18,32,1]{3,2,1,0:T(8,128)} %copy.122), kind=kLoop, calls=%fused_computation.20 | loop fusion | flops 2545920 | bytes 2471040 | tf_op jit(solution)/shard_map/concatenate | solution.py:25
  53.9 1.6 %scatter_fusion.2 = f32[3,512,128]{2,0,1:T(4,128)S(1)} fusion(f32[3,512,128]{2,0,1:T(4,128)S(1)} %broadcast_in_dim.18, s32[32]{0:T(128)S(1)} %copy-done.12, f32[32,3,128]{2,1,0:T(4,128)S(1)} %fusion.13), kind=kCustom, calls=%fused_computation.3 | custom fusion | flops 12288 | bytes 147584 | tf_op jit(solution)/shard_map/scatter-add | solution.py:147
  55.7 1.3 %collective-permute-start.5 = (f32[3,1,32,128]{3,2,1,0:T(8,128)S(1)}, f32[3,1,32,128]{3,2,1,0:T(8,128)S(1)}, u32[]{:S(2)}, u32[]{:S(2)}) collective-permute-start(f32[3,1,32,128]{3,2,1,0:T(8,128)S(1)} %get-tuple-element.82), channel_id=1, source_target_pairs={{4,0},{8,4},{12,8},{16,12},{20,16},{24,20},{28,24},{5,1},{9,5},{13... | collective-permute-start | bytes 147464 | tf_op jit(solution)/shard_map/ppermute | solution.py:24
  57.0 3.0 %collective-permute-start.4 = (f32[3,1,32,128]{3,2,1,0:T(8,128)S(1)}, f32[3,1,32,128]{3,2,1,0:T(8,128)S(1)}, u32[]{:S(2)}, u32[]{:S(2)}) collective-permute-start(f32[3,1,32,128]{3,2,1,0:T(8,128)S(1)} %get-tuple-element.81), channel_id=1, source_target_pairs={{0,4},{4,8},{8,12},{12,16},{16,20},{20,24},{24,28},{1,5},{5,9},{9,... | collective-permute-start | bytes 147464 | tf_op jit(solution)/shard_map/ppermute | solution.py:21
  60.0 2.2 %copy.135 = f32[3,16,32,128]{2,1,3,0:T(8,128)} copy(f32[3,16,32,128]{3,0,2,1:T(4,128)S(1)} %bitcast.54) | data formatting | bytes 1572864 | tf_op jit(solution)/shard_map/reshape | solution.py:149
  62.5 2.9 %pad_maximum_fusion = f32[3,18,32,128]{2,1,3,0:T(8,128)S(1)} fusion(f32[3,1,32,128]{2,1,3,0:T(1,128)S(1)} %copy.136, f32[3,16,32,128]{2,1,3,0:T(8,128)} %copy.135, f32[3,1,32,128]{2,1,3,0:T(1,128)S(1)} %copy.134), kind=kLoop, calls=%fused_computation.15 | loop fusion | flops 442368 | bytes 1769472 | tf_op jit(solution)/shard_map/concatenate | solution.py:25
  65.5 2.1 %copy-done = f32[3,18,32,128]{2,1,3,0:T(8,128)} copy-done((f32[3,18,32,128]{2,1,3,0:T(8,128)}, f32[3,18,32,128]{2,1,3,0:T(8,128)S(1)}, u32[]{:S(2)}) %copy-start) | copy-done | bytes 884760
  68.2 1.3 %collective-permute-start.7 = (f32[3,18,32,1]{2,1,3,0:T(8,128)S(1)}, f32[3,18,32,1]{2,1,3,0:T(8,128)}, u32[]{:S(2)}, u32[]{:S(2)}) collective-permute-start(f32[3,18,32,1]{2,1,3,0:T(8,128)S(1)} %get-tuple-element.64), channel_id=1, source_target_pairs={{1,0},{2,1},{3,2},{5,4},{6,5},{7,6},{9,8},{10,9},{11,10},{13,12},{... | collective-permute-start | bytes 20744 | tf_op jit(solution)/shard_map/ppermute | solution.py:24
  69.5 5.2 %collective-permute-start.6 = (f32[3,18,32,1]{2,1,3,0:T(8,128)}, f32[3,18,32,1]{2,1,3,0:T(8,128)}, u32[]{:S(2)}, u32[]{:S(2)}) collective-permute-start(f32[3,18,32,1]{2,1,3,0:T(8,128)} %get-tuple-element.63), channel_id=1, source_target_pairs={{0,1},{1,2},{2,3},{4,5},{5,6},{6,7},{8,9},{9,10},{10,11},{12,13},{... | collective-permute-start | bytes 20744 | tf_op jit(solution)/shard_map/ppermute | solution.py:21
  76.1 4.5 %copy.138 = f32[3,18,32,128]{3,2,1,0:T(8,128)} copy(f32[3,18,32,128]{2,1,3,0:T(8,128)} %copy-done) | data formatting | bytes 1769472 | tf_op jit(solution)/shard_map/concatenate | solution.py:25
  81.8 2.1 %copy.137 = f32[3,18,32,1]{3,2,1,0:T(8,128)} copy(f32[3,18,32,1]{2,1,3,0:T(8,128)} %collective-permute-done.6) | data formatting | bytes 13824 | tf_op jit(solution)/shard_map/ppermute | solution.py:21
  83.9 2.4 %select_maximum_fusion.2 = f32[3,18,34,130]{3,2,1,0:T(8,128)S(1)} fusion(f32[3,18,32,1]{3,2,1,0:T(8,128)S(1)} %copy.139, f32[3,18,32,128]{3,2,1,0:T(8,128)} %copy.138, f32[3,18,32,1]{3,2,1,0:T(8,128)} %copy.137), kind=kLoop, calls=%fused_computation.23 | loop fusion | flops 1909440 | bytes 1853280 | tf_op jit(solution)/shard_map/concatenate | solution.py:25
  89.9 1.4 %multiply_reduce_fusion.3 = (f32[16,32,128]{2,1,0:T(8,128)S(1)}, f32[3,16,32,128]{3,2,1,0:T(8,128)}) fusion(f32[3,16,32,128]{3,2,1,0:T(8,128)S(1)} %get-tuple-element.62, f32[3,16,32,129]{3,2,1,0:T(8,128)S(1)} %fusion.11, f32[3,16,33,128]{3,2,1,0:T(8,128)S(1)} %fusion.14, f32[3,17,32,128]{3,2,1,0:T(8,128)S(1)} %fusion.15, f32[3,16,32,128]{3,0,2,1:T(4,128)S(1)} %bitcast.55), kind=kLoop, calls=%fused_computation.56 | loop fusion | flops 1703936 | bytes 7340032 | tf_op jit(solution)/shard_map/reduce_sum | solution.py:153
  91.4 16.6 %while.11 = (s32[]{:T(128)}, f32[64]{0:T(128)S(1)}, f32[16,4096]{1,0:T(8,128)S(1)}, s32[16,4096]{1,0:T(8,128)S(1)}, s32[]{:T(128)}, /*index=5*/s32[]{:T(128)}) while((s32[]{:T(128)}, f32[64]{0:T(128)S(1)}, f32[16,4096]{1,0:T(8,128)S(1)}, s32[16,4096]{1,0:T(8,128)S(1)}, s32[]{:T(128)}, /*index=5*/s32[]{:T(128)}) %tuple.44), condition=%wide.region_9.10_spmd.clone, body=%wide.region_8.9_spmd.clone.sunk | while | flops 3408003 | bytes 66399 | solution.py:162
  108.1 10.0 %all-reduce.2 = f32[64]{0:T(128)S(1)} all-reduce(f32[64]{0:T(128)S(1)} %get-tuple-element.30), channel_id=2, replica_groups=mesh['fluid'=8,'wall'=4] {'wall'}, use_global_device_ids=true, to_apply=%region_10.11.clone | all-reduce | flops 64 | bytes 512
  (132 shorter events, 45.3 us)
Async XLA Ops:
  0.6 19.0 %copy-start.8 = (bf16[1,1,32,128,128]{4,3,2,1,0:T(8,128)(2,1)S(1)}, bf16[1,1,32,128,128]{4,3,2,1,0:T(8,128)(2,1)}, u32[]{:S(2)}) copy-start(bf16[1,1,32,128,128]{4,3,2,1,0:T(8,128)(2,1)} %param.10) | copy-start | bytes 3145732
  1.6 23.3 %collective-permute-start = (f32[4,1,32,128]{3,2,1,0:T(8,128)S(1)}, f32[4,1,32,128]{3,2,1,0:T(8,128)S(1)}, u32[]{:S(2)}, u32[]{:S(2)}) collective-permute-start(f32[4,1,32,128]{3,2,1,0:T(8,128)S(1)} %get-tuple-element.80), channel_id=1, source_target_pairs={{0,4},{4,8},{8,12},{12,16},{16,20},{20,24},{24,28},{1,5},{5,9},{9,... | collective-permute-start | bytes 196616 | tf_op jit(solution)/shard_map/ppermute | solution.py:21
  4.0 21.0 %collective-permute-start.1 = (f32[4,1,32,128]{3,2,1,0:T(8,128)S(1)}, f32[4,1,32,128]{3,2,1,0:T(8,128)S(1)}, u32[]{:S(2)}, u32[]{:S(2)}) collective-permute-start(f32[4,1,32,128]{3,2,1,0:T(8,128)S(1)} %get-tuple-element.79), channel_id=1, source_target_pairs={{4,0},{8,4},{12,8},{16,12},{20,16},{24,20},{28,24},{5,1},{9,5},{13... | collective-permute-start | bytes 196616 | tf_op jit(solution)/shard_map/ppermute | solution.py:24
  9.8 15.1 %copy-start.1 = (f32[4,16,32,128]{3,2,1,0:T(8,128)S(1)}, f32[4,16,32,128]{3,2,1,0:T(8,128)}, u32[]{:S(2)}) copy-start(f32[4,16,32,128]{3,2,1,0:T(8,128)} %param.8) | copy-start | bytes 3145732
  9.8 23.4 %all-to-all-start.1 = ((bf16[8,4,3,128]{3,1,2,0:T(4,128)(2,1)}), bf16[8,4,3,128]{3,1,2,0:T(4,128)(2,1)}, u32[]{:S(2)}, u32[]{:S(2)}) async-start(bf16[8,4,3,128]{3,1,2,0:T(4,128)(2,1)} %copy.128), calls=%async_computation.1 | async-start | bytes 49152 | tf_op jit(solution)/shard_map/all_to_all | solution.py:124
  17.9 7.0 %copy-start.11 = (s32[32]{0:T(128)}, s32[32]{0:T(128)S(1)}, u32[]{:S(2)}) copy-start(s32[32]{0:T(128)S(1)} %fusion.34) | copy-start | bytes 388
  26.7 12.0 %collective-permute-start.3 = (f32[4,18,32,1]{2,1,3,0:T(8,128)}, f32[4,18,32,1]{2,1,3,0:T(8,128)S(1)}, u32[]{:S(2)}, u32[]{:S(2)}) collective-permute-start(f32[4,18,32,1]{2,1,3,0:T(8,128)} %copy.145), channel_id=1, source_target_pairs={{1,0},{2,1},{3,2},{5,4},{6,5},{7,6},{9,8},{10,9},{11,10},{13,12},{... | collective-permute-start | bytes 27656 | tf_op jit(solution)/shard_map/ppermute | solution.py:24
  28.6 10.6 %collective-permute-start.2 = (f32[4,18,32,1]{2,1,3,0:T(8,128)S(1)}, f32[4,18,32,1]{2,1,3,0:T(8,128)S(1)}, u32[]{:S(2)}, u32[]{:S(2)}) collective-permute-start(f32[4,18,32,1]{2,1,3,0:T(8,128)S(1)} %copy.144), channel_id=1, source_target_pairs={{0,1},{1,2},{2,3},{4,5},{5,6},{6,7},{8,9},{9,10},{10,11},{12,13},{... | collective-permute-start | bytes 27656 | tf_op jit(solution)/shard_map/ppermute | solution.py:21
  33.2 19.6 %all-to-all-start = ((bf16[8,4,128,128]{3,2,1,0:T(8,128)(2,1)}), bf16[8,4,128,128]{3,2,1,0:T(8,128)(2,1)S(1)}, u32[]{:S(2)}, u32[]{:S(2)}) async-start(bf16[8,4,128,128]{3,2,1,0:T(8,128)(2,1)} %bitcast.8), calls=%async_computation | async-start | bytes 2097152 | tf_op jit(solution)/shard_map/all_to_all | solution.py:117
  46.7 1.2 copy-start.4
  48.1 1.1 copy-start.6
  49.2 1.2 %copy-start.2 = (f32[4,16,32,128]{3,2,1,0:T(8,128)S(1)}, f32[4,16,32,128]{3,2,1,0:T(8,128)}, u32[]{:S(2)}) copy-start(f32[4,16,32,128]{3,2,1,0:T(8,128)} %param.8) | copy-start | bytes 3145732
  50.4 2.3 %copy-start.9 = (f32[8,4,3,128]{3,1,0,2:T(4,128)S(1)}, f32[8,4,3,128]{3,1,0,2:T(4,128)}, u32[]{:S(2)}) copy-start(f32[8,4,3,128]{3,1,0,2:T(4,128)} %copy.130) | copy-start | bytes 147460
  50.4 2.3 %copy-start.13 = (pred[32]{0:T(512)(128)(4,1)S(1)}, pred[32]{0:T(512)(128)(4,1)}, u32[]{:S(2)}) copy-start(pred[32]{0:T(512)(128)(4,1)} %compare_and_fusion) | copy-start | bytes 100
  50.9 39.0 %copy-start.3 = (f32[3,16,32,128]{3,2,1,0:T(8,128)}, f32[3,16,32,128]{3,2,1,0:T(8,128)S(1)}, u32[]{:S(2)}) copy-start(f32[3,16,32,128]{3,2,1,0:T(8,128)S(1)} %get-tuple-element.62) | copy-start | bytes 2359300
  50.9 2.9 %copy-start.12 = (s32[32]{0:T(128)S(1)}, s32[32]{0:T(128)}, u32[]{:S(2)}) copy-start(s32[32]{0:T(128)} %copy-done.11) | copy-start | bytes 388
  55.7 6.6 %collective-permute-start.5 = (f32[3,1,32,128]{3,2,1,0:T(8,128)S(1)}, f32[3,1,32,128]{3,2,1,0:T(8,128)S(1)}, u32[]{:S(2)}, u32[]{:S(2)}) collective-permute-start(f32[3,1,32,128]{3,2,1,0:T(8,128)S(1)} %get-tuple-element.82), channel_id=1, source_target_pairs={{4,0},{8,4},{12,8},{16,12},{20,16},{24,20},{28,24},{5,1},{9,5},{13... | collective-permute-start | bytes 147464 | tf_op jit(solution)/shard_map/ppermute | solution.py:24
  57.0 5.4 %collective-permute-start.4 = (f32[3,1,32,128]{3,2,1,0:T(8,128)S(1)}, f32[3,1,32,128]{3,2,1,0:T(8,128)S(1)}, u32[]{:S(2)}, u32[]{:S(2)}) collective-permute-start(f32[3,1,32,128]{3,2,1,0:T(8,128)S(1)} %get-tuple-element.81), channel_id=1, source_target_pairs={{0,4},{4,8},{8,12},{12,16},{16,20},{20,24},{24,28},{1,5},{5,9},{9,... | collective-permute-start | bytes 147464 | tf_op jit(solution)/shard_map/ppermute | solution.py:21
  62.5 12.2 %copy-start.10 = (s32[16,32,128]{2,1,0:T(8,128)S(1)}, s32[16,32,128]{2,1,0:T(8,128)}, u32[]{:S(2)}) copy-start(s32[16,32,128]{2,1,0:T(8,128)} %param.9) | copy-start | bytes 786436
  62.5 12.3 %copy-start.14 = (u32[32]{0:T(128)S(1)}, u32[32]{0:T(128)}, u32[]{:S(2)}) copy-start(u32[32]{0:T(128)} %constant.76) | copy-start | bytes 388
  65.5 2.1 %copy-start = (f32[3,18,32,128]{2,1,3,0:T(8,128)}, f32[3,18,32,128]{2,1,3,0:T(8,128)S(1)}, u32[]{:S(2)}) copy-start(f32[3,18,32,128]{2,1,3,0:T(8,128)S(1)} %pad_maximum_fusion) | copy-start | bytes 2654212
  68.2 12.4 %collective-permute-start.7 = (f32[3,18,32,1]{2,1,3,0:T(8,128)S(1)}, f32[3,18,32,1]{2,1,3,0:T(8,128)}, u32[]{:S(2)}, u32[]{:S(2)}) collective-permute-start(f32[3,18,32,1]{2,1,3,0:T(8,128)S(1)} %get-tuple-element.64), channel_id=1, source_target_pairs={{1,0},{2,1},{3,2},{5,4},{6,5},{7,6},{9,8},{10,9},{11,10},{13,12},{... | collective-permute-start | bytes 20744 | tf_op jit(solution)/shard_map/ppermute | solution.py:24
  69.5 12.3 %collective-permute-start.6 = (f32[3,18,32,1]{2,1,3,0:T(8,128)}, f32[3,18,32,1]{2,1,3,0:T(8,128)}, u32[]{:S(2)}, u32[]{:S(2)}) collective-permute-start(f32[3,18,32,1]{2,1,3,0:T(8,128)} %get-tuple-element.63), channel_id=1, source_target_pairs={{0,1},{1,2},{2,3},{4,5},{5,6},{6,7},{8,9},{9,10},{10,11},{12,13},{... | collective-permute-start | bytes 20744 | tf_op jit(solution)/shard_map/ppermute | solution.py:21
  88.2 1.1 copy-start.7
  (1 other events, 1.0 us)
where the time goes:
time: 121 us; the launch traced here: 119 us
  local copies, waits for them, and re-layouts  35.5 us (29%)
  starting transfers between devices  31.7 us (26%)
  other arithmetic  21.7 us (18%)
  matrix products  16.8 us (14%)
  blocking collectives  10 us (8%)
  between operations  1.78 us (1%)
    dot_general x16, matrix products, add_slab(): jnp.dot(values, onehot, precision=lax.Precision.HIGHEST)  15.8 us
    ppermute x4, starting transfers between devices, with_halo(): lax.ppermute(lax.slice_in_dim(block, block.shape[dim] - width, None, axis...  15.1 us
    unnamed x1, blocking collectives  10 us
    concatenate x3, other arithmetic, with_halo(): block = jnp.concatenate([low, block, high], axis=dim)  7.81 us
    all_to_all x1, starting transfers between devices, body(): lax.all_to_all(outgoing_measurements.reshape(block_groups, slot_limit, 3,...  7.21 us
    unnamed x38, local copies, waits for them, and re-layouts  7.17 us
    ppermute x4, starting transfers between devices, with_halo(): lax.ppermute(lax.slice_in_dim(block, 0, width, axis=dim), axis, backward)  5.14 us
    scatter x1, local copies, waits for them, and re-layouts, body(): send_tiles = jnp.zeros((total_slots, depth_width, depth_width), jnp.bfloa...  4.64 us
  transfers between devices with their start and end apart: 10, of which 1 were waited for; matrix products, arithmetic and copies ran while one was open for 31% of the time, Pallas kernels for 0%

commit v1 on v0

v1 whole, which is shorter than its diff:
```python
import functools

import jax
import jax.numpy as jnp
from jax import lax
from jax.experimental import pallas as pl
from jax.experimental.pallas import tpu as pltpu
from jax.sharding import PartitionSpec as P

REG_DEV = 16

time_step = 0.12
nu_floor = 0.1
nu_spread = 0.9
relax_sq = 4.0
sens_scale = 0.03

VMEM = pl.BlockSpec(memory_space=pltpu.VMEM)
SMEM = pl.BlockSpec(memory_space=pltpu.SMEM)
ANY = pl.BlockSpec(memory_space=pl.ANY)
LIMIT = 24 * 1024 * 1024


def call(kernel, outs, ins, operands, scratch=(), flops=1, moved=1, out_specs=None):
    return pl.pallas_call(
        kernel,
        out_shape=outs,
        in_specs=ins,
        out_specs=out_specs if out_specs is not None else jax.tree.map(lambda _: VMEM, outs),
        scratch_shapes=list(scratch),
        compiler_params=pltpu.CompilerParams(vmem_limit_bytes=LIMIT),
        cost_estimate=pl.CostEstimate(flops=flops, bytes_accessed=moved, transcendentals=0),
    )(*operands)


def f32(*shape):
    return jax.ShapeDtypeStruct(shape, jnp.float32)


def bf16(*shape):
    return jax.ShapeDtypeStruct(shape, jnp.bfloat16)


def swap(block, axis, turn):
    count = lax.axis_size(axis)
    pairs = [(i, (i + 1) % count if (i + turn) % 2 == 0 else (i - 1) % count) for i in range(count)]
    return lax.ppermute(block, axis, pairs)


def cross(block, axis, mask):
    return lax.ppermute(block, axis, [(i, i ^ mask) for i in range(lax.axis_size(axis))])


def from_neighbours(index, count, first, second):
    even = index % 2 == 0
    above = jnp.where(even, first, second)
    below = jnp.where(even, second, first)
    above = jnp.where(index == count - 1, jnp.zeros_like(above), above)
    below = jnp.where(index == 0, jnp.zeros_like(below), below)
    return below, above


def pack_edges(packed, plane, m, lane):
    width = lane.shape[1]
    here = (lane == 2 * m) | (lane == (2 * m + width - 1) % width)
    return jnp.where(here, pltpu.roll(plane, 2 * m, 1), packed)


def mix_edges(below, above, lane):
    return jnp.where(lane % 2 == 0, above, pltpu.roll(below, 2, 1))


def edge_of(mixed, m):
    width = mixed.shape[1]
    return pltpu.roll(mixed, (2 * width - (2 * m + 1)) % width, 1)


def viscosity(jumps):
    shear_sq = jumps[0] * jumps[0] + jumps[1] * jumps[1] + jumps[2] * jumps[2]
    root = lax.rsqrt(1.0 + relax_sq * shear_sq)
    return nu_floor + nu_spread * (root * lax.rsqrt(root))


def iotas(rows, width):
    shape = (rows, width)
    return lax.broadcasted_iota(jnp.int32, shape, 0), lax.broadcasted_iota(jnp.int32, shape, 1)


def group_kernel(cap, dest_ref, tiles_ref, meas_ref, send_ref, count_ref, rows_ref, blank_ref, tile_sems, row_sem, blank_sem):
    count_tiles, width, _ = tiles_ref.shape
    groups = send_ref.shape[0]
    slots = groups * cap
    extra = rows_ref.shape[0] // groups

    def clear(b, carry):
        count_ref[b] = 0
        return carry

    lax.fori_loop(0, groups, clear, 0)
    _, tile_lane = iotas(8, count_tiles)

    def tile_copy(t, b, k):
        return pltpu.make_async_copy(
            tiles_ref.at[t], send_ref.at[b, pl.ds(pl.multiple_of(k * width, width), width), :], tile_sems.at[t]
        )

    def send_one(t, slot_of):
        b = dest_ref[t]
        k = count_ref[b]
        count_ref[b] = k + 1
        tile_copy(t, b, k).start()
        return jnp.where(tile_lane == t, b * cap + k, slot_of)

    slot_of = lax.fori_loop(0, count_tiles, send_one, jnp.full((8, count_tiles), -1, jnp.int32), unroll=4)

    def blank_copy(b, k):
        return pltpu.make_async_copy(
            blank_ref, send_ref.at[b, pl.ds(pl.multiple_of(k * width, width), width), :], blank_sem
        )

    if slots > count_tiles:
        blank_ref[...] = jnp.zeros_like(blank_ref)

        def blanks(b, carry):
            def one(k, inner):
                copy = blank_copy(b, k)
                copy.start()
                copy.wait()
                return inner

            return lax.fori_loop(count_ref[b], cap, one, carry)

        lax.fori_loop(0, groups, blanks, 0)

    meas = meas_ref[...].astype(jnp.float32)
    row = lax.broadcasted_iota(jnp.int32, (groups * extra, count_tiles), 0)
    within = row % extra
    row_slot = (row // extra) * cap + within // 3
    used = within < cap * 3
    total = jnp.zeros((groups * extra, width), jnp.float32)
    for c in range(3):
        pick = (row_slot == slot_of[0:1, :]) & used & (within % 3 == c)
        total += jnp.dot(
            pick.astype(jnp.float32).astype(jnp.bfloat16),
            meas[:, c, :].astype(jnp.bfloat16),
            preferred_element_type=jnp.float32,
        )
    rows_ref[...] = total.astype(jnp.bfloat16)
    for b in range(groups):
        pltpu.make_async_copy(
            rows_ref.at[pl.ds(b * extra, extra), :], send_ref.at[b, pl.ds(cap * width, extra), :], row_sem.at[b]
        ).start()

    def finish(t, carry):
        tile_copy(t, 0, 0).wait()
        return carry

    lax.fori_loop(0, count_tiles, finish, 0, unroll=4)
    for b in range(groups):
        pltpu.make_async_copy(
            rows_ref.at[pl.ds(b * extra, extra), :], send_ref.at[b, pl.ds(cap * width, extra), :], row_sem.at[b]
        ).wait()


def faces_kernel(pos_ref, flow_ref, first_ref, second_ref, edges_ref):
    fields, planes, rows, width = flow_ref.shape
    even = pos_ref[0] % 2 == 0
    _, lane = iotas(rows, width)
    for c in range(fields):
        low, high = flow_ref[c, 0], flow_ref[c, planes - 1]
        first_ref[c] = jnp.where(even, high, low)
        second_ref[c] = jnp.where(even, low, high)
    packed = jnp.zeros((rows, width), jnp.float32)
    for c in range(fields):
        for x in range(planes):
            packed = pack_edges(packed, flow_ref[c, x], c * planes + x, lane)
    edges_ref[...] = packed


def forward_kernel(
    sizes, cap, pos_ref, cells_ref, flow_ref, regions_ref, x0_ref, x1_ref, z0_ref, z1_ref,
    next_ref, nux_ref, nuyu_ref, nuyd_ref, nuzu_ref, nuzd_ref, kz_ref, kpack_ref, vpack_ref, values_ref, pick_ref,
    padded_ref, taken_ref,
):
    _, planes, rows, width = flow_ref.shape
    groups, walls = sizes
    extra = values_ref.shape[1]
    row, lane = iotas(rows, width)
    below, above = from_neighbours(pos_ref[1], walls, z0_ref[...], z1_ref[...])
    halo = mix_edges(below, above, lane)
    for c in range(4):
        low, high = from_neighbours(pos_ref[0], groups, x0_ref[c], x1_ref[c])
        padded_ref[c, 0] = low
        padded_ref[c, planes + 1] = high
        padded_ref[c, 1 : planes + 1] = flow_ref[c]
    nux_ref[0] = viscosity([padded_ref[c, 1] - padded_ref[c, 0] for c in range(3)])

    def up_y(value):
        return jnp.where(row == rows - 1, 0.0, pltpu.roll(value, rows - 1, 0))

    def down_y(value):
        return jnp.where(row == 0, 0.0, pltpu.roll(value, 1, 0))

    def plane(x, carry):
        kpack, vpack = carry
        here = [padded_ref[c, x + 1] for c in range(4)]
        over = [padded_ref[c, x + 2] for c in range(4)]
        under = [padded_ref[c, x] for c in range(4)]
        total = [None] * 3
        pressure = [None] * 3

        def add(axis, nu_up, nu_down):
            for c in range(3):
                flux = nu_up * (over[c] - here[c]) - nu_down * (here[c] - under[c])
                total[c] = flux if total[c] is None else total[c] + flux
            pressure[axis] = 0.5 * (over[3] - under[3])

        nu_up = viscosity([over[c] - here[c] for c in range(3)])
        nux_ref[x + 1] = nu_up
        add(0, nu_up, nux_ref[x])
        over = [up_y(here[c]) for c in range(4)]
        under = [down_y(here[c]) for c in range(4)]
        nu_up = viscosity([over[c] - here[c] for c in range(3)])
        nu_down = viscosity([here[c] - under[c] for c in range(3)])
        nuyu_ref[x] = nu_up
        nuyd_ref[x] = nu_down
        add(1, nu_up, nu_down)
        rim = [edge_of(halo, c * planes + x) for c in range(4)]
        over = [jnp.where(lane == width - 1, rim[c], pltpu.roll(here[c], width - 1, 1)) for c in range(4)]
        under = [jnp.where(lane == 0, rim[c], pltpu.roll(here[c], 1, 1)) for c in range(4)]
        nu_up = viscosity([over[c] - here[c] for c in range(3)])
        nu_down = viscosity([here[c] - under[c] for c in range(3)])
        nuzu_ref[x] = nu_up
        nuzd_ref[x] = nu_down
        add(2, nu_up, nu_down)
        edge_nu = time_step * jnp.where(lane == width - 1, nu_up, jnp.where(lane == 0, nu_down, 0.0))
        kz_ref[x] = edge_nu
        kpack = pack_edges(kpack, edge_nu, x, lane)
        for c in range(3):
            value = here[c] + time_step * (total[c] - pressure[c])
            next_ref[c, x] = value
            vpack = pack_edges(vpack, value, c * planes + x, lane)
        vpack = pack_edges(vpack, regions_ref[x].astype(jnp.float32), 3 * planes + x, lane)
        return kpack, vpack

    blank = jnp.zeros((rows, width), jnp.float32)
    kpack, vpack = lax.fori_loop(0, planes, plane, (blank, blank))
    kpack_ref[...] = kpack
    vpack_ref[...] = vpack

    taken_ref[...] = jnp.zeros_like(taken_ref)
    slot_rows = groups * extra
    _, slot_lane = iotas(8, slot_rows)

    def slot(s, cell_of):
        b = s // cap
        first = b * extra + (s - b * cap) * 3
        cell = cells_ref[s]
        for c in range(3):
            taken_ref[pl.ds(first + c, 1), :] = next_ref[c, cell // rows, pl.ds(cell % rows, 1), :]
        return jnp.where((slot_lane >= first) & (slot_lane < first + 3), cell, cell_of)

    cell_of = lax.fori_loop(0, groups * cap, slot, jnp.full((8, slot_rows), -1, jnp.int32), unroll=4)
    values_ref[...] = taken_ref[...].astype(jnp.bfloat16).reshape(values_ref.shape)
    lines, slot_lane = iotas(planes * rows, slot_rows)
    hit = lines == cell_of[0:1, :]
    part = (slot_lane % extra) % 3
    for c in range(3):
        pick_ref[c] = (hit & (part == c)).astype(jnp.float32).astype(jnp.bfloat16)


def forcing_kernel(cap, pos_ref, recv_ref, values_ref, pick_ref, forcing_ref, first_ref, second_ref, high_ref, low_ref):
    groups, extra, width = values_ref.shape
    _, planes, rows, _ = forcing_ref.shape
    depth = cap * width
    row, lane = iotas(extra, depth)
    own = row // 3 == lane // width
    for b in range(groups):
        weights = recv_ref[b, pl.ds(0, depth), :]
        predicted = lax.dot_general(
            values_ref[b], weights, (((1,), (1,)), ((), ())), preferred_element_type=jnp.float32
        )
        seen = recv_ref[b, pl.ds(depth, extra), :].astype(jnp.float32)
        misfit = jnp.where(own, predicted - jnp.concatenate([seen] * cap, axis=1), 0.0).astype(jnp.bfloat16)
        contrib = jnp.dot(misfit, weights, preferred_element_type=jnp.float32)
        high = contrib.astype(jnp.bfloat16)
        high_ref[pl.ds(b * extra, extra), :] = high
        low_ref[pl.ds(b * extra, extra), :] = (contrib - high.astype(jnp.float32)).astype(jnp.bfloat16)
    even = pos_ref[0] % 2 == 0
    for c in range(3):
        total = jnp.dot(pick_ref[c], high_ref[...], preferred_element_type=jnp.float32)
        total += jnp.dot(pick_ref[c], low_ref[...], preferred_element_type=jnp.float32)
        forcing_ref[c] = total.reshape(planes, rows, width)
        low, high = total[:rows], total[(planes - 1) * rows :]
        first_ref[c] = jnp.where(even, high, low)
        second_ref[c] = jnp.where(even, low, high)


def region_sums(product_ref, region_ref, sums_ref, plus_ref=None):
    count = sums_ref.shape[0]
    rows, width = product_ref.shape
    step = 32

    def group(g, carry):
        sums = [jnp.zeros((8, width), jnp.float32)] * 8
        for r in range(0, rows, step):
            values = product_ref[r : r + step, :]
            ids = region_ref[r : r + step, :] - g * 8
            for i in range(8):
                chosen = jnp.where(ids == i, values, 0.0)
                for s in range(0, step, 8):
                    sums[i] = sums[i] + chosen[s : s + 8]
        block = jnp.concatenate([jnp.sum(part, axis=0, keepdims=True) for part in sums], axis=0)
        at = pl.ds(pl.multiple_of(g * 8, 8), 8)
        sums_ref[at, :] = block if plus_ref is None else block + plus_ref[at, :]
        return carry

    lax.fori_loop(0, count // 8, group, 0)


def inner_kernel(
    walls, pos_ref, forcing_ref, next_ref, nux_ref, nuyu_ref, nuyd_ref, nuzu_ref, nuzd_ref, kpack_ref, regions_ref, v0_ref, v1_ref,
    adjoint_ref, fpack_ref, sums_ref, product_ref, ids_ref,
):
    _, planes, rows, width = forcing_ref.shape
    row, lane = iotas(rows, width)

    def plane(x, fpack):
        nus = (nux_ref[x + 1], nux_ref[x], nuyu_ref[x], nuyd_ref[x], nuzu_ref[x], nuzd_ref[x])
        next_up, next_down = jnp.minimum(x + 1, planes - 1), jnp.maximum(x - 1, 0)
        at_top, at_bottom = x == planes - 1, x == 0
        product = None
        for c in range(3):
            here = forcing_ref[c, x]
            over = jnp.where(at_top, 0.0, forcing_ref[c, next_up])
            under = jnp.where(at_bottom, 0.0, forcing_ref[c, next_down])
            total = nus[0] * (over - here) - nus[1] * (here - under)
            over = jnp.where(row == rows - 1, 0.0, pltpu.roll(here, rows - 1, 0))
            under = jnp.where(row == 0, 0.0, pltpu.roll(here, 1, 0))
            total += nus[2] * (over - here) - nus[3] * (here - under)
            over = jnp.where(lane == width - 1, 0.0, pltpu.roll(here, width - 1, 1))
            under = jnp.where(lane == 0, 0.0, pltpu.roll(here, 1, 1))
            total += nus[4] * (over - here) - nus[5] * (here - under)
            value = here + time_step * total
            adjoint_ref[c, x] = value
            part = value * next_ref[c, x]
            product = part if product is None else product + part
            fpack = pack_edges(fpack, here, c * planes + x, lane)
        at = pl.ds(pl.multiple_of(x * rows, rows), rows)
        product_ref[at, :] = product
        ids_ref[at, :] = regions_ref[x]
        return fpack

    fpack = lax.fori_loop(0, planes, plane, jnp.zeros((rows, width), jnp.float32))
    fpack_ref[...] = fpack
    below, above = from_neighbours(pos_ref[1], walls, v0_ref[...], v1_ref[...])
    mixed = mix_edges(below, above, lane)
    reach = pltpu.roll(fpack, 1, 1) * mixed
    reach = reach + pltpu.roll(reach, width - 2 * planes, 1) + pltpu.roll(reach, width - 4 * planes, 1)
    reach = jnp.where(lane < 2 * planes, reach * pltpu.roll(kpack_ref[...], 1, 1), 0.0)
    product_ref[pl.ds(planes * rows, rows), :] = reach
    ids_ref[pl.ds(planes * rows, rows), :] = pltpu.roll(mixed, (width - 6 * planes) % width, 1).astype(jnp.int32)
    region_sums(product_ref, ids_ref, sums_ref)


def edge_kernel(
    sizes, masks, pos_ref, x0_ref, x1_ref, nux_ref, next_ref, regions_ref, sums_ref, fpack_ref, *refs
):
    groups, walls = sizes
    outs, (product_ref, ids_ref, total_ref) = refs[:-3], refs[-3:]
    _, planes, rows, width = next_ref.shape
    low, high = 0.0, 0.0
    for c in range(3):
        below, above = from_neighbours(pos_ref[0], groups, x0_ref[c], x1_ref[c])
        low += below * next_ref[c, 0]
        high += above * next_ref[c, planes - 1]
    product_ref[:rows, :] = time_step * nux_ref[0] * low
    product_ref[rows:, :] = time_step * nux_ref[planes] * high
    ids_ref[:rows, :] = regions_ref[0]
    ids_ref[rows:, :] = regions_ref[planes - 1]
    region_sums(product_ref, ids_ref, total_ref, sums_ref)
    per = total_ref.shape[0] // walls
    for mask, out_ref in zip((0,) + masks, outs):
        target = pos_ref[1] ^ mask
        out_ref[:per, :] = total_ref[pl.ds(pl.multiple_of(target * per, per), per), :]
        if out_ref.shape[0] > per:
            out_ref[per:, :] = fpack_ref[...]


def final_kernel(sizes, pos_ref, inner_ref, x0_ref, x1_ref, nux_ref, kz_ref, own_ref, *refs):
    groups, walls = sizes
    arrived, adjoint_ref, sens_ref = refs[:-2], refs[-2], refs[-1]
    _, planes, rows, width = inner_ref.shape
    per = own_ref.shape[0]
    _, lane = iotas(rows, width)
    me = pos_ref[1]
    total = own_ref[...]
    below = jnp.zeros((rows, width), jnp.float32)
    above = jnp.zeros((rows, width), jnp.float32)
    for mask, ref in zip(range(1, walls), arrived):
        total = total + ref[:per, :]
        if ref.shape[0] > per:
            edges = ref[per:, :]
            above = jnp.where((me ^ mask) == me + 1, edges, above)
            below = jnp.where((me ^ mask) == me - 1, edges, below)
    sens_ref[...] = sens_scale * lax.dot_general(
        jnp.ones((8, width), jnp.float32), total, (((1,), (1,)), ((), ())),
        precision=lax.Precision.HIGHEST, preferred_element_type=jnp.float32,
    )[:1]
    mixed = mix_edges(below, above, lane)

    def plane(x, carry):
        edge_nu = kz_ref[x]
        for c in range(3):
            adjoint_ref[c, x] = inner_ref[c, x] + edge_nu * edge_of(mixed, c * planes + x)
        return carry

    lax.fori_loop(0, planes, plane, 0, unroll=4)
    for c in range(3):
        low, high = from_neighbours(pos_ref[0], groups, x0_ref[c], x1_ref[c])
        adjoint_ref[c, 0] += time_step * nux_ref[0] * low
        adjoint_ref[c, planes - 1] += time_step * nux_ref[planes] * high


def body(flow_state, regions, obs_tiles, measured, tile_dest, cell_list):
    groups, walls = lax.axis_size("fluid"), lax.axis_size("wall")
    sizes = (groups, walls)
    _, planes, rows, width = flow_state.shape
    count_tiles = obs_tiles.shape[2]
    cap = cell_list.shape[3]
    extra = -(-cap * 3 // 16) * 16
    reg_count = REG_DEV * walls
    cells = groups * cap
    grid = planes * rows * width
    pos = jnp.stack([lax.axis_index("fluid"), lax.axis_index("wall")]).astype(jnp.int32)

    send = call(
        functools.partial(group_kernel, cap),
        bf16(groups, cap * width + extra, width),
        [SMEM, ANY, VMEM],
        (tile_dest[0, 0], obs_tiles[0, 0], measured[0, 0]),
        (
            pltpu.SMEM((groups,), jnp.int32),
            pltpu.VMEM((groups * extra, width), jnp.bfloat16),
            pltpu.VMEM((width, width), jnp.bfloat16),
            pltpu.SemaphoreType.DMA((count_tiles,)),
            pltpu.SemaphoreType.DMA((groups,)),
            pltpu.SemaphoreType.DMA,
        ),
        moved=4 * count_tiles * width * width,
        out_specs=ANY,
    )
    recv = lax.all_to_all(send, "fluid", split_axis=0, concat_axis=0, tiled=True)

    xs0, xs1, zs = call(
        faces_kernel,
        (f32(4, rows, width), f32(4, rows, width), f32(rows, width)),
        [SMEM, VMEM],
        (pos, flow_state),
        moved=16 * grid,
    )
    x0, x1 = swap(xs0, "fluid", 0), swap(xs1, "fluid", 1)
    z0, z1 = swap(zs, "wall", 0), swap(zs, "wall", 1)
    velocity_next, nux, nuyu, nuyd, nuzu, nuzd, kz, kpack, vpack, values, pick = call(
        functools.partial(forward_kernel, sizes, cap),
        (f32(3, planes, rows, width), f32(planes + 1, rows, width))
        + (f32(planes, rows, width),) * 5
        + (f32(rows, width),) * 2
        + (bf16(groups, extra, width), bf16(3, planes * rows, groups * extra)),
        [SMEM, SMEM] + [VMEM] * 6,
        (pos, cell_list[0, 0].reshape(cells), flow_state, regions, x0, x1, z0, z1),
        (pltpu.VMEM((4, planes + 2, rows, width), jnp.float32), pltpu.VMEM((groups * extra, width), jnp.float32)),
        flops=200 * grid,
        moved=60 * grid,
    )
    v0, v1 = swap(vpack, "wall", 0), swap(vpack, "wall", 1)

    forcing, fs0, fs1 = call(
        functools.partial(forcing_kernel, cap),
        (f32(3, planes, rows, width), f32(3, rows, width), f32(3, rows, width)),
        [SMEM] + [VMEM] * 3,
        (pos, recv, values, pick),
        (pltpu.VMEM((groups * extra, width), jnp.bfloat16),) * 2,
        flops=4 * cells * 16 * width * width,
        moved=2 * cells * width * width + 12 * grid,
    )
    f0, f1 = swap(fs0, "fluid", 0), swap(fs1, "fluid", 1)
    inner, fpack, sums = call(
        functools.partial(inner_kernel, walls),
        (f32(3, planes, rows, width), f32(rows, width), f32(reg_count, width)),
        [SMEM] + [VMEM] * 11,
        (pos, forcing, velocity_next, nux, nuyu, nuyd, nuzu, nuzd, kpack, regions, v0, v1),
        (pltpu.VMEM(((planes + 1) * rows, width), jnp.float32), pltpu.VMEM(((planes + 1) * rows, width), jnp.int32)),
        flops=300 * grid,
        moved=60 * grid,
    )
    masks = tuple(range(1, walls))
    heights = [REG_DEV] + [REG_DEV + (rows if mask & (mask + 1) == 0 else 0) for mask in masks]
    own, *parts = call(
        functools.partial(edge_kernel, sizes, masks),
        tuple(f32(height, width) for height in heights),
        [SMEM] + [VMEM] * 7,
        (pos, f0, f1, nux, velocity_next, regions, sums, fpack),
        (
            pltpu.VMEM((2 * rows, width), jnp.float32),
            pltpu.VMEM((2 * rows, width), jnp.int32),
            pltpu.VMEM((reg_count, width), jnp.float32),
        ),
        flops=20 * grid,
        moved=4 * grid,
    )
    arrived = [cross(part, "wall", mask) for part, mask in zip(parts, masks)]
    adjoint, sens = call(
        functools.partial(final_kernel, sizes),
        (f32(3, planes, rows, width), f32(1, REG_DEV)),
        [SMEM] + [VMEM] * (6 + len(arrived)),
        (pos, inner, f0, f1, nux, kz, own, *arrived),
        flops=10 * grid,
        moved=24 * grid,
    )
    return velocity_next, adjoint, sens.reshape(REG_DEV)


def solution(mesh):
    in_specs = (
        P(None, "fluid", None, "wall"),
        P("fluid", None, "wall"),
        P("fluid", "wall", None, None, None),
        P("fluid", "wall", None, None, None),
        P("fluid", "wall", None),
        P("fluid", "wall", None, None),
    )
    out_specs = (
        P(None, "fluid", None, "wall"),
        P(None, "fluid", None, "wall"),
        P(("fluid", "wall")),
    )
    return jax.shard_map(body, mesh=mesh, in_specs=in_specs, out_specs=out_specs, check_vma=False)
```

time: 121 us -> 62.6 us (0.52); the launches traced: 119 us -> 62.2 us
  local copies, waits for them, and re-layouts: 35.5 us -> 8.12 us
  other arithmetic: 21.7 us -> 0.08 us
  Pallas kernels: 0 us -> 17.7 us
  matrix products: 16.8 us -> 0 us
  waiting for transfers between devices: 0.77 us -> 15.5 us
  starting transfers between devices: 31.7 us -> 19.9 us
  blocking collectives: 10 us -> 0 us
    pallas_call x0 -> x7, Pallas kernels: none -> 17.7 us  [call(): pl.pallas_call(kernel, out_shape=outs, in_specs=ins, out_specs=out_specs...]
    dot_general x17 -> x0, matrix products: 16.8 us -> none  [the longest x16 15.8 us: add_slab(): jnp.dot(values, onehot, precision=lax.Precision.HIGHEST)]
    ppermute x8 -> x11, waiting for transfers between devices: 0.02 us -> 15.5 us  [the longest x8 12.6 us: swap(): return lax.ppermute(block, axis, pairs)]
    unnamed x1 -> x0, blocking collectives: 10 us -> none
    concatenate x3 -> x0, other arithmetic: 7.81 us -> none  [with_halo(): block = jnp.concatenate([low, block, high], axis=dim)]
    scatter x2 -> x0, local copies, waits for them, and re-layouts: 6.12 us -> none  [the longest x1 4.64 us: body(): send_tiles = jnp.zeros((total_slots, depth_width, depth_width), jnp.bfloa...]
    all_to_all x2 -> x1, starting transfers between devices: 11.4 us -> 5.31 us  [body(): lax.all_to_all(send, 'fluid', split_axis=0, concat_axis=0, tiled=True)]
    ppermute x8 -> x11, starting transfers between devices: 20.3 us -> 14.6 us  [the longest x8 11.1 us: swap(): return lax.ppermute(block, axis, pairs)]
  transfers between devices with their start and end apart: 10 -> 12, of which waited for: 1 -> 6; matrix products, arithmetic and copies ran while one was open for 31% -> 0% of each run, Pallas kernels for 0% -> 17%
where the time goes in v1:
time: 62.6 us; the launch traced here: 62.2 us
  starting transfers between devices  19.9 us (32%)
  Pallas kernels  17.7 us (28%)
  waiting for transfers between devices  15.5 us (25%)
  local copies, waits for them, and re-layouts  8.12 us (13%)
  between operations  0.77 us (1%)
    pallas_call x7, Pallas kernels, call(): pl.pallas_call(kernel, out_shape=outs, in_specs=ins, out_specs=out_specs...  17.7 us
    ppermute x8, waiting for transfers between devices, swap(): return lax.ppermute(block, axis, pairs)  12.6 us
    ppermute x8, starting transfers between devices, swap(): return lax.ppermute(block, axis, pairs)  11.1 us
    unnamed x34, local copies, waits for them, and re-layouts  8.04 us
    all_to_all x1, starting transfers between devices, body(): lax.all_to_all(send, 'fluid', split_axis=0, concat_axis=0, tiled=True)  5.31 us
    ppermute x3, starting transfers between devices, cross(): lax.ppermute(block, axis, [(i, i ^ mask) for i in range(lax.axis_size(axi...  3.55 us
    ppermute x3, waiting for transfers between devices, cross(): lax.ppermute(block, axis, [(i, i ^ mask) for i in range(lax.axis_size(axi...  2.95 us
  transfers between devices with their start and end apart: 12, of which 6 were waited for; matrix products, arithmetic and copies ran while one was open for 0% of the time, Pallas kernels for 17%

profile of v1, /device:TPU:0, one launch (start us, length us, event | category | flops | bytes accessed | tf_op | source)
XLA Modules:
  0.0 62.2 jit_solution(17571741840797167030)
XLA Ops:
  0.6 0.8 %copy.14 = bf16[1,1,32,3,128]{4,3,2,1,0:T(4,128)(2,1)S(1)} copy(bf16[1,1,32,3,128]{4,2,3,1,0:T(8,128)(2,1)} %param.9) | data formatting | bytes 49152 | tf_op args[3]
  1.4 1.2 %copy-done.3 = bf16[1,1,32,128,128]{4,3,2,1,0:T(8,128)(2,1)S(1)} copy-done((bf16[1,1,32,128,128]{4,3,2,1,0:T(8,128)(2,1)S(1)}, bf16[1,1,32,128,128]{4,3,2,1,0:T(8,128)(2,1)}, u32[]{:S(2)}) %copy-start.3) | copy-done | bytes 1048600
  3.3 2.0 %shard_map.87 = bf16[8,528,128]{2,1,0:T(8,128)(2,1)} custom-call(s32[32]{0:T(128)S(1)} %bitcast.12, bf16[32,128,128]{2,1,0:T(8,128)(2,1)S(1)} %bitcast.10, bf16[32,3,128]{2,1,0:T(4,128)(2,1)S(1)} %bitcast.11), custom_call_target="tpu_custom_call" | custom-call | flops 1 | bytes 2097152 | tf_op jit(solution)/shard_map/pallas_call | solution.py:25
  5.3 5.3 %all-to-all-start = ((bf16[8,528,128]{2,1,0:T(8,128)(2,1)}), bf16[8,528,128]{2,1,0:T(8,128)(2,1)S(1)}, u32[]{:S(2)}, u32[]{:S(2)}) async-start(bf16[8,528,128]{2,1,0:T(8,128)(2,1)} %shard_map.87), calls=%async_computation | async-start | bytes 2162688 | tf_op jit(solution)/shard_map/all_to_all | solution.py:453
  10.7 0.9 %shard_map.85 = (f32[4,32,128]{2,1,0:T(8,128)S(1)}, f32[4,32,128]{2,1,0:T(8,128)S(1)}, f32[32,128]{1,0:T(8,128)S(1)}) custom-call(s32[2]{0:T(128)S(1)} %pad_add_fusion.pos_ref, f32[4,16,32,128]{3,2,1,0:T(8,128)S(1)} %copy-done), custom_call_target="tpu_custom_call" | custom-call | flops 1 | bytes 1048576 | tf_op jit(solution)/shard_map/pallas_call | solution.py:25
  12.2 2.5 %collective-permute-start.1 = (f32[4,32,128]{2,1,0:T(8,128)S(1)}, f32[4,32,128]{2,1,0:T(8,128)S(1)}, u32[]{:S(2)}, u32[]{:S(2)}) collective-permute-start(f32[4,32,128]{2,1,0:T(8,128)S(1)} %get-tuple-element.30), channel_id=1, source_target_pairs={{0,28},{4,8},{8,4},{12,16},{16,12},{20,24},{24,20},{28,0},{1,29},{... | collective-permute-start | bytes 196616 | tf_op jit(solution)/shard_map/ppermute | solution.py:47
  14.7 3.6 %collective-permute-start.3 = (f32[32,128]{1,0:T(8,128)S(1)}, f32[32,128]{1,0:T(8,128)S(1)}, u32[]{:S(2)}, u32[]{:S(2)}) collective-permute-start(f32[32,128]{1,0:T(8,128)S(1)} %get-tuple-element.31), channel_id=1, source_target_pairs={{0,3},{1,2},{2,1},{3,0},{4,7},{5,6},{6,5},{7,4},{8,11},{9,10},{10,... | collective-permute-start | bytes 49160 | tf_op jit(solution)/shard_map/ppermute | solution.py:47
  18.5 1.8 %collective-permute-done.3.z1_ref = f32[32,128]{1,0:T(8,128)S(1)} collective-permute-done((f32[32,128]{1,0:T(8,128)S(1)}, f32[32,128]{1,0:T(8,128)S(1)}, u32[]{:S(2)}, u32[]{:S(2)}) %collective-permute-start.3) | collective-permute-done | bytes 16416 | tf_op jit(solution)/shard_map/ppermute | solution.py:47
  20.2 1.8 %collective-permute-done.2.z0_ref = f32[32,128]{1,0:T(8,128)S(1)} collective-permute-done((f32[32,128]{1,0:T(8,128)S(1)}, f32[32,128]{1,0:T(8,128)S(1)}, u32[]{:S(2)}, u32[]{:S(2)}) %collective-permute-start.2) | collective-permute-done | bytes 16416 | tf_op jit(solution)/shard_map/ppermute | solution.py:47
  22.0 5.3 %collective-permute-done.1.x1_ref = f32[4,32,128]{2,1,0:T(8,128)S(1)} collective-permute-done((f32[4,32,128]{2,1,0:T(8,128)S(1)}, f32[4,32,128]{2,1,0:T(8,128)S(1)}, u32[]{:S(2)}, u32[]{:S(2)}) %collective-permute-start.1) | collective-permute-done | bytes 65568 | tf_op jit(solution)/shard_map/ppermute | solution.py:47
  27.3 5.4 %shard_map.86 = (f32[3,16,32,128]{3,2,1,0:T(8,128)}, f32[17,32,128]{2,1,0:T(8,128)S(1)}, f32[16,32,128]{2,1,0:T(8,128)S(1)}, f32[16,32,128]{2,1,0:T(8,128)S(1)},...) custom-call(s32[2]{0:T(128)S(1)} %pad_add_fusion.pos_ref, ...), custom_call_target="tpu_custom_call" | custom-call | flops 13107200 | bytes 3932160 | tf_op jit(solution)/shard_map/pallas_call | solution.py:25
  34.8 0.7 %copy-done.10 = f32[16,32,128]{2,1,0:T(8,128)} copy-done((f32[16,32,128]{2,1,0:T(8,128)}, f32[16,32,128]{2,1,0:T(8,128)S(1)}, u32[]{:S(2)}) %copy-start.10) | copy-done | bytes 262168
  36.2 2.2 %shard_map.88 = (f32[3,16,32,128]{3,2,1,0:T(8,128)S(1)}, f32[3,32,128]{2,1,0:T(8,128)S(1)}, f32[3,32,128]{2,1,0:T(8,128)S(1)}) custom-call(s32[2]{0:T(128)S(1)} %pad_add_fusion.pos_ref, bf16[8,528,128]{2,1,0:T(8,128)(2,1)S(1)} %all-to-all-done.recv_ref, bf16[8,16,128]{2,1,0:T(8,128)(2,1)S(1)} %get-tuple-element.33.values_ref, ...), custom_call_target="tpu_custom_call" | custom-call | flops 33554432 | bytes 1835008 | tf_op jit(solution)/shard_map/pallas_call | solution.py:25
  39.2 3.6 %collective-permute-start.5 = (f32[32,128]{1,0:T(8,128)S(1)}, f32[32,128]{1,0:T(8,128)S(1)}, u32[]{:S(2)}, u32[]{:S(2)}) collective-permute-start(f32[32,128]{1,0:T(8,128)S(1)} %copy-done.14), channel_id=1, source_target_pairs={{0,3},{1,2},{2,1},{3,0},{4,7},{5,6},{6,5},{7,4},{8,11},{9,10},{10,... | collective-permute-start | bytes 49160 | tf_op jit(solution)/shard_map/ppermute | solution.py:47
  42.8 1.9 %collective-permute-done.5.v1_ref = f32[32,128]{1,0:T(8,128)S(1)} collective-permute-done((f32[32,128]{1,0:T(8,128)S(1)}, f32[32,128]{1,0:T(8,128)S(1)}, u32[]{:S(2)}, u32[]{:S(2)}) %collective-permute-start.5) | collective-permute-done | bytes 16416 | tf_op jit(solution)/shard_map/ppermute | solution.py:47
  44.7 1.8 %collective-permute-done.4.v0_ref = f32[32,128]{1,0:T(8,128)S(1)} collective-permute-done((f32[32,128]{1,0:T(8,128)S(1)}, f32[32,128]{1,0:T(8,128)S(1)}, u32[]{:S(2)}, u32[]{:S(2)}) %collective-permute-start.4) | collective-permute-done | bytes 16416 | tf_op jit(solution)/shard_map/ppermute | solution.py:47
  46.5 0.9 %copy-done.9 = f32[16,32,128]{2,1,0:T(8,128)S(1)} copy-done((f32[16,32,128]{2,1,0:T(8,128)S(1)}, f32[16,32,128]{2,1,0:T(8,128)}, u32[]{:S(2)}) %copy-start.9) | copy-done | bytes 262168
  47.5 0.9 %copy-done.11 = f32[16,32,128]{2,1,0:T(8,128)S(1)} copy-done((f32[16,32,128]{2,1,0:T(8,128)S(1)}, f32[16,32,128]{2,1,0:T(8,128)}, u32[]{:S(2)}) %copy-start.11) | copy-done | bytes 262168
  48.4 4.3 %shard_map.89 = (f32[3,16,32,128]{3,2,1,0:T(8,128)S(1)}, f32[32,128]{1,0:T(8,128)S(1)}, f32[64,128]{1,0:T(8,128)S(1)}) custom-call(s32[2]{0:T(128)S(1)} %pad_add_fusion.pos_ref, f32[3,16,32,128]{3,2,1,0:T(8,128)S(1)} %get-tuple-element.35.forcing_ref, f32[3,16,32,128]{3,2,1,0:T(8,128)S(1)} %copy-done.1, f32[17,32,128]{2,1,0:T(8,128)S(1)} %get-tuple-element.36.nux_ref, ...), custom_call_target="tpu_custom_call" | custom-call | flops 19660800 | bytes 3932160 | tf_op jit(solution)/shard_map/pallas_call | solution.py:25
  52.7 0.9 %shard_map.90 = (f32[16,128]{1,0:T(8,128)S(1)}, f32[48,128]{1,0:T(8,128)S(1)}, f32[16,128]{1,0:T(8,128)S(1)}, f32[48,128]{1,0:T(8,128)S(1)}) custom-call(s32[2]{0:T(128)S(1)} %pad_add_fusion.pos_ref, f32[3,32,128]{2,1,0:T(8,128)S(1)} %collective-permute-done.6.x0_ref, f32[3,32,128]{2,1,0:T(8,128)S(1)} %collective-permute-done.7.x1_ref, ...), custom_call_target="tpu_custom_call" | custom-call | flops 1310720 | bytes 262144 | tf_op jit(solution)/shard_map/pallas_call | solution.py:25
  53.9 1.7 %collective-permute-start.10 = (f32[48,128]{1,0:T(8,128)S(1)}, f32[48,128]{1,0:T(8,128)S(1)}, u32[]{:S(2)}, u32[]{:S(2)}) collective-permute-start(f32[48,128]{1,0:T(8,128)S(1)} %get-tuple-element.52), channel_id=1, source_target_pairs={{0,3},{1,2},{2,1},{3,0},{4,7},{5,6},{6,5},{7,4},{8,11},{9,10},{10,... | collective-permute-start | bytes 73736 | tf_op jit(solution)/shard_map/ppermute | solution.py:51
  55.6 1.6 %collective-permute-start.9 = (f32[16,128]{1,0:T(8,128)S(1)}, f32[16,128]{1,0:T(8,128)S(1)}, u32[]{:S(2)}, u32[]{:S(2)}) collective-permute-start(f32[16,128]{1,0:T(8,128)S(1)} %get-tuple-element.51), channel_id=1, source_target_pairs={{0,2},{1,3},{2,0},{3,1},{4,6},{5,7},{6,4},{7,5},{8,10},{9,11},{10,... | collective-permute-start | bytes 24584 | tf_op jit(solution)/shard_map/ppermute | solution.py:51
  57.2 2.9 %collective-permute-done.9.refs_1_ = f32[16,128]{1,0:T(8,128)S(1)} collective-permute-done((f32[16,128]{1,0:T(8,128)S(1)}, f32[16,128]{1,0:T(8,128)S(1)}, u32[]{:S(2)}, u32[]{:S(2)}) %collective-permute-start.9) | collective-permute-done | bytes 8224 | tf_op jit(solution)/shard_map/ppermute | solution.py:51
  60.2 2.1 %shard_map.91 = (f32[3,16,32,128]{3,2,1,0:T(8,128)}, f32[1,16]{1,0:T(1,128)}) custom-call(s32[2]{0:T(128)S(1)} %pad_add_fusion.pos_ref, f32[3,16,32,128]{3,2,1,0:T(8,128)S(1)} %get-tuple-element.43.inner_ref, f32[3,32,128]{2,1,0:T(8,128)S(1)} %collective-permute-done.6.x0_ref, f32[3,32,128]{2,1,0:T(8,128)S(1)} %collective-permute-done.7.x1_ref, ...), custom_call_target="tpu_custom_call" | custom-call | flops 655360 | bytes 1572864 | tf_op jit(solution)/shard_map/pallas_call | solution.py:25
  (43 shorter events, 5.2 us)
Async XLA Ops:
  1.4 1.2 %copy-start.3 = (bf16[1,1,32,128,128]{4,3,2,1,0:T(8,128)(2,1)S(1)}, bf16[1,1,32,128,128]{4,3,2,1,0:T(8,128)(2,1)}, u32[]{:S(2)}) copy-start(bf16[1,1,32,128,128]{4,3,2,1,0:T(8,128)(2,1)} %param.8) | copy-start | bytes 3145732
  5.3 5.4 %copy-start = (f32[4,16,32,128]{3,2,1,0:T(8,128)S(1)}, f32[4,16,32,128]{3,2,1,0:T(8,128)}, u32[]{:S(2)}) copy-start(f32[4,16,32,128]{3,2,1,0:T(8,128)} %flow_ref.3) | copy-start | bytes 3145732
  5.3 13.0 %copy-start.15 = (s32[1,1,8,4]{2,3,1,0:T(4,128)S(1)}, s32[1,1,8,4]{2,3,1,0:T(4,128)}, u32[]{:S(2)}) copy-start(s32[1,1,8,4]{2,3,1,0:T(4,128)} %param.11) | copy-start | bytes 388
  5.3 30.8 %all-to-all-start = ((bf16[8,528,128]{2,1,0:T(8,128)(2,1)}), bf16[8,528,128]{2,1,0:T(8,128)(2,1)S(1)}, u32[]{:S(2)}, u32[]{:S(2)}) async-start(bf16[8,528,128]{2,1,0:T(8,128)(2,1)} %shard_map.87), calls=%async_computation | async-start | bytes 2162688 | tf_op jit(solution)/shard_map/all_to_all | solution.py:453
  10.6 16.7 %copy-start.2 = (s32[16,32,128]{2,1,0:T(8,128)S(1)}, s32[16,32,128]{2,1,0:T(8,128)}, u32[]{:S(2)}) copy-start(s32[16,32,128]{2,1,0:T(8,128)} %regions_ref.5) | copy-start | bytes 786436
  11.6 10.4 %collective-permute-start = (f32[4,32,128]{2,1,0:T(8,128)S(1)}, f32[4,32,128]{2,1,0:T(8,128)S(1)}, u32[]{:S(2)}, u32[]{:S(2)}) collective-permute-start(f32[4,32,128]{2,1,0:T(8,128)S(1)} %get-tuple-element.29), channel_id=1, source_target_pairs={{0,4},{4,0},{8,12},{12,8},{16,20},{20,16},{24,28},{28,24},{1,5},{5... | collective-permute-start | bytes 196616 | tf_op jit(solution)/shard_map/ppermute | solution.py:47
  12.2 15.2 %collective-permute-start.1 = (f32[4,32,128]{2,1,0:T(8,128)S(1)}, f32[4,32,128]{2,1,0:T(8,128)S(1)}, u32[]{:S(2)}, u32[]{:S(2)}) collective-permute-start(f32[4,32,128]{2,1,0:T(8,128)S(1)} %get-tuple-element.30), channel_id=1, source_target_pairs={{0,28},{4,8},{8,4},{12,16},{16,12},{20,24},{24,20},{28,0},{1,29},{... | collective-permute-start | bytes 196616 | tf_op jit(solution)/shard_map/ppermute | solution.py:47
  14.7 5.5 %collective-permute-start.3 = (f32[32,128]{1,0:T(8,128)S(1)}, f32[32,128]{1,0:T(8,128)S(1)}, u32[]{:S(2)}, u32[]{:S(2)}) collective-permute-start(f32[32,128]{1,0:T(8,128)S(1)} %get-tuple-element.31), channel_id=1, source_target_pairs={{0,3},{1,2},{2,1},{3,0},{4,7},{5,6},{6,5},{7,4},{8,11},{9,10},{10,... | collective-permute-start | bytes 49160 | tf_op jit(solution)/shard_map/ppermute | solution.py:47
  18.3 3.7 %collective-permute-start.2 = (f32[32,128]{1,0:T(8,128)S(1)}, f32[32,128]{1,0:T(8,128)S(1)}, u32[]{:S(2)}, u32[]{:S(2)}) collective-permute-start(f32[32,128]{1,0:T(8,128)S(1)} %get-tuple-element.31), channel_id=1, source_target_pairs={{0,1},{1,0},{2,3},{3,2},{4,5},{5,4},{6,7},{7,6},{8,9},{9,8},{10,11... | collective-permute-start | bytes 49160 | tf_op jit(solution)/shard_map/ppermute | solution.py:47
  34.1 0.7 %copy-start.8 = (f32[16,32,128]{2,1,0:T(8,128)}, f32[16,32,128]{2,1,0:T(8,128)S(1)}, u32[]{:S(2)}) copy-start(f32[16,32,128]{2,1,0:T(8,128)S(1)} %get-tuple-element.39.nuzu_ref) | copy-start | bytes 786436
  34.8 0.7 %copy-start.10 = (f32[16,32,128]{2,1,0:T(8,128)}, f32[16,32,128]{2,1,0:T(8,128)S(1)}, u32[]{:S(2)}) copy-start(f32[16,32,128]{2,1,0:T(8,128)S(1)} %get-tuple-element.40.nuzd_ref) | copy-start | bytes 786436
  36.1 10.4 %copy-start.1 = (f32[3,16,32,128]{3,2,1,0:T(8,128)S(1)}, f32[3,16,32,128]{3,2,1,0:T(8,128)}, u32[]{:S(2)}) copy-start(f32[3,16,32,128]{3,2,1,0:T(8,128)} %get-tuple-element.26.next_ref) | copy-start | bytes 2359300
  36.2 3.0 %copy-start.14 = (f32[32,128]{1,0:T(8,128)S(1)}, f32[32,128]{1,0:T(8,128)}, u32[]{:S(2)}) copy-start(f32[32,128]{1,0:T(8,128)} %copy-done.13) | copy-start | bytes 49156
  36.2 10.4 %copy-start.5 = (f32[16,32,128]{2,1,0:T(8,128)S(1)}, f32[16,32,128]{2,1,0:T(8,128)}, u32[]{:S(2)}) copy-start(f32[16,32,128]{2,1,0:T(8,128)} %copy-done.4) | copy-start | bytes 786436
  36.2 10.4 %copy-start.7 = (f32[16,32,128]{2,1,0:T(8,128)S(1)}, f32[16,32,128]{2,1,0:T(8,128)}, u32[]{:S(2)}) copy-start(f32[16,32,128]{2,1,0:T(8,128)} %copy-done.6) | copy-start | bytes 786436
  38.4 14.3 %collective-permute-start.6 = (f32[3,32,128]{2,1,0:T(8,128)S(1)}, f32[3,32,128]{2,1,0:T(8,128)S(1)}, u32[]{:S(2)}, u32[]{:S(2)}) collective-permute-start(f32[3,32,128]{2,1,0:T(8,128)S(1)} %get-tuple-element.44), channel_id=1, source_target_pairs={{0,4},{4,0},{8,12},{12,8},{16,20},{20,16},{24,28},{28,24},{1,5},{5... | collective-permute-start | bytes 147464 | tf_op jit(solution)/shard_map/ppermute | solution.py:47
  38.5 14.3 %collective-permute-start.7 = (f32[3,32,128]{2,1,0:T(8,128)S(1)}, f32[3,32,128]{2,1,0:T(8,128)S(1)}, u32[]{:S(2)}, u32[]{:S(2)}) collective-permute-start(f32[3,32,128]{2,1,0:T(8,128)S(1)} %get-tuple-element.45), channel_id=1, source_target_pairs={{0,28},{4,8},{8,4},{12,16},{16,12},{20,24},{24,20},{28,0},{1,29},{... | collective-permute-start | bytes 147464 | tf_op jit(solution)/shard_map/ppermute | solution.py:47
  39.2 5.5 %collective-permute-start.5 = (f32[32,128]{1,0:T(8,128)S(1)}, f32[32,128]{1,0:T(8,128)S(1)}, u32[]{:S(2)}, u32[]{:S(2)}) collective-permute-start(f32[32,128]{1,0:T(8,128)S(1)} %copy-done.14), channel_id=1, source_target_pairs={{0,3},{1,2},{2,1},{3,0},{4,7},{5,6},{6,5},{7,4},{8,11},{9,10},{10,... | collective-permute-start | bytes 49160 | tf_op jit(solution)/shard_map/ppermute | solution.py:47
  42.8 3.7 %collective-permute-start.4 = (f32[32,128]{1,0:T(8,128)S(1)}, f32[32,128]{1,0:T(8,128)S(1)}, u32[]{:S(2)}, u32[]{:S(2)}) collective-permute-start(f32[32,128]{1,0:T(8,128)S(1)} %copy-done.14), channel_id=1, source_target_pairs={{0,1},{1,0},{2,3},{3,2},{4,5},{5,4},{6,7},{7,6},{8,9},{9,8},{10,11... | collective-permute-start | bytes 49160 | tf_op jit(solution)/shard_map/ppermute | solution.py:47
  46.5 1.0 %copy-start.9 = (f32[16,32,128]{2,1,0:T(8,128)S(1)}, f32[16,32,128]{2,1,0:T(8,128)}, u32[]{:S(2)}) copy-start(f32[16,32,128]{2,1,0:T(8,128)} %copy-done.8) | copy-start | bytes 786436
  47.5 0.9 %copy-start.11 = (f32[16,32,128]{2,1,0:T(8,128)S(1)}, f32[16,32,128]{2,1,0:T(8,128)}, u32[]{:S(2)}) copy-start(f32[16,32,128]{2,1,0:T(8,128)} %copy-done.10) | copy-start | bytes 786436
  53.6 6.5 %collective-permute-start.8 = (f32[48,128]{1,0:T(8,128)S(1)}, f32[48,128]{1,0:T(8,128)S(1)}, u32[]{:S(2)}, u32[]{:S(2)}) collective-permute-start(f32[48,128]{1,0:T(8,128)S(1)} %get-tuple-element.50), channel_id=1, source_target_pairs={{0,1},{1,0},{2,3},{3,2},{4,5},{5,4},{6,7},{7,6},{8,9},{9,8},{10,11... | collective-permute-start | bytes 73736 | tf_op jit(solution)/shard_map/ppermute | solution.py:51
  53.9 6.3 %collective-permute-start.10 = (f32[48,128]{1,0:T(8,128)S(1)}, f32[48,128]{1,0:T(8,128)S(1)}, u32[]{:S(2)}, u32[]{:S(2)}) collective-permute-start(f32[48,128]{1,0:T(8,128)S(1)} %get-tuple-element.52), channel_id=1, source_target_pairs={{0,3},{1,2},{2,1},{3,0},{4,7},{5,6},{6,5},{7,4},{8,11},{9,10},{10,... | collective-permute-start | bytes 73736 | tf_op jit(solution)/shard_map/ppermute | solution.py:51
  55.6 4.5 %collective-permute-start.9 = (f32[16,128]{1,0:T(8,128)S(1)}, f32[16,128]{1,0:T(8,128)S(1)}, u32[]{:S(2)}, u32[]{:S(2)}) collective-permute-start(f32[16,128]{1,0:T(8,128)S(1)} %get-tuple-element.51), channel_id=1, source_target_pairs={{0,2},{1,3},{2,0},{3,1},{4,6},{5,7},{6,4},{7,5},{8,10},{9,11},{10,... | collective-permute-start | bytes 24584 | tf_op jit(solution)/shard_map/ppermute | solution.py:51
  (4 other events, 2.7 us)

commit v2 on v1

v2 whole, which is shorter than its diff:
```python
import functools

import jax
import jax.numpy as jnp
from jax import lax
from jax.experimental import pallas as pl
from jax.experimental.pallas import tpu as pltpu
from jax.sharding import PartitionSpec as P

REG_DEV = 16

time_step = 0.12
nu_floor = 0.1
nu_spread = 0.9
relax_sq = 4.0
sens_scale = 0.03

VMEM = pl.BlockSpec(memory_space=pltpu.VMEM)
SMEM = pl.BlockSpec(memory_space=pltpu.SMEM)
ANY = pl.BlockSpec(memory_space=pl.ANY)
HBM = pl.BlockSpec(memory_space=pltpu.HBM)
LIMIT = 24 * 1024 * 1024


def call(kernel, outs, ins, operands, scratch=(), flops=1, moved=1, out_specs=None, limit=LIMIT):
    return pl.pallas_call(
        kernel,
        out_shape=outs,
        in_specs=ins,
        out_specs=out_specs if out_specs is not None else jax.tree.map(lambda _: VMEM, outs),
        scratch_shapes=list(scratch),
        compiler_params=pltpu.CompilerParams(vmem_limit_bytes=limit),
        cost_estimate=pl.CostEstimate(flops=flops, bytes_accessed=moved, transcendentals=0),
    )(*operands)


def f32(*shape):
    return jax.ShapeDtypeStruct(shape, jnp.float32)


def bf16(*shape):
    return jax.ShapeDtypeStruct(shape, jnp.bfloat16)


def swap(block, axis, turn):
    count = lax.axis_size(axis)
    pairs = [(i, (i + 1) % count if (i + turn) % 2 == 0 else (i - 1) % count) for i in range(count)]
    return lax.ppermute(block, axis, pairs)


def cross(block, axis, mask):
    return lax.ppermute(block, axis, [(i, i ^ mask) for i in range(lax.axis_size(axis))])


def from_neighbours(index, count, first, second):
    even = index % 2 == 0
    above = jnp.where(even, first, second)
    below = jnp.where(even, second, first)
    above = jnp.where(index == count - 1, jnp.zeros_like(above), above)
    below = jnp.where(index == 0, jnp.zeros_like(below), below)
    return below, above


def pack_edges(packed, plane, m, lane):
    width = lane.shape[1]
    here = (lane == 2 * m) | (lane == (2 * m + width - 1) % width)
    return jnp.where(here, pltpu.roll(plane, 2 * m, 1), packed)


def mix_edges(below, above, lane):
    return jnp.where(lane % 2 == 0, above, pltpu.roll(below, 2, 1))


def edge_of(mixed, m):
    width = mixed.shape[1]
    return pltpu.roll(mixed, (2 * width - (2 * m + 1)) % width, 1)


def viscosity(jumps):
    shear_sq = jumps[0] * jumps[0] + jumps[1] * jumps[1] + jumps[2] * jumps[2]
    root = lax.rsqrt(1.0 + relax_sq * shear_sq)
    return nu_floor + nu_spread * (root * lax.rsqrt(root))


def iotas(rows, width):
    shape = (rows, width)
    return lax.broadcasted_iota(jnp.int32, shape, 0), lax.broadcasted_iota(jnp.int32, shape, 1)


def faces_kernel(flow_ref, first_ref, second_ref, sems):
    last = flow_ref.shape[1] - 1
    odd = lax.axis_index("fluid") % 2
    copies = [
        pltpu.make_async_copy(flow_ref.at[:, plane], out_ref, sems.at[i])
        for i, (plane, out_ref) in enumerate(((last - last * odd, first_ref), (last * odd, second_ref)))
    ]
    for copy in copies:
        copy.start()
    for copy in copies:
        copy.wait()


def edges_kernel(groups, flow_ref, regions_ref, x0_ref, x1_ref, edges_ref):
    fields, planes, rows, width = flow_ref.shape
    _, lane = iotas(rows, width)
    outer = jnp.zeros((rows, width), jnp.float32)
    second, beside = outer, outer
    for c in range(fields):
        for x in range(planes):
            m, plane = c * planes + x, flow_ref[c, x]
            outer = pack_edges(outer, plane, m, lane)
            second = jnp.where(lane == 2 * m, pltpu.roll(plane, (2 * m - 1) % width, 1), second)
            second = jnp.where(lane == (2 * m - 1) % width, pltpu.roll(plane, (2 * m + 1) % width, 1), second)
        for side, plane in enumerate(from_neighbours(lax.axis_index("fluid"), groups, x0_ref[c], x1_ref[c])):
            beside = pack_edges(beside, plane, 2 * c + side, lane)
    for x in range(planes):
        beside = pack_edges(beside, regions_ref[x].astype(jnp.float32), 2 * fields + x, lane)
    edges_ref[0], edges_ref[1], edges_ref[2] = outer, second, beside


def outside_edges(walls, planes, halo, second, beside, inside, rim_nu):
    rows, width = halo.shape
    row, lane = iotas(rows, width)
    x, field = (lane // 2) % planes, (lane // 2) // planes

    def spread(nu):
        nu = jnp.where(field == 0, nu, 0.0)
        return nu + pltpu.roll(nu, 2 * planes, 1) + pltpu.roll(nu, 4 * planes, 1)

    def nu_of(jump):
        return spread(viscosity([jump] + [pltpu.roll(jump, width - 2 * c * planes, 1) for c in (1, 2)]))

    over_x, under_x = pltpu.roll(halo, width - 2, 1), pltpu.roll(halo, 2, 1)
    for c in range(4):
        low = pltpu.roll(beside, (2 * c * planes - 4 * c) % width, 1)
        high = pltpu.roll(beside, (2 * (c * planes + planes - 1) - 4 * c - 2) % width, 1)
        under_x = jnp.where((x == 0) & (field == c), low, under_x)
        over_x = jnp.where((x == planes - 1) & (field == c), high, over_x)
    over_y = jnp.where(row == rows - 1, 0.0, pltpu.roll(halo, rows - 1, 0))
    under_y = jnp.where(row == 0, 0.0, pltpu.roll(halo, 1, 0))
    total = spread(rim_nu) * (inside - halo)
    for other in (over_x, under_x, over_y, under_y, second):
        total += nu_of(other - halo) * (other - halo)
    above = lane % 2 == 0
    gradient_x = pltpu.roll(0.5 * (over_x - under_x), width - 6 * planes, 1)
    gradient_y = pltpu.roll(0.5 * (over_y - under_y), width - 4 * planes, 1)
    gradient_z = pltpu.roll(0.5 * jnp.where(above, second - inside, inside - second), width - 2 * planes, 1)
    gradient = jnp.where(field == 0, gradient_x, jnp.where(field == 1, gradient_y, gradient_z))
    value = halo + time_step * (total - gradient)
    value = jnp.where(field == 3, pltpu.roll(beside, 6 * planes - 16, 1), value)
    me = lax.axis_index("wall")
    exists = jnp.where(above, jnp.where(me < walls - 1, 1, 0), jnp.where(me > 0, 1, 0)) == 1
    return jnp.where(exists & (field < 4), value, 0.0)


def group_kernel(
    cap, dest_ref, tiles_ref, meas_ref, after_ref, send_ref,
    list_ref, held_ref, seen_ref, count_ref, rows_ref, blank_ref, list_sem, seen_sem, in_sems, out_sems, row_sems, blank_sem,
):
    count_tiles, width, _ = tiles_ref.shape
    groups = send_ref.shape[0]
    slots = groups * cap
    extra = rows_ref.shape[0] // groups
    listed = pltpu.make_async_copy(dest_ref, list_ref, list_sem)
    listed.start()

    piece = count_tiles // in_sems.shape[0]

    def load(p):
        part = pl.ds(p * piece, piece)
        return pltpu.make_async_copy(tiles_ref.at[part], held_ref.at[part], in_sems.at[p])

    for p in range(in_sems.shape[0]):
        load(p).start()
    seen = pltpu.make_async_copy(meas_ref, seen_ref, seen_sem)
    seen.start()

    def clear(b, carry):
        count_ref[b] = 0
        return carry

    lax.fori_loop(0, groups, clear, 0)
    _, tile_lane = iotas(8, count_tiles)
    listed.wait()

    def store(t, b, k):
        return pltpu.make_async_copy(
            held_ref.at[t], send_ref.at[b, pl.ds(pl.multiple_of(k * width, width), width), :], out_sems.at[t]
        )

    def send_one(t, slot_of):
        b = list_ref[t]
        k = count_ref[b]
        count_ref[b] = k + 1
        store(t, b, k).start()
        return jnp.where(tile_lane == t, b * cap + k, slot_of)

    slot_of = jnp.full((8, count_tiles), -1, jnp.int32)
    for p in range(in_sems.shape[0]):
        load(p).wait()
        slot_of = lax.fori_loop(p * piece, (p + 1) * piece, send_one, slot_of, unroll=True)

    if slots > count_tiles:
        blank_ref[...] = jnp.zeros_like(blank_ref)

        def blanks(b, carry):
            def one(k, inner):
                copy = pltpu.make_async_copy(
                    blank_ref, send_ref.at[b, pl.ds(pl.multiple_of(k * width, width), width), :], blank_sem
                )
                copy.start()
                copy.wait()
                return inner

            return lax.fori_loop(count_ref[b], cap, one, carry)

        lax.fori_loop(0, groups, blanks, 0)

    seen.wait()
    row = lax.broadcasted_iota(jnp.int32, (groups * extra, count_tiles), 0)
    within = row % extra
    row_slot = (row // extra) * cap + within // 3
    used = within < cap * 3
    total = jnp.zeros((groups * extra, width), jnp.float32)
    for c in range(3):
        pick = (row_slot == slot_of[0:1, :]) & used & (within % 3 == c)
        total += jnp.dot(
            pick.astype(jnp.float32).astype(jnp.bfloat16), seen_ref[c], preferred_element_type=jnp.float32
        )
    rows_ref[...] = total.astype(jnp.bfloat16)

    def row_copy(b):
        return pltpu.make_async_copy(
            rows_ref.at[pl.ds(b * extra, extra), :], send_ref.at[b, pl.ds(cap * width, extra), :], row_sems.at[b]
        )

    for b in range(groups):
        row_copy(b).start()

    def finish(t, carry):
        store(t, 0, 0).wait()
        return carry

    lax.fori_loop(0, count_tiles, finish, 0, unroll=4)
    for b in range(groups):
        row_copy(b).wait()


def forward_kernel(
    sizes, cap, cells_ref, flow_ref, x0_ref, x1_ref, z0_ref, z1_ref, edges_ref,
    next_ref, nux_ref, nuy_ref, nuz_ref, nuy0_ref, rim_ref, outside_ref, values_ref, pick_ref,
    padded_ref, taken_ref,
):
    _, planes, rows, width = flow_ref.shape
    groups, walls = sizes
    extra = values_ref.shape[1]
    row, lane = iotas(rows, width)
    halo, second, beside = (
        mix_edges(*from_neighbours(lax.axis_index("wall"), walls, z0_ref[i], z1_ref[i]), lane) for i in range(3)
    )
    inside = pltpu.roll(edges_ref[0], 1, 1)
    jump = halo - inside
    rim_nu = viscosity([jump] + [pltpu.roll(jump, width - 2 * c * planes, 1) for c in (1, 2)])
    rim_nu = jnp.where(lane < 2 * planes, rim_nu, 0.0)
    rim_ref[...] = rim_nu
    outside_ref[...] = outside_edges(walls, planes, halo, second, beside, inside, rim_nu)
    for c in range(4):
        low, high = from_neighbours(lax.axis_index("fluid"), groups, x0_ref[c], x1_ref[c])
        padded_ref[c, 0] = low
        padded_ref[c, planes + 1] = high
        padded_ref[c, 1 : planes + 1] = flow_ref[c]
    nux_ref[0] = viscosity([padded_ref[c, 1] - padded_ref[c, 0] for c in range(3)])

    def plane(x, carry):
        here = [padded_ref[c, x + 1] for c in range(4)]
        over = [padded_ref[c, x + 2] for c in range(4)]
        under = [padded_ref[c, x] for c in range(4)]
        total = [None] * 3
        pressure = [None] * 3

        def add(axis, nu_up, nu_down):
            for c in range(3):
                flux = nu_up * (over[c] - here[c]) - nu_down * (here[c] - under[c])
                total[c] = flux if total[c] is None else total[c] + flux
            pressure[axis] = 0.5 * (over[3] - under[3])

        nu_up = viscosity([over[c] - here[c] for c in range(3)])
        nux_ref[x + 1] = nu_up
        add(0, nu_up, nux_ref[x])
        over = [jnp.where(row == rows - 1, 0.0, pltpu.roll(here[c], rows - 1, 0)) for c in range(4)]
        under = [jnp.where(row == 0, 0.0, pltpu.roll(here[c], 1, 0)) for c in range(4)]
        nu_up = viscosity([over[c] - here[c] for c in range(3)])
        nu_first = viscosity([here[c][:1] for c in range(3)])
        nuy_ref[x] = nu_up
        nuy0_ref[pl.ds(x, 1), :] = nu_first
        add(1, nu_up, jnp.where(row == 0, nu_first, pltpu.roll(nu_up, 1, 0)))
        rim = [edge_of(halo, c * planes + x) for c in range(4)]
        over = [jnp.where(lane == width - 1, rim[c], pltpu.roll(here[c], width - 1, 1)) for c in range(4)]
        under = [jnp.where(lane == 0, rim[c], pltpu.roll(here[c], 1, 1)) for c in range(4)]
        nu_up = viscosity([over[c] - here[c] for c in range(3)])
        nuz_ref[x] = nu_up
        add(2, nu_up, jnp.where(lane == 0, edge_of(rim_nu, x), pltpu.roll(nu_up, 1, 1)))
        for c in range(3):
            value = here[c] + time_step * (total[c] - pressure[c])
            next_ref[c, x] = value
        return carry

    lax.fori_loop(0, planes, plane, 0, unroll=4)

    taken_ref[...] = jnp.zeros_like(taken_ref)
    slot_rows = groups * extra
    _, slot_lane = iotas(8, slot_rows)

    def slot(s, cell_of):
        b = s // cap
        first = b * extra + (s - b * cap) * 3
        cell = cells_ref[s - b * cap, b]
        for c in range(3):
            taken_ref[pl.ds(first + c, 1), :] = next_ref[c, cell // rows, pl.ds(cell % rows, 1), :]
        return jnp.where((slot_lane >= first) & (slot_lane < first + 3), cell, cell_of)

    cell_of = lax.fori_loop(0, groups * cap, slot, jnp.full((8, slot_rows), -1, jnp.int32), unroll=4)
    values_ref[...] = taken_ref[...].astype(jnp.bfloat16).reshape(values_ref.shape)
    lines, slot_lane = iotas(planes * rows, slot_rows)
    hit = lines == cell_of[0:1, :]
    part = (slot_lane % extra) % 3
    for c in range(3):
        pick_ref[c] = (hit & (part == c)).astype(jnp.float32).astype(jnp.bfloat16)


def forcing_kernel(
    cap, recv_ref, values_ref, pick_ref, forcing_ref, first_ref, second_ref, high_ref, low_ref
):
    groups, extra, width = values_ref.shape
    _, planes, rows, _ = forcing_ref.shape
    depth = cap * width
    row, lane = iotas(extra, depth)
    own = row // 3 == lane // width
    for b in range(groups):
        weights = recv_ref[b, pl.ds(0, depth), :]
        predicted = lax.dot_general(
            values_ref[b], weights, (((1,), (1,)), ((), ())), preferred_element_type=jnp.float32
        )
        seen = recv_ref[b, pl.ds(depth, extra), :].astype(jnp.float32)
        misfit = jnp.where(own, predicted - jnp.concatenate([seen] * cap, axis=1), 0.0).astype(jnp.bfloat16)
        contrib = jnp.dot(misfit, weights, preferred_element_type=jnp.float32)
        high = contrib.astype(jnp.bfloat16)
        high_ref[pl.ds(b * extra, extra), :] = high
        low_ref[pl.ds(b * extra, extra), :] = (contrib - high.astype(jnp.float32)).astype(jnp.bfloat16)
    even = lax.axis_index("fluid") % 2 == 0
    for c in range(3):
        total = jnp.dot(pick_ref[c], high_ref[...], preferred_element_type=jnp.float32)
        total += jnp.dot(pick_ref[c], low_ref[...], preferred_element_type=jnp.float32)
        forcing_ref[c] = total.reshape(planes, rows, width)
        low, high = total[:rows], total[(planes - 1) * rows :]
        first_ref[c] = jnp.where(even, high, low)
        second_ref[c] = jnp.where(even, low, high)


def region_sums(product_ref, region_ref, sums_ref, plus_ref=None):
    count = sums_ref.shape[0]
    rows, width = product_ref.shape
    step = 32

    def group(g, carry):
        sums = [jnp.zeros((8, width), jnp.float32)] * 8
        for r in range(0, rows, step):
            values = product_ref[r : r + step, :]
            ids = region_ref[r : r + step, :] - g * 8
            for i in range(8):
                chosen = jnp.where(ids == i, values, 0.0)
                for s in range(0, step, 8):
                    sums[i] = sums[i] + chosen[s : s + 8]
        block = jnp.concatenate([jnp.sum(part, axis=0, keepdims=True) for part in sums], axis=0)
        at = pl.ds(pl.multiple_of(g * 8, 8), 8)
        sums_ref[at, :] = block if plus_ref is None else block + plus_ref[at, :]
        return carry

    lax.fori_loop(0, count // 8, group, 0)


def inner_kernel(
    forcing_ref, next_ref, nux_ref, nuy_ref, nuz_ref, nuy0_ref, rim_ref, regions_ref, outside_ref,
    adjoint_ref, fpack_ref, sums_ref, product_ref, ids_ref,
):
    _, planes, rows, width = forcing_ref.shape
    row, lane = iotas(rows, width)
    rim_nu = rim_ref[...]

    def plane(x, fpack):
        nuy, nuz = nuy_ref[x], nuz_ref[x]
        nuy_down = jnp.where(row == 0, nuy0_ref[pl.ds(x, 1), :], pltpu.roll(nuy, 1, 0))
        nuz_down = jnp.where(lane == 0, edge_of(rim_nu, x), pltpu.roll(nuz, 1, 1))
        nus = (nux_ref[x + 1], nux_ref[x], nuy, nuy_down, nuz, nuz_down)
        next_up, next_down = jnp.minimum(x + 1, planes - 1), jnp.maximum(x - 1, 0)
        at_top, at_bottom = x == planes - 1, x == 0
        product = None
        for c in range(3):
            here = forcing_ref[c, x]
            over = jnp.where(at_top, 0.0, forcing_ref[c, next_up])
            under = jnp.where(at_bottom, 0.0, forcing_ref[c, next_down])
            total = nus[0] * (over - here) - nus[1] * (here - under)
            over = jnp.where(row == rows - 1, 0.0, pltpu.roll(here, rows - 1, 0))
            under = jnp.where(row == 0, 0.0, pltpu.roll(here, 1, 0))
            total += nus[2] * (over - here) - nus[3] * (here - under)
            over = jnp.where(lane == width - 1, 0.0, pltpu.roll(here, width - 1, 1))
            under = jnp.where(lane == 0, 0.0, pltpu.roll(here, 1, 1))
            total += nus[4] * (over - here) - nus[5] * (here - under)
            value = here + time_step * total
            adjoint_ref[c, x] = value
            part = value * next_ref[c, x]
            product = part if product is None else product + part
            fpack = pack_edges(fpack, here, c * planes + x, lane)
        at = pl.ds(pl.multiple_of(x * rows, rows), rows)
        product_ref[at, :] = product
        ids_ref[at, :] = regions_ref[x]
        return fpack

    fpack = lax.fori_loop(0, planes, plane, jnp.zeros((rows, width), jnp.float32), unroll=4)
    fpack_ref[...] = fpack
    mixed = outside_ref[...]
    reach = pltpu.roll(fpack, 1, 1) * mixed
    reach = reach + pltpu.roll(reach, width - 2 * planes, 1) + pltpu.roll(reach, width - 4 * planes, 1)
    reach = time_step * reach * rim_nu
    product_ref[pl.ds(planes * rows, rows), :] = reach
    ids_ref[pl.ds(planes * rows, rows), :] = pltpu.roll(mixed, (width - 6 * planes) % width, 1).astype(jnp.int32)
    region_sums(product_ref, ids_ref, sums_ref)


def edge_kernel(
    sizes, masks, x0_ref, x1_ref, nux_ref, next_ref, regions_ref, sums_ref, fpack_ref, *refs
):
    groups, walls = sizes
    outs, (product_ref, ids_ref, total_ref) = refs[:-3], refs[-3:]
    _, planes, rows, width = next_ref.shape
    low, high = 0.0, 0.0
    for c in range(3):
        below, above = from_neighbours(lax.axis_index("fluid"), groups, x0_ref[c], x1_ref[c])
        low += below * next_ref[c, 0]
        high += above * next_ref[c, planes - 1]
    product_ref[:rows, :] = time_step * nux_ref[0] * low
    product_ref[rows:, :] = time_step * nux_ref[planes] * high
    ids_ref[:rows, :] = regions_ref[0]
    ids_ref[rows:, :] = regions_ref[planes - 1]
    region_sums(product_ref, ids_ref, total_ref, sums_ref)
    per = total_ref.shape[0] // walls
    for mask, out_ref in zip((0,) + masks, outs):
        target = lax.axis_index("wall") ^ mask
        out_ref[:per, :] = total_ref[pl.ds(pl.multiple_of(target * per, per), per), :]
        if out_ref.shape[0] > per:
            out_ref[per:, :] = fpack_ref[...]


def final_kernel(sizes, inner_ref, x0_ref, x1_ref, nux_ref, rim_ref, own_ref, *refs):
    groups, walls = sizes
    arrived, adjoint_ref, sens_ref = refs[:-2], refs[-2], refs[-1]
    _, planes, rows, width = inner_ref.shape
    per = own_ref.shape[0]
    _, lane = iotas(rows, width)
    me = lax.axis_index("wall")
    total = own_ref[...]
    below = jnp.zeros((rows, width), jnp.float32)
    above = jnp.zeros((rows, width), jnp.float32)
    for mask, ref in zip(range(1, walls), arrived):
        total = total + ref[:per, :]
        if ref.shape[0] > per:
            edges = ref[per:, :]
            above = jnp.where((me ^ mask) == me + 1, edges, above)
            below = jnp.where((me ^ mask) == me - 1, edges, below)
    sens_ref[...] = sens_scale * lax.dot_general(
        jnp.ones((8, width), jnp.float32), total, (((1,), (1,)), ((), ())),
        precision=lax.Precision.HIGHEST, preferred_element_type=jnp.float32,
    )[:1]
    mixed = mix_edges(below, above, lane)
    edge_nu = time_step * rim_ref[...]
    edge_nu = edge_nu + pltpu.roll(edge_nu, 2 * planes, 1) + pltpu.roll(edge_nu, 4 * planes, 1)
    edge_flux = mixed * edge_nu
    on_edge = (lane == 0) | (lane == width - 1)

    def plane(x, carry):
        for c in range(3):
            edge = edge_of(edge_flux, c * planes + x)
            adjoint_ref[c, x] = inner_ref[c, x] + jnp.where(on_edge, edge, 0.0)
        return carry

    lax.fori_loop(0, planes, plane, 0, unroll=4)
    for c in range(3):
        low, high = from_neighbours(lax.axis_index("fluid"), groups, x0_ref[c], x1_ref[c])
        adjoint_ref[c, 0] += time_step * nux_ref[0] * low
        adjoint_ref[c, planes - 1] += time_step * nux_ref[planes] * high


def body(flow_state, regions, obs_tiles, measured, tile_dest, cell_list):
    groups, walls = lax.axis_size("fluid"), lax.axis_size("wall")
    sizes = (groups, walls)
    _, planes, rows, width = flow_state.shape
    count_tiles = obs_tiles.shape[2]
    cap = cell_list.shape[3]
    extra = -(-cap * 3 // 16) * 16
    reg_count = REG_DEV * walls
    cells = groups * cap
    grid = planes * rows * width

    xs0, xs1 = call(
        faces_kernel,
        (f32(4, rows, width), f32(4, rows, width)),
        [HBM],
        (flow_state,),
        (pltpu.SemaphoreType.DMA((2,)),),
        limit=60 * 1024 * 1024,
    )
    x0, x1 = swap(xs0, "fluid", 0), swap(xs1, "fluid", 1)
    send = call(
        functools.partial(group_kernel, cap),
        bf16(groups, cap * width + extra, width),
        [HBM, HBM, HBM, ANY],
        (tile_dest[0, 0], obs_tiles[0, 0], jnp.transpose(measured[0, 0], (1, 0, 2)), xs1),
        (
            pltpu.SMEM((count_tiles,), jnp.int32),
            pltpu.VMEM((count_tiles, width, width), jnp.bfloat16),
            pltpu.VMEM((3, count_tiles, width), jnp.bfloat16),
            pltpu.SMEM((groups,), jnp.int32),
            pltpu.VMEM((groups * extra, width), jnp.bfloat16),
            pltpu.VMEM((width, width), jnp.bfloat16),
            pltpu.SemaphoreType.DMA,
            pltpu.SemaphoreType.DMA,
            pltpu.SemaphoreType.DMA((4,)),
            pltpu.SemaphoreType.DMA((count_tiles,)),
            pltpu.SemaphoreType.DMA((groups,)),
            pltpu.SemaphoreType.DMA,
        ),
        moved=4 * count_tiles * width * width,
        out_specs=HBM,
        limit=60 * 1024 * 1024,
    )
    send, x0, x1 = lax.optimization_barrier((send, x0, x1))
    recv = lax.all_to_all(send, "fluid", split_axis=0, concat_axis=0, tiled=True)
    zs = call(
        functools.partial(edges_kernel, groups),
        f32(3, rows, width),
        [VMEM] * 4,
        (flow_state, regions, x0, x1),
        moved=16 * grid,
    )
    z0, z1 = swap(zs, "wall", 0), swap(zs, "wall", 1)
    velocity_next, nux, nuy, nuz, nuy0, rim, outside, values, pick = call(
        functools.partial(forward_kernel, sizes, cap),
        (f32(3, planes, rows, width), f32(planes + 1, rows, width), f32(planes, rows, width), f32(planes, rows, width))
        + (f32(planes, width), f32(rows, width), f32(rows, width))
        + (bf16(groups, extra, width), bf16(3, planes * rows, groups * extra)),
        [SMEM] + [VMEM] * 6,
        (cell_list[0, 0].T, flow_state, x0, x1, z0, z1, zs),
        (pltpu.VMEM((4, planes + 2, rows, width), jnp.float32), pltpu.VMEM((groups * extra, width), jnp.float32)),
        flops=200 * grid,
        moved=60 * grid,
    )

    forcing, fs0, fs1 = call(
        functools.partial(forcing_kernel, cap),
        (f32(3, planes, rows, width), f32(3, rows, width), f32(3, rows, width)),
        [VMEM] * 3,
        (recv, values, pick),
        (pltpu.VMEM((groups * extra, width), jnp.bfloat16),) * 2,
    )
    f0, f1 = swap(fs0, "fluid", 0), swap(fs1, "fluid", 1)
    inner, fpack, sums = call(
        inner_kernel,
        (f32(3, planes, rows, width), f32(rows, width), f32(reg_count, width)),
        [VMEM] * 9,
        (forcing, velocity_next, nux, nuy, nuz, nuy0, rim, regions, outside),
        (pltpu.VMEM(((planes + 1) * rows, width), jnp.float32), pltpu.VMEM(((planes + 1) * rows, width), jnp.int32)),
    )
    masks = tuple(range(1, walls))
    heights = [REG_DEV] + [REG_DEV + (rows if mask & (mask + 1) == 0 else 0) for mask in masks]
    own, *parts = call(
        functools.partial(edge_kernel, sizes, masks),
        tuple(f32(height, width) for height in heights),
        [VMEM] * 7,
        (f0, f1, nux, velocity_next, regions, sums, fpack),
        (
            pltpu.VMEM((2 * rows, width), jnp.float32),
            pltpu.VMEM((2 * rows, width), jnp.int32),
            pltpu.VMEM((reg_count, width), jnp.float32),
        ),
        flops=20 * grid,
        moved=4 * grid,
    )
    arrived = [cross(part, "wall", mask) for part, mask in zip(parts, masks)]
    adjoint, sens = call(
        functools.partial(final_kernel, sizes),
        (f32(3, planes, rows, width), f32(1, REG_DEV)),
        [VMEM] * (6 + len(arrived)),
        (inner, f0, f1, nux, rim, own, *arrived),
        flops=10 * grid,
        moved=24 * grid,
    )
    return velocity_next, adjoint, sens.reshape(REG_DEV)


def solution(mesh):
    in_specs = (
        P(None, "fluid", None, "wall"),
        P("fluid", None, "wall"),
        P("fluid", "wall", None, None, None),
        P("fluid", "wall", None, None, None),
        P("fluid", "wall", None),
        P("fluid", "wall", None, None),
    )
    out_specs = (
        P(None, "fluid", None, "wall"),
        P(None, "fluid", None, "wall"),
        P(("fluid", "wall")),
    )
    return jax.shard_map(body, mesh=mesh, in_specs=in_specs, out_specs=out_specs, check_vma=False)
```

time: 62.6 us -> 45.4 us (0.73)
  local copies, waits for them, and re-layouts: 8.12 us -> 0.73 us
  waiting for transfers between devices: 15.5 us -> 11.3 us
  starting transfers between devices: 19.9 us -> 16.6 us
  Pallas kernels: 17.7 us -> 15.7 us
    ppermute x8 -> x6, waiting for transfers between devices: 12.6 us -> 4.82 us  [swap(): return lax.ppermute(block, axis, pairs)]
    unnamed x34 -> x12, local copies, waits for them, and re-layouts: 8.04 us -> 0.73 us
    ppermute x8 -> x6, starting transfers between devices: 11.1 us -> 8.7 us  [swap(): return lax.ppermute(block, axis, pairs)]
    all_to_all x1, waiting for transfers between devices: 0.01 us -> 2.06 us  [body(): lax.all_to_all(send, 'fluid', split_axis=0, concat_axis=0, tiled=True)]
    pallas_call x7 -> x8, Pallas kernels: 17.7 us -> 15.7 us  [call(): pl.pallas_call(kernel, out_shape=outs, in_specs=ins, out_specs=out_specs...]
    all_to_all x1, starting transfers between devices: 5.31 us -> 3.7 us  [body(): lax.all_to_all(send, 'fluid', split_axis=0, concat_axis=0, tiled=True)]
    ppermute x3, waiting for transfers between devices: 2.95 us -> 4.44 us  [cross(): lax.ppermute(block, axis, [(i, i ^ mask) for i in range(lax.axis_size(axi...]
    ppermute x3, starting transfers between devices: 3.55 us -> 4.23 us  [cross(): lax.ppermute(block, axis, [(i, i ^ mask) for i in range(lax.axis_size(axi...]
  transfers between devices with their start and end apart: 12 -> 10, of which waited for: 6 -> 5; matrix products, arithmetic and copies ran while one was open for 0% -> 0% of each run, Pallas kernels for 17% -> 24%
where the time goes in v2:
time: 45.4 us; the launch traced here: 45.1 us
  starting transfers between devices  16.6 us (37%)
  Pallas kernels  15.7 us (35%)
  waiting for transfers between devices  11.3 us (25%)
  between operations  0.76 us (2%)
  local copies, waits for them, and re-layouts  0.73 us (2%)
    pallas_call x8, Pallas kernels, call(): pl.pallas_call(kernel, out_shape=outs, in_specs=ins, out_specs=out_specs...  15.7 us
    ppermute x6, starting transfers between devices, swap(): return lax.ppermute(block, axis, pairs)  8.7 us
    ppermute x6, waiting for transfers between devices, swap(): return lax.ppermute(block, axis, pairs)  4.82 us
    ppermute x3, waiting for transfers between devices, cross(): lax.ppermute(block, axis, [(i, i ^ mask) for i in range(lax.axis_size(axi...  4.44 us
    ppermute x3, starting transfers between devices, cross(): lax.ppermute(block, axis, [(i, i ^ mask) for i in range(lax.axis_size(axi...  4.23 us
    all_to_all x1, starting transfers between devices, body(): lax.all_to_all(send, 'fluid', split_axis=0, concat_axis=0, tiled=True)  3.7 us
    all_to_all x1, waiting for transfers between devices, body(): lax.all_to_all(send, 'fluid', split_axis=0, concat_axis=0, tiled=True)  2.06 us
  transfers between devices with their start and end apart: 10, of which 5 were waited for; matrix products, arithmetic and copies ran while one was open for 0% of the time, Pallas kernels for 24%

profile of v2, /device:TPU:0, one launch (start us, length us, event | category | flops | bytes accessed | tf_op | source)
XLA Modules:
  0.0 45.1 jit_solution(70642852516913646)
XLA Ops:
  0.6 1.6 %shard_map.85 = (f32[4,32,128]{2,1,0:T(8,128)}, f32[4,32,128]{2,1,0:T(8,128)}) custom-call(f32[4,16,32,128]{3,2,1,0:T(8,128)} %flow_ref.5), custom_call_target="tpu_custom_call" | custom-call | flops 1 | bytes 1 | tf_op jit(solution)/shard_map/pallas_call | solution.py:26
  2.2 0.5 %collective-permute-start = (f32[4,32,128]{2,1,0:T(8,128)}, f32[4,32,128]{2,1,0:T(8,128)S(1)}, u32[]{:S(2)}, u32[]{:S(2)}) collective-permute-start(f32[4,32,128]{2,1,0:T(8,128)} %get-tuple-element.30), channel_id=1, source_target_pairs={{0,4},{4,0},{8,12},{12,8},{16,20},{20,16},{24,28},{28,24},{1,5},{5... | collective-permute-start | bytes 196616 | tf_op jit(solution)/shard_map/ppermute | solution.py:48
  2.7 3.6 %collective-permute-start.1 = (f32[4,32,128]{2,1,0:T(8,128)}, f32[4,32,128]{2,1,0:T(8,128)S(1)}, u32[]{:S(2)}, u32[]{:S(2)}) collective-permute-start(f32[4,32,128]{2,1,0:T(8,128)} %get-tuple-element.29.after_ref), channel_id=1, source_target_pairs={{0,28},{4,8},{8,4},{12,16},{16,12},{20,24},{24,20},{28,0},{1,29},{... | collective-permute-start | bytes 196616 | tf_op jit(solution)/shard_map/ppermute | solution.py:48
  6.3 2.4 %shard_map.86 = bf16[8,528,128]{2,1,0:T(8,128)(2,1)} custom-call(s32[32]{0:T(128)} %bitcast.12, bf16[32,128,128]{2,1,0:T(8,128)(2,1)} %bitcast.10, bf16[3,32,128]{2,1,0:T(8,128)(2,1)} %bitcast.11, f32[4,32,128]{2,1,0:T(8,128)} %get-tuple-element.29.after_ref), custom_call_target="tpu_custom_call" | custom-call | flops 1 | bytes 2097152 | tf_op jit(solution)/shard_map/pallas_call | solution.py:26
  8.7 0.0 copy-start
  8.8 3.7 %all-to-all-start = ((bf16[8,528,128]{2,1,0:T(8,128)(2,1)}), bf16[8,528,128]{2,1,0:T(8,128)(2,1)S(1)}, u32[]{:S(2)}, u32[]{:S(2)}) async-start(bf16[8,528,128]{2,1,0:T(8,128)(2,1)} %shard_map.86), calls=%async_computation | async-start | bytes 2162688 | tf_op jit(solution)/shard_map/all_to_all | solution.py:537
  12.5 1.1 %shard_map.87.edges_ref = f32[3,32,128]{2,1,0:T(8,128)S(1)} custom-call(f32[4,16,32,128]{3,2,1,0:T(8,128)S(1)} %copy-done, s32[16,32,128]{2,1,0:T(8,128)S(1)} %copy-done.2, f32[4,32,128]{2,1,0:T(8,128)S(1)} %collective-permute-done.x0_ref, f32[4,32,128]{2,1,0:T(8,128)S(1)} %collective-permute-done.1.x1_ref), custom_call_target="tpu_custom_call" | custom-call | flops 1 | bytes 1048576 | tf_op jit(solution)/shard_map/pallas_call | solution.py:26
  13.6 3.7 %collective-permute-start.3 = (f32[3,32,128]{2,1,0:T(8,128)S(1)}, f32[3,32,128]{2,1,0:T(8,128)S(1)}, u32[]{:S(2)}, u32[]{:S(2)}) collective-permute-start(f32[3,32,128]{2,1,0:T(8,128)S(1)} %shard_map.87.edges_ref), channel_id=1, source_target_pairs={{0,3},{1,2},{2,1},{3,0},{4,7},{5,6},{6,5},{7,4},{8,11},{9,10},{10,... | collective-permute-start | bytes 147464 | tf_op jit(solution)/shard_map/ppermute | solution.py:48
  17.3 2.7 %collective-permute-done.3.z1_ref = f32[3,32,128]{2,1,0:T(8,128)S(1)} collective-permute-done((f32[3,32,128]{2,1,0:T(8,128)S(1)}, f32[3,32,128]{2,1,0:T(8,128)S(1)}, u32[]{:S(2)}, u32[]{:S(2)}) %collective-permute-start.3) | collective-permute-done | bytes 49184 | tf_op jit(solution)/shard_map/ppermute | solution.py:48
  20.0 1.3 %collective-permute-done.2.z0_ref = f32[3,32,128]{2,1,0:T(8,128)S(1)} collective-permute-done((f32[3,32,128]{2,1,0:T(8,128)S(1)}, f32[3,32,128]{2,1,0:T(8,128)S(1)}, u32[]{:S(2)}, u32[]{:S(2)}) %collective-permute-start.2) | collective-permute-done | bytes 49184 | tf_op jit(solution)/shard_map/ppermute | solution.py:48
  21.3 4.0 %shard_map.88 = (f32[3,16,32,128]{3,2,1,0:T(8,128)}, f32[17,32,128]{2,1,0:T(8,128)S(1)}, f32[16,32,128]{2,1,0:T(8,128)S(1)}, f32[16,32,128]{2,1,0:T(8,128)S(1)},...) custom-call(s32[4,8]{1,0:T(4,128)S(1)} %bitcast.9, ...), custom_call_target="tpu_custom_call" | custom-call | flops 13107200 | bytes 3932160 | tf_op jit(solution)/shard_map/pallas_call | solution.py:26
  25.4 0.7 %copy-done.3 = f32[16,32,128]{2,1,0:T(8,128)} copy-done((f32[16,32,128]{2,1,0:T(8,128)}, f32[16,32,128]{2,1,0:T(8,128)S(1)}, u32[]{:S(2)}) %copy-start.3) | copy-done | bytes 262168
  26.1 2.1 %all-to-all-done.recv_ref = bf16[8,528,128]{2,1,0:T(8,128)(2,1)S(1)} async-done(((bf16[8,528,128]{2,1,0:T(8,128)(2,1)}), bf16[8,528,128]{2,1,0:T(8,128)(2,1)S(1)}, u32[]{:S(2)}, u32[]{:S(2)}) %all-to-all-start) | async-done | bytes 1081376 | tf_op jit(solution)/shard_map/all_to_all | solution.py:537
  28.2 1.7 %shard_map.89 = (f32[3,16,32,128]{3,2,1,0:T(8,128)S(1)}, f32[3,32,128]{2,1,0:T(8,128)S(1)}, f32[3,32,128]{2,1,0:T(8,128)S(1)}) custom-call(bf16[8,528,128]{2,1,0:T(8,128)(2,1)S(1)} %all-to-all-done.recv_ref, bf16[8,16,128]{2,1,0:T(8,128)(2,1)S(1)} %get-tuple-element.35.values_ref, bf16[3,512,128]{2,1,0:T(8,128)(2,1)S(1)} %get-tuple-element.36.pick_ref), custom_call_target="tpu_custom_call" | custom-call | flops 1 | bytes 1 | tf_op jit(solution)/shard_map/pallas_call | solution.py:26
  29.8 0.1 collective-permute-start.4
  29.9 0.9 %collective-permute-start.5 = (f32[3,32,128]{2,1,0:T(8,128)S(1)}, f32[3,32,128]{2,1,0:T(8,128)S(1)}, u32[]{:S(2)}, u32[]{:S(2)}) collective-permute-start(f32[3,32,128]{2,1,0:T(8,128)S(1)} %get-tuple-element.46), channel_id=1, source_target_pairs={{0,28},{4,8},{8,4},{12,16},{16,12},{20,24},{24,20},{28,0},{1,29},{... | collective-permute-start | bytes 147464 | tf_op jit(solution)/shard_map/ppermute | solution.py:48
  30.8 3.1 %shard_map.90 = (f32[3,16,32,128]{3,2,1,0:T(8,128)S(1)}, f32[32,128]{1,0:T(8,128)S(1)}, f32[64,128]{1,0:T(8,128)S(1)}) custom-call(f32[3,16,32,128]{3,2,1,0:T(8,128)S(1)} %get-tuple-element.37.forcing_ref, f32[3,16,32,128]{3,2,1,0:T(8,128)S(1)} %copy-done.1, f32[17,32,128]{2,1,0:T(8,128)S(1)} %get-tuple-element.38.nux_ref, ...), custom_call_target="tpu_custom_call" | custom-call | flops 1 | bytes 1 | tf_op jit(solution)/shard_map/pallas_call | solution.py:26
  33.9 0.7 %collective-permute-done.5.x1_ref = f32[3,32,128]{2,1,0:T(8,128)S(1)} collective-permute-done((f32[3,32,128]{2,1,0:T(8,128)S(1)}, f32[3,32,128]{2,1,0:T(8,128)S(1)}, u32[]{:S(2)}, u32[]{:S(2)}) %collective-permute-start.5) | collective-permute-done | bytes 49184 | tf_op jit(solution)/shard_map/ppermute | solution.py:48
  34.6 0.3 shard_map.91
  35.0 1.6 %collective-permute-start.6 = (f32[48,128]{1,0:T(8,128)S(1)}, f32[48,128]{1,0:T(8,128)S(1)}, u32[]{:S(2)}, u32[]{:S(2)}) collective-permute-start(f32[48,128]{1,0:T(8,128)S(1)} %get-tuple-element.50), channel_id=1, source_target_pairs={{0,1},{1,0},{2,3},{3,2},{4,5},{5,4},{6,7},{7,6},{8,9},{9,8},{10,11... | collective-permute-start | bytes 73736 | tf_op jit(solution)/shard_map/ppermute | solution.py:52
  36.6 2.5 %collective-permute-start.8 = (f32[48,128]{1,0:T(8,128)S(1)}, f32[48,128]{1,0:T(8,128)S(1)}, u32[]{:S(2)}, u32[]{:S(2)}) collective-permute-start(f32[48,128]{1,0:T(8,128)S(1)} %get-tuple-element.52), channel_id=1, source_target_pairs={{0,3},{1,2},{2,1},{3,0},{4,7},{5,6},{6,5},{7,4},{8,11},{9,10},{10,... | collective-permute-start | bytes 73736 | tf_op jit(solution)/shard_map/ppermute | solution.py:52
  39.1 0.1 collective-permute-start.7
  39.2 4.4 %collective-permute-done.7.refs_1_ = f32[16,128]{1,0:T(8,128)S(1)} collective-permute-done((f32[16,128]{1,0:T(8,128)S(1)}, f32[16,128]{1,0:T(8,128)S(1)}, u32[]{:S(2)}, u32[]{:S(2)}) %collective-permute-start.7) | collective-permute-done | bytes 8224 | tf_op jit(solution)/shard_map/ppermute | solution.py:52
  43.6 1.5 %shard_map.92 = (f32[3,16,32,128]{3,2,1,0:T(8,128)}, f32[1,16]{1,0:T(1,128)}) custom-call(f32[3,16,32,128]{3,2,1,0:T(8,128)S(1)} %get-tuple-element.44.inner_ref, f32[3,32,128]{2,1,0:T(8,128)S(1)} %collective-permute-done.4.x0_ref, f32[3,32,128]{2,1,0:T(8,128)S(1)} %collective-permute-done.5.x1_ref, f32[17,32,128]{2,1,0:T(8,128)S(1)} %get-tuple-element.38.nux_ref, ...), custom_call_target="tpu_custom_call" | custom-call | flops 655360 | bytes 1572864 | tf_op jit(solution)/shard_map/pallas_call | solution.py:26
  (16 shorter events, 0.0 us)
Async XLA Ops:
  2.2 6.5 %collective-permute-start = (f32[4,32,128]{2,1,0:T(8,128)}, f32[4,32,128]{2,1,0:T(8,128)S(1)}, u32[]{:S(2)}, u32[]{:S(2)}) collective-permute-start(f32[4,32,128]{2,1,0:T(8,128)} %get-tuple-element.30), channel_id=1, source_target_pairs={{0,4},{4,0},{8,12},{12,8},{16,20},{20,16},{24,28},{28,24},{1,5},{5... | collective-permute-start | bytes 196616 | tf_op jit(solution)/shard_map/ppermute | solution.py:48
  2.7 6.0 %collective-permute-start.1 = (f32[4,32,128]{2,1,0:T(8,128)}, f32[4,32,128]{2,1,0:T(8,128)S(1)}, u32[]{:S(2)}, u32[]{:S(2)}) collective-permute-start(f32[4,32,128]{2,1,0:T(8,128)} %get-tuple-element.29.after_ref), channel_id=1, source_target_pairs={{0,28},{4,8},{8,4},{12,16},{16,12},{20,24},{24,20},{28,0},{1,29},{... | collective-permute-start | bytes 196616 | tf_op jit(solution)/shard_map/ppermute | solution.py:48
  8.7 3.8 %copy-start = (f32[4,16,32,128]{3,2,1,0:T(8,128)S(1)}, f32[4,16,32,128]{3,2,1,0:T(8,128)}, u32[]{:S(2)}) copy-start(f32[4,16,32,128]{3,2,1,0:T(8,128)} %flow_ref.5) | copy-start | bytes 3145732
  8.7 3.8 %copy-start.2 = (s32[16,32,128]{2,1,0:T(8,128)S(1)}, s32[16,32,128]{2,1,0:T(8,128)}, u32[]{:S(2)}) copy-start(s32[16,32,128]{2,1,0:T(8,128)} %regions_ref.5) | copy-start | bytes 786436
  8.8 19.4 %all-to-all-start = ((bf16[8,528,128]{2,1,0:T(8,128)(2,1)}), bf16[8,528,128]{2,1,0:T(8,128)(2,1)S(1)}, u32[]{:S(2)}, u32[]{:S(2)}) async-start(bf16[8,528,128]{2,1,0:T(8,128)(2,1)} %shard_map.86), calls=%async_computation | async-start | bytes 2162688 | tf_op jit(solution)/shard_map/all_to_all | solution.py:537
  12.5 8.9 %copy-start.5 = (s32[1,1,8,4]{2,3,1,0:T(4,128)S(1)}, s32[1,1,8,4]{2,3,1,0:T(4,128)}, u32[]{:S(2)}) copy-start(s32[1,1,8,4]{2,3,1,0:T(4,128)} %param.11) | copy-start | bytes 388
  13.6 6.4 %collective-permute-start.3 = (f32[3,32,128]{2,1,0:T(8,128)S(1)}, f32[3,32,128]{2,1,0:T(8,128)S(1)}, u32[]{:S(2)}, u32[]{:S(2)}) collective-permute-start(f32[3,32,128]{2,1,0:T(8,128)S(1)} %shard_map.87.edges_ref), channel_id=1, source_target_pairs={{0,3},{1,2},{2,1},{3,0},{4,7},{5,6},{6,5},{7,4},{8,11},{9,10},{10,... | collective-permute-start | bytes 147464 | tf_op jit(solution)/shard_map/ppermute | solution.py:48
  17.3 4.1 %collective-permute-start.2 = (f32[3,32,128]{2,1,0:T(8,128)S(1)}, f32[3,32,128]{2,1,0:T(8,128)S(1)}, u32[]{:S(2)}, u32[]{:S(2)}) collective-permute-start(f32[3,32,128]{2,1,0:T(8,128)S(1)} %shard_map.87.edges_ref), channel_id=1, source_target_pairs={{0,1},{1,0},{2,3},{3,2},{4,5},{5,4},{6,7},{7,6},{8,9},{9,8},{10,11... | collective-permute-start | bytes 147464 | tf_op jit(solution)/shard_map/ppermute | solution.py:48
  25.4 0.7 %copy-start.3 = (f32[16,32,128]{2,1,0:T(8,128)}, f32[16,32,128]{2,1,0:T(8,128)S(1)}, u32[]{:S(2)}) copy-start(f32[16,32,128]{2,1,0:T(8,128)S(1)} %get-tuple-element.40.nuz_ref) | copy-start | bytes 786436
  26.1 4.7 %copy-start.1 = (f32[3,16,32,128]{3,2,1,0:T(8,128)S(1)}, f32[3,16,32,128]{3,2,1,0:T(8,128)}, u32[]{:S(2)}) copy-start(f32[3,16,32,128]{3,2,1,0:T(8,128)} %get-tuple-element.26.next_ref) | copy-start | bytes 2359300
  28.2 2.6 %copy-start.4 = (f32[16,32,128]{2,1,0:T(8,128)S(1)}, f32[16,32,128]{2,1,0:T(8,128)}, u32[]{:S(2)}) copy-start(f32[16,32,128]{2,1,0:T(8,128)} %copy-done.3) | copy-start | bytes 786436
  29.8 4.0 %collective-permute-start.4 = (f32[3,32,128]{2,1,0:T(8,128)S(1)}, f32[3,32,128]{2,1,0:T(8,128)S(1)}, u32[]{:S(2)}, u32[]{:S(2)}) collective-permute-start(f32[3,32,128]{2,1,0:T(8,128)S(1)} %get-tuple-element.45), channel_id=1, source_target_pairs={{0,4},{4,0},{8,12},{12,8},{16,20},{20,16},{24,28},{28,24},{1,5},{5... | collective-permute-start | bytes 147464 | tf_op jit(solution)/shard_map/ppermute | solution.py:48
  29.9 4.7 %collective-permute-start.5 = (f32[3,32,128]{2,1,0:T(8,128)S(1)}, f32[3,32,128]{2,1,0:T(8,128)S(1)}, u32[]{:S(2)}, u32[]{:S(2)}) collective-permute-start(f32[3,32,128]{2,1,0:T(8,128)S(1)} %get-tuple-element.46), channel_id=1, source_target_pairs={{0,28},{4,8},{8,4},{12,16},{16,12},{20,24},{24,20},{28,0},{1,29},{... | collective-permute-start | bytes 147464 | tf_op jit(solution)/shard_map/ppermute | solution.py:48
  35.0 8.7 %collective-permute-start.6 = (f32[48,128]{1,0:T(8,128)S(1)}, f32[48,128]{1,0:T(8,128)S(1)}, u32[]{:S(2)}, u32[]{:S(2)}) collective-permute-start(f32[48,128]{1,0:T(8,128)S(1)} %get-tuple-element.50), channel_id=1, source_target_pairs={{0,1},{1,0},{2,3},{3,2},{4,5},{5,4},{6,7},{7,6},{8,9},{9,8},{10,11... | collective-permute-start | bytes 73736 | tf_op jit(solution)/shard_map/ppermute | solution.py:52
  36.6 7.0 %collective-permute-start.8 = (f32[48,128]{1,0:T(8,128)S(1)}, f32[48,128]{1,0:T(8,128)S(1)}, u32[]{:S(2)}, u32[]{:S(2)}) collective-permute-start(f32[48,128]{1,0:T(8,128)S(1)} %get-tuple-element.52), channel_id=1, source_target_pairs={{0,3},{1,2},{2,1},{3,0},{4,7},{5,6},{6,5},{7,4},{8,11},{9,10},{10,... | collective-permute-start | bytes 73736 | tf_op jit(solution)/shard_map/ppermute | solution.py:52
  39.1 4.5 %collective-permute-start.7 = (f32[16,128]{1,0:T(8,128)S(1)}, f32[16,128]{1,0:T(8,128)S(1)}, u32[]{:S(2)}, u32[]{:S(2)}) collective-permute-start(f32[16,128]{1,0:T(8,128)S(1)} %get-tuple-element.51), channel_id=1, source_target_pairs={{0,2},{1,3},{2,0},{3,1},{4,6},{5,7},{6,4},{7,5},{8,10},{9,11},{10,... | collective-permute-start | bytes 24584 | tf_op jit(solution)/shard_map/ppermute | solution.py:52

commit v3 on v2

--- a/solution.py
+++ b/solution.py
@@ -43,9 +43,20 @@
 
 
 def swap(block, axis, turn):
-    count = lax.axis_size(axis)
-    pairs = [(i, (i + 1) % count if (i + turn) % 2 == 0 else (i - 1) % count) for i in range(count)]
-    return lax.ppermute(block, axis, pairs)
+    groups, walls = lax.axis_size("fluid"), lax.axis_size("wall")
+
+    def partner(f, w):
+        if axis == "fluid":
+            return (f + 1 if (f + turn) % 2 == 0 else f - 1) % groups, w
+        other = w + 1 if (w + turn) % 2 == 0 else w - 1
+        return (f, other) if 0 <= other < walls else (f ^ 1, w)
+
+    pairs = []
+    for f in range(groups):
+        for w in range(walls):
+            to_f, to_w = partner(f, w)
+            pairs.append((f * walls + w, to_f * walls + to_w))
+    return lax.ppermute(block, ("fluid", "wall"), pairs)
 
 
 def cross(block, axis, mask):
@@ -67,8 +78,8 @@
     return jnp.where(here, pltpu.roll(plane, 2 * m, 1), packed)
 
 
-def mix_edges(below, above, lane):
-    return jnp.where(lane % 2 == 0, above, pltpu.roll(below, 2, 1))
+def mix_edges(below, above, lane, shift=2):
+    return jnp.where(lane % 2 == 0, above, pltpu.roll(below, shift, 1))
 
 
 def edge_of(mixed, m):
@@ -91,8 +102,9 @@
     last = flow_ref.shape[1] - 1
     odd = lax.axis_index("fluid") % 2
     copies = [
-        pltpu.make_async_copy(flow_ref.at[:, plane], out_ref, sems.at[i])
+        pltpu.make_async_copy(flow_ref.at[c, plane], out_ref.at[c], sems.at[i, c])
         for i, (plane, out_ref) in enumerate(((last - last * odd, first_ref), (last * odd, second_ref)))
+        for c in range(flow_ref.shape[0])
     ]
     for copy in copies:
         copy.start()
@@ -109,8 +121,8 @@
         for x in range(planes):
             m, plane = c * planes + x, flow_ref[c, x]
             outer = pack_edges(outer, plane, m, lane)
-            second = jnp.where(lane == 2 * m, pltpu.roll(plane, (2 * m - 1) % width, 1), second)
-            second = jnp.where(lane == (2 * m - 1) % width, pltpu.roll(plane, (2 * m + 1) % width, 1), second)
+            here = (lane == 2 * m) | (lane == (2 * m - 3) % width)
+            second = jnp.where(here, pltpu.roll(plane, (2 * m - 1) % width, 1), second)
         for side, plane in enumerate(from_neighbours(lax.axis_index("fluid"), groups, x0_ref[c], x1_ref[c])):
             beside = pack_edges(beside, plane, 2 * c + side, lane)
     for x in range(planes):
@@ -153,17 +165,19 @@
     return jnp.where(exists & (field < 4), value, 0.0)
 
 
-def group_kernel(
-    cap, dest_ref, tiles_ref, meas_ref, after_ref, send_ref,
-    list_ref, held_ref, seen_ref, count_ref, rows_ref, blank_ref, list_sem, seen_sem, in_sems, out_sems, row_sems, blank_sem,
-):
+def group_kernel(cap, dest_ref, tiles_ref, meas_ref, after_ref, *refs):
+    chips = len(refs) - 12
+    sends = refs[:chips]
+    (list_ref, held_ref, seen_ref, count_ref, slot_ref, rows_ref, blank_ref,
+     list_sem, seen_sem, in_sems, out_sems, row_sems) = refs[chips:]
     count_tiles, width, _ = tiles_ref.shape
-    groups = send_ref.shape[0]
+    groups = 2 * chips
     slots = groups * cap
     extra = rows_ref.shape[0] // groups
+    depth = cap * width
+    me = lax.axis_index("fluid")
     listed = pltpu.make_async_copy(dest_ref, list_ref, list_sem)
     listed.start()
-
     piece = count_tiles // in_sems.shape[0]
 
     def load(p):
@@ -177,44 +191,51 @@
 
     def clear(b, carry):
         count_ref[b] = 0
+        for k in range(cap):
+            slot_ref[b * cap + k] = -1
         return carry
 
     lax.fori_loop(0, groups, clear, 0)
+    if slots > count_tiles:
+        blank_ref[...] = jnp.zeros_like(blank_ref)
     _, tile_lane = iotas(8, count_tiles)
     listed.wait()
 
-    def store(t, b, k):
-        return pltpu.make_async_copy(
-            held_ref.at[t], send_ref.at[b, pl.ds(pl.multiple_of(k * width, width), width), :], out_sems.at[t]
-        )
-
-    def send_one(t, slot_of):
+    def place(t, slot_of):
         b = list_ref[t]
         k = count_ref[b]
         count_ref[b] = k + 1
-        store(t, b, k).start()
+        slot_ref[b * cap + k] = t
         return jnp.where(tile_lane == t, b * cap + k, slot_of)
 
-    slot_of = jnp.full((8, count_tiles), -1, jnp.int32)
+    slot_of = lax.fori_loop(
+        0, count_tiles, place, jnp.full((8, count_tiles), -1, jnp.int32), unroll=True
+    )
     for p in range(in_sems.shape[0]):
         load(p).wait()
-        slot_of = lax.fori_loop(p * piece, (p + 1) * piece, send_one, slot_of, unroll=True)
-
-    if slots > count_tiles:
-        blank_ref[...] = jnp.zeros_like(blank_ref)
-
-        def blanks(b, carry):
-            def one(k, inner):
-                copy = pltpu.make_async_copy(
-                    blank_ref, send_ref.at[b, pl.ds(pl.multiple_of(k * width, width), width), :], blank_sem
-                )
-                copy.start()
-                copy.wait()
-                return inner
-
-            return lax.fori_loop(count_ref[b], cap, one, carry)
-
-        lax.fori_loop(0, groups, blanks, 0)
+
+    def each(act):
+        for m in list(range(1, chips)) + [0]:
+            for j in range(2):
+                b = me ^ (2 * m + j)
+                for k in range(cap):
+                    t = slot_ref[b * cap + k]
+                    at = sends[m].at[j, pl.ds(k * width, width), :]
+                    sem = out_sems.at[(2 * m + j) * cap + k]
+                    if slots > count_tiles:
+
+                        @pl.when(t >= 0)
+                        def _():
+                            act(pltpu.make_async_copy(held_ref.at[t], at, sem))
+
+                        @pl.when(t < 0)
+                        def _():
+                            act(pltpu.make_async_copy(blank_ref, at, sem))
+
+                    else:
+                        act(pltpu.make_async_copy(held_ref.at[t], at, sem))
+
+    each(lambda copy: copy.start())
 
     seen.wait()
     row = lax.broadcasted_iota(jnp.int32, (groups * extra, count_tiles), 0)
@@ -229,41 +250,40 @@
         )
     rows_ref[...] = total.astype(jnp.bfloat16)
 
-    def row_copy(b):
+    def row_copy(m, j):
+        b = me ^ (2 * m + j)
         return pltpu.make_async_copy(
-            rows_ref.at[pl.ds(b * extra, extra), :], send_ref.at[b, pl.ds(cap * width, extra), :], row_sems.at[b]
+            rows_ref.at[pl.ds(pl.multiple_of(b * extra, extra), extra), :],
+            sends[m].at[j, pl.ds(depth, extra), :],
+            row_sems.at[2 * m + j],
         )
 
-    for b in range(groups):
-        row_copy(b).start()
-
-    def finish(t, carry):
-        store(t, 0, 0).wait()
-        return carry
-
-    lax.fori_loop(0, count_tiles, finish, 0, unroll=4)
-    for b in range(groups):
-        row_copy(b).wait()
+    for m in range(chips):
+        for j in range(2):
+            row_copy(m, j).start()
+    each(lambda copy: copy.wait())
+    for m in range(chips):
+        for j in range(2):
+            row_copy(m, j).wait()
 
 
 def forward_kernel(
     sizes, cap, cells_ref, flow_ref, x0_ref, x1_ref, z0_ref, z1_ref, edges_ref,
-    next_ref, nux_ref, nuy_ref, nuz_ref, nuy0_ref, rim_ref, outside_ref, values_ref, pick_ref,
-    padded_ref, taken_ref,
+    out_ref, next_ref, nux_ref, nuy_ref, nuz_ref, nuy0_ref, rim_ref, mine_ref, lent_ref, cells_of_ref,
+    list_ref, padded_ref, taken_ref, list_sem, out_sems,
 ):
     _, planes, rows, width = flow_ref.shape
     groups, walls = sizes
-    extra = values_ref.shape[1]
+    chips, extra, _ = mine_ref.shape
+    listed = pltpu.make_async_copy(cells_ref, list_ref, list_sem)
+    listed.start()
     row, lane = iotas(rows, width)
-    halo, second, beside = (
-        mix_edges(*from_neighbours(lax.axis_index("wall"), walls, z0_ref[i], z1_ref[i]), lane) for i in range(3)
-    )
+    halo = mix_edges(*from_neighbours(lax.axis_index("wall"), walls, z0_ref[0], z1_ref[0]), lane)
     inside = pltpu.roll(edges_ref[0], 1, 1)
     jump = halo - inside
     rim_nu = viscosity([jump] + [pltpu.roll(jump, width - 2 * c * planes, 1) for c in (1, 2)])
     rim_nu = jnp.where(lane < 2 * planes, rim_nu, 0.0)
     rim_ref[...] = rim_nu
-    outside_ref[...] = outside_edges(walls, planes, halo, second, beside, inside, rim_nu)
     for c in range(4):
         low, high = from_neighbours(lax.axis_index("fluid"), groups, x0_ref[c], x1_ref[c])
         padded_ref[c, 0] = low
@@ -305,52 +325,94 @@
             next_ref[c, x] = value
         return carry
 
-    lax.fori_loop(0, planes, plane, 0, unroll=4)
+    pieces = out_sems.shape[0]
+    step = planes // pieces
+
+    def store(i):
+        part = pl.ds(i * step, step)
+        return pltpu.make_async_copy(next_ref.at[:, part], out_ref.at[:, part], out_sems.at[i])
+
+    for i in range(pieces):
+        lax.fori_loop(i * step, (i + 1) * step, plane, 0, unroll=True)
+        store(i).start()
 
     taken_ref[...] = jnp.zeros_like(taken_ref)
-    slot_rows = groups * extra
-    _, slot_lane = iotas(8, slot_rows)
-
-    def slot(s, cell_of):
-        b = s // cap
-        first = b * extra + (s - b * cap) * 3
-        cell = cells_ref[s - b * cap, b]
-        for c in range(3):
-            taken_ref[pl.ds(first + c, 1), :] = next_ref[c, cell // rows, pl.ds(cell % rows, 1), :]
-        return jnp.where((slot_lane >= first) & (slot_lane < first + 3), cell, cell_of)
-
-    cell_of = lax.fori_loop(0, groups * cap, slot, jnp.full((8, slot_rows), -1, jnp.int32), unroll=4)
-    values_ref[...] = taken_ref[...].astype(jnp.bfloat16).reshape(values_ref.shape)
-    lines, slot_lane = iotas(planes * rows, slot_rows)
-    hit = lines == cell_of[0:1, :]
+    listed.wait()
+    _, slot_lane = iotas(8, groups * extra)
+    cell_of = jnp.full((8, groups * extra), -1, jnp.int32)
+    odd = lax.axis_index("fluid") % 2
+    for b in range(groups):
+        part = (odd if b % 2 == 0 else 1 - odd) * chips + b // 2
+        for k in range(cap):
+            cell = list_ref[k, b]
+            x, y = lax.div(cell, rows), lax.rem(cell, rows)
+            first = part * extra + 3 * k
+            for c in range(3):
+                taken_ref[pl.ds(first + c, 1), :] = next_ref[c, x, pl.ds(y, 1), :]
+            cell_of = jnp.where((slot_lane >= first) & (slot_lane < first + 3), cell, cell_of)
+    cells_of_ref[...] = cell_of
+    taken = taken_ref[...].astype(jnp.bfloat16).reshape((2,) + mine_ref.shape)
+    mine_ref[...] = taken[0]
+    lent_ref[...] = taken[1]
+    for i in range(pieces):
+        store(i).wait()
+
+
+def pick_kernel(
+    sizes, cells_of_ref, z0_ref, z1_ref, edges_ref, rim_ref, outside_ref, pick_ref
+):
+    _, rows, width = edges_ref.shape
+    groups, walls = sizes
+    _, lines, slot_rows = pick_ref.shape
+    planes = lines // rows
+    extra = slot_rows // groups
+    _, lane = iotas(rows, width)
+    halo, second, beside = (
+        mix_edges(*from_neighbours(lax.axis_index("wall"), walls, z0_ref[i], z1_ref[i]), lane, shift)
+        for i, shift in enumerate((2, 4, 2))
+    )
+    inside = pltpu.roll(edges_ref[0], 1, 1)
+    outside_ref[...] = outside_edges(walls, planes, halo, second, beside, inside, rim_ref[...])
+    line, slot_lane = iotas(lines, slot_rows)
+    hit = line == cells_of_ref[0:1, :]
     part = (slot_lane % extra) % 3
     for c in range(3):
         pick_ref[c] = (hit & (part == c)).astype(jnp.float32).astype(jnp.bfloat16)
 
 
-def forcing_kernel(
-    cap, recv_ref, values_ref, pick_ref, forcing_ref, first_ref, second_ref, high_ref, low_ref
-):
-    groups, extra, width = values_ref.shape
-    _, planes, rows, _ = forcing_ref.shape
+def product_kernel(cap, block, values_ref, after_ref, *refs):
+    chips, extra, width = values_ref.shape
+    recvs, out_ref = refs[:chips], refs[chips]
     depth = cap * width
     row, lane = iotas(extra, depth)
     own = row // 3 == lane // width
-    for b in range(groups):
-        weights = recv_ref[b, pl.ds(0, depth), :]
+    here = lax.axis_index("fluid") // 2
+    for m, recv_ref in enumerate(recvs):
+        source = here ^ m
+        at = pl.ds(pl.multiple_of(source * extra, extra), extra)
+        weights = recv_ref[block, pl.ds(0, depth), :]
         predicted = lax.dot_general(
-            values_ref[b], weights, (((1,), (1,)), ((), ())), preferred_element_type=jnp.float32
+            values_ref[source], weights, (((1,), (1,)), ((), ())), preferred_element_type=jnp.float32
         )
-        seen = recv_ref[b, pl.ds(depth, extra), :].astype(jnp.float32)
+        seen = recv_ref[block, pl.ds(depth, extra), :].astype(jnp.float32)
         misfit = jnp.where(own, predicted - jnp.concatenate([seen] * cap, axis=1), 0.0).astype(jnp.bfloat16)
         contrib = jnp.dot(misfit, weights, preferred_element_type=jnp.float32)
         high = contrib.astype(jnp.bfloat16)
-        high_ref[pl.ds(b * extra, extra), :] = high
-        low_ref[pl.ds(b * extra, extra), :] = (contrib - high.astype(jnp.float32)).astype(jnp.bfloat16)
+        out_ref[0, at, :] = high
+        out_ref[1, at, :] = (contrib - high.astype(jnp.float32)).astype(jnp.bfloat16)
+
+
+def forcing_kernel(mine_ref, other_ref, pick_ref, forcing_ref, first_ref, second_ref):
+    _, planes, rows, width = forcing_ref.shape
+    half = mine_ref.shape[1]
     even = lax.axis_index("fluid") % 2 == 0
     for c in range(3):
-        total = jnp.dot(pick_ref[c], high_ref[...], preferred_element_type=jnp.float32)
-        total += jnp.dot(pick_ref[c], low_ref[...], preferred_element_type=jnp.float32)
+        total = None
+        for i, part_ref in enumerate((mine_ref, other_ref)):
+            pick = pick_ref[c, :, i * half : (i + 1) * half]
+            for part in range(2):
+                product = jnp.dot(pick, part_ref[part], preferred_element_type=jnp.float32)
+                total = product if total is None else total + product
         forcing_ref[c] = total.reshape(planes, rows, width)
         low, high = total[:rows], total[(planes - 1) * rows :]
         first_ref[c] = jnp.where(even, high, low)
@@ -453,7 +515,7 @@
 
 def final_kernel(sizes, inner_ref, x0_ref, x1_ref, nux_ref, rim_ref, own_ref, *refs):
     groups, walls = sizes
-    arrived, adjoint_ref, sens_ref = refs[:-2], refs[-2], refs[-1]
+    arrived, (adjoint_ref, sens_ref, value_ref, sems) = refs[:-4], refs[-4:]
     _, planes, rows, width = inner_ref.shape
     per = own_ref.shape[0]
     _, lane = iotas(rows, width)
@@ -467,27 +529,35 @@
             edges = ref[per:, :]
             above = jnp.where((me ^ mask) == me + 1, edges, above)
             below = jnp.where((me ^ mask) == me - 1, edges, below)
-    sens_ref[...] = sens_scale * lax.dot_general(
-        jnp.ones((8, width), jnp.float32), total, (((1,), (1,)), ((), ())),
-        precision=lax.Precision.HIGHEST, preferred_element_type=jnp.float32,
-    )[:1]
     mixed = mix_edges(below, above, lane)
     edge_nu = time_step * rim_ref[...]
     edge_nu = edge_nu + pltpu.roll(edge_nu, 2 * planes, 1) + pltpu.roll(edge_nu, 4 * planes, 1)
     edge_flux = mixed * edge_nu
     on_edge = (lane == 0) | (lane == width - 1)
 
-    def plane(x, carry):
-        for c in range(3):
-            edge = edge_of(edge_flux, c * planes + x)
-            adjoint_ref[c, x] = inner_ref[c, x] + jnp.where(on_edge, edge, 0.0)
-        return carry
-
-    lax.fori_loop(0, planes, plane, 0, unroll=4)
-    for c in range(3):
-        low, high = from_neighbours(lax.axis_index("fluid"), groups, x0_ref[c], x1_ref[c])
-        adjoint_ref[c, 0] += time_step * nux_ref[0] * low
-        adjoint_ref[c, planes - 1] += time_step * nux_ref[planes] * high
+    beside = [from_neighbours(lax.axis_index("fluid"), groups, x0_ref[c], x1_ref[c]) for c in range(3)]
+    step = planes // sems.shape[0]
+
+    def store(i):
+        part = pl.ds(i * step, step)
+        return pltpu.make_async_copy(value_ref.at[:, part], adjoint_ref.at[:, part], sems.at[i])
+
+    for i in range(sems.shape[0]):
+        for x in range(i * step, (i + 1) * step):
+            for c in range(3):
+                value = inner_ref[c, x] + jnp.where(on_edge, edge_of(edge_flux, c * planes + x), 0.0)
+                if x == 0:
+                    value += time_step * nux_ref[0] * beside[c][0]
+                if x == planes - 1:
+                    value += time_step * nux_ref[planes] * beside[c][1]
+                value_ref[c, x] = value
+        store(i).start()
+    sens_ref[...] = sens_scale * lax.dot_general(
+        jnp.ones((8, width), jnp.float32), total, (((1,), (1,)), ((), ())),
+        precision=lax.Precision.HIGHEST, preferred_element_type=jnp.float32,
+    )[:1]
+    for i in range(sems.shape[0]):
+        store(i).wait()
 
 
 def body(flow_state, regions, obs_tiles, measured, tile_dest, cell_list):
@@ -501,73 +571,98 @@
     cells = groups * cap
     grid = planes * rows * width
 
+    chips = groups // 2
+    height = cap * width + extra
     xs0, xs1 = call(
         faces_kernel,
         (f32(4, rows, width), f32(4, rows, width)),
         [HBM],
         (flow_state,),
-        (pltpu.SemaphoreType.DMA((2,)),),
+        (pltpu.SemaphoreType.DMA((2, 4)),),
         limit=60 * 1024 * 1024,
     )
     x0, x1 = swap(xs0, "fluid", 0), swap(xs1, "fluid", 1)
-    send = call(
+    sends = call(
         functools.partial(group_kernel, cap),
-        bf16(groups, cap * width + extra, width),
-        [HBM, HBM, HBM, ANY],
+        (bf16(2, height, width),) * chips,
+        [HBM] * 3 + [ANY],
         (tile_dest[0, 0], obs_tiles[0, 0], jnp.transpose(measured[0, 0], (1, 0, 2)), xs1),
         (
             pltpu.SMEM((count_tiles,), jnp.int32),
             pltpu.VMEM((count_tiles, width, width), jnp.bfloat16),
             pltpu.VMEM((3, count_tiles, width), jnp.bfloat16),
             pltpu.SMEM((groups,), jnp.int32),
+            pltpu.SMEM((cells,), jnp.int32),
             pltpu.VMEM((groups * extra, width), jnp.bfloat16),
             pltpu.VMEM((width, width), jnp.bfloat16),
             pltpu.SemaphoreType.DMA,
             pltpu.SemaphoreType.DMA,
             pltpu.SemaphoreType.DMA((4,)),
-            pltpu.SemaphoreType.DMA((count_tiles,)),
+            pltpu.SemaphoreType.DMA((cells,)),
             pltpu.SemaphoreType.DMA((groups,)),
-            pltpu.SemaphoreType.DMA,
         ),
-        moved=4 * count_tiles * width * width,
-        out_specs=HBM,
+        out_specs=(HBM,) * chips,
         limit=60 * 1024 * 1024,
     )
-    send, x0, x1 = lax.optimization_barrier((send, x0, x1))
-    recv = lax.all_to_all(send, "fluid", split_axis=0, concat_axis=0, tiled=True)
+    *sends, x0, x1 = lax.optimization_barrier((*sends, x0, x1))
+    recvs = [sends[0]] + [cross(sends[m], "fluid", 2 * m) for m in range(1, chips)]
     zs = call(
         functools.partial(edges_kernel, groups),
         f32(3, rows, width),
         [VMEM] * 4,
         (flow_state, regions, x0, x1),
-        moved=16 * grid,
     )
     z0, z1 = swap(zs, "wall", 0), swap(zs, "wall", 1)
-    velocity_next, nux, nuy, nuz, nuy0, rim, outside, values, pick = call(
+    slot_rows = groups * extra
+    velocity_next, velocity, nux, nuy, nuz, nuy0, rim, mine, lent, cells_of = call(
         functools.partial(forward_kernel, sizes, cap),
-        (f32(3, planes, rows, width), f32(planes + 1, rows, width), f32(planes, rows, width), f32(planes, rows, width))
-        + (f32(planes, width), f32(rows, width), f32(rows, width))
-        + (bf16(groups, extra, width), bf16(3, planes * rows, groups * extra)),
-        [SMEM] + [VMEM] * 6,
+        (f32(3, planes, rows, width),) * 2
+        + (f32(planes + 1, rows, width), f32(planes, rows, width), f32(planes, rows, width))
+        + (f32(planes, width), f32(rows, width))
+        + (bf16(chips, extra, width),) * 2
+        + (jax.ShapeDtypeStruct((8, slot_rows), jnp.int32),),
+        [ANY] + [VMEM] * 6,
         (cell_list[0, 0].T, flow_state, x0, x1, z0, z1, zs),
-        (pltpu.VMEM((4, planes + 2, rows, width), jnp.float32), pltpu.VMEM((groups * extra, width), jnp.float32)),
-        flops=200 * grid,
-        moved=60 * grid,
-    )
-
+        (
+            pltpu.SMEM((cap, groups), jnp.int32),
+            pltpu.VMEM((4, planes + 2, rows, width), jnp.float32),
+            pltpu.VMEM((slot_rows, width), jnp.float32),
+            pltpu.SemaphoreType.DMA,
+            pltpu.SemaphoreType.DMA((4,)),
+        ),
+        out_specs=(HBM,) + (VMEM,) * 9,
+    )
+    borrowed = cross(lent, "fluid", 1)
+    outside, pick = call(
+        functools.partial(pick_kernel, sizes),
+        (f32(rows, width), bf16(3, planes * rows, slot_rows)),
+        [VMEM] * 5,
+        (cells_of, z0, z1, zs, rim),
+    )
+
+    def products(block, values, after):
+        return call(
+            functools.partial(product_kernel, cap, block),
+            bf16(2, chips * extra, width),
+            [VMEM, ANY] + [VMEM] * chips,
+            (values, after, *recvs),
+        )
+
+    given = products(1, borrowed, pick)
+    other = cross(given, "fluid", 1)
+    held = products(0, mine, given)
     forcing, fs0, fs1 = call(
-        functools.partial(forcing_kernel, cap),
+        forcing_kernel,
         (f32(3, planes, rows, width), f32(3, rows, width), f32(3, rows, width)),
         [VMEM] * 3,
-        (recv, values, pick),
-        (pltpu.VMEM((groups * extra, width), jnp.bfloat16),) * 2,
+        (held, other, pick),
     )
     f0, f1 = swap(fs0, "fluid", 0), swap(fs1, "fluid", 1)
     inner, fpack, sums = call(
         inner_kernel,
         (f32(3, planes, rows, width), f32(rows, width), f32(reg_count, width)),
         [VMEM] * 9,
-        (forcing, velocity_next, nux, nuy, nuz, nuy0, rim, regions, outside),
+        (forcing, velocity, nux, nuy, nuz, nuy0, rim, regions, outside),
         (pltpu.VMEM(((planes + 1) * rows, width), jnp.float32), pltpu.VMEM(((planes + 1) * rows, width), jnp.int32)),
     )
     masks = tuple(range(1, walls))
@@ -576,7 +671,7 @@
         functools.partial(edge_kernel, sizes, masks),
         tuple(f32(height, width) for height in heights),
         [VMEM] * 7,
-        (f0, f1, nux, velocity_next, regions, sums, fpack),
+        (f0, f1, nux, velocity, regions, sums, fpack),
         (
             pltpu.VMEM((2 * rows, width), jnp.float32),
             pltpu.VMEM((2 * rows, width), jnp.int32),
@@ -591,6 +686,8 @@
         (f32(3, planes, rows, width), f32(1, REG_DEV)),
         [VMEM] * (6 + len(arrived)),
         (inner, f0, f1, nux, rim, own, *arrived),
+        (pltpu.VMEM((3, planes, rows, width), jnp.float32), pltpu.SemaphoreType.DMA((4,))),
+        out_specs=(HBM, VMEM),
         flops=10 * grid,
         moved=24 * grid,
     )

time: 45.4 us -> 42.7 us (0.941)
  waiting for transfers between devices: 11.3 us -> 9.52 us
  local copies, waits for them, and re-layouts: 0.73 us -> 0.02 us
  Pallas kernels: 15.7 us -> 15.2 us
    ppermute x3 -> x8, starting transfers between devices: 4.23 us -> 7.98 us  [cross(): lax.ppermute(block, axis, [(i, i ^ mask) for i in range(lax.axis_size(axi...]
    all_to_all x1 -> x0, starting transfers between devices: 3.7 us -> none  [body(): lax.all_to_all(send, 'fluid', split_axis=0, concat_axis=0, tiled=True)]
    ppermute x3 -> x8, waiting for transfers between devices: 4.44 us -> 7.44 us  [cross(): lax.ppermute(block, axis, [(i, i ^ mask) for i in range(lax.axis_size(axi...]
    ppermute x6, waiting for transfers between devices: 4.82 us -> 2.08 us  [swap(): return lax.ppermute(block, ('fluid', 'wall'), pairs)]
    all_to_all x1 -> x0, waiting for transfers between devices: 2.06 us -> none  [body(): lax.all_to_all(send, 'fluid', split_axis=0, concat_axis=0, tiled=True)]
    unnamed x12 -> x8, local copies, waits for them, and re-layouts: 0.73 us -> 0.02 us
    pallas_call x8 -> x11, Pallas kernels: 15.7 us -> 15.2 us  [call(): pl.pallas_call(kernel, out_shape=outs, in_specs=ins, out_specs=out_specs...]
  transfers between devices with their start and end apart: 10 -> 14, of which waited for: 5 -> 5; matrix products, arithmetic and copies ran while one was open for 0% -> 0% of each run, Pallas kernels for 24% -> 24%
where the time goes in v3:
time: 42.7 us; the launch traced here: 42.5 us
  starting transfers between devices  17 us (40%)
  Pallas kernels  15.2 us (36%)
  waiting for transfers between devices  9.52 us (22%)
  between operations  0.76 us (2%)
    pallas_call x11, Pallas kernels, call(): pl.pallas_call(kernel, out_shape=outs, in_specs=ins, out_specs=out_specs...  15.2 us
    ppermute x6, starting transfers between devices, swap(): return lax.ppermute(block, ('fluid', 'wall'), pairs)  9.02 us
    ppermute x8, starting transfers between devices, cross(): lax.ppermute(block, axis, [(i, i ^ mask) for i in range(lax.axis_size(axi...  7.98 us
    ppermute x8, waiting for transfers between devices, cross(): lax.ppermute(block, axis, [(i, i ^ mask) for i in range(lax.axis_size(axi...  7.44 us
    ppermute x6, waiting for transfers between devices, swap(): return lax.ppermute(block, ('fluid', 'wall'), pairs)  2.08 us
  transfers between devices with their start and end apart: 14, of which 5 were waited for; matrix products, arithmetic and copies ran while one was open for 0% of the time, Pallas kernels for 24%

profile of v3, /device:TPU:0, one launch (start us, length us, event | category | flops | bytes accessed | tf_op | source)
XLA Modules:
  0.0 42.5 jit_solution(12007062110293732006)
XLA Ops:
  0.6 1.6 %shard_map.85 = (f32[4,32,128]{2,1,0:T(8,128)}, f32[4,32,128]{2,1,0:T(8,128)}) custom-call(f32[4,16,32,128]{3,2,1,0:T(8,128)} %flow_ref.5), custom_call_target="tpu_custom_call" | custom-call | flops 1 | bytes 1 | tf_op jit(solution)/shard_map/pallas_call | solution.py:26
  2.3 0.5 %collective-permute-start = (f32[4,32,128]{2,1,0:T(8,128)}, f32[4,32,128]{2,1,0:T(8,128)S(1)}, u32[]{:S(2)}, u32[]{:S(2)}) collective-permute-start(f32[4,32,128]{2,1,0:T(8,128)} %get-tuple-element.44), channel_id=1, source_target_pairs={{0,4},{1,5},{2,6},{3,7},{4,0},{5,1},{6,2},{7,3},{8,12},{9,13},{10,... | collective-permute-start | bytes 196616 | tf_op jit(solution)/shard_map/ppermute | solution.py:59
  2.8 3.6 %collective-permute-start.1 = (f32[4,32,128]{2,1,0:T(8,128)}, f32[4,32,128]{2,1,0:T(8,128)S(1)}, u32[]{:S(2)}, u32[]{:S(2)}) collective-permute-start(f32[4,32,128]{2,1,0:T(8,128)} %get-tuple-element.39.after_ref), channel_id=1, source_target_pairs={{0,28},{1,29},{2,30},{3,31},{4,8},{5,9},{6,10},{7,11},{8,4},{9,5},... | collective-permute-start | bytes 196616 | tf_op jit(solution)/shard_map/ppermute | solution.py:59
  6.4 2.6 %shard_map.86 = (bf16[2,528,128]{2,1,0:T(8,128)(2,1)}, bf16[2,528,128]{2,1,0:T(8,128)(2,1)}, bf16[2,528,128]{2,1,0:T(8,128)(2,1)}, bf16[2,528,128]{2,1,0:T(8,128)(2,1)}) custom-call(s32[32]{0:T(128)} %bitcast.12, bf16[32,128,128]{2,1,0:T(8,128)(2,1)} %bitcast.10, bf16[3,32,128]{2,1,0:T(8,128)(2,1)} %bitcast.11, f32[4,32,128]{2,1,0:T(8,128)} %get-tuple-element.39.after_ref), custom_call_target="tpu_custom_call" | custom-call | flops 1 | bytes 1 | tf_op jit(solution)/shard_map/pallas_call | solution.py:26
  9.3 1.7 %collective-permute-start.6 = (bf16[2,528,128]{2,1,0:T(8,128)(2,1)}, bf16[2,528,128]{2,1,0:T(8,128)(2,1)S(1)}, u32[]{:S(2)}, u32[]{:S(2)}) collective-permute-start(bf16[2,528,128]{2,1,0:T(8,128)(2,1)} %get-tuple-element.55), channel_id=1, source_target_pairs={{0,16},{4,20},{8,24},{12,28},{16,0},{20,4},{24,8},{28,12},{1,17},{... | collective-permute-start | bytes 811016 | tf_op jit(solution)/shard_map/ppermute | solution.py:63
  11.0 1.5 %collective-permute-start.7 = (bf16[2,528,128]{2,1,0:T(8,128)(2,1)}, bf16[2,528,128]{2,1,0:T(8,128)(2,1)S(1)}, u32[]{:S(2)}, u32[]{:S(2)}) collective-permute-start(bf16[2,528,128]{2,1,0:T(8,128)(2,1)} %get-tuple-element.56), channel_id=1, source_target_pairs={{0,24},{4,28},{8,16},{12,20},{16,8},{20,12},{24,0},{28,4},{1,25},{... | collective-permute-start | bytes 811016 | tf_op jit(solution)/shard_map/ppermute | solution.py:63
  12.6 0.7 %shard_map.87.edges_ref = f32[3,32,128]{2,1,0:T(8,128)S(1)} custom-call(f32[4,16,32,128]{3,2,1,0:T(8,128)S(1)} %copy-done, s32[16,32,128]{2,1,0:T(8,128)S(1)} %copy-done.1, f32[4,32,128]{2,1,0:T(8,128)S(1)} %collective-permute-done.x0_ref, f32[4,32,128]{2,1,0:T(8,128)S(1)} %collective-permute-done.1.x1_ref), custom_call_target="tpu_custom_call" | custom-call | flops 1 | bytes 1 | tf_op jit(solution)/shard_map/pallas_call | solution.py:26
  13.4 3.1 %collective-permute-start.2 = (f32[3,32,128]{2,1,0:T(8,128)S(1)}, f32[3,32,128]{2,1,0:T(8,128)S(1)}, u32[]{:S(2)}, u32[]{:S(2)}) collective-permute-start(f32[3,32,128]{2,1,0:T(8,128)S(1)} %shard_map.87.edges_ref), channel_id=1, source_target_pairs={{0,1},{1,0},{2,3},{3,2},{4,5},{5,4},{6,7},{7,6},{8,9},{9,8},{10,11... | collective-permute-start | bytes 147464 | tf_op jit(solution)/shard_map/ppermute | solution.py:59
  16.5 2.1 %collective-permute-done.2.z0_ref = f32[3,32,128]{2,1,0:T(8,128)S(1)} collective-permute-done((f32[3,32,128]{2,1,0:T(8,128)S(1)}, f32[3,32,128]{2,1,0:T(8,128)S(1)}, u32[]{:S(2)}, u32[]{:S(2)}) %collective-permute-start.2) | collective-permute-done | bytes 49184 | tf_op jit(solution)/shard_map/ppermute | solution.py:59
  18.6 2.6 %shard_map.88 = (f32[3,16,32,128]{3,2,1,0:T(8,128)}, f32[3,16,32,128]{3,2,1,0:T(8,128)S(1)}, f32[17,32,128]{2,1,0:T(8,128)S(1)}, f32[16,32,128]{2,1,0:T(8,128)S(...) custom-call(s32[4,8]{1,0:T(4,128)S(1)} %bitcast.9, ...), custom_call_target="tpu_custom_call" | custom-call | flops 1 | bytes 1 | tf_op jit(solution)/shard_map/pallas_call | solution.py:26
  21.3 0.5 %shard_map.89 = (f32[32,128]{1,0:T(8,128)S(1)}, bf16[3,512,128]{2,1,0:T(8,128)(2,1)S(1)}) custom-call(s32[8,128]{1,0:T(8,128)S(1)} %get-tuple-element.50.cells_of_ref, f32[3,32,128]{2,1,0:T(8,128)S(1)} %collective-permute-done.2.z0_ref, f32[3,32,128]{2,1,0:T(8,128)S(1)} %collective-permute-done.3.z1_ref, f32[3,32,128]{2,1,0:T(8,128)S(1)} %shard_map.87.edges_ref, ...), custom_call_target="tpu_custom_call" | custom-call | flops 1 | bytes 1 | tf_op jit(solution)/shard_map/pallas_call | solution.py:26
  21.8 0.7 %collective-permute-done.4.values_ref = bf16[4,16,128]{2,1,0:T(8,128)(2,1)S(1)} collective-permute-done((bf16[4,16,128]{2,1,0:T(8,128)(2,1)S(1)}, bf16[4,16,128]{2,1,0:T(8,128)(2,1)S(1)}, u32[]{:S(2)}, u32[]{:S(2)}) %collective-permute-start.4) | collective-permute-done | bytes 16416 | tf_op jit(solution)/shard_map/ppermute | solution.py:63
  22.5 1.9 %collective-permute-done.6.refs_2_ = bf16[2,528,128]{2,1,0:T(8,128)(2,1)S(1)} collective-permute-done((bf16[2,528,128]{2,1,0:T(8,128)(2,1)}, bf16[2,528,128]{2,1,0:T(8,128)(2,1)S(1)}, u32[]{:S(2)}, u32[]{:S(2)}) %collective-permute-start.6) | collective-permute-done | bytes 270368 | tf_op jit(solution)/shard_map/ppermute | solution.py:63
  24.4 0.7 %shard_map.90.after_ref = bf16[2,64,128]{2,1,0:T(8,128)(2,1)S(1)} custom-call(bf16[4,16,128]{2,1,0:T(8,128)(2,1)S(1)} %collective-permute-done.4.values_ref, bf16[3,512,128]{2,1,0:T(8,128)(2,1)S(1)} %get-tuple-element.52.after_ref.pick_ref, bf16[2,528,128]{2,1,0:T(8,128)(2,1)S(1)} %copy-done.2, bf16[2,528,128]{2,1,0:T(8,128)(2,1)S(1)} %collective-permute-done.5.refs_1_, ...), custom_call_target="tpu_custom_call" | custom-call | flops 1 | bytes 1 | tf_op jit(solution)/shard_map/pallas_call | solution.py:26
  25.3 0.7 %shard_map.91.mine_ref = bf16[2,64,128]{2,1,0:T(8,128)(2,1)S(1)} custom-call(bf16[4,16,128]{2,1,0:T(8,128)(2,1)S(1)} %get-tuple-element.48.values_ref, bf16[2,64,128]{2,1,0:T(8,128)(2,1)S(1)} %shard_map.90.after_ref, bf16[2,528,128]{2,1,0:T(8,128)(2,1)S(1)} %copy-done.2, bf16[2,528,128]{2,1,0:T(8,128)(2,1)S(1)} %collective-permute-done.5.refs_1_, ...), custom_call_target="tpu_custom_call" | custom-call | flops 1 | bytes 1 | tf_op jit(solution)/shard_map/pallas_call | solution.py:26
  26.0 0.4 collective-permute-done.8.other_ref
  26.4 0.6 %shard_map.92 = (f32[3,16,32,128]{3,2,1,0:T(8,128)S(1)}, f32[3,32,128]{2,1,0:T(8,128)S(1)}, f32[3,32,128]{2,1,0:T(8,128)S(1)}) custom-call(bf16[2,64,128]{2,1,0:T(8,128)(2,1)S(1)} %shard_map.91.mine_ref, bf16[2,64,128]{2,1,0:T(8,128)(2,1)S(1)} %collective-permute-done.8.other_ref, bf16[3,512,128]{2,1,0:T(8,128)(2,1)S(1)} %get-tuple-element.52.after_ref.pick_ref), custom_call_target="tpu_custom_call" | custom-call | flops 1 | bytes 1 | tf_op jit(solution)/shard_map/pallas_call | solution.py:26
  27.2 1.5 %collective-permute-start.10 = (f32[3,32,128]{2,1,0:T(8,128)S(1)}, f32[3,32,128]{2,1,0:T(8,128)S(1)}, u32[]{:S(2)}, u32[]{:S(2)}) collective-permute-start(f32[3,32,128]{2,1,0:T(8,128)S(1)} %get-tuple-element.66), channel_id=1, source_target_pairs={{0,28},{1,29},{2,30},{3,31},{4,8},{5,9},{6,10},{7,11},{8,4},{9,5},... | collective-permute-start | bytes 147464 | tf_op jit(solution)/shard_map/ppermute | solution.py:59
  28.7 3.1 %shard_map.93 = (f32[3,16,32,128]{3,2,1,0:T(8,128)S(1)}, f32[32,128]{1,0:T(8,128)S(1)}, f32[64,128]{1,0:T(8,128)S(1)}) custom-call(f32[3,16,32,128]{3,2,1,0:T(8,128)S(1)} %get-tuple-element.57.forcing_ref, f32[3,16,32,128]{3,2,1,0:T(8,128)S(1)} %get-tuple-element.58.next_ref, f32[17,32,128]{2,1,0:T(8,128)S(1)} %get-tuple-element.59.nux_ref, ...), custom_call_target="tpu_custom_call" | custom-call | flops 1 | bytes 1 | tf_op jit(solution)/shard_map/pallas_call | solution.py:26
  31.8 0.4 shard_map.94
  32.2 1.6 %collective-permute-start.11 = (f32[48,128]{1,0:T(8,128)S(1)}, f32[48,128]{1,0:T(8,128)S(1)}, u32[]{:S(2)}, u32[]{:S(2)}) collective-permute-start(f32[48,128]{1,0:T(8,128)S(1)} %get-tuple-element.70), channel_id=1, source_target_pairs={{0,1},{1,0},{2,3},{3,2},{4,5},{5,4},{6,7},{7,6},{8,9},{9,8},{10,11... | collective-permute-start | bytes 73736 | tf_op jit(solution)/shard_map/ppermute | solution.py:63
  33.8 2.5 %collective-permute-start.13 = (f32[48,128]{1,0:T(8,128)S(1)}, f32[48,128]{1,0:T(8,128)S(1)}, u32[]{:S(2)}, u32[]{:S(2)}) collective-permute-start(f32[48,128]{1,0:T(8,128)S(1)} %get-tuple-element.72), channel_id=1, source_target_pairs={{0,3},{1,2},{2,1},{3,0},{4,7},{5,6},{6,5},{7,4},{8,11},{9,10},{10,... | collective-permute-start | bytes 73736 | tf_op jit(solution)/shard_map/ppermute | solution.py:63
  36.4 4.4 %collective-permute-done.12.refs_1_ = f32[16,128]{1,0:T(8,128)S(1)} collective-permute-done((f32[16,128]{1,0:T(8,128)S(1)}, f32[16,128]{1,0:T(8,128)S(1)}, u32[]{:S(2)}, u32[]{:S(2)}) %collective-permute-start.12) | collective-permute-done | bytes 8224 | tf_op jit(solution)/shard_map/ppermute | solution.py:63
  40.9 1.6 %shard_map.95 = (f32[3,16,32,128]{3,2,1,0:T(8,128)}, f32[1,16]{1,0:T(1,128)}) custom-call(f32[3,16,32,128]{3,2,1,0:T(8,128)S(1)} %get-tuple-element.64.inner_ref, f32[3,32,128]{2,1,0:T(8,128)S(1)} %collective-permute-done.9.x0_ref, f32[3,32,128]{2,1,0:T(8,128)S(1)} %collective-permute-done.10.x1_ref, f32[17,32,128]{2,1,0:T(8,128)S(1)} %get-tuple-element.59.nux_ref, ...), custom_call_target="tpu_custom_call" | custom-call | flops 655360 | bytes 1572864 | tf_op jit(solution)/shard_map/pallas_call | solution.py:26
  (23 shorter events, 0.9 us)
Async XLA Ops:
  0.6 11.9 %copy-start = (f32[4,16,32,128]{3,2,1,0:T(8,128)S(1)}, f32[4,16,32,128]{3,2,1,0:T(8,128)}, u32[]{:S(2)}) copy-start(f32[4,16,32,128]{3,2,1,0:T(8,128)} %flow_ref.5) | copy-start | bytes 3145732
  2.3 6.7 %collective-permute-start = (f32[4,32,128]{2,1,0:T(8,128)}, f32[4,32,128]{2,1,0:T(8,128)S(1)}, u32[]{:S(2)}, u32[]{:S(2)}) collective-permute-start(f32[4,32,128]{2,1,0:T(8,128)} %get-tuple-element.44), channel_id=1, source_target_pairs={{0,4},{1,5},{2,6},{3,7},{4,0},{5,1},{6,2},{7,3},{8,12},{9,13},{10,... | collective-permute-start | bytes 196616 | tf_op jit(solution)/shard_map/ppermute | solution.py:59
  2.8 6.2 %collective-permute-start.1 = (f32[4,32,128]{2,1,0:T(8,128)}, f32[4,32,128]{2,1,0:T(8,128)S(1)}, u32[]{:S(2)}, u32[]{:S(2)}) collective-permute-start(f32[4,32,128]{2,1,0:T(8,128)} %get-tuple-element.39.after_ref), channel_id=1, source_target_pairs={{0,28},{1,29},{2,30},{3,31},{4,8},{5,9},{6,10},{7,11},{8,4},{9,5},... | collective-permute-start | bytes 196616 | tf_op jit(solution)/shard_map/ppermute | solution.py:59
  6.4 6.2 %copy-start.1 = (s32[16,32,128]{2,1,0:T(8,128)S(1)}, s32[16,32,128]{2,1,0:T(8,128)}, u32[]{:S(2)}) copy-start(s32[16,32,128]{2,1,0:T(8,128)} %regions_ref.5) | copy-start | bytes 786436
  9.0 13.5 %collective-permute-start.5 = (bf16[2,528,128]{2,1,0:T(8,128)(2,1)}, bf16[2,528,128]{2,1,0:T(8,128)(2,1)S(1)}, u32[]{:S(2)}, u32[]{:S(2)}) collective-permute-start(bf16[2,528,128]{2,1,0:T(8,128)(2,1)} %get-tuple-element.54), channel_id=1, source_target_pairs={{0,8},{4,12},{8,0},{12,4},{16,24},{20,28},{24,16},{28,20},{1,9},{5... | collective-permute-start | bytes 811016 | tf_op jit(solution)/shard_map/ppermute | solution.py:63
  9.3 15.1 %collective-permute-start.6 = (bf16[2,528,128]{2,1,0:T(8,128)(2,1)}, bf16[2,528,128]{2,1,0:T(8,128)(2,1)S(1)}, u32[]{:S(2)}, u32[]{:S(2)}) collective-permute-start(bf16[2,528,128]{2,1,0:T(8,128)(2,1)} %get-tuple-element.55), channel_id=1, source_target_pairs={{0,16},{4,20},{8,24},{12,28},{16,0},{20,4},{24,8},{28,12},{1,17},{... | collective-permute-start | bytes 811016 | tf_op jit(solution)/shard_map/ppermute | solution.py:63
  11.0 13.4 %collective-permute-start.7 = (bf16[2,528,128]{2,1,0:T(8,128)(2,1)}, bf16[2,528,128]{2,1,0:T(8,128)(2,1)S(1)}, u32[]{:S(2)}, u32[]{:S(2)}) collective-permute-start(bf16[2,528,128]{2,1,0:T(8,128)(2,1)} %get-tuple-element.56), channel_id=1, source_target_pairs={{0,24},{4,28},{8,16},{12,20},{16,8},{20,12},{24,0},{28,4},{1,25},{... | collective-permute-start | bytes 811016 | tf_op jit(solution)/shard_map/ppermute | solution.py:63
  12.6 6.0 %copy-start.3 = (s32[1,1,8,4]{2,3,1,0:T(4,128)S(1)}, s32[1,1,8,4]{2,3,1,0:T(4,128)}, u32[]{:S(2)}) copy-start(s32[1,1,8,4]{2,3,1,0:T(4,128)} %param.11) | copy-start | bytes 388
  13.3 3.2 %collective-permute-start.3 = (f32[3,32,128]{2,1,0:T(8,128)S(1)}, f32[3,32,128]{2,1,0:T(8,128)S(1)}, u32[]{:S(2)}, u32[]{:S(2)}) collective-permute-start(f32[3,32,128]{2,1,0:T(8,128)S(1)} %shard_map.87.edges_ref), channel_id=1, source_target_pairs={{0,4},{1,2},{2,1},{3,7},{4,0},{5,6},{6,5},{7,3},{8,12},{9,10},{10,... | collective-permute-start | bytes 147464 | tf_op jit(solution)/shard_map/ppermute | solution.py:59
  13.4 5.2 %collective-permute-start.2 = (f32[3,32,128]{2,1,0:T(8,128)S(1)}, f32[3,32,128]{2,1,0:T(8,128)S(1)}, u32[]{:S(2)}, u32[]{:S(2)}) collective-permute-start(f32[3,32,128]{2,1,0:T(8,128)S(1)} %shard_map.87.edges_ref), channel_id=1, source_target_pairs={{0,1},{1,0},{2,3},{3,2},{4,5},{5,4},{6,7},{7,6},{8,9},{9,8},{10,11... | collective-permute-start | bytes 147464 | tf_op jit(solution)/shard_map/ppermute | solution.py:59
  18.6 5.8 %copy-start.2 = (bf16[2,528,128]{2,1,0:T(8,128)(2,1)S(1)}, bf16[2,528,128]{2,1,0:T(8,128)(2,1)}, u32[]{:S(2)}) copy-start(bf16[2,528,128]{2,1,0:T(8,128)(2,1)} %get-tuple-element.53.refs_0_) | copy-start | bytes 811012
  21.2 1.2 %collective-permute-start.4 = (bf16[4,16,128]{2,1,0:T(8,128)(2,1)S(1)}, bf16[4,16,128]{2,1,0:T(8,128)(2,1)S(1)}, u32[]{:S(2)}, u32[]{:S(2)}) collective-permute-start(bf16[4,16,128]{2,1,0:T(8,128)(2,1)S(1)} %get-tuple-element.49), channel_id=1, source_target_pairs={{0,4},{4,0},{8,12},{12,8},{16,20},{20,16},{24,28},{28,24},{1,5},{5... | collective-permute-start | bytes 49160 | tf_op jit(solution)/shard_map/ppermute | solution.py:63
  25.1 1.2 %collective-permute-start.8 = (bf16[2,64,128]{2,1,0:T(8,128)(2,1)S(1)}, bf16[2,64,128]{2,1,0:T(8,128)(2,1)S(1)}, u32[]{:S(2)}, u32[]{:S(2)}) collective-permute-start(bf16[2,64,128]{2,1,0:T(8,128)(2,1)S(1)} %shard_map.90.after_ref), channel_id=1, source_target_pairs={{0,4},{4,0},{8,12},{12,8},{16,20},{20,16},{24,28},{28,24},{1,5},{5... | collective-permute-start | bytes 98312 | tf_op jit(solution)/shard_map/ppermute | solution.py:63
  27.0 4.9 %collective-permute-start.9 = (f32[3,32,128]{2,1,0:T(8,128)S(1)}, f32[3,32,128]{2,1,0:T(8,128)S(1)}, u32[]{:S(2)}, u32[]{:S(2)}) collective-permute-start(f32[3,32,128]{2,1,0:T(8,128)S(1)} %get-tuple-element.65), channel_id=1, source_target_pairs={{0,4},{1,5},{2,6},{3,7},{4,0},{5,1},{6,2},{7,3},{8,12},{9,13},{10,... | collective-permute-start | bytes 147464 | tf_op jit(solution)/shard_map/ppermute | solution.py:59
  27.2 4.6 %collective-permute-start.10 = (f32[3,32,128]{2,1,0:T(8,128)S(1)}, f32[3,32,128]{2,1,0:T(8,128)S(1)}, u32[]{:S(2)}, u32[]{:S(2)}) collective-permute-start(f32[3,32,128]{2,1,0:T(8,128)S(1)} %get-tuple-element.66), channel_id=1, source_target_pairs={{0,28},{1,29},{2,30},{3,31},{4,8},{5,9},{6,10},{7,11},{8,4},{9,5},... | collective-permute-start | bytes 147464 | tf_op jit(solution)/shard_map/ppermute | solution.py:59
  32.2 8.7 %collective-permute-start.11 = (f32[48,128]{1,0:T(8,128)S(1)}, f32[48,128]{1,0:T(8,128)S(1)}, u32[]{:S(2)}, u32[]{:S(2)}) collective-permute-start(f32[48,128]{1,0:T(8,128)S(1)} %get-tuple-element.70), channel_id=1, source_target_pairs={{0,1},{1,0},{2,3},{3,2},{4,5},{5,4},{6,7},{7,6},{8,9},{9,8},{10,11... | collective-permute-start | bytes 73736 | tf_op jit(solution)/shard_map/ppermute | solution.py:63
  33.8 7.0 %collective-permute-start.13 = (f32[48,128]{1,0:T(8,128)S(1)}, f32[48,128]{1,0:T(8,128)S(1)}, u32[]{:S(2)}, u32[]{:S(2)}) collective-permute-start(f32[48,128]{1,0:T(8,128)S(1)} %get-tuple-element.72), channel_id=1, source_target_pairs={{0,3},{1,2},{2,1},{3,0},{4,7},{5,6},{6,5},{7,4},{8,11},{9,10},{10,... | collective-permute-start | bytes 73736 | tf_op jit(solution)/shard_map/ppermute | solution.py:63
  36.3 4.5 %collective-permute-start.12 = (f32[16,128]{1,0:T(8,128)S(1)}, f32[16,128]{1,0:T(8,128)S(1)}, u32[]{:S(2)}, u32[]{:S(2)}) collective-permute-start(f32[16,128]{1,0:T(8,128)S(1)} %get-tuple-element.71), channel_id=1, source_target_pairs={{0,2},{1,3},{2,0},{3,1},{4,6},{5,7},{6,4},{7,5},{8,10},{9,11},{10,... | collective-permute-start | bytes 24584 | tf_op jit(solution)/shard_map/ppermute | solution.py:63

commit v4 on v3

--- a/solution.py
+++ b/solution.py
@@ -402,52 +402,69 @@
         out_ref[1, at, :] = (contrib - high.astype(jnp.float32)).astype(jnp.bfloat16)
 
 
-def forcing_kernel(mine_ref, other_ref, pick_ref, forcing_ref, first_ref, second_ref):
-    _, planes, rows, width = forcing_ref.shape
+def forcing_rows(c, part, mine_ref, other_ref, pick_ref):
     half = mine_ref.shape[1]
+    total = None
+    for i, share_ref in enumerate((mine_ref, other_ref)):
+        pick = pick_ref[c, part, i * half : (i + 1) * half]
+        for share in range(2):
+            product = jnp.dot(pick, share_ref[share], preferred_element_type=jnp.float32)
+            total = product if total is None else total + product
+    return total
+
+
+def ends_kernel(mine_ref, other_ref, pick_ref, first_ref, second_ref):
+    _, rows, _ = first_ref.shape
+    lines = pick_ref.shape[1]
     even = lax.axis_index("fluid") % 2 == 0
     for c in range(3):
-        total = None
-        for i, part_ref in enumerate((mine_ref, other_ref)):
-            pick = pick_ref[c, :, i * half : (i + 1) * half]
-            for part in range(2):
-                product = jnp.dot(pick, part_ref[part], preferred_element_type=jnp.float32)
-                total = product if total is None else total + product
-        forcing_ref[c] = total.reshape(planes, rows, width)
-        low, high = total[:rows], total[(planes - 1) * rows :]
-        first_ref[c] = jnp.where(even, high, low)
-        second_ref[c] = jnp.where(even, low, high)
-
-
-def region_sums(product_ref, region_ref, sums_ref, plus_ref=None):
-    count = sums_ref.shape[0]
-    rows, width = product_ref.shape
-    step = 32
-
-    def group(g, carry):
-        sums = [jnp.zeros((8, width), jnp.float32)] * 8
-        for r in range(0, rows, step):
-            values = product_ref[r : r + step, :]
-            ids = region_ref[r : r + step, :] - g * 8
-            for i in range(8):
-                chosen = jnp.where(ids == i, values, 0.0)
-                for s in range(0, step, 8):
-                    sums[i] = sums[i] + chosen[s : s + 8]
-        block = jnp.concatenate([jnp.sum(part, axis=0, keepdims=True) for part in sums], axis=0)
-        at = pl.ds(pl.multiple_of(g * 8, 8), 8)
-        sums_ref[at, :] = block if plus_ref is None else block + plus_ref[at, :]
-        return carry
-
-    lax.fori_loop(0, count // 8, group, 0)
+        low = forcing_rows(c, slice(0, rows), mine_ref, other_ref, pick_ref)
+        high = forcing_rows(c, slice(lines - rows, lines), mine_ref, other_ref, pick_ref)
+        first_ref[c] = jnp.where(even, high, low).astype(jnp.bfloat16)
+        second_ref[c] = jnp.where(even, low, high).astype(jnp.bfloat16)
+
+
+def forcing_kernel(mine_ref, other_ref, pick_ref, after_ref, forcing_ref):
+    for c in range(3):
+        forcing_ref[c] = forcing_rows(c, slice(None), mine_ref, other_ref, pick_ref).reshape(forcing_ref.shape[1:])
+
+
+def region_rows(values, ids, tops):
+    top, low = (ids // 8).astype(jnp.float32).astype(jnp.bfloat16), (ids % 8).astype(jnp.float32).astype(jnp.bfloat16)
+    main = values.astype(jnp.bfloat16)
+    rest = (values - main.astype(jnp.float32)).astype(jnp.bfloat16)
+    zero = jnp.zeros_like(main)
+    one = jnp.ones_like(main)
+    hits = [top == jnp.bfloat16(h) for h in range(tops)]
+    return (
+        jnp.concatenate([jnp.where(hit, main, zero) for hit in hits], axis=0),
+        jnp.concatenate([jnp.where(hit, rest, zero) for hit in hits], axis=0),
+        jnp.concatenate([jnp.where(low == jnp.bfloat16(l), one, zero) for l in range(8)], axis=0),
+    )
+
+
+def region_sums(main, rest, ones, rows):
+    over_lanes = (((1,), (1,)), ((), ()))
+    total = lax.dot_general(main, ones, over_lanes, preferred_element_type=jnp.float32)
+    total += lax.dot_general(rest, ones, over_lanes, preferred_element_type=jnp.float32)
+    row, column = iotas(*total.shape)
+    total = jnp.where(row % rows == column % rows, total, 0.0)
+    return jnp.sum(total.reshape(total.shape[0] // rows, rows, total.shape[1]), axis=1)
 
 
 def inner_kernel(
     forcing_ref, next_ref, nux_ref, nuy_ref, nuz_ref, nuy0_ref, rim_ref, regions_ref, outside_ref,
-    adjoint_ref, fpack_ref, sums_ref, product_ref, ids_ref,
+    adjoint_ref, fpack_ref, sums_ref, main_ref, rest_ref, ones_ref,
 ):
     _, planes, rows, width = forcing_ref.shape
     row, lane = iotas(rows, width)
     rim_nu = rim_ref[...]
+    tops = sums_ref.shape[0]
+
+    def add_up(x, values, ids):
+        at = pl.ds(pl.multiple_of(x * width, width), width)
+        for part_ref, part in zip((main_ref, rest_ref, ones_ref), region_rows(values, ids, tops)):
+            part_ref[:, at] = part
 
     def plane(x, fpack):
         nuy, nuz = nuy_ref[x], nuz_ref[x]
@@ -473,9 +490,7 @@
             part = value * next_ref[c, x]
             product = part if product is None else product + part
             fpack = pack_edges(fpack, here, c * planes + x, lane)
-        at = pl.ds(pl.multiple_of(x * rows, rows), rows)
-        product_ref[at, :] = product
-        ids_ref[at, :] = regions_ref[x]
+        add_up(x, product, regions_ref[x])
         return fpack
 
     fpack = lax.fori_loop(0, planes, plane, jnp.zeros((rows, width), jnp.float32), unroll=4)
@@ -484,33 +499,37 @@
     reach = pltpu.roll(fpack, 1, 1) * mixed
     reach = reach + pltpu.roll(reach, width - 2 * planes, 1) + pltpu.roll(reach, width - 4 * planes, 1)
     reach = time_step * reach * rim_nu
-    product_ref[pl.ds(planes * rows, rows), :] = reach
-    ids_ref[pl.ds(planes * rows, rows), :] = pltpu.roll(mixed, (width - 6 * planes) % width, 1).astype(jnp.int32)
-    region_sums(product_ref, ids_ref, sums_ref)
-
-
-def edge_kernel(
-    sizes, masks, x0_ref, x1_ref, nux_ref, next_ref, regions_ref, sums_ref, fpack_ref, *refs
-):
-    groups, walls = sizes
-    outs, (product_ref, ids_ref, total_ref) = refs[:-3], refs[-3:]
+    add_up(planes, reach, pltpu.roll(mixed, (width - 6 * planes) % width, 1).astype(jnp.int32))
+    sums_ref[...] = region_sums(main_ref[...], rest_ref[...], ones_ref[...], rows)
+
+
+def edge_kernel(groups, masks, x0_ref, x1_ref, nux_ref, next_ref, regions_ref, sums_ref, fpack_ref, *outs):
     _, planes, rows, width = next_ref.shape
+    tops, columns = sums_ref.shape
     low, high = 0.0, 0.0
     for c in range(3):
-        below, above = from_neighbours(lax.axis_index("fluid"), groups, x0_ref[c], x1_ref[c])
+        below, above = beside_of(c, groups, x0_ref, x1_ref)
         low += below * next_ref[c, 0]
         high += above * next_ref[c, planes - 1]
-    product_ref[:rows, :] = time_step * nux_ref[0] * low
-    product_ref[rows:, :] = time_step * nux_ref[planes] * high
-    ids_ref[:rows, :] = regions_ref[0]
-    ids_ref[rows:, :] = regions_ref[planes - 1]
-    region_sums(product_ref, ids_ref, total_ref, sums_ref)
-    per = total_ref.shape[0] // walls
+    ends = [
+        region_rows(time_step * nux_ref[0] * low, regions_ref[0], tops),
+        region_rows(time_step * nux_ref[planes] * high, regions_ref[planes - 1], tops),
+    ]
+    total = sums_ref[...] + region_sums(*(jnp.concatenate(both, axis=1) for both in zip(*ends)), rows)
+    height = tops * (columns // width)
     for mask, out_ref in zip((0,) + masks, outs):
-        target = lax.axis_index("wall") ^ mask
-        out_ref[:per, :] = total_ref[pl.ds(pl.multiple_of(target * per, per), per), :]
-        if out_ref.shape[0] > per:
-            out_ref[per:, :] = fpack_ref[...]
+        for i in range(columns // width):
+            out_ref[i * tops : (i + 1) * tops, :] = total[:, i * width : (i + 1) * width]
+        if mask:
+            out_ref[height : height + rows, :] = fpack_ref[...]
+            if out_ref.shape[0] > height + rows:
+                out_ref[height + rows :, :] = jnp.zeros((out_ref.shape[0] - height - rows, width), jnp.float32)
+
+
+def beside_of(c, groups, x0_ref, x1_ref):
+    return from_neighbours(
+        lax.axis_index("fluid"), groups, x0_ref[c].astype(jnp.float32), x1_ref[c].astype(jnp.float32)
+    )
 
 
 def final_kernel(sizes, inner_ref, x0_ref, x1_ref, nux_ref, rim_ref, own_ref, *refs):
@@ -525,8 +544,8 @@
     above = jnp.zeros((rows, width), jnp.float32)
     for mask, ref in zip(range(1, walls), arrived):
         total = total + ref[:per, :]
-        if ref.shape[0] > per:
-            edges = ref[per:, :]
+        if mask & (mask + 1) == 0:
+            edges = ref[per : per + rows, :]
             above = jnp.where((me ^ mask) == me + 1, edges, above)
             below = jnp.where((me ^ mask) == me - 1, edges, below)
     mixed = mix_edges(below, above, lane)
@@ -535,7 +554,7 @@
     edge_flux = mixed * edge_nu
     on_edge = (lane == 0) | (lane == width - 1)
 
-    beside = [from_neighbours(lax.axis_index("fluid"), groups, x0_ref[c], x1_ref[c]) for c in range(3)]
+    beside = [beside_of(c, groups, x0_ref, x1_ref) for c in range(3)]
     step = planes // sems.shape[0]
 
     def store(i):
@@ -552,10 +571,21 @@
                     value += time_step * nux_ref[planes] * beside[c][1]
                 value_ref[c, x] = value
         store(i).start()
-    sens_ref[...] = sens_scale * lax.dot_general(
-        jnp.ones((8, width), jnp.float32), total, (((1,), (1,)), ((), ())),
-        precision=lax.Precision.HIGHEST, preferred_element_type=jnp.float32,
-    )[:1]
+    parts = width // rows
+    tops = REG_DEV * walls // 8
+    owned = REG_DEV // 8
+    top, _ = iotas(tops, width)
+    region, lane = iotas(REG_DEV, width)
+    sens = jnp.zeros((8, REG_DEV), jnp.float32)
+    for i in range(8 // parts):
+        for h in range(owned):
+            mine = jnp.where(top == me * owned + h, total[i * tops : (i + 1) * tops], 0.0)
+            gather = (region == h * 8 + i * parts + lane // rows).astype(jnp.float32)
+            sens += lax.dot_general(
+                jnp.broadcast_to(jnp.sum(mine, axis=0, keepdims=True), (8, width)), gather, (((1,), (1,)), ((), ())),
+                precision=lax.Precision.HIGHEST, preferred_element_type=jnp.float32,
+            )
+    sens_ref[...] = sens_scale * sens[:1]
     for i in range(sems.shape[0]):
         store(i).wait()
 
@@ -573,14 +603,9 @@
 
     chips = groups // 2
     height = cap * width + extra
-    xs0, xs1 = call(
-        faces_kernel,
-        (f32(4, rows, width), f32(4, rows, width)),
-        [HBM],
-        (flow_state,),
-        (pltpu.SemaphoreType.DMA((2, 4)),),
-        limit=60 * 1024 * 1024,
-    )
+    even = lax.axis_index("fluid") % 2 == 0
+    low, high = flow_state[:, 0], flow_state[:, planes - 1]
+    xs0, xs1 = jnp.where(even, high, low), jnp.where(even, low, high)
     x0, x1 = swap(xs0, "fluid", 0), swap(xs1, "fluid", 1)
     sends = call(
         functools.partial(group_kernel, cap),
@@ -651,34 +676,30 @@
     given = products(1, borrowed, pick)
     other = cross(given, "fluid", 1)
     held = products(0, mine, given)
-    forcing, fs0, fs1 = call(
-        forcing_kernel,
-        (f32(3, planes, rows, width), f32(3, rows, width), f32(3, rows, width)),
-        [VMEM] * 3,
-        (held, other, pick),
-    )
+    fs0, fs1 = call(ends_kernel, (bf16(3, rows, width),) * 2, [VMEM] * 3, (held, other, pick))
     f0, f1 = swap(fs0, "fluid", 0), swap(fs1, "fluid", 1)
+    forcing = call(forcing_kernel, f32(3, planes, rows, width), [VMEM] * 3 + [ANY], (held, other, pick, fs1))
+    tops = reg_count // 8
+    columns = 8 * rows
+    sum_rows = tops * (columns // width)
     inner, fpack, sums = call(
         inner_kernel,
-        (f32(3, planes, rows, width), f32(rows, width), f32(reg_count, width)),
+        (f32(3, planes, rows, width), f32(rows, width), f32(tops, columns)),
         [VMEM] * 9,
         (forcing, velocity, nux, nuy, nuz, nuy0, rim, regions, outside),
-        (pltpu.VMEM(((planes + 1) * rows, width), jnp.float32), pltpu.VMEM(((planes + 1) * rows, width), jnp.int32)),
+        (
+            pltpu.VMEM((tops * rows, (planes + 1) * width), jnp.bfloat16),
+            pltpu.VMEM((tops * rows, (planes + 1) * width), jnp.bfloat16),
+            pltpu.VMEM((columns, (planes + 1) * width), jnp.bfloat16),
+        ),
     )
     masks = tuple(range(1, walls))
-    heights = [REG_DEV] + [REG_DEV + (rows if mask & (mask + 1) == 0 else 0) for mask in masks]
+    heights = [sum_rows] + [sum_rows + rows + 8 * (mask - 1) for mask in masks]
     own, *parts = call(
-        functools.partial(edge_kernel, sizes, masks),
+        functools.partial(edge_kernel, groups, masks),
         tuple(f32(height, width) for height in heights),
         [VMEM] * 7,
         (f0, f1, nux, velocity, regions, sums, fpack),
-        (
-            pltpu.VMEM((2 * rows, width), jnp.float32),
-            pltpu.VMEM((2 * rows, width), jnp.int32),
-            pltpu.VMEM((reg_count, width), jnp.float32),
-        ),
-        flops=20 * grid,
-        moved=4 * grid,
     )
     arrived = [cross(part, "wall", mask) for part, mask in zip(parts, masks)]
     adjoint, sens = call(

time: 42.7 us -> 41.2 us (0.965)
  Pallas kernels: 15.2 us -> 13.2 us
  other arithmetic: 0 us -> 0.97 us
  waiting for transfers between devices: 9.52 us -> 8.99 us
    pallas_call x11, Pallas kernels: 15.2 us -> 13.2 us  [call(): pl.pallas_call(kernel, out_shape=outs, in_specs=ins, out_specs=out_specs...]
    select_n x0 -> x1, other arithmetic: none -> 0.97 us  [body(): xs0, xs1 = (jnp.where(even, high, low), jnp.where(even, low, high))]
    ppermute x8, waiting for transfers between devices: 7.44 us -> 6.91 us  [cross(): lax.ppermute(block, axis, [(i, i ^ mask) for i in range(lax.axis_size(axi...]
  transfers between devices with their start and end apart: 14 -> 14, of which waited for: 5 -> 6; matrix products, arithmetic and copies ran while one was open for 0% -> 0% of each run, Pallas kernels for 24% -> 25%
where the time goes in v4:
time: 41.2 us; the launch traced here: 41 us
  starting transfers between devices  17.1 us (42%)
  Pallas kernels  13.2 us (32%)
  waiting for transfers between devices  8.99 us (22%)
  other arithmetic  0.97 us (2%)
  between operations  0.78 us (2%)
    pallas_call x11, Pallas kernels, call(): pl.pallas_call(kernel, out_shape=outs, in_specs=ins, out_specs=out_specs...  13.2 us
    ppermute x6, starting transfers between devices, swap(): return lax.ppermute(block, ('fluid', 'wall'), pairs)  8.87 us
    ppermute x8, starting transfers between devices, cross(): lax.ppermute(block, axis, [(i, i ^ mask) for i in range(lax.axis_size(axi...  8.2 us
    ppermute x8, waiting for transfers between devices, cross(): lax.ppermute(block, axis, [(i, i ^ mask) for i in range(lax.axis_size(axi...  6.91 us
    ppermute x6, waiting for transfers between devices, swap(): return lax.ppermute(block, ('fluid', 'wall'), pairs)  2.08 us
    select_n x1, other arithmetic, body(): xs0, xs1 = (jnp.where(even, high, low), jnp.where(even, low, high))  0.97 us
  transfers between devices with their start and end apart: 14, of which 6 were waited for; matrix products, arithmetic and copies ran while one was open for 0% of the time, Pallas kernels for 25%

profile of v4, /device:TPU:0, one launch (start us, length us, event | category | flops | bytes accessed | tf_op | source)
XLA Modules:
  0.0 41.0 jit_solution(4603954818868713379)
XLA Ops:
  0.7 1.0 %fusion.1 = (f32[4,32,128]{2,1,0:T(8,128)S(1)}, f32[4,32,128]{2,1,0:T(8,128)S(1)}) fusion(f32[4,16,32,128]{3,2,1,0:T(8,128)} %flow_ref.3, pred[]{:T(512)S(6)} %eq.5), kind=kLoop, calls=%fused_computation.3 | loop fusion | flops 32768 | bytes 262145 | tf_op jit(solution)/shard_map/jit(_where)/select_n | solution.py:608
  1.6 0.5 %collective-permute-start = (f32[4,32,128]{2,1,0:T(8,128)S(1)}, f32[4,32,128]{2,1,0:T(8,128)S(1)}, u32[]{:S(2)}, u32[]{:S(2)}) collective-permute-start(f32[4,32,128]{2,1,0:T(8,128)S(1)} %get-tuple-element.69), channel_id=1, source_target_pairs={{0,4},{1,5},{2,6},{3,7},{4,0},{5,1},{6,2},{7,3},{8,12},{9,13},{10,... | collective-permute-start | bytes 196616 | tf_op jit(solution)/shard_map/ppermute | solution.py:59
  2.2 3.6 %collective-permute-start.1 = (f32[4,32,128]{2,1,0:T(8,128)S(1)}, f32[4,32,128]{2,1,0:T(8,128)S(1)}, u32[]{:S(2)}, u32[]{:S(2)}) collective-permute-start(f32[4,32,128]{2,1,0:T(8,128)S(1)} %get-tuple-element.70.after_ref), channel_id=1, source_target_pairs={{0,28},{1,29},{2,30},{3,31},{4,8},{5,9},{6,10},{7,11},{8,4},{9,5},... | collective-permute-start | bytes 196616 | tf_op jit(solution)/shard_map/ppermute | solution.py:59
  5.7 2.6 %shard_map.85 = (bf16[2,528,128]{2,1,0:T(8,128)(2,1)}, bf16[2,528,128]{2,1,0:T(8,128)(2,1)}, bf16[2,528,128]{2,1,0:T(8,128)(2,1)}, bf16[2,528,128]{2,1,0:T(8,128)(2,1)}) custom-call(s32[32]{0:T(128)} %bitcast.26, bf16[32,128,128]{2,1,0:T(8,128)(2,1)} %bitcast.24, bf16[3,32,128]{2,1,0:T(8,128)(2,1)} %bitcast.25, f32[4,32,128]{2,1,0:T(8,128)} %copy-done.4), custom_call_target="tpu_custom_call" | custom-call | flops 1 | bytes 1 | tf_op jit(solution)/shard_map/pallas_call | solution.py:26
  8.4 1.7 %collective-permute-start.6 = (bf16[2,528,128]{2,1,0:T(8,128)(2,1)}, bf16[2,528,128]{2,1,0:T(8,128)(2,1)S(1)}, u32[]{:S(2)}, u32[]{:S(2)}) collective-permute-start(bf16[2,528,128]{2,1,0:T(8,128)(2,1)} %get-tuple-element.50), channel_id=1, source_target_pairs={{0,16},{4,20},{8,24},{12,28},{16,0},{20,4},{24,8},{28,12},{1,17},{... | collective-permute-start | bytes 811016 | tf_op jit(solution)/shard_map/ppermute | solution.py:63
  10.1 1.7 %collective-permute-start.7 = (bf16[2,528,128]{2,1,0:T(8,128)(2,1)}, bf16[2,528,128]{2,1,0:T(8,128)(2,1)S(1)}, u32[]{:S(2)}, u32[]{:S(2)}) collective-permute-start(bf16[2,528,128]{2,1,0:T(8,128)(2,1)} %get-tuple-element.51), channel_id=1, source_target_pairs={{0,24},{4,28},{8,16},{12,20},{16,8},{20,12},{24,0},{28,4},{1,25},{... | collective-permute-start | bytes 811016 | tf_op jit(solution)/shard_map/ppermute | solution.py:63
  11.9 0.7 %shard_map.86.edges_ref = f32[3,32,128]{2,1,0:T(8,128)S(1)} custom-call(f32[4,16,32,128]{3,2,1,0:T(8,128)S(1)} %copy-done, s32[16,32,128]{2,1,0:T(8,128)S(1)} %copy-done.1, f32[4,32,128]{2,1,0:T(8,128)S(1)} %collective-permute-done.x0_ref, f32[4,32,128]{2,1,0:T(8,128)S(1)} %collective-permute-done.1.x1_ref), custom_call_target="tpu_custom_call" | custom-call | flops 1 | bytes 1 | tf_op jit(solution)/shard_map/pallas_call | solution.py:26
  12.7 3.1 %collective-permute-start.2 = (f32[3,32,128]{2,1,0:T(8,128)S(1)}, f32[3,32,128]{2,1,0:T(8,128)S(1)}, u32[]{:S(2)}, u32[]{:S(2)}) collective-permute-start(f32[3,32,128]{2,1,0:T(8,128)S(1)} %shard_map.86.edges_ref), channel_id=1, source_target_pairs={{0,1},{1,0},{2,3},{3,2},{4,5},{5,4},{6,7},{7,6},{8,9},{9,8},{10,11... | collective-permute-start | bytes 147464 | tf_op jit(solution)/shard_map/ppermute | solution.py:59
  15.9 2.1 %collective-permute-done.2.z0_ref = f32[3,32,128]{2,1,0:T(8,128)S(1)} collective-permute-done((f32[3,32,128]{2,1,0:T(8,128)S(1)}, f32[3,32,128]{2,1,0:T(8,128)S(1)}, u32[]{:S(2)}, u32[]{:S(2)}) %collective-permute-start.2) | collective-permute-done | bytes 49184 | tf_op jit(solution)/shard_map/ppermute | solution.py:59
  17.9 2.6 %shard_map.87 = (f32[3,16,32,128]{3,2,1,0:T(8,128)}, f32[3,16,32,128]{3,2,1,0:T(8,128)S(1)}, f32[17,32,128]{2,1,0:T(8,128)S(1)}, f32[16,32,128]{2,1,0:T(8,128)S(...) custom-call(s32[4,8]{1,0:T(4,128)S(1)} %bitcast.23, ...), custom_call_target="tpu_custom_call" | custom-call | flops 1 | bytes 1 | tf_op jit(solution)/shard_map/pallas_call | solution.py:26
  20.6 0.5 %shard_map.88 = (f32[32,128]{1,0:T(8,128)S(1)}, bf16[3,512,128]{2,1,0:T(8,128)(2,1)S(1)}) custom-call(s32[8,128]{1,0:T(8,128)S(1)} %get-tuple-element.45.cells_of_ref, f32[3,32,128]{2,1,0:T(8,128)S(1)} %collective-permute-done.2.z0_ref, f32[3,32,128]{2,1,0:T(8,128)S(1)} %collective-permute-done.3.z1_ref, f32[3,32,128]{2,1,0:T(8,128)S(1)} %shard_map.86.edges_ref, ...), custom_call_target="tpu_custom_call" | custom-call | flops 1 | bytes 1 | tf_op jit(solution)/shard_map/pallas_call | solution.py:26
  21.1 0.7 %collective-permute-done.4.values_ref = bf16[4,16,128]{2,1,0:T(8,128)(2,1)S(1)} collective-permute-done((bf16[4,16,128]{2,1,0:T(8,128)(2,1)S(1)}, bf16[4,16,128]{2,1,0:T(8,128)(2,1)S(1)}, u32[]{:S(2)}, u32[]{:S(2)}) %collective-permute-start.4) | collective-permute-done | bytes 16416 | tf_op jit(solution)/shard_map/ppermute | solution.py:63
  21.8 1.9 %collective-permute-done.6.refs_2_ = bf16[2,528,128]{2,1,0:T(8,128)(2,1)S(1)} collective-permute-done((bf16[2,528,128]{2,1,0:T(8,128)(2,1)}, bf16[2,528,128]{2,1,0:T(8,128)(2,1)S(1)}, u32[]{:S(2)}, u32[]{:S(2)}) %collective-permute-start.6) | collective-permute-done | bytes 270368 | tf_op jit(solution)/shard_map/ppermute | solution.py:63
  23.7 0.7 %shard_map.89.after_ref = bf16[2,64,128]{2,1,0:T(8,128)(2,1)S(1)} custom-call(bf16[4,16,128]{2,1,0:T(8,128)(2,1)S(1)} %collective-permute-done.4.values_ref, bf16[3,512,128]{2,1,0:T(8,128)(2,1)S(1)} %get-tuple-element.47.after_ref.pick_ref, bf16[2,528,128]{2,1,0:T(8,128)(2,1)S(1)} %copy-done.2, bf16[2,528,128]{2,1,0:T(8,128)(2,1)S(1)} %collective-permute-done.5.refs_1_, ...), custom_call_target="tpu_custom_call" | custom-call | flops 1 | bytes 1 | tf_op jit(solution)/shard_map/pallas_call | solution.py:26
  24.5 0.7 %shard_map.90.mine_ref = bf16[2,64,128]{2,1,0:T(8,128)(2,1)S(1)} custom-call(bf16[4,16,128]{2,1,0:T(8,128)(2,1)S(1)} %get-tuple-element.43.values_ref, bf16[2,64,128]{2,1,0:T(8,128)(2,1)S(1)} %shard_map.89.after_ref, bf16[2,528,128]{2,1,0:T(8,128)(2,1)S(1)} %copy-done.2, bf16[2,528,128]{2,1,0:T(8,128)(2,1)S(1)} %collective-permute-done.5.refs_1_, ...), custom_call_target="tpu_custom_call" | custom-call | flops 1 | bytes 1 | tf_op jit(solution)/shard_map/pallas_call | solution.py:26
  25.3 0.4 collective-permute-done.8.other_ref
  26.1 1.4 %collective-permute-start.10 = (bf16[3,32,128]{2,1,0:T(8,128)(2,1)S(1)}, bf16[3,32,128]{2,1,0:T(8,128)(2,1)S(1)}, u32[]{:S(2)}, u32[]{:S(2)}) collective-permute-start(bf16[3,32,128]{2,1,0:T(8,128)(2,1)S(1)} %get-tuple-element.52.after_ref), channel_id=1, source_target_pairs={{0,28},{1,29},{2,30},{3,31},{4,8},{5,9},{6,10},{7,11},{8,4},{9,5},... | collective-permute-start | bytes 73736 | tf_op jit(solution)/shard_map/ppermute | solution.py:59
  27.5 0.6 %shard_map.92.forcing_ref = f32[3,16,32,128]{3,2,1,0:T(8,128)S(1)} custom-call(bf16[2,64,128]{2,1,0:T(8,128)(2,1)S(1)} %shard_map.90.mine_ref, bf16[2,64,128]{2,1,0:T(8,128)(2,1)S(1)} %collective-permute-done.8.other_ref, bf16[3,512,128]{2,1,0:T(8,128)(2,1)S(1)} %get-tuple-element.47.after_ref.pick_ref, bf16[3,32,128]{2,1,0:T(8,128)(2,1)S(1)} %get-tuple-element.52.after_ref), custom_call_target="tpu_custom_call" | custom-call | flops 1 | bytes 1 | tf_op jit(solution)/shard_map/pallas_call | solution.py:26
  28.1 2.5 %shard_map.93 = (f32[3,16,32,128]{3,2,1,0:T(8,128)S(1)}, f32[32,128]{1,0:T(8,128)S(1)}, f32[8,256]{1,0:T(8,128)S(1)}) custom-call(f32[3,16,32,128]{3,2,1,0:T(8,128)S(1)} %shard_map.92.forcing_ref, f32[3,16,32,128]{3,2,1,0:T(8,128)S(1)} %get-tuple-element.53.next_ref, f32[17,32,128]{2,1,0:T(8,128)S(1)} %get-tuple-element.54.nux_ref, ...), custom_call_target="tpu_custom_call" | custom-call | flops 1 | bytes 1 | tf_op jit(solution)/shard_map/pallas_call | solution.py:26
  30.9 3.7 %collective-permute-start.13 = (f32[64,128]{1,0:T(8,128)S(1)}, f32[64,128]{1,0:T(8,128)S(1)}, u32[]{:S(2)}, u32[]{:S(2)}) collective-permute-start(f32[64,128]{1,0:T(8,128)S(1)} %get-tuple-element.66), channel_id=1, source_target_pairs={{0,3},{1,2},{2,1},{3,0},{4,7},{5,6},{6,5},{7,4},{8,11},{9,10},{10,... | collective-permute-start | bytes 98312 | tf_op jit(solution)/shard_map/ppermute | solution.py:63
  34.6 0.8 %collective-permute-start.11 = (f32[48,128]{1,0:T(8,128)S(1)}, f32[48,128]{1,0:T(8,128)S(1)}, u32[]{:S(2)}, u32[]{:S(2)}) collective-permute-start(f32[48,128]{1,0:T(8,128)S(1)} %get-tuple-element.64), channel_id=1, source_target_pairs={{0,1},{1,0},{2,3},{3,2},{4,5},{5,4},{6,7},{7,6},{8,9},{9,8},{10,11... | collective-permute-start | bytes 73736 | tf_op jit(solution)/shard_map/ppermute | solution.py:63
  35.4 3.0 %collective-permute-done.11.refs_0_ = f32[48,128]{1,0:T(8,128)S(1)} collective-permute-done((f32[48,128]{1,0:T(8,128)S(1)}, f32[48,128]{1,0:T(8,128)S(1)}, u32[]{:S(2)}, u32[]{:S(2)}) %collective-permute-start.11) | collective-permute-done | bytes 24608 | tf_op jit(solution)/shard_map/ppermute | solution.py:63
  38.4 0.9 %collective-permute-done.12.refs_1_ = f32[56,128]{1,0:T(8,128)S(1)} collective-permute-done((f32[56,128]{1,0:T(8,128)S(1)}, f32[56,128]{1,0:T(8,128)S(1)}, u32[]{:S(2)}, u32[]{:S(2)}) %collective-permute-start.12) | collective-permute-done | bytes 28704 | tf_op jit(solution)/shard_map/ppermute | solution.py:63
  39.4 1.6 %shard_map.95 = (f32[3,16,32,128]{3,2,1,0:T(8,128)}, f32[1,16]{1,0:T(1,128)}) custom-call(f32[3,16,32,128]{3,2,1,0:T(8,128)S(1)} %get-tuple-element.59.inner_ref, bf16[3,32,128]{2,1,0:T(8,128)(2,1)S(1)} %collective-permute-done.9.x0_ref, bf16[3,32,128]{2,1,0:T(8,128)(2,1)S(1)} %collective-permute-done.10.x1_ref, ...), custom_call_target="tpu_custom_call" | custom-call | flops 655360 | bytes 1572864 | tf_op jit(solution)/shard_map/pallas_call | solution.py:26
  (26 shorter events, 1.2 us)
Async XLA Ops:
  0.6 11.3 %copy-start = (f32[4,16,32,128]{3,2,1,0:T(8,128)S(1)}, f32[4,16,32,128]{3,2,1,0:T(8,128)}, u32[]{:S(2)}) copy-start(f32[4,16,32,128]{3,2,1,0:T(8,128)} %flow_ref.3) | copy-start | bytes 3145732
  1.6 4.1 %copy-start.4 = (f32[4,32,128]{2,1,0:T(8,128)}, f32[4,32,128]{2,1,0:T(8,128)S(1)}, u32[]{:S(2)}) copy-start(f32[4,32,128]{2,1,0:T(8,128)S(1)} %get-tuple-element.70.after_ref) | copy-start | bytes 196612
  1.6 6.7 %collective-permute-start = (f32[4,32,128]{2,1,0:T(8,128)S(1)}, f32[4,32,128]{2,1,0:T(8,128)S(1)}, u32[]{:S(2)}, u32[]{:S(2)}) collective-permute-start(f32[4,32,128]{2,1,0:T(8,128)S(1)} %get-tuple-element.69), channel_id=1, source_target_pairs={{0,4},{1,5},{2,6},{3,7},{4,0},{5,1},{6,2},{7,3},{8,12},{9,13},{10,... | collective-permute-start | bytes 196616 | tf_op jit(solution)/shard_map/ppermute | solution.py:59
  2.2 6.2 %collective-permute-start.1 = (f32[4,32,128]{2,1,0:T(8,128)S(1)}, f32[4,32,128]{2,1,0:T(8,128)S(1)}, u32[]{:S(2)}, u32[]{:S(2)}) collective-permute-start(f32[4,32,128]{2,1,0:T(8,128)S(1)} %get-tuple-element.70.after_ref), channel_id=1, source_target_pairs={{0,28},{1,29},{2,30},{3,31},{4,8},{5,9},{6,10},{7,11},{8,4},{9,5},... | collective-permute-start | bytes 196616 | tf_op jit(solution)/shard_map/ppermute | solution.py:59
  5.7 6.2 %copy-start.1 = (s32[16,32,128]{2,1,0:T(8,128)S(1)}, s32[16,32,128]{2,1,0:T(8,128)}, u32[]{:S(2)}) copy-start(s32[16,32,128]{2,1,0:T(8,128)} %regions_ref.5) | copy-start | bytes 786436
  8.3 13.5 %collective-permute-start.5 = (bf16[2,528,128]{2,1,0:T(8,128)(2,1)}, bf16[2,528,128]{2,1,0:T(8,128)(2,1)S(1)}, u32[]{:S(2)}, u32[]{:S(2)}) collective-permute-start(bf16[2,528,128]{2,1,0:T(8,128)(2,1)} %get-tuple-element.49), channel_id=1, source_target_pairs={{0,8},{4,12},{8,0},{12,4},{16,24},{20,28},{24,16},{28,20},{1,9},{5... | collective-permute-start | bytes 811016 | tf_op jit(solution)/shard_map/ppermute | solution.py:63
  8.4 15.3 %collective-permute-start.6 = (bf16[2,528,128]{2,1,0:T(8,128)(2,1)}, bf16[2,528,128]{2,1,0:T(8,128)(2,1)S(1)}, u32[]{:S(2)}, u32[]{:S(2)}) collective-permute-start(bf16[2,528,128]{2,1,0:T(8,128)(2,1)} %get-tuple-element.50), channel_id=1, source_target_pairs={{0,16},{4,20},{8,24},{12,28},{16,0},{20,4},{24,8},{28,12},{1,17},{... | collective-permute-start | bytes 811016 | tf_op jit(solution)/shard_map/ppermute | solution.py:63
  10.1 13.5 %collective-permute-start.7 = (bf16[2,528,128]{2,1,0:T(8,128)(2,1)}, bf16[2,528,128]{2,1,0:T(8,128)(2,1)S(1)}, u32[]{:S(2)}, u32[]{:S(2)}) collective-permute-start(bf16[2,528,128]{2,1,0:T(8,128)(2,1)} %get-tuple-element.51), channel_id=1, source_target_pairs={{0,24},{4,28},{8,16},{12,20},{16,8},{20,12},{24,0},{28,4},{1,25},{... | collective-permute-start | bytes 811016 | tf_op jit(solution)/shard_map/ppermute | solution.py:63
  11.9 6.0 %copy-start.3 = (s32[1,1,8,4]{2,3,1,0:T(4,128)S(1)}, s32[1,1,8,4]{2,3,1,0:T(4,128)}, u32[]{:S(2)}) copy-start(s32[1,1,8,4]{2,3,1,0:T(4,128)} %param.11) | copy-start | bytes 388
  12.6 3.2 %collective-permute-start.3 = (f32[3,32,128]{2,1,0:T(8,128)S(1)}, f32[3,32,128]{2,1,0:T(8,128)S(1)}, u32[]{:S(2)}, u32[]{:S(2)}) collective-permute-start(f32[3,32,128]{2,1,0:T(8,128)S(1)} %shard_map.86.edges_ref), channel_id=1, source_target_pairs={{0,4},{1,2},{2,1},{3,7},{4,0},{5,6},{6,5},{7,3},{8,12},{9,10},{10,... | collective-permute-start | bytes 147464 | tf_op jit(solution)/shard_map/ppermute | solution.py:59
  12.7 5.2 %collective-permute-start.2 = (f32[3,32,128]{2,1,0:T(8,128)S(1)}, f32[3,32,128]{2,1,0:T(8,128)S(1)}, u32[]{:S(2)}, u32[]{:S(2)}) collective-permute-start(f32[3,32,128]{2,1,0:T(8,128)S(1)} %shard_map.86.edges_ref), channel_id=1, source_target_pairs={{0,1},{1,0},{2,3},{3,2},{4,5},{5,4},{6,7},{7,6},{8,9},{9,8},{10,11... | collective-permute-start | bytes 147464 | tf_op jit(solution)/shard_map/ppermute | solution.py:59
  17.9 5.8 %copy-start.2 = (bf16[2,528,128]{2,1,0:T(8,128)(2,1)S(1)}, bf16[2,528,128]{2,1,0:T(8,128)(2,1)}, u32[]{:S(2)}) copy-start(bf16[2,528,128]{2,1,0:T(8,128)(2,1)} %get-tuple-element.48.refs_0_) | copy-start | bytes 811012
  20.6 1.2 %collective-permute-start.4 = (bf16[4,16,128]{2,1,0:T(8,128)(2,1)S(1)}, bf16[4,16,128]{2,1,0:T(8,128)(2,1)S(1)}, u32[]{:S(2)}, u32[]{:S(2)}) collective-permute-start(bf16[4,16,128]{2,1,0:T(8,128)(2,1)S(1)} %get-tuple-element.44), channel_id=1, source_target_pairs={{0,4},{4,0},{8,12},{12,8},{16,20},{20,16},{24,28},{28,24},{1,5},{5... | collective-permute-start | bytes 49160 | tf_op jit(solution)/shard_map/ppermute | solution.py:63
  24.4 1.2 %collective-permute-start.8 = (bf16[2,64,128]{2,1,0:T(8,128)(2,1)S(1)}, bf16[2,64,128]{2,1,0:T(8,128)(2,1)S(1)}, u32[]{:S(2)}, u32[]{:S(2)}) collective-permute-start(bf16[2,64,128]{2,1,0:T(8,128)(2,1)S(1)} %shard_map.89.after_ref), channel_id=1, source_target_pairs={{0,4},{4,0},{8,12},{12,8},{16,20},{20,16},{24,28},{28,24},{1,5},{5... | collective-permute-start | bytes 98312 | tf_op jit(solution)/shard_map/ppermute | solution.py:63
  25.9 4.7 %collective-permute-start.9 = (bf16[3,32,128]{2,1,0:T(8,128)(2,1)S(1)}, bf16[3,32,128]{2,1,0:T(8,128)(2,1)S(1)}, u32[]{:S(2)}, u32[]{:S(2)}) collective-permute-start(bf16[3,32,128]{2,1,0:T(8,128)(2,1)S(1)} %get-tuple-element.60), channel_id=1, source_target_pairs={{0,4},{1,5},{2,6},{3,7},{4,0},{5,1},{6,2},{7,3},{8,12},{9,13},{10,... | collective-permute-start | bytes 73736 | tf_op jit(solution)/shard_map/ppermute | solution.py:59
  26.1 4.5 %collective-permute-start.10 = (bf16[3,32,128]{2,1,0:T(8,128)(2,1)S(1)}, bf16[3,32,128]{2,1,0:T(8,128)(2,1)S(1)}, u32[]{:S(2)}, u32[]{:S(2)}) collective-permute-start(bf16[3,32,128]{2,1,0:T(8,128)(2,1)S(1)} %get-tuple-element.52.after_ref), channel_id=1, source_target_pairs={{0,28},{1,29},{2,30},{3,31},{4,8},{5,9},{6,10},{7,11},{8,4},{9,5},... | collective-permute-start | bytes 73736 | tf_op jit(solution)/shard_map/ppermute | solution.py:59
  30.9 8.4 %collective-permute-start.13 = (f32[64,128]{1,0:T(8,128)S(1)}, f32[64,128]{1,0:T(8,128)S(1)}, u32[]{:S(2)}, u32[]{:S(2)}) collective-permute-start(f32[64,128]{1,0:T(8,128)S(1)} %get-tuple-element.66), channel_id=1, source_target_pairs={{0,3},{1,2},{2,1},{3,0},{4,7},{5,6},{6,5},{7,4},{8,11},{9,10},{10,... | collective-permute-start | bytes 98312 | tf_op jit(solution)/shard_map/ppermute | solution.py:63
  34.6 4.8 %collective-permute-start.12 = (f32[56,128]{1,0:T(8,128)S(1)}, f32[56,128]{1,0:T(8,128)S(1)}, u32[]{:S(2)}, u32[]{:S(2)}) collective-permute-start(f32[56,128]{1,0:T(8,128)S(1)} %get-tuple-element.65), channel_id=1, source_target_pairs={{0,2},{1,3},{2,0},{3,1},{4,6},{5,7},{6,4},{7,5},{8,10},{9,11},{10,... | collective-permute-start | bytes 86024 | tf_op jit(solution)/shard_map/ppermute | solution.py:63
  34.6 3.8 %collective-permute-start.11 = (f32[48,128]{1,0:T(8,128)S(1)}, f32[48,128]{1,0:T(8,128)S(1)}, u32[]{:S(2)}, u32[]{:S(2)}) collective-permute-start(f32[48,128]{1,0:T(8,128)S(1)} %get-tuple-element.64), channel_id=1, source_target_pairs={{0,1},{1,0},{2,3},{3,2},{4,5},{5,4},{6,7},{7,6},{8,9},{9,8},{10,11... | collective-permute-start | bytes 73736 | tf_op jit(solution)/shard_map/ppermute | solution.py:63

commit v5 on v4

--- a/solution.py
+++ b/solution.py
@@ -20,6 +20,7 @@
 ANY = pl.BlockSpec(memory_space=pl.ANY)
 HBM = pl.BlockSpec(memory_space=pltpu.HBM)
 LIMIT = 24 * 1024 * 1024
+HIDES = 100_000_000_000
 
 
 def call(kernel, outs, ins, operands, scratch=(), flops=1, moved=1, out_specs=None, limit=LIMIT):
@@ -46,10 +47,11 @@
     groups, walls = lax.axis_size("fluid"), lax.axis_size("wall")
 
     def partner(f, w):
+        at, count = (f, groups) if axis == "fluid" else (w, walls)
+        other = at + 1 if (at + turn) % 2 == 0 else at - 1
         if axis == "fluid":
-            return (f + 1 if (f + turn) % 2 == 0 else f - 1) % groups, w
-        other = w + 1 if (w + turn) % 2 == 0 else w - 1
-        return (f, other) if 0 <= other < walls else (f ^ 1, w)
+            return (other, w) if 0 <= other < count else (f, w ^ 1)
+        return (f, other) if 0 <= other < count else (f ^ 1, w)
 
     pairs = []
     for f in range(groups):
@@ -629,13 +631,13 @@
         out_specs=(HBM,) * chips,
         limit=60 * 1024 * 1024,
     )
-    *sends, x0, x1 = lax.optimization_barrier((*sends, x0, x1))
     recvs = [sends[0]] + [cross(sends[m], "fluid", 2 * m) for m in range(1, chips)]
     zs = call(
         functools.partial(edges_kernel, groups),
         f32(3, rows, width),
         [VMEM] * 4,
         (flow_state, regions, x0, x1),
+        flops=HIDES,
     )
     z0, z1 = swap(zs, "wall", 0), swap(zs, "wall", 1)
     slot_rows = groups * extra

time: 41.2 us -> 40.1 us (0.973)
  starting transfers between devices: 17.1 us -> 16.3 us
    ppermute x6, starting transfers between devices: 8.87 us -> 8.18 us  [swap(): return lax.ppermute(block, ('fluid', 'wall'), pairs)]
  transfers between devices with their start and end apart: 14 -> 14, of which waited for: 6 -> 6; matrix products, arithmetic and copies ran while one was open for 0% -> 0% of each run, Pallas kernels for 25% -> 26%
where the time goes in v5:
time: 40.1 us; the launch traced here: 39.9 us
  starting transfers between devices  16.3 us (41%)
  Pallas kernels  13.2 us (33%)
  waiting for transfers between devices  8.73 us (22%)
  other arithmetic  0.97 us (2%)
  between operations  0.78 us (2%)
    pallas_call x11, Pallas kernels, call(): pl.pallas_call(kernel, out_shape=outs, in_specs=ins, out_specs=out_specs...  13.2 us
    ppermute x6, starting transfers between devices, swap(): return lax.ppermute(block, ('fluid', 'wall'), pairs)  8.18 us
    ppermute x8, starting transfers between devices, cross(): lax.ppermute(block, axis, [(i, i ^ mask) for i in range(lax.axis_size(axi...  8.08 us
    ppermute x8, waiting for transfers between devices, cross(): lax.ppermute(block, axis, [(i, i ^ mask) for i in range(lax.axis_size(axi...  6.65 us
    ppermute x6, waiting for transfers between devices, swap(): return lax.ppermute(block, ('fluid', 'wall'), pairs)  2.08 us
    select_n x1, other arithmetic, body(): xs0, xs1 = (jnp.where(even, high, low), jnp.where(even, low, high))  0.97 us
  transfers between devices with their start and end apart: 14, of which 6 were waited for; matrix products, arithmetic and copies ran while one was open for 0% of the time, Pallas kernels for 26%

profile of v5, /device:TPU:0, one launch (start us, length us, event | category | flops | bytes accessed | tf_op | source)
XLA Modules:
  0.0 39.9 jit_solution(5384070278154261560)
XLA Ops:
  0.7 1.0 %fusion.1 = (f32[4,32,128]{2,1,0:T(8,128)S(1)}, f32[4,32,128]{2,1,0:T(8,128)S(1)}) fusion(f32[4,16,32,128]{3,2,1,0:T(8,128)} %flow_ref.3, pred[]{:T(512)S(6)} %eq.5), kind=kLoop, calls=%fused_computation.3 | loop fusion | flops 32768 | bytes 262145 | tf_op jit(solution)/shard_map/jit(_where)/select_n | solution.py:610
  1.6 0.5 %collective-permute-start = (f32[4,32,128]{2,1,0:T(8,128)S(1)}, f32[4,32,128]{2,1,0:T(8,128)S(1)}, u32[]{:S(2)}, u32[]{:S(2)}) collective-permute-start(f32[4,32,128]{2,1,0:T(8,128)S(1)} %get-tuple-element.58), channel_id=1, source_target_pairs={{0,4},{1,5},{2,6},{3,7},{4,0},{5,1},{6,2},{7,3},{8,12},{9,13},{10,... | collective-permute-start | bytes 196616 | tf_op jit(solution)/shard_map/ppermute | solution.py:61
  2.2 2.6 %collective-permute-start.1 = (f32[4,32,128]{2,1,0:T(8,128)S(1)}, f32[4,32,128]{2,1,0:T(8,128)S(1)}, u32[]{:S(2)}, u32[]{:S(2)}) collective-permute-start(f32[4,32,128]{2,1,0:T(8,128)S(1)} %get-tuple-element.57.after_ref), channel_id=1, source_target_pairs={{0,1},{1,0},{2,3},{3,2},{4,8},{5,9},{6,10},{7,11},{8,4},{9,5},{10,... | collective-permute-start | bytes 196616 | tf_op jit(solution)/shard_map/ppermute | solution.py:61
  4.8 2.6 %shard_map.88 = (bf16[2,528,128]{2,1,0:T(8,128)(2,1)}, bf16[2,528,128]{2,1,0:T(8,128)(2,1)}, bf16[2,528,128]{2,1,0:T(8,128)(2,1)}, bf16[2,528,128]{2,1,0:T(8,128)(2,1)}) custom-call(s32[32]{0:T(128)} %bitcast.26, bf16[32,128,128]{2,1,0:T(8,128)(2,1)} %bitcast.24, bf16[3,32,128]{2,1,0:T(8,128)(2,1)} %bitcast.25, f32[4,32,128]{2,1,0:T(8,128)} %copy-done.4), custom_call_target="tpu_custom_call" | custom-call | flops 1 | bytes 1 | tf_op jit(solution)/shard_map/pallas_call | solution.py:27
  7.9 1.6 %collective-permute-start.6 = (bf16[2,528,128]{2,1,0:T(8,128)(2,1)}, bf16[2,528,128]{2,1,0:T(8,128)(2,1)S(1)}, u32[]{:S(2)}, u32[]{:S(2)}) collective-permute-start(bf16[2,528,128]{2,1,0:T(8,128)(2,1)} %get-tuple-element.38), channel_id=1, source_target_pairs={{0,16},{4,20},{8,24},{12,28},{16,0},{20,4},{24,8},{28,12},{1,17},{... | collective-permute-start | bytes 811016 | tf_op jit(solution)/shard_map/ppermute | solution.py:65
  9.5 1.5 %collective-permute-start.7 = (bf16[2,528,128]{2,1,0:T(8,128)(2,1)}, bf16[2,528,128]{2,1,0:T(8,128)(2,1)S(1)}, u32[]{:S(2)}, u32[]{:S(2)}) collective-permute-start(bf16[2,528,128]{2,1,0:T(8,128)(2,1)} %get-tuple-element.39), channel_id=1, source_target_pairs={{0,24},{4,28},{8,16},{12,20},{16,8},{20,12},{24,0},{28,4},{1,25},{... | collective-permute-start | bytes 811016 | tf_op jit(solution)/shard_map/ppermute | solution.py:65
  11.0 0.7 %shard_map.85.edges_ref = f32[3,32,128]{2,1,0:T(8,128)S(1)} custom-call(f32[4,16,32,128]{3,2,1,0:T(8,128)S(1)} %copy-done, s32[16,32,128]{2,1,0:T(8,128)S(1)} %copy-done.2, f32[4,32,128]{2,1,0:T(8,128)S(1)} %collective-permute-done.x0_ref, f32[4,32,128]{2,1,0:T(8,128)S(1)} %collective-permute-done.1.x1_ref), custom_call_target="tpu_custom_call" | custom-call | flops 99999997952 | bytes 1 | tf_op jit(solution)/shard_map/pallas_call | solution.py:27
  11.8 3.1 %collective-permute-start.2 = (f32[3,32,128]{2,1,0:T(8,128)S(1)}, f32[3,32,128]{2,1,0:T(8,128)S(1)}, u32[]{:S(2)}, u32[]{:S(2)}) collective-permute-start(f32[3,32,128]{2,1,0:T(8,128)S(1)} %shard_map.85.edges_ref), channel_id=1, source_target_pairs={{0,1},{1,0},{2,3},{3,2},{4,5},{5,4},{6,7},{7,6},{8,9},{9,8},{10,11... | collective-permute-start | bytes 147464 | tf_op jit(solution)/shard_map/ppermute | solution.py:61
  15.0 2.1 %collective-permute-done.2.z0_ref = f32[3,32,128]{2,1,0:T(8,128)S(1)} collective-permute-done((f32[3,32,128]{2,1,0:T(8,128)S(1)}, f32[3,32,128]{2,1,0:T(8,128)S(1)}, u32[]{:S(2)}, u32[]{:S(2)}) %collective-permute-start.2) | collective-permute-done | bytes 49184 | tf_op jit(solution)/shard_map/ppermute | solution.py:61
  17.0 2.6 %shard_map.86 = (f32[3,16,32,128]{3,2,1,0:T(8,128)}, f32[3,16,32,128]{3,2,1,0:T(8,128)S(1)}, f32[17,32,128]{2,1,0:T(8,128)S(1)}, f32[16,32,128]{2,1,0:T(8,128)S(...) custom-call(s32[4,8]{1,0:T(4,128)S(1)} %bitcast.23, ...), custom_call_target="tpu_custom_call" | custom-call | flops 1 | bytes 1 | tf_op jit(solution)/shard_map/pallas_call | solution.py:27
  19.7 0.5 %shard_map.87 = (f32[32,128]{1,0:T(8,128)S(1)}, bf16[3,512,128]{2,1,0:T(8,128)(2,1)S(1)}) custom-call(s32[8,128]{1,0:T(8,128)S(1)} %get-tuple-element.33.cells_of_ref, f32[3,32,128]{2,1,0:T(8,128)S(1)} %collective-permute-done.2.z0_ref, f32[3,32,128]{2,1,0:T(8,128)S(1)} %collective-permute-done.3.z1_ref, f32[3,32,128]{2,1,0:T(8,128)S(1)} %shard_map.85.edges_ref, ...), custom_call_target="tpu_custom_call" | custom-call | flops 1 | bytes 1 | tf_op jit(solution)/shard_map/pallas_call | solution.py:27
  20.2 0.7 %collective-permute-done.4.values_ref = bf16[4,16,128]{2,1,0:T(8,128)(2,1)S(1)} collective-permute-done((bf16[4,16,128]{2,1,0:T(8,128)(2,1)S(1)}, bf16[4,16,128]{2,1,0:T(8,128)(2,1)S(1)}, u32[]{:S(2)}, u32[]{:S(2)}) %collective-permute-start.4) | collective-permute-done | bytes 16416 | tf_op jit(solution)/shard_map/ppermute | solution.py:65
  20.9 2.2 %collective-permute-done.6.refs_2_ = bf16[2,528,128]{2,1,0:T(8,128)(2,1)S(1)} collective-permute-done((bf16[2,528,128]{2,1,0:T(8,128)(2,1)}, bf16[2,528,128]{2,1,0:T(8,128)(2,1)S(1)}, u32[]{:S(2)}, u32[]{:S(2)}) %collective-permute-start.6) | collective-permute-done | bytes 270368 | tf_op jit(solution)/shard_map/ppermute | solution.py:65
  23.1 0.7 %shard_map.89.after_ref = bf16[2,64,128]{2,1,0:T(8,128)(2,1)S(1)} custom-call(bf16[4,16,128]{2,1,0:T(8,128)(2,1)S(1)} %collective-permute-done.4.values_ref, bf16[3,512,128]{2,1,0:T(8,128)(2,1)S(1)} %get-tuple-element.35.after_ref.pick_ref, bf16[2,528,128]{2,1,0:T(8,128)(2,1)S(1)} %copy-done.1, bf16[2,528,128]{2,1,0:T(8,128)(2,1)S(1)} %collective-permute-done.5.refs_1_, ...), custom_call_target="tpu_custom_call" | custom-call | flops 1 | bytes 1 | tf_op jit(solution)/shard_map/pallas_call | solution.py:27
  23.8 0.7 %shard_map.90.mine_ref = bf16[2,64,128]{2,1,0:T(8,128)(2,1)S(1)} custom-call(bf16[4,16,128]{2,1,0:T(8,128)(2,1)S(1)} %get-tuple-element.31.values_ref, bf16[2,64,128]{2,1,0:T(8,128)(2,1)S(1)} %shard_map.89.after_ref, bf16[2,528,128]{2,1,0:T(8,128)(2,1)S(1)} %copy-done.1, bf16[2,528,128]{2,1,0:T(8,128)(2,1)S(1)} %collective-permute-done.5.refs_1_, ...), custom_call_target="tpu_custom_call" | custom-call | flops 1 | bytes 1 | tf_op jit(solution)/shard_map/pallas_call | solution.py:27
  24.6 0.5 %collective-permute-done.8.other_ref = bf16[2,64,128]{2,1,0:T(8,128)(2,1)S(1)} collective-permute-done((bf16[2,64,128]{2,1,0:T(8,128)(2,1)S(1)}, bf16[2,64,128]{2,1,0:T(8,128)(2,1)S(1)}, u32[]{:S(2)}, u32[]{:S(2)}) %collective-permute-start.8) | collective-permute-done | bytes 32800 | tf_op jit(solution)/shard_map/ppermute | solution.py:65
  25.5 1.6 %collective-permute-start.10 = (bf16[3,32,128]{2,1,0:T(8,128)(2,1)S(1)}, bf16[3,32,128]{2,1,0:T(8,128)(2,1)S(1)}, u32[]{:S(2)}, u32[]{:S(2)}) collective-permute-start(bf16[3,32,128]{2,1,0:T(8,128)(2,1)S(1)} %get-tuple-element.40.after_ref), channel_id=1, source_target_pairs={{0,1},{1,0},{2,3},{3,2},{4,8},{5,9},{6,10},{7,11},{8,4},{9,5},{10,... | collective-permute-start | bytes 73736 | tf_op jit(solution)/shard_map/ppermute | solution.py:61
  27.1 0.6 %shard_map.92.forcing_ref = f32[3,16,32,128]{3,2,1,0:T(8,128)S(1)} custom-call(bf16[2,64,128]{2,1,0:T(8,128)(2,1)S(1)} %shard_map.90.mine_ref, bf16[2,64,128]{2,1,0:T(8,128)(2,1)S(1)} %collective-permute-done.8.other_ref, bf16[3,512,128]{2,1,0:T(8,128)(2,1)S(1)} %get-tuple-element.35.after_ref.pick_ref, bf16[3,32,128]{2,1,0:T(8,128)(2,1)S(1)} %get-tuple-element.40.after_ref), custom_call_target="tpu_custom_call" | custom-call | flops 1 | bytes 1 | tf_op jit(solution)/shard_map/pallas_call | solution.py:27
  27.7 2.5 %shard_map.93 = (f32[3,16,32,128]{3,2,1,0:T(8,128)S(1)}, f32[32,128]{1,0:T(8,128)S(1)}, f32[8,256]{1,0:T(8,128)S(1)}) custom-call(f32[3,16,32,128]{3,2,1,0:T(8,128)S(1)} %shard_map.92.forcing_ref, f32[3,16,32,128]{3,2,1,0:T(8,128)S(1)} %get-tuple-element.41.next_ref, f32[17,32,128]{2,1,0:T(8,128)S(1)} %get-tuple-element.42.nux_ref, ...), custom_call_target="tpu_custom_call" | custom-call | flops 1 | bytes 1 | tf_op jit(solution)/shard_map/pallas_call | solution.py:27
  30.6 2.7 %collective-permute-start.13 = (f32[64,128]{1,0:T(8,128)S(1)}, f32[64,128]{1,0:T(8,128)S(1)}, u32[]{:S(2)}, u32[]{:S(2)}) collective-permute-start(f32[64,128]{1,0:T(8,128)S(1)} %get-tuple-element.54), channel_id=1, source_target_pairs={{0,3},{1,2},{2,1},{3,0},{4,7},{5,6},{6,5},{7,4},{8,11},{9,10},{10,... | collective-permute-start | bytes 98312 | tf_op jit(solution)/shard_map/ppermute | solution.py:65
  33.3 1.7 %collective-permute-start.11 = (f32[48,128]{1,0:T(8,128)S(1)}, f32[48,128]{1,0:T(8,128)S(1)}, u32[]{:S(2)}, u32[]{:S(2)}) collective-permute-start(f32[48,128]{1,0:T(8,128)S(1)} %get-tuple-element.52), channel_id=1, source_target_pairs={{0,1},{1,0},{2,3},{3,2},{4,5},{5,4},{6,7},{7,6},{8,9},{9,8},{10,11... | collective-permute-start | bytes 73736 | tf_op jit(solution)/shard_map/ppermute | solution.py:65
  35.0 2.2 %collective-permute-done.11.refs_0_ = f32[48,128]{1,0:T(8,128)S(1)} collective-permute-done((f32[48,128]{1,0:T(8,128)S(1)}, f32[48,128]{1,0:T(8,128)S(1)}, u32[]{:S(2)}, u32[]{:S(2)}) %collective-permute-start.11) | collective-permute-done | bytes 24608 | tf_op jit(solution)/shard_map/ppermute | solution.py:65
  37.2 1.1 %collective-permute-done.12.refs_1_ = f32[56,128]{1,0:T(8,128)S(1)} collective-permute-done((f32[56,128]{1,0:T(8,128)S(1)}, f32[56,128]{1,0:T(8,128)S(1)}, u32[]{:S(2)}, u32[]{:S(2)}) %collective-permute-start.12) | collective-permute-done | bytes 28704 | tf_op jit(solution)/shard_map/ppermute | solution.py:65
  38.3 1.6 %shard_map.95 = (f32[3,16,32,128]{3,2,1,0:T(8,128)}, f32[1,16]{1,0:T(1,128)}) custom-call(f32[3,16,32,128]{3,2,1,0:T(8,128)S(1)} %get-tuple-element.47.inner_ref, bf16[3,32,128]{2,1,0:T(8,128)(2,1)S(1)} %collective-permute-done.9.x0_ref, bf16[3,32,128]{2,1,0:T(8,128)(2,1)S(1)} %collective-permute-done.10.x1_ref, ...), custom_call_target="tpu_custom_call" | custom-call | flops 655360 | bytes 1572864 | tf_op jit(solution)/shard_map/pallas_call | solution.py:27
  (26 shorter events, 1.4 us)
Async XLA Ops:
  0.6 10.3 %copy-start = (f32[4,16,32,128]{3,2,1,0:T(8,128)S(1)}, f32[4,16,32,128]{3,2,1,0:T(8,128)}, u32[]{:S(2)}) copy-start(f32[4,16,32,128]{3,2,1,0:T(8,128)} %flow_ref.3) | copy-start | bytes 3145732
  1.6 3.2 %copy-start.4 = (f32[4,32,128]{2,1,0:T(8,128)}, f32[4,32,128]{2,1,0:T(8,128)S(1)}, u32[]{:S(2)}) copy-start(f32[4,32,128]{2,1,0:T(8,128)S(1)} %get-tuple-element.57.after_ref) | copy-start | bytes 196612
  1.6 9.3 %collective-permute-start = (f32[4,32,128]{2,1,0:T(8,128)S(1)}, f32[4,32,128]{2,1,0:T(8,128)S(1)}, u32[]{:S(2)}, u32[]{:S(2)}) collective-permute-start(f32[4,32,128]{2,1,0:T(8,128)S(1)} %get-tuple-element.58), channel_id=1, source_target_pairs={{0,4},{1,5},{2,6},{3,7},{4,0},{5,1},{6,2},{7,3},{8,12},{9,13},{10,... | collective-permute-start | bytes 196616 | tf_op jit(solution)/shard_map/ppermute | solution.py:61
  2.2 8.8 %collective-permute-start.1 = (f32[4,32,128]{2,1,0:T(8,128)S(1)}, f32[4,32,128]{2,1,0:T(8,128)S(1)}, u32[]{:S(2)}, u32[]{:S(2)}) collective-permute-start(f32[4,32,128]{2,1,0:T(8,128)S(1)} %get-tuple-element.57.after_ref), channel_id=1, source_target_pairs={{0,1},{1,0},{2,3},{3,2},{4,8},{5,9},{6,10},{7,11},{8,4},{9,5},{10,... | collective-permute-start | bytes 196616 | tf_op jit(solution)/shard_map/ppermute | solution.py:61
  4.8 6.2 %copy-start.2 = (s32[16,32,128]{2,1,0:T(8,128)S(1)}, s32[16,32,128]{2,1,0:T(8,128)}, u32[]{:S(2)}) copy-start(s32[16,32,128]{2,1,0:T(8,128)} %regions_ref.5) | copy-start | bytes 786436
  7.4 13.5 %collective-permute-start.5 = (bf16[2,528,128]{2,1,0:T(8,128)(2,1)}, bf16[2,528,128]{2,1,0:T(8,128)(2,1)S(1)}, u32[]{:S(2)}, u32[]{:S(2)}) collective-permute-start(bf16[2,528,128]{2,1,0:T(8,128)(2,1)} %get-tuple-element.37), channel_id=1, source_target_pairs={{0,8},{4,12},{8,0},{12,4},{16,24},{20,28},{24,16},{28,20},{1,9},{5... | collective-permute-start | bytes 811016 | tf_op jit(solution)/shard_map/ppermute | solution.py:65
  7.9 15.2 %collective-permute-start.6 = (bf16[2,528,128]{2,1,0:T(8,128)(2,1)}, bf16[2,528,128]{2,1,0:T(8,128)(2,1)S(1)}, u32[]{:S(2)}, u32[]{:S(2)}) collective-permute-start(bf16[2,528,128]{2,1,0:T(8,128)(2,1)} %get-tuple-element.38), channel_id=1, source_target_pairs={{0,16},{4,20},{8,24},{12,28},{16,0},{20,4},{24,8},{28,12},{1,17},{... | collective-permute-start | bytes 811016 | tf_op jit(solution)/shard_map/ppermute | solution.py:65
  9.5 13.6 %collective-permute-start.7 = (bf16[2,528,128]{2,1,0:T(8,128)(2,1)}, bf16[2,528,128]{2,1,0:T(8,128)(2,1)S(1)}, u32[]{:S(2)}, u32[]{:S(2)}) collective-permute-start(bf16[2,528,128]{2,1,0:T(8,128)(2,1)} %get-tuple-element.39), channel_id=1, source_target_pairs={{0,24},{4,28},{8,16},{12,20},{16,8},{20,12},{24,0},{28,4},{1,25},{... | collective-permute-start | bytes 811016 | tf_op jit(solution)/shard_map/ppermute | solution.py:65
  11.0 6.0 %copy-start.3 = (s32[1,1,8,4]{2,3,1,0:T(4,128)S(1)}, s32[1,1,8,4]{2,3,1,0:T(4,128)}, u32[]{:S(2)}) copy-start(s32[1,1,8,4]{2,3,1,0:T(4,128)} %param.11) | copy-start | bytes 388
  11.7 3.2 %collective-permute-start.3 = (f32[3,32,128]{2,1,0:T(8,128)S(1)}, f32[3,32,128]{2,1,0:T(8,128)S(1)}, u32[]{:S(2)}, u32[]{:S(2)}) collective-permute-start(f32[3,32,128]{2,1,0:T(8,128)S(1)} %shard_map.85.edges_ref), channel_id=1, source_target_pairs={{0,4},{1,2},{2,1},{3,7},{4,0},{5,6},{6,5},{7,3},{8,12},{9,10},{10,... | collective-permute-start | bytes 147464 | tf_op jit(solution)/shard_map/ppermute | solution.py:61
  11.8 5.2 %collective-permute-start.2 = (f32[3,32,128]{2,1,0:T(8,128)S(1)}, f32[3,32,128]{2,1,0:T(8,128)S(1)}, u32[]{:S(2)}, u32[]{:S(2)}) collective-permute-start(f32[3,32,128]{2,1,0:T(8,128)S(1)} %shard_map.85.edges_ref), channel_id=1, source_target_pairs={{0,1},{1,0},{2,3},{3,2},{4,5},{5,4},{6,7},{7,6},{8,9},{9,8},{10,11... | collective-permute-start | bytes 147464 | tf_op jit(solution)/shard_map/ppermute | solution.py:61
  17.0 6.1 %copy-start.1 = (bf16[2,528,128]{2,1,0:T(8,128)(2,1)S(1)}, bf16[2,528,128]{2,1,0:T(8,128)(2,1)}, u32[]{:S(2)}) copy-start(bf16[2,528,128]{2,1,0:T(8,128)(2,1)} %get-tuple-element.36.refs_0_) | copy-start | bytes 811012
  19.7 1.2 %collective-permute-start.4 = (bf16[4,16,128]{2,1,0:T(8,128)(2,1)S(1)}, bf16[4,16,128]{2,1,0:T(8,128)(2,1)S(1)}, u32[]{:S(2)}, u32[]{:S(2)}) collective-permute-start(bf16[4,16,128]{2,1,0:T(8,128)(2,1)S(1)} %get-tuple-element.32), channel_id=1, source_target_pairs={{0,4},{4,0},{8,12},{12,8},{16,20},{20,16},{24,28},{28,24},{1,5},{5... | collective-permute-start | bytes 49160 | tf_op jit(solution)/shard_map/ppermute | solution.py:65
  23.8 1.2 %collective-permute-start.8 = (bf16[2,64,128]{2,1,0:T(8,128)(2,1)S(1)}, bf16[2,64,128]{2,1,0:T(8,128)(2,1)S(1)}, u32[]{:S(2)}, u32[]{:S(2)}) collective-permute-start(bf16[2,64,128]{2,1,0:T(8,128)(2,1)S(1)} %shard_map.89.after_ref), channel_id=1, source_target_pairs={{0,4},{4,0},{8,12},{12,8},{16,20},{20,16},{24,28},{28,24},{1,5},{5... | collective-permute-start | bytes 98312 | tf_op jit(solution)/shard_map/ppermute | solution.py:65
  25.3 5.0 %collective-permute-start.9 = (bf16[3,32,128]{2,1,0:T(8,128)(2,1)S(1)}, bf16[3,32,128]{2,1,0:T(8,128)(2,1)S(1)}, u32[]{:S(2)}, u32[]{:S(2)}) collective-permute-start(bf16[3,32,128]{2,1,0:T(8,128)(2,1)S(1)} %get-tuple-element.48), channel_id=1, source_target_pairs={{0,4},{1,5},{2,6},{3,7},{4,0},{5,1},{6,2},{7,3},{8,12},{9,13},{10,... | collective-permute-start | bytes 73736 | tf_op jit(solution)/shard_map/ppermute | solution.py:61
  25.5 4.7 %collective-permute-start.10 = (bf16[3,32,128]{2,1,0:T(8,128)(2,1)S(1)}, bf16[3,32,128]{2,1,0:T(8,128)(2,1)S(1)}, u32[]{:S(2)}, u32[]{:S(2)}) collective-permute-start(bf16[3,32,128]{2,1,0:T(8,128)(2,1)S(1)} %get-tuple-element.40.after_ref), channel_id=1, source_target_pairs={{0,1},{1,0},{2,3},{3,2},{4,8},{5,9},{6,10},{7,11},{8,4},{9,5},{10,... | collective-permute-start | bytes 73736 | tf_op jit(solution)/shard_map/ppermute | solution.py:61
  30.6 7.7 %collective-permute-start.13 = (f32[64,128]{1,0:T(8,128)S(1)}, f32[64,128]{1,0:T(8,128)S(1)}, u32[]{:S(2)}, u32[]{:S(2)}) collective-permute-start(f32[64,128]{1,0:T(8,128)S(1)} %get-tuple-element.54), channel_id=1, source_target_pairs={{0,3},{1,2},{2,1},{3,0},{4,7},{5,6},{6,5},{7,4},{8,11},{9,10},{10,... | collective-permute-start | bytes 98312 | tf_op jit(solution)/shard_map/ppermute | solution.py:65
  33.3 5.0 %collective-permute-start.12 = (f32[56,128]{1,0:T(8,128)S(1)}, f32[56,128]{1,0:T(8,128)S(1)}, u32[]{:S(2)}, u32[]{:S(2)}) collective-permute-start(f32[56,128]{1,0:T(8,128)S(1)} %get-tuple-element.53), channel_id=1, source_target_pairs={{0,2},{1,3},{2,0},{3,1},{4,6},{5,7},{6,4},{7,5},{8,10},{9,11},{10,... | collective-permute-start | bytes 86024 | tf_op jit(solution)/shard_map/ppermute | solution.py:65
  33.3 3.9 %collective-permute-start.11 = (f32[48,128]{1,0:T(8,128)S(1)}, f32[48,128]{1,0:T(8,128)S(1)}, u32[]{:S(2)}, u32[]{:S(2)}) collective-permute-start(f32[48,128]{1,0:T(8,128)S(1)} %get-tuple-element.52), channel_id=1, source_target_pairs={{0,1},{1,0},{2,3},{3,2},{4,5},{5,4},{6,7},{7,6},{8,9},{9,8},{10,11... | collective-permute-start | bytes 73736 | tf_op jit(solution)/shard_map/ppermute | solution.py:65

commit v6 on v5

--- a/solution.py
+++ b/solution.py
@@ -167,11 +167,11 @@
     return jnp.where(exists & (field < 4), value, 0.0)
 
 
-def group_kernel(cap, dest_ref, tiles_ref, meas_ref, after_ref, *refs):
+def group_kernel(cap, dest_ref, tiles_ref, meas_ref, flow_ref, *refs):
     chips = len(refs) - 12
-    sends = refs[:chips]
-    (list_ref, held_ref, seen_ref, count_ref, slot_ref, rows_ref, blank_ref,
-     list_sem, seen_sem, in_sems, out_sems, row_sems) = refs[chips:]
+    sends, halo_refs = refs[:chips], refs[chips : chips + 2]
+    (list_ref, held_ref, seen_ref, count_ref, slot_ref, rows_ref,
+     list_sem, seen_sem, in_sems, face_sems) = refs[chips + 2 :]
     count_tiles, width, _ = tiles_ref.shape
     groups = 2 * chips
     slots = groups * cap
@@ -190,6 +190,15 @@
         load(p).start()
     seen = pltpu.make_async_copy(meas_ref, seen_ref, seen_sem)
     seen.start()
+    last = flow_ref.shape[1] - 1
+    fields = flow_ref.shape[0]
+    faces = [
+        pltpu.make_async_copy(flow_ref.at[c, plane], halo_refs[i].at[c], face_sems.at[i * fields + c])
+        for i, plane in enumerate((last * (1 - me % 2), last * (me % 2)))
+        for c in range(fields)
+    ]
+    for face in faces:
+        face.start()
 
     def clear(b, carry):
         count_ref[b] = 0
@@ -198,8 +207,6 @@
         return carry
 
     lax.fori_loop(0, groups, clear, 0)
-    if slots > count_tiles:
-        blank_ref[...] = jnp.zeros_like(blank_ref)
     _, tile_lane = iotas(8, count_tiles)
     listed.wait()
 
@@ -216,29 +223,16 @@
     for p in range(in_sems.shape[0]):
         load(p).wait()
 
-    def each(act):
-        for m in list(range(1, chips)) + [0]:
-            for j in range(2):
-                b = me ^ (2 * m + j)
-                for k in range(cap):
-                    t = slot_ref[b * cap + k]
-                    at = sends[m].at[j, pl.ds(k * width, width), :]
-                    sem = out_sems.at[(2 * m + j) * cap + k]
-                    if slots > count_tiles:
-
-                        @pl.when(t >= 0)
-                        def _():
-                            act(pltpu.make_async_copy(held_ref.at[t], at, sem))
-
-                        @pl.when(t < 0)
-                        def _():
-                            act(pltpu.make_async_copy(blank_ref, at, sem))
-
-                    else:
-                        act(pltpu.make_async_copy(held_ref.at[t], at, sem))
-
-    each(lambda copy: copy.start())
-
+    for m in list(range(1, chips)) + [0]:
+        for j in range(2):
+            b = me ^ (2 * m + j)
+            for k in range(cap):
+                t = slot_ref[b * cap + k]
+                at = (j, slice(k * width, (k + 1) * width))
+                if slots > count_tiles:
+                    sends[m][at] = jnp.where(t >= 0, held_ref[jnp.maximum(t, 0)], jnp.zeros((width, width), jnp.bfloat16))
+                else:
+                    sends[m][at] = held_ref[t]
     seen.wait()
     row = lax.broadcasted_iota(jnp.int32, (groups * extra, count_tiles), 0)
     within = row % extra
@@ -252,21 +246,12 @@
         )
     rows_ref[...] = total.astype(jnp.bfloat16)
 
-    def row_copy(m, j):
-        b = me ^ (2 * m + j)
-        return pltpu.make_async_copy(
-            rows_ref.at[pl.ds(pl.multiple_of(b * extra, extra), extra), :],
-            sends[m].at[j, pl.ds(depth, extra), :],
-            row_sems.at[2 * m + j],
-        )
-
     for m in range(chips):
         for j in range(2):
-            row_copy(m, j).start()
-    each(lambda copy: copy.wait())
-    for m in range(chips):
-        for j in range(2):
-            row_copy(m, j).wait()
+            b = me ^ (2 * m + j)
+            sends[m][j, depth:, :] = rows_ref[pl.ds(pl.multiple_of(b * extra, extra), extra), :]
+    for face in faces:
+        face.wait()
 
 
 def forward_kernel(
@@ -361,7 +346,7 @@
 
 
 def pick_kernel(
-    sizes, cells_of_ref, z0_ref, z1_ref, edges_ref, rim_ref, outside_ref, pick_ref
+    sizes, cells_of_ref, z0_ref, z1_ref, edges_ref, rim_ref, outside_ref, rims_ref, pick_ref
 ):
     _, rows, width = edges_ref.shape
     groups, walls = sizes
@@ -374,7 +359,9 @@
         for i, shift in enumerate((2, 4, 2))
     )
     inside = pltpu.roll(edges_ref[0], 1, 1)
-    outside_ref[...] = outside_edges(walls, planes, halo, second, beside, inside, rim_ref[...])
+    rim_nu = rim_ref[...]
+    outside_ref[...] = outside_edges(walls, planes, halo, second, beside, inside, rim_nu)
+    rims_ref[...] = time_step * (rim_nu + pltpu.roll(rim_nu, 2 * planes, 1) + pltpu.roll(rim_nu, 4 * planes, 1))
     line, slot_lane = iotas(lines, slot_rows)
     hit = line == cells_of_ref[0:1, :]
     part = (slot_lane % extra) % 3
@@ -534,9 +521,9 @@
     )
 
 
-def final_kernel(sizes, inner_ref, x0_ref, x1_ref, nux_ref, rim_ref, own_ref, *refs):
+def final_kernel(sizes, inner_ref, x0_ref, x1_ref, nux_ref, rims_ref, own_ref, *refs):
     groups, walls = sizes
-    arrived, (adjoint_ref, sens_ref, value_ref, sems) = refs[:-4], refs[-4:]
+    arrived, (adjoint_ref, sens_ref, value_ref, owned_ref, sems, owned_sem) = refs[:-6], refs[-6:]
     _, planes, rows, width = inner_ref.shape
     per = own_ref.shape[0]
     _, lane = iotas(rows, width)
@@ -551,9 +538,7 @@
             above = jnp.where((me ^ mask) == me + 1, edges, above)
             below = jnp.where((me ^ mask) == me - 1, edges, below)
     mixed = mix_edges(below, above, lane)
-    edge_nu = time_step * rim_ref[...]
-    edge_nu = edge_nu + pltpu.roll(edge_nu, 2 * planes, 1) + pltpu.roll(edge_nu, 4 * planes, 1)
-    edge_flux = mixed * edge_nu
+    edge_flux = mixed * rims_ref[...]
     on_edge = (lane == 0) | (lane == width - 1)
 
     beside = [beside_of(c, groups, x0_ref, x1_ref) for c in range(3)]
@@ -587,9 +572,12 @@
                 jnp.broadcast_to(jnp.sum(mine, axis=0, keepdims=True), (8, width)), gather, (((1,), (1,)), ((), ())),
                 precision=lax.Precision.HIGHEST, preferred_element_type=jnp.float32,
             )
-    sens_ref[...] = sens_scale * sens[:1]
+    owned_ref[...] = sens_scale * sens[:1]
+    owned_copy = pltpu.make_async_copy(owned_ref, sens_ref, owned_sem)
+    owned_copy.start()
     for i in range(sems.shape[0]):
         store(i).wait()
+    owned_copy.wait()
 
 
 def body(flow_state, regions, obs_tiles, measured, tile_dest, cell_list):
@@ -605,15 +593,14 @@
 
     chips = groups // 2
     height = cap * width + extra
-    even = lax.axis_index("fluid") % 2 == 0
-    low, high = flow_state[:, 0], flow_state[:, planes - 1]
-    xs0, xs1 = jnp.where(even, high, low), jnp.where(even, low, high)
-    x0, x1 = swap(xs0, "fluid", 0), swap(xs1, "fluid", 1)
-    sends = call(
+    *sends, xs0, xs1 = call(
         functools.partial(group_kernel, cap),
-        (bf16(2, height, width),) * chips,
-        [HBM] * 3 + [ANY],
-        (tile_dest[0, 0], obs_tiles[0, 0], jnp.transpose(measured[0, 0], (1, 0, 2)), xs1),
+        (bf16(2, height, width),) * chips + (f32(4, rows, width),) * 2,
+        [HBM] * 4,
+        tuple(
+            pltpu.with_memory_space_constraint(operand, pltpu.HBM)
+            for operand in (tile_dest[0, 0], obs_tiles[0, 0], jnp.transpose(measured[0, 0], (1, 0, 2)), flow_state)
+        ),
         (
             pltpu.SMEM((count_tiles,), jnp.int32),
             pltpu.VMEM((count_tiles, width, width), jnp.bfloat16),
@@ -621,16 +608,14 @@
             pltpu.SMEM((groups,), jnp.int32),
             pltpu.SMEM((cells,), jnp.int32),
             pltpu.VMEM((groups * extra, width), jnp.bfloat16),
-            pltpu.VMEM((width, width), jnp.bfloat16),
             pltpu.SemaphoreType.DMA,
             pltpu.SemaphoreType.DMA,
             pltpu.SemaphoreType.DMA((4,)),
-            pltpu.SemaphoreType.DMA((cells,)),
-            pltpu.SemaphoreType.DMA((groups,)),
+            pltpu.SemaphoreType.DMA((8,)),
         ),
-        out_specs=(HBM,) * chips,
-        limit=60 * 1024 * 1024,
-    )
+        out_specs=(VMEM,) * (chips + 2),
+    )
+    x0, x1 = swap(xs0, "fluid", 0), swap(xs1, "fluid", 1)
     recvs = [sends[0]] + [cross(sends[m], "fluid", 2 * m) for m in range(1, chips)]
     zs = call(
         functools.partial(edges_kernel, groups),
@@ -660,9 +645,9 @@
         out_specs=(HBM,) + (VMEM,) * 9,
     )
     borrowed = cross(lent, "fluid", 1)
-    outside, pick = call(
+    outside, rims, pick = call(
         functools.partial(pick_kernel, sizes),
-        (f32(rows, width), bf16(3, planes * rows, slot_rows)),
+        (f32(rows, width), f32(rows, width), bf16(3, planes * rows, slot_rows)),
         [VMEM] * 5,
         (cells_of, z0, z1, zs, rim),
     )
@@ -708,9 +693,14 @@
         functools.partial(final_kernel, sizes),
         (f32(3, planes, rows, width), f32(1, REG_DEV)),
         [VMEM] * (6 + len(arrived)),
-        (inner, f0, f1, nux, rim, own, *arrived),
-        (pltpu.VMEM((3, planes, rows, width), jnp.float32), pltpu.SemaphoreType.DMA((4,))),
-        out_specs=(HBM, VMEM),
+        (inner, f0, f1, nux, rims, own, *arrived),
+        (
+            pltpu.VMEM((3, planes, rows, width), jnp.float32),
+            pltpu.VMEM((1, REG_DEV), jnp.float32),
+            pltpu.SemaphoreType.DMA((4,)),
+            pltpu.SemaphoreType.DMA,
+        ),
+        out_specs=(HBM, HBM),
         flops=10 * grid,
         moved=24 * grid,
     )

time: 40.1 us -> 37.5 us (0.935)
  Pallas kernels: 13.2 us -> 11.8 us
  other arithmetic: 0.97 us -> 0 us
    pallas_call x11, Pallas kernels: 13.2 us -> 11.8 us  [call(): pl.pallas_call(kernel, out_shape=outs, in_specs=ins, out_specs=out_specs...]
    select_n x1 -> x0, other arithmetic: 0.97 us -> none  [body(): xs0, xs1 = (jnp.where(even, high, low), jnp.where(even, low, high))]
  transfers between devices with their start and end apart: 14 -> 14, of which waited for: 6 -> 7; matrix products, arithmetic and copies ran while one was open for 0% -> 0% of each run, Pallas kernels for 26% -> 21%
where the time goes in v6:
time: 37.5 us; the launch traced here: 37.4 us
  starting transfers between devices  16.3 us (43%)
  Pallas kernels  11.8 us (31%)
  waiting for transfers between devices  8.41 us (22%)
  between operations  0.76 us (2%)
    pallas_call x11, Pallas kernels, call(): pl.pallas_call(kernel, out_shape=outs, in_specs=ins, out_specs=out_specs...  11.8 us
    ppermute x6, starting transfers between devices, swap(): return lax.ppermute(block, ('fluid', 'wall'), pairs)  8.33 us
    ppermute x8, starting transfers between devices, cross(): lax.ppermute(block, axis, [(i, i ^ mask) for i in range(lax.axis_size(axi...  8.01 us
    ppermute x8, waiting for transfers between devices, cross(): lax.ppermute(block, axis, [(i, i ^ mask) for i in range(lax.axis_size(axi...  6.33 us
    ppermute x6, waiting for transfers between devices, swap(): return lax.ppermute(block, ('fluid', 'wall'), pairs)  2.08 us
  transfers between devices with their start and end apart: 14, of which 7 were waited for; matrix products, arithmetic and copies ran while one was open for 0% of the time, Pallas kernels for 21%

profile of v6, /device:TPU:0, one launch (start us, length us, event | category | flops | bytes accessed | tf_op | source)
XLA Modules:
  0.0 37.4 jit_solution(7081756300837347729)
XLA Ops:
  0.7 1.8 %shard_map.85 = (bf16[2,528,128]{2,1,0:T(8,128)(2,1)S(1)}, bf16[2,528,128]{2,1,0:T(8,128)(2,1)S(1)}, bf16[2,528,128]{2,1,0:T(8,128)(2,1)S(1)}, bf16[2,528,128]{2...) custom-call(s32[32]{0:T(128)} %bitcast.12, bf16[32,128,128]{2,1,0:T(8,128)(2,1)} %bitcast.10, ...), custom_call_target="tpu_custom_call" | custom-call | flops 1 | bytes 1 | tf_op jit(solution)/shard_map/pallas_call | solution.py:27
  2.4 0.5 %collective-permute-start = (f32[4,32,128]{2,1,0:T(8,128)S(1)}, f32[4,32,128]{2,1,0:T(8,128)S(1)}, u32[]{:S(2)}, u32[]{:S(2)}) collective-permute-start(f32[4,32,128]{2,1,0:T(8,128)S(1)} %get-tuple-element.33), channel_id=1, source_target_pairs={{0,4},{1,5},{2,6},{3,7},{4,0},{5,1},{6,2},{7,3},{8,12},{9,13},{10,... | collective-permute-start | bytes 196616 | tf_op jit(solution)/shard_map/ppermute | solution.py:61
  2.9 2.6 %collective-permute-start.1 = (f32[4,32,128]{2,1,0:T(8,128)S(1)}, f32[4,32,128]{2,1,0:T(8,128)S(1)}, u32[]{:S(2)}, u32[]{:S(2)}) collective-permute-start(f32[4,32,128]{2,1,0:T(8,128)S(1)} %get-tuple-element.34), channel_id=1, source_target_pairs={{0,1},{1,0},{2,3},{3,2},{4,8},{5,9},{6,10},{7,11},{8,4},{9,5},{10,... | collective-permute-start | bytes 196616 | tf_op jit(solution)/shard_map/ppermute | solution.py:61
  5.6 2.0 %collective-permute-start.6 = (bf16[2,528,128]{2,1,0:T(8,128)(2,1)S(1)}, bf16[2,528,128]{2,1,0:T(8,128)(2,1)S(1)}, u32[]{:S(2)}, u32[]{:S(2)}) collective-permute-start(bf16[2,528,128]{2,1,0:T(8,128)(2,1)S(1)} %get-tuple-element.43), channel_id=1, source_target_pairs={{0,16},{4,20},{8,24},{12,28},{16,0},{20,4},{24,8},{28,12},{1,17},{... | collective-permute-start | bytes 811016 | tf_op jit(solution)/shard_map/ppermute | solution.py:65
  7.6 1.5 %collective-permute-start.7 = (bf16[2,528,128]{2,1,0:T(8,128)(2,1)S(1)}, bf16[2,528,128]{2,1,0:T(8,128)(2,1)S(1)}, u32[]{:S(2)}, u32[]{:S(2)}) collective-permute-start(bf16[2,528,128]{2,1,0:T(8,128)(2,1)S(1)} %get-tuple-element.44), channel_id=1, source_target_pairs={{0,24},{4,28},{8,16},{12,20},{16,8},{20,12},{24,0},{28,4},{1,25},{... | collective-permute-start | bytes 811016 | tf_op jit(solution)/shard_map/ppermute | solution.py:65
  9.1 0.8 %shard_map.86.edges_ref = f32[3,32,128]{2,1,0:T(8,128)S(1)} custom-call(f32[4,16,32,128]{3,2,1,0:T(8,128)S(1)} %copy-done, s32[16,32,128]{2,1,0:T(8,128)S(1)} %copy-done.1, f32[4,32,128]{2,1,0:T(8,128)S(1)} %collective-permute-done.x0_ref, f32[4,32,128]{2,1,0:T(8,128)S(1)} %collective-permute-done.1.x1_ref), custom_call_target="tpu_custom_call" | custom-call | flops 99999997952 | bytes 1 | tf_op jit(solution)/shard_map/pallas_call | solution.py:27
  9.9 3.1 %collective-permute-start.2 = (f32[3,32,128]{2,1,0:T(8,128)S(1)}, f32[3,32,128]{2,1,0:T(8,128)S(1)}, u32[]{:S(2)}, u32[]{:S(2)}) collective-permute-start(f32[3,32,128]{2,1,0:T(8,128)S(1)} %shard_map.86.edges_ref), channel_id=1, source_target_pairs={{0,1},{1,0},{2,3},{3,2},{4,5},{5,4},{6,7},{7,6},{8,9},{9,8},{10,11... | collective-permute-start | bytes 147464 | tf_op jit(solution)/shard_map/ppermute | solution.py:61
  13.1 2.1 %collective-permute-done.2.z0_ref = f32[3,32,128]{2,1,0:T(8,128)S(1)} collective-permute-done((f32[3,32,128]{2,1,0:T(8,128)S(1)}, f32[3,32,128]{2,1,0:T(8,128)S(1)}, u32[]{:S(2)}, u32[]{:S(2)}) %collective-permute-start.2) | collective-permute-done | bytes 49184 | tf_op jit(solution)/shard_map/ppermute | solution.py:61
  15.2 2.6 %shard_map.87 = (f32[3,16,32,128]{3,2,1,0:T(8,128)}, f32[3,16,32,128]{3,2,1,0:T(8,128)S(1)}, f32[17,32,128]{2,1,0:T(8,128)S(1)}, f32[16,32,128]{2,1,0:T(8,128)S(...) custom-call(s32[4,8]{1,0:T(4,128)S(1)} %bitcast.9, ...), custom_call_target="tpu_custom_call" | custom-call | flops 1 | bytes 1 | tf_op jit(solution)/shard_map/pallas_call | solution.py:27
  17.9 0.4 %shard_map.88 = (f32[32,128]{1,0:T(8,128)S(1)}, f32[32,128]{1,0:T(8,128)S(1)}, bf16[3,512,128]{2,1,0:T(8,128)(2,1)S(1)}) custom-call(s32[8,128]{1,0:T(8,128)S(1)} %get-tuple-element.38.cells_of_ref, f32[3,32,128]{2,1,0:T(8,128)S(1)} %collective-permute-done.2.z0_ref, f32[3,32,128]{2,1,0:T(8,128)S(1)} %collective-permute-done.3.z1_ref, ...), custom_call_target="tpu_custom_call" | custom-call | flops 1 | bytes 1 | tf_op jit(solution)/shard_map/pallas_call | solution.py:27
  18.3 0.7 %collective-permute-done.4.values_ref = bf16[4,16,128]{2,1,0:T(8,128)(2,1)S(1)} collective-permute-done((bf16[4,16,128]{2,1,0:T(8,128)(2,1)S(1)}, bf16[4,16,128]{2,1,0:T(8,128)(2,1)S(1)}, u32[]{:S(2)}, u32[]{:S(2)}) %collective-permute-start.4) | collective-permute-done | bytes 16416 | tf_op jit(solution)/shard_map/ppermute | solution.py:65
  19.0 1.1 %collective-permute-done.6.refs_2_ = bf16[2,528,128]{2,1,0:T(8,128)(2,1)S(1)} collective-permute-done((bf16[2,528,128]{2,1,0:T(8,128)(2,1)S(1)}, bf16[2,528,128]{2,1,0:T(8,128)(2,1)S(1)}, u32[]{:S(2)}, u32[]{:S(2)}) %collective-permute-start.6) | collective-permute-done | bytes 270368 | tf_op jit(solution)/shard_map/ppermute | solution.py:65
  20.2 0.7 %collective-permute-done.7.refs_3_ = bf16[2,528,128]{2,1,0:T(8,128)(2,1)S(1)} collective-permute-done((bf16[2,528,128]{2,1,0:T(8,128)(2,1)S(1)}, bf16[2,528,128]{2,1,0:T(8,128)(2,1)S(1)}, u32[]{:S(2)}, u32[]{:S(2)}) %collective-permute-start.7) | collective-permute-done | bytes 270368 | tf_op jit(solution)/shard_map/ppermute | solution.py:65
  20.9 0.7 %shard_map.89.after_ref = bf16[2,64,128]{2,1,0:T(8,128)(2,1)S(1)} custom-call(bf16[4,16,128]{2,1,0:T(8,128)(2,1)S(1)} %collective-permute-done.4.values_ref, bf16[3,512,128]{2,1,0:T(8,128)(2,1)S(1)} %get-tuple-element.40.after_ref.pick_ref, bf16[2,528,128]{2,1,0:T(8,128)(2,1)S(1)} %get-tuple-element.41.refs_0_, ...), custom_call_target="tpu_custom_call" | custom-call | flops 1 | bytes 1 | tf_op jit(solution)/shard_map/pallas_call | solution.py:27
  21.6 0.7 %shard_map.90.mine_ref = bf16[2,64,128]{2,1,0:T(8,128)(2,1)S(1)} custom-call(bf16[4,16,128]{2,1,0:T(8,128)(2,1)S(1)} %get-tuple-element.36.values_ref, bf16[2,64,128]{2,1,0:T(8,128)(2,1)S(1)} %shard_map.89.after_ref, bf16[2,528,128]{2,1,0:T(8,128)(2,1)S(1)} %get-tuple-element.41.refs_0_, bf16[2,528,128]{2,1,0:T(8,128)(2,1)S(1)} %collective-permute-done.5.refs_1_, ...), custom_call_target="tpu_custom_call" | custom-call | flops 1 | bytes 1 | tf_op jit(solution)/shard_map/pallas_call | solution.py:27
  22.3 0.5 %collective-permute-done.8.other_ref = bf16[2,64,128]{2,1,0:T(8,128)(2,1)S(1)} collective-permute-done((bf16[2,64,128]{2,1,0:T(8,128)(2,1)S(1)}, bf16[2,64,128]{2,1,0:T(8,128)(2,1)S(1)}, u32[]{:S(2)}, u32[]{:S(2)}) %collective-permute-start.8) | collective-permute-done | bytes 32800 | tf_op jit(solution)/shard_map/ppermute | solution.py:65
  23.3 1.7 %collective-permute-start.10 = (bf16[3,32,128]{2,1,0:T(8,128)(2,1)S(1)}, bf16[3,32,128]{2,1,0:T(8,128)(2,1)S(1)}, u32[]{:S(2)}, u32[]{:S(2)}) collective-permute-start(bf16[3,32,128]{2,1,0:T(8,128)(2,1)S(1)} %get-tuple-element.45.after_ref), channel_id=1, source_target_pairs={{0,1},{1,0},{2,3},{3,2},{4,8},{5,9},{6,10},{7,11},{8,4},{9,5},{10,... | collective-permute-start | bytes 73736 | tf_op jit(solution)/shard_map/ppermute | solution.py:61
  25.0 0.6 %shard_map.92.forcing_ref = f32[3,16,32,128]{3,2,1,0:T(8,128)S(1)} custom-call(bf16[2,64,128]{2,1,0:T(8,128)(2,1)S(1)} %shard_map.90.mine_ref, bf16[2,64,128]{2,1,0:T(8,128)(2,1)S(1)} %collective-permute-done.8.other_ref, bf16[3,512,128]{2,1,0:T(8,128)(2,1)S(1)} %get-tuple-element.40.after_ref.pick_ref, bf16[3,32,128]{2,1,0:T(8,128)(2,1)S(1)} %get-tuple-element.45.after_ref), custom_call_target="tpu_custom_call" | custom-call | flops 1 | bytes 1 | tf_op jit(solution)/shard_map/pallas_call | solution.py:27
  25.6 2.6 %shard_map.93 = (f32[3,16,32,128]{3,2,1,0:T(8,128)S(1)}, f32[32,128]{1,0:T(8,128)S(1)}, f32[8,256]{1,0:T(8,128)S(1)}) custom-call(f32[3,16,32,128]{3,2,1,0:T(8,128)S(1)} %shard_map.92.forcing_ref, f32[3,16,32,128]{3,2,1,0:T(8,128)S(1)} %get-tuple-element.46.next_ref, f32[17,32,128]{2,1,0:T(8,128)S(1)} %get-tuple-element.47.nux_ref, ...), custom_call_target="tpu_custom_call" | custom-call | flops 1 | bytes 1 | tf_op jit(solution)/shard_map/pallas_call | solution.py:27
  28.5 2.7 %collective-permute-start.13 = (f32[64,128]{1,0:T(8,128)S(1)}, f32[64,128]{1,0:T(8,128)S(1)}, u32[]{:S(2)}, u32[]{:S(2)}) collective-permute-start(f32[64,128]{1,0:T(8,128)S(1)} %get-tuple-element.60), channel_id=1, source_target_pairs={{0,3},{1,2},{2,1},{3,0},{4,7},{5,6},{6,5},{7,4},{8,11},{9,10},{10,... | collective-permute-start | bytes 98312 | tf_op jit(solution)/shard_map/ppermute | solution.py:65
  31.2 1.7 %collective-permute-start.11 = (f32[48,128]{1,0:T(8,128)S(1)}, f32[48,128]{1,0:T(8,128)S(1)}, u32[]{:S(2)}, u32[]{:S(2)}) collective-permute-start(f32[48,128]{1,0:T(8,128)S(1)} %get-tuple-element.58), channel_id=1, source_target_pairs={{0,1},{1,0},{2,3},{3,2},{4,5},{5,4},{6,7},{7,6},{8,9},{9,8},{10,11... | collective-permute-start | bytes 73736 | tf_op jit(solution)/shard_map/ppermute | solution.py:65
  32.9 2.1 %collective-permute-done.11.refs_0_ = f32[48,128]{1,0:T(8,128)S(1)} collective-permute-done((f32[48,128]{1,0:T(8,128)S(1)}, f32[48,128]{1,0:T(8,128)S(1)}, u32[]{:S(2)}, u32[]{:S(2)}) %collective-permute-start.11) | collective-permute-done | bytes 24608 | tf_op jit(solution)/shard_map/ppermute | solution.py:65
  35.1 1.2 %collective-permute-done.12.refs_1_ = f32[56,128]{1,0:T(8,128)S(1)} collective-permute-done((f32[56,128]{1,0:T(8,128)S(1)}, f32[56,128]{1,0:T(8,128)S(1)}, u32[]{:S(2)}, u32[]{:S(2)}) %collective-permute-start.12) | collective-permute-done | bytes 28704 | tf_op jit(solution)/shard_map/ppermute | solution.py:65
  36.3 1.1 %shard_map.95 = (f32[3,16,32,128]{3,2,1,0:T(8,128)}, f32[1,16]{1,0:T(1,128)}) custom-call(f32[3,16,32,128]{3,2,1,0:T(8,128)S(1)} %get-tuple-element.52.inner_ref, bf16[3,32,128]{2,1,0:T(8,128)(2,1)S(1)} %collective-permute-done.9.x0_ref, bf16[3,32,128]{2,1,0:T(8,128)(2,1)S(1)} %collective-permute-done.10.x1_ref, ...), custom_call_target="tpu_custom_call" | custom-call | flops 655360 | bytes 1572864 | tf_op jit(solution)/shard_map/pallas_call | solution.py:27
  (21 shorter events, 0.9 us)
Async XLA Ops:
  0.6 8.5 %copy-start = (f32[4,16,32,128]{3,2,1,0:T(8,128)S(1)}, f32[4,16,32,128]{3,2,1,0:T(8,128)}, u32[]{:S(2)}) copy-start(f32[4,16,32,128]{3,2,1,0:T(8,128)} %flow_ref.5) | copy-start | bytes 3145732
  0.6 8.5 %copy-start.1 = (s32[16,32,128]{2,1,0:T(8,128)S(1)}, s32[16,32,128]{2,1,0:T(8,128)}, u32[]{:S(2)}) copy-start(s32[16,32,128]{2,1,0:T(8,128)} %regions_ref.5) | copy-start | bytes 786436
  2.4 6.7 %collective-permute-start = (f32[4,32,128]{2,1,0:T(8,128)S(1)}, f32[4,32,128]{2,1,0:T(8,128)S(1)}, u32[]{:S(2)}, u32[]{:S(2)}) collective-permute-start(f32[4,32,128]{2,1,0:T(8,128)S(1)} %get-tuple-element.33), channel_id=1, source_target_pairs={{0,4},{1,5},{2,6},{3,7},{4,0},{5,1},{6,2},{7,3},{8,12},{9,13},{10,... | collective-permute-start | bytes 196616 | tf_op jit(solution)/shard_map/ppermute | solution.py:61
  2.9 6.1 %collective-permute-start.1 = (f32[4,32,128]{2,1,0:T(8,128)S(1)}, f32[4,32,128]{2,1,0:T(8,128)S(1)}, u32[]{:S(2)}, u32[]{:S(2)}) collective-permute-start(f32[4,32,128]{2,1,0:T(8,128)S(1)} %get-tuple-element.34), channel_id=1, source_target_pairs={{0,1},{1,0},{2,3},{3,2},{4,8},{5,9},{6,10},{7,11},{8,4},{9,5},{10,... | collective-permute-start | bytes 196616 | tf_op jit(solution)/shard_map/ppermute | solution.py:61
  5.6 13.5 %collective-permute-start.5 = (bf16[2,528,128]{2,1,0:T(8,128)(2,1)S(1)}, bf16[2,528,128]{2,1,0:T(8,128)(2,1)S(1)}, u32[]{:S(2)}, u32[]{:S(2)}) collective-permute-start(bf16[2,528,128]{2,1,0:T(8,128)(2,1)S(1)} %get-tuple-element.42), channel_id=1, source_target_pairs={{0,8},{4,12},{8,0},{12,4},{16,24},{20,28},{24,16},{28,20},{1,9},{5... | collective-permute-start | bytes 811016 | tf_op jit(solution)/shard_map/ppermute | solution.py:65
  5.6 14.6 %collective-permute-start.6 = (bf16[2,528,128]{2,1,0:T(8,128)(2,1)S(1)}, bf16[2,528,128]{2,1,0:T(8,128)(2,1)S(1)}, u32[]{:S(2)}, u32[]{:S(2)}) collective-permute-start(bf16[2,528,128]{2,1,0:T(8,128)(2,1)S(1)} %get-tuple-element.43), channel_id=1, source_target_pairs={{0,16},{4,20},{8,24},{12,28},{16,0},{20,4},{24,8},{28,12},{1,17},{... | collective-permute-start | bytes 811016 | tf_op jit(solution)/shard_map/ppermute | solution.py:65
  7.6 13.3 %collective-permute-start.7 = (bf16[2,528,128]{2,1,0:T(8,128)(2,1)S(1)}, bf16[2,528,128]{2,1,0:T(8,128)(2,1)S(1)}, u32[]{:S(2)}, u32[]{:S(2)}) collective-permute-start(bf16[2,528,128]{2,1,0:T(8,128)(2,1)S(1)} %get-tuple-element.44), channel_id=1, source_target_pairs={{0,24},{4,28},{8,16},{12,20},{16,8},{20,12},{24,0},{28,4},{1,25},{... | collective-permute-start | bytes 811016 | tf_op jit(solution)/shard_map/ppermute | solution.py:65
  9.1 6.1 %copy-start.2 = (s32[1,1,8,4]{2,3,1,0:T(4,128)S(1)}, s32[1,1,8,4]{2,3,1,0:T(4,128)}, u32[]{:S(2)}) copy-start(s32[1,1,8,4]{2,3,1,0:T(4,128)} %param.11) | copy-start | bytes 388
  9.9 3.2 %collective-permute-start.3 = (f32[3,32,128]{2,1,0:T(8,128)S(1)}, f32[3,32,128]{2,1,0:T(8,128)S(1)}, u32[]{:S(2)}, u32[]{:S(2)}) collective-permute-start(f32[3,32,128]{2,1,0:T(8,128)S(1)} %shard_map.86.edges_ref), channel_id=1, source_target_pairs={{0,4},{1,2},{2,1},{3,7},{4,0},{5,6},{6,5},{7,3},{8,12},{9,10},{10,... | collective-permute-start | bytes 147464 | tf_op jit(solution)/shard_map/ppermute | solution.py:61
  9.9 5.2 %collective-permute-start.2 = (f32[3,32,128]{2,1,0:T(8,128)S(1)}, f32[3,32,128]{2,1,0:T(8,128)S(1)}, u32[]{:S(2)}, u32[]{:S(2)}) collective-permute-start(f32[3,32,128]{2,1,0:T(8,128)S(1)} %shard_map.86.edges_ref), channel_id=1, source_target_pairs={{0,1},{1,0},{2,3},{3,2},{4,5},{5,4},{6,7},{7,6},{8,9},{9,8},{10,11... | collective-permute-start | bytes 147464 | tf_op jit(solution)/shard_map/ppermute | solution.py:61
  17.8 1.2 %collective-permute-start.4 = (bf16[4,16,128]{2,1,0:T(8,128)(2,1)S(1)}, bf16[4,16,128]{2,1,0:T(8,128)(2,1)S(1)}, u32[]{:S(2)}, u32[]{:S(2)}) collective-permute-start(bf16[4,16,128]{2,1,0:T(8,128)(2,1)S(1)} %get-tuple-element.37), channel_id=1, source_target_pairs={{0,4},{4,0},{8,12},{12,8},{16,20},{20,16},{24,28},{28,24},{1,5},{5... | collective-permute-start | bytes 49160 | tf_op jit(solution)/shard_map/ppermute | solution.py:65
  21.6 1.2 %collective-permute-start.8 = (bf16[2,64,128]{2,1,0:T(8,128)(2,1)S(1)}, bf16[2,64,128]{2,1,0:T(8,128)(2,1)S(1)}, u32[]{:S(2)}, u32[]{:S(2)}) collective-permute-start(bf16[2,64,128]{2,1,0:T(8,128)(2,1)S(1)} %shard_map.89.after_ref), channel_id=1, source_target_pairs={{0,4},{4,0},{8,12},{12,8},{16,20},{20,16},{24,28},{28,24},{1,5},{5... | collective-permute-start | bytes 98312 | tf_op jit(solution)/shard_map/ppermute | solution.py:65
  23.1 5.1 %collective-permute-start.9 = (bf16[3,32,128]{2,1,0:T(8,128)(2,1)S(1)}, bf16[3,32,128]{2,1,0:T(8,128)(2,1)S(1)}, u32[]{:S(2)}, u32[]{:S(2)}) collective-permute-start(bf16[3,32,128]{2,1,0:T(8,128)(2,1)S(1)} %get-tuple-element.53), channel_id=1, source_target_pairs={{0,4},{1,5},{2,6},{3,7},{4,0},{5,1},{6,2},{7,3},{8,12},{9,13},{10,... | collective-permute-start | bytes 73736 | tf_op jit(solution)/shard_map/ppermute | solution.py:61
  23.3 4.9 %collective-permute-start.10 = (bf16[3,32,128]{2,1,0:T(8,128)(2,1)S(1)}, bf16[3,32,128]{2,1,0:T(8,128)(2,1)S(1)}, u32[]{:S(2)}, u32[]{:S(2)}) collective-permute-start(bf16[3,32,128]{2,1,0:T(8,128)(2,1)S(1)} %get-tuple-element.45.after_ref), channel_id=1, source_target_pairs={{0,1},{1,0},{2,3},{3,2},{4,8},{5,9},{6,10},{7,11},{8,4},{9,5},{10,... | collective-permute-start | bytes 73736 | tf_op jit(solution)/shard_map/ppermute | solution.py:61
  28.5 7.8 %collective-permute-start.13 = (f32[64,128]{1,0:T(8,128)S(1)}, f32[64,128]{1,0:T(8,128)S(1)}, u32[]{:S(2)}, u32[]{:S(2)}) collective-permute-start(f32[64,128]{1,0:T(8,128)S(1)} %get-tuple-element.60), channel_id=1, source_target_pairs={{0,3},{1,2},{2,1},{3,0},{4,7},{5,6},{6,5},{7,4},{8,11},{9,10},{10,... | collective-permute-start | bytes 98312 | tf_op jit(solution)/shard_map/ppermute | solution.py:65
  31.2 5.0 %collective-permute-start.12 = (f32[56,128]{1,0:T(8,128)S(1)}, f32[56,128]{1,0:T(8,128)S(1)}, u32[]{:S(2)}, u32[]{:S(2)}) collective-permute-start(f32[56,128]{1,0:T(8,128)S(1)} %get-tuple-element.59), channel_id=1, source_target_pairs={{0,2},{1,3},{2,0},{3,1},{4,6},{5,7},{6,4},{7,5},{8,10},{9,11},{10,... | collective-permute-start | bytes 86024 | tf_op jit(solution)/shard_map/ppermute | solution.py:65
  31.2 3.8 %collective-permute-start.11 = (f32[48,128]{1,0:T(8,128)S(1)}, f32[48,128]{1,0:T(8,128)S(1)}, u32[]{:S(2)}, u32[]{:S(2)}) collective-permute-start(f32[48,128]{1,0:T(8,128)S(1)} %get-tuple-element.58), channel_id=1, source_target_pairs={{0,1},{1,0},{2,3},{3,2},{4,5},{5,4},{6,7},{7,6},{8,9},{9,8},{10,11... | collective-permute-start | bytes 73736 | tf_op jit(solution)/shard_map/ppermute | solution.py:65

commit v7 on v6

--- a/solution.py
+++ b/solution.py
@@ -418,7 +418,14 @@
         forcing_ref[c] = forcing_rows(c, slice(None), mine_ref, other_ref, pick_ref).reshape(forcing_ref.shape[1:])
 
 
+FOLD = 16
+
+
 def region_rows(values, ids, tops):
+    def folded(plane):
+        return jnp.concatenate([plane[y : y + FOLD] for y in range(0, plane.shape[0], FOLD)], axis=1)
+
+    values, ids = folded(values), folded(ids)
     top, low = (ids // 8).astype(jnp.float32).astype(jnp.bfloat16), (ids % 8).astype(jnp.float32).astype(jnp.bfloat16)
     main = values.astype(jnp.bfloat16)
     rest = (values - main.astype(jnp.float32)).astype(jnp.bfloat16)
@@ -432,13 +439,13 @@
     )
 
 
-def region_sums(main, rest, ones, rows):
+def region_sums(main, rest, ones):
     over_lanes = (((1,), (1,)), ((), ()))
     total = lax.dot_general(main, ones, over_lanes, preferred_element_type=jnp.float32)
     total += lax.dot_general(rest, ones, over_lanes, preferred_element_type=jnp.float32)
     row, column = iotas(*total.shape)
-    total = jnp.where(row % rows == column % rows, total, 0.0)
-    return jnp.sum(total.reshape(total.shape[0] // rows, rows, total.shape[1]), axis=1)
+    total = jnp.where(row % FOLD == column % FOLD, total, 0.0)
+    return jnp.sum(total.reshape(total.shape[0] // FOLD, FOLD, total.shape[1]), axis=1)
 
 
 def inner_kernel(
@@ -451,7 +458,8 @@
     tops = sums_ref.shape[0]
 
     def add_up(x, values, ids):
-        at = pl.ds(pl.multiple_of(x * width, width), width)
+        span = rows // FOLD * width
+        at = pl.ds(pl.multiple_of(x * span, span), span)
         for part_ref, part in zip((main_ref, rest_ref, ones_ref), region_rows(values, ids, tops)):
             part_ref[:, at] = part
 
@@ -489,7 +497,7 @@
     reach = reach + pltpu.roll(reach, width - 2 * planes, 1) + pltpu.roll(reach, width - 4 * planes, 1)
     reach = time_step * reach * rim_nu
     add_up(planes, reach, pltpu.roll(mixed, (width - 6 * planes) % width, 1).astype(jnp.int32))
-    sums_ref[...] = region_sums(main_ref[...], rest_ref[...], ones_ref[...], rows)
+    sums_ref[...] = region_sums(main_ref[...], rest_ref[...], ones_ref[...])
 
 
 def edge_kernel(groups, masks, x0_ref, x1_ref, nux_ref, next_ref, regions_ref, sums_ref, fpack_ref, *outs):
@@ -504,7 +512,7 @@
         region_rows(time_step * nux_ref[0] * low, regions_ref[0], tops),
         region_rows(time_step * nux_ref[planes] * high, regions_ref[planes - 1], tops),
     ]
-    total = sums_ref[...] + region_sums(*(jnp.concatenate(both, axis=1) for both in zip(*ends)), rows)
+    total = sums_ref[...] + region_sums(*(jnp.concatenate(both, axis=1) for both in zip(*ends)))
     height = tops * (columns // width)
     for mask, out_ref in zip((0,) + masks, outs):
         for i in range(columns // width):
@@ -558,7 +566,7 @@
                     value += time_step * nux_ref[planes] * beside[c][1]
                 value_ref[c, x] = value
         store(i).start()
-    parts = width // rows
+    parts = width // FOLD
     tops = REG_DEV * walls // 8
     owned = REG_DEV // 8
     top, _ = iotas(tops, width)
@@ -567,7 +575,7 @@
     for i in range(8 // parts):
         for h in range(owned):
             mine = jnp.where(top == me * owned + h, total[i * tops : (i + 1) * tops], 0.0)
-            gather = (region == h * 8 + i * parts + lane // rows).astype(jnp.float32)
+            gather = (region == h * 8 + i * parts + lane // FOLD).astype(jnp.float32)
             sens += lax.dot_general(
                 jnp.broadcast_to(jnp.sum(mine, axis=0, keepdims=True), (8, width)), gather, (((1,), (1,)), ((), ())),
                 precision=lax.Precision.HIGHEST, preferred_element_type=jnp.float32,
@@ -667,7 +675,8 @@
     f0, f1 = swap(fs0, "fluid", 0), swap(fs1, "fluid", 1)
     forcing = call(forcing_kernel, f32(3, planes, rows, width), [VMEM] * 3 + [ANY], (held, other, pick, fs1))
     tops = reg_count // 8
-    columns = 8 * rows
+    columns = 8 * FOLD
+    span = (planes + 1) * rows // FOLD * width
     sum_rows = tops * (columns // width)
     inner, fpack, sums = call(
         inner_kernel,
@@ -675,9 +684,9 @@
         [VMEM] * 9,
         (forcing, velocity, nux, nuy, nuz, nuy0, rim, regions, outside),
         (
-            pltpu.VMEM((tops * rows, (planes + 1) * width), jnp.bfloat16),
-            pltpu.VMEM((tops * rows, (planes + 1) * width), jnp.bfloat16),
-            pltpu.VMEM((columns, (planes + 1) * width), jnp.bfloat16),
+            pltpu.VMEM((tops * FOLD, span), jnp.bfloat16),
+            pltpu.VMEM((tops * FOLD, span), jnp.bfloat16),
+            pltpu.VMEM((columns, span), jnp.bfloat16),
         ),
     )
     masks = tuple(range(1, walls))

time: 37.5 us -> 37.2 us (level)
  transfers between devices with their start and end apart: 14 -> 14, of which waited for: 7 -> 7; matrix products, arithmetic and copies ran while one was open for 0% -> 0% of each run, Pallas kernels for 21% -> 20%
where the time goes in v7:
time: 37.2 us; the launch traced here: 37 us
  starting transfers between devices  16.3 us (44%)
  Pallas kernels  11.6 us (31%)
  waiting for transfers between devices  8.37 us (22%)
  between operations  0.75 us (2%)
    pallas_call x11, Pallas kernels, call(): pl.pallas_call(kernel, out_shape=outs, in_specs=ins, out_specs=out_specs...  11.6 us
    ppermute x6, starting transfers between devices, swap(): return lax.ppermute(block, ('fluid', 'wall'), pairs)  8.33 us
    ppermute x8, starting transfers between devices, cross(): lax.ppermute(block, axis, [(i, i ^ mask) for i in range(lax.axis_size(axi...  8.01 us
    ppermute x8, waiting for transfers between devices, cross(): lax.ppermute(block, axis, [(i, i ^ mask) for i in range(lax.axis_size(axi...  6.3 us
    ppermute x6, waiting for transfers between devices, swap(): return lax.ppermute(block, ('fluid', 'wall'), pairs)  2.08 us
  transfers between devices with their start and end apart: 14, of which 7 were waited for; matrix products, arithmetic and copies ran while one was open for 0% of the time, Pallas kernels for 20%

profile of v7, /device:TPU:0, one launch (start us, length us, event | category | flops | bytes accessed | tf_op | source)
XLA Modules:
  0.0 37.0 jit_solution(3669571662842803595)
XLA Ops:
  0.7 1.8 %shard_map.85 = (bf16[2,528,128]{2,1,0:T(8,128)(2,1)S(1)}, bf16[2,528,128]{2,1,0:T(8,128)(2,1)S(1)}, bf16[2,528,128]{2,1,0:T(8,128)(2,1)S(1)}, bf16[2,528,128]{2...) custom-call(s32[32]{0:T(128)} %bitcast.12, bf16[32,128,128]{2,1,0:T(8,128)(2,1)} %bitcast.10, ...), custom_call_target="tpu_custom_call" | custom-call | flops 1 | bytes 1 | tf_op jit(solution)/shard_map/pallas_call | solution.py:27
  2.4 0.5 %collective-permute-start = (f32[4,32,128]{2,1,0:T(8,128)S(1)}, f32[4,32,128]{2,1,0:T(8,128)S(1)}, u32[]{:S(2)}, u32[]{:S(2)}) collective-permute-start(f32[4,32,128]{2,1,0:T(8,128)S(1)} %get-tuple-element.33), channel_id=1, source_target_pairs={{0,4},{1,5},{2,6},{3,7},{4,0},{5,1},{6,2},{7,3},{8,12},{9,13},{10,... | collective-permute-start | bytes 196616 | tf_op jit(solution)/shard_map/ppermute | solution.py:61
  2.9 2.6 %collective-permute-start.1 = (f32[4,32,128]{2,1,0:T(8,128)S(1)}, f32[4,32,128]{2,1,0:T(8,128)S(1)}, u32[]{:S(2)}, u32[]{:S(2)}) collective-permute-start(f32[4,32,128]{2,1,0:T(8,128)S(1)} %get-tuple-element.34), channel_id=1, source_target_pairs={{0,1},{1,0},{2,3},{3,2},{4,8},{5,9},{6,10},{7,11},{8,4},{9,5},{10,... | collective-permute-start | bytes 196616 | tf_op jit(solution)/shard_map/ppermute | solution.py:61
  5.6 2.0 %collective-permute-start.6 = (bf16[2,528,128]{2,1,0:T(8,128)(2,1)S(1)}, bf16[2,528,128]{2,1,0:T(8,128)(2,1)S(1)}, u32[]{:S(2)}, u32[]{:S(2)}) collective-permute-start(bf16[2,528,128]{2,1,0:T(8,128)(2,1)S(1)} %get-tuple-element.43), channel_id=1, source_target_pairs={{0,16},{4,20},{8,24},{12,28},{16,0},{20,4},{24,8},{28,12},{1,17},{... | collective-permute-start | bytes 811016 | tf_op jit(solution)/shard_map/ppermute | solution.py:65
  7.6 1.5 %collective-permute-start.7 = (bf16[2,528,128]{2,1,0:T(8,128)(2,1)S(1)}, bf16[2,528,128]{2,1,0:T(8,128)(2,1)S(1)}, u32[]{:S(2)}, u32[]{:S(2)}) collective-permute-start(bf16[2,528,128]{2,1,0:T(8,128)(2,1)S(1)} %get-tuple-element.44), channel_id=1, source_target_pairs={{0,24},{4,28},{8,16},{12,20},{16,8},{20,12},{24,0},{28,4},{1,25},{... | collective-permute-start | bytes 811016 | tf_op jit(solution)/shard_map/ppermute | solution.py:65
  9.1 0.8 %shard_map.86.edges_ref = f32[3,32,128]{2,1,0:T(8,128)S(1)} custom-call(f32[4,16,32,128]{3,2,1,0:T(8,128)S(1)} %copy-done, s32[16,32,128]{2,1,0:T(8,128)S(1)} %copy-done.1, f32[4,32,128]{2,1,0:T(8,128)S(1)} %collective-permute-done.x0_ref, f32[4,32,128]{2,1,0:T(8,128)S(1)} %collective-permute-done.1.x1_ref), custom_call_target="tpu_custom_call" | custom-call | flops 99999997952 | bytes 1 | tf_op jit(solution)/shard_map/pallas_call | solution.py:27
  9.9 3.1 %collective-permute-start.2 = (f32[3,32,128]{2,1,0:T(8,128)S(1)}, f32[3,32,128]{2,1,0:T(8,128)S(1)}, u32[]{:S(2)}, u32[]{:S(2)}) collective-permute-start(f32[3,32,128]{2,1,0:T(8,128)S(1)} %shard_map.86.edges_ref), channel_id=1, source_target_pairs={{0,1},{1,0},{2,3},{3,2},{4,5},{5,4},{6,7},{7,6},{8,9},{9,8},{10,11... | collective-permute-start | bytes 147464 | tf_op jit(solution)/shard_map/ppermute | solution.py:61
  13.1 2.1 %collective-permute-done.2.z0_ref = f32[3,32,128]{2,1,0:T(8,128)S(1)} collective-permute-done((f32[3,32,128]{2,1,0:T(8,128)S(1)}, f32[3,32,128]{2,1,0:T(8,128)S(1)}, u32[]{:S(2)}, u32[]{:S(2)}) %collective-permute-start.2) | collective-permute-done | bytes 49184 | tf_op jit(solution)/shard_map/ppermute | solution.py:61
  15.2 2.6 %shard_map.87 = (f32[3,16,32,128]{3,2,1,0:T(8,128)}, f32[3,16,32,128]{3,2,1,0:T(8,128)S(1)}, f32[17,32,128]{2,1,0:T(8,128)S(1)}, f32[16,32,128]{2,1,0:T(8,128)S(...) custom-call(s32[4,8]{1,0:T(4,128)S(1)} %bitcast.9, ...), custom_call_target="tpu_custom_call" | custom-call | flops 1 | bytes 1 | tf_op jit(solution)/shard_map/pallas_call | solution.py:27
  17.9 0.4 %shard_map.88 = (f32[32,128]{1,0:T(8,128)S(1)}, f32[32,128]{1,0:T(8,128)S(1)}, bf16[3,512,128]{2,1,0:T(8,128)(2,1)S(1)}) custom-call(s32[8,128]{1,0:T(8,128)S(1)} %get-tuple-element.38.cells_of_ref, f32[3,32,128]{2,1,0:T(8,128)S(1)} %collective-permute-done.2.z0_ref, f32[3,32,128]{2,1,0:T(8,128)S(1)} %collective-permute-done.3.z1_ref, ...), custom_call_target="tpu_custom_call" | custom-call | flops 1 | bytes 1 | tf_op jit(solution)/shard_map/pallas_call | solution.py:27
  18.3 0.7 %collective-permute-done.4.values_ref = bf16[4,16,128]{2,1,0:T(8,128)(2,1)S(1)} collective-permute-done((bf16[4,16,128]{2,1,0:T(8,128)(2,1)S(1)}, bf16[4,16,128]{2,1,0:T(8,128)(2,1)S(1)}, u32[]{:S(2)}, u32[]{:S(2)}) %collective-permute-start.4) | collective-permute-done | bytes 16416 | tf_op jit(solution)/shard_map/ppermute | solution.py:65
  19.0 1.1 %collective-permute-done.6.refs_2_ = bf16[2,528,128]{2,1,0:T(8,128)(2,1)S(1)} collective-permute-done((bf16[2,528,128]{2,1,0:T(8,128)(2,1)S(1)}, bf16[2,528,128]{2,1,0:T(8,128)(2,1)S(1)}, u32[]{:S(2)}, u32[]{:S(2)}) %collective-permute-start.6) | collective-permute-done | bytes 270368 | tf_op jit(solution)/shard_map/ppermute | solution.py:65
  20.2 0.7 %collective-permute-done.7.refs_3_ = bf16[2,528,128]{2,1,0:T(8,128)(2,1)S(1)} collective-permute-done((bf16[2,528,128]{2,1,0:T(8,128)(2,1)S(1)}, bf16[2,528,128]{2,1,0:T(8,128)(2,1)S(1)}, u32[]{:S(2)}, u32[]{:S(2)}) %collective-permute-start.7) | collective-permute-done | bytes 270368 | tf_op jit(solution)/shard_map/ppermute | solution.py:65
  20.9 0.7 %shard_map.89.after_ref = bf16[2,64,128]{2,1,0:T(8,128)(2,1)S(1)} custom-call(bf16[4,16,128]{2,1,0:T(8,128)(2,1)S(1)} %collective-permute-done.4.values_ref, bf16[3,512,128]{2,1,0:T(8,128)(2,1)S(1)} %get-tuple-element.40.after_ref.pick_ref, bf16[2,528,128]{2,1,0:T(8,128)(2,1)S(1)} %get-tuple-element.41.refs_0_, ...), custom_call_target="tpu_custom_call" | custom-call | flops 1 | bytes 1 | tf_op jit(solution)/shard_map/pallas_call | solution.py:27
  21.6 0.7 %shard_map.90.mine_ref = bf16[2,64,128]{2,1,0:T(8,128)(2,1)S(1)} custom-call(bf16[4,16,128]{2,1,0:T(8,128)(2,1)S(1)} %get-tuple-element.36.values_ref, bf16[2,64,128]{2,1,0:T(8,128)(2,1)S(1)} %shard_map.89.after_ref, bf16[2,528,128]{2,1,0:T(8,128)(2,1)S(1)} %get-tuple-element.41.refs_0_, bf16[2,528,128]{2,1,0:T(8,128)(2,1)S(1)} %collective-permute-done.5.refs_1_, ...), custom_call_target="tpu_custom_call" | custom-call | flops 1 | bytes 1 | tf_op jit(solution)/shard_map/pallas_call | solution.py:27
  22.3 0.5 %collective-permute-done.8.other_ref = bf16[2,64,128]{2,1,0:T(8,128)(2,1)S(1)} collective-permute-done((bf16[2,64,128]{2,1,0:T(8,128)(2,1)S(1)}, bf16[2,64,128]{2,1,0:T(8,128)(2,1)S(1)}, u32[]{:S(2)}, u32[]{:S(2)}) %collective-permute-start.8) | collective-permute-done | bytes 32800 | tf_op jit(solution)/shard_map/ppermute | solution.py:65
  23.3 1.7 %collective-permute-start.10 = (bf16[3,32,128]{2,1,0:T(8,128)(2,1)S(1)}, bf16[3,32,128]{2,1,0:T(8,128)(2,1)S(1)}, u32[]{:S(2)}, u32[]{:S(2)}) collective-permute-start(bf16[3,32,128]{2,1,0:T(8,128)(2,1)S(1)} %get-tuple-element.45.after_ref), channel_id=1, source_target_pairs={{0,1},{1,0},{2,3},{3,2},{4,8},{5,9},{6,10},{7,11},{8,4},{9,5},{10,... | collective-permute-start | bytes 73736 | tf_op jit(solution)/shard_map/ppermute | solution.py:61
  25.0 0.6 %shard_map.92.forcing_ref = f32[3,16,32,128]{3,2,1,0:T(8,128)S(1)} custom-call(bf16[2,64,128]{2,1,0:T(8,128)(2,1)S(1)} %shard_map.90.mine_ref, bf16[2,64,128]{2,1,0:T(8,128)(2,1)S(1)} %collective-permute-done.8.other_ref, bf16[3,512,128]{2,1,0:T(8,128)(2,1)S(1)} %get-tuple-element.40.after_ref.pick_ref, bf16[3,32,128]{2,1,0:T(8,128)(2,1)S(1)} %get-tuple-element.45.after_ref), custom_call_target="tpu_custom_call" | custom-call | flops 1 | bytes 1 | tf_op jit(solution)/shard_map/pallas_call | solution.py:27
  25.6 2.3 %shard_map.93 = (f32[3,16,32,128]{3,2,1,0:T(8,128)S(1)}, f32[32,128]{1,0:T(8,128)S(1)}, f32[8,128]{1,0:T(8,128)S(1)}) custom-call(f32[3,16,32,128]{3,2,1,0:T(8,128)S(1)} %shard_map.92.forcing_ref, f32[3,16,32,128]{3,2,1,0:T(8,128)S(1)} %get-tuple-element.46.next_ref, f32[17,32,128]{2,1,0:T(8,128)S(1)} %get-tuple-element.47.nux_ref, ...), custom_call_target="tpu_custom_call" | custom-call | flops 1 | bytes 1 | tf_op jit(solution)/shard_map/pallas_call | solution.py:27
  28.2 3.0 %collective-permute-start.13 = (f32[56,128]{1,0:T(8,128)S(1)}, f32[56,128]{1,0:T(8,128)S(1)}, u32[]{:S(2)}, u32[]{:S(2)}) collective-permute-start(f32[56,128]{1,0:T(8,128)S(1)} %get-tuple-element.60), channel_id=1, source_target_pairs={{0,3},{1,2},{2,1},{3,0},{4,7},{5,6},{6,5},{7,4},{8,11},{9,10},{10,... | collective-permute-start | bytes 86024 | tf_op jit(solution)/shard_map/ppermute | solution.py:65
  31.2 1.5 %collective-permute-start.11 = (f32[40,128]{1,0:T(8,128)S(1)}, f32[40,128]{1,0:T(8,128)S(1)}, u32[]{:S(2)}, u32[]{:S(2)}) collective-permute-start(f32[40,128]{1,0:T(8,128)S(1)} %get-tuple-element.58), channel_id=1, source_target_pairs={{0,1},{1,0},{2,3},{3,2},{4,5},{5,4},{6,7},{7,6},{8,9},{9,8},{10,11... | collective-permute-start | bytes 61448 | tf_op jit(solution)/shard_map/ppermute | solution.py:65
  32.6 2.3 %collective-permute-done.11.refs_0_ = f32[40,128]{1,0:T(8,128)S(1)} collective-permute-done((f32[40,128]{1,0:T(8,128)S(1)}, f32[40,128]{1,0:T(8,128)S(1)}, u32[]{:S(2)}, u32[]{:S(2)}) %collective-permute-start.11) | collective-permute-done | bytes 20512 | tf_op jit(solution)/shard_map/ppermute | solution.py:65
  35.0 0.9 %collective-permute-done.12.refs_1_ = f32[48,128]{1,0:T(8,128)S(1)} collective-permute-done((f32[48,128]{1,0:T(8,128)S(1)}, f32[48,128]{1,0:T(8,128)S(1)}, u32[]{:S(2)}, u32[]{:S(2)}) %collective-permute-start.12) | collective-permute-done | bytes 24608 | tf_op jit(solution)/shard_map/ppermute | solution.py:65
  35.9 1.1 %shard_map.95 = (f32[3,16,32,128]{3,2,1,0:T(8,128)}, f32[1,16]{1,0:T(1,128)}) custom-call(f32[3,16,32,128]{3,2,1,0:T(8,128)S(1)} %get-tuple-element.52.inner_ref, bf16[3,32,128]{2,1,0:T(8,128)(2,1)S(1)} %collective-permute-done.9.x0_ref, bf16[3,32,128]{2,1,0:T(8,128)(2,1)S(1)} %collective-permute-done.10.x1_ref, ...), custom_call_target="tpu_custom_call" | custom-call | flops 655360 | bytes 1572864 | tf_op jit(solution)/shard_map/pallas_call | solution.py:27
  (21 shorter events, 0.9 us)
Async XLA Ops:
  0.6 8.5 %copy-start = (f32[4,16,32,128]{3,2,1,0:T(8,128)S(1)}, f32[4,16,32,128]{3,2,1,0:T(8,128)}, u32[]{:S(2)}) copy-start(f32[4,16,32,128]{3,2,1,0:T(8,128)} %flow_ref.5) | copy-start | bytes 3145732
  0.6 8.5 %copy-start.1 = (s32[16,32,128]{2,1,0:T(8,128)S(1)}, s32[16,32,128]{2,1,0:T(8,128)}, u32[]{:S(2)}) copy-start(s32[16,32,128]{2,1,0:T(8,128)} %regions_ref.5) | copy-start | bytes 786436
  2.4 6.7 %collective-permute-start = (f32[4,32,128]{2,1,0:T(8,128)S(1)}, f32[4,32,128]{2,1,0:T(8,128)S(1)}, u32[]{:S(2)}, u32[]{:S(2)}) collective-permute-start(f32[4,32,128]{2,1,0:T(8,128)S(1)} %get-tuple-element.33), channel_id=1, source_target_pairs={{0,4},{1,5},{2,6},{3,7},{4,0},{5,1},{6,2},{7,3},{8,12},{9,13},{10,... | collective-permute-start | bytes 196616 | tf_op jit(solution)/shard_map/ppermute | solution.py:61
  2.9 6.1 %collective-permute-start.1 = (f32[4,32,128]{2,1,0:T(8,128)S(1)}, f32[4,32,128]{2,1,0:T(8,128)S(1)}, u32[]{:S(2)}, u32[]{:S(2)}) collective-permute-start(f32[4,32,128]{2,1,0:T(8,128)S(1)} %get-tuple-element.34), channel_id=1, source_target_pairs={{0,1},{1,0},{2,3},{3,2},{4,8},{5,9},{6,10},{7,11},{8,4},{9,5},{10,... | collective-permute-start | bytes 196616 | tf_op jit(solution)/shard_map/ppermute | solution.py:61
  5.6 13.5 %collective-permute-start.5 = (bf16[2,528,128]{2,1,0:T(8,128)(2,1)S(1)}, bf16[2,528,128]{2,1,0:T(8,128)(2,1)S(1)}, u32[]{:S(2)}, u32[]{:S(2)}) collective-permute-start(bf16[2,528,128]{2,1,0:T(8,128)(2,1)S(1)} %get-tuple-element.42), channel_id=1, source_target_pairs={{0,8},{4,12},{8,0},{12,4},{16,24},{20,28},{24,16},{28,20},{1,9},{5... | collective-permute-start | bytes 811016 | tf_op jit(solution)/shard_map/ppermute | solution.py:65
  5.6 14.6 %collective-permute-start.6 = (bf16[2,528,128]{2,1,0:T(8,128)(2,1)S(1)}, bf16[2,528,128]{2,1,0:T(8,128)(2,1)S(1)}, u32[]{:S(2)}, u32[]{:S(2)}) collective-permute-start(bf16[2,528,128]{2,1,0:T(8,128)(2,1)S(1)} %get-tuple-element.43), channel_id=1, source_target_pairs={{0,16},{4,20},{8,24},{12,28},{16,0},{20,4},{24,8},{28,12},{1,17},{... | collective-permute-start | bytes 811016 | tf_op jit(solution)/shard_map/ppermute | solution.py:65
  7.6 13.3 %collective-permute-start.7 = (bf16[2,528,128]{2,1,0:T(8,128)(2,1)S(1)}, bf16[2,528,128]{2,1,0:T(8,128)(2,1)S(1)}, u32[]{:S(2)}, u32[]{:S(2)}) collective-permute-start(bf16[2,528,128]{2,1,0:T(8,128)(2,1)S(1)} %get-tuple-element.44), channel_id=1, source_target_pairs={{0,24},{4,28},{8,16},{12,20},{16,8},{20,12},{24,0},{28,4},{1,25},{... | collective-permute-start | bytes 811016 | tf_op jit(solution)/shard_map/ppermute | solution.py:65
  9.1 6.1 %copy-start.2 = (s32[1,1,8,4]{2,3,1,0:T(4,128)S(1)}, s32[1,1,8,4]{2,3,1,0:T(4,128)}, u32[]{:S(2)}) copy-start(s32[1,1,8,4]{2,3,1,0:T(4,128)} %param.11) | copy-start | bytes 388
  9.9 3.2 %collective-permute-start.3 = (f32[3,32,128]{2,1,0:T(8,128)S(1)}, f32[3,32,128]{2,1,0:T(8,128)S(1)}, u32[]{:S(2)}, u32[]{:S(2)}) collective-permute-start(f32[3,32,128]{2,1,0:T(8,128)S(1)} %shard_map.86.edges_ref), channel_id=1, source_target_pairs={{0,4},{1,2},{2,1},{3,7},{4,0},{5,6},{6,5},{7,3},{8,12},{9,10},{10,... | collective-permute-start | bytes 147464 | tf_op jit(solution)/shard_map/ppermute | solution.py:61
  9.9 5.2 %collective-permute-start.2 = (f32[3,32,128]{2,1,0:T(8,128)S(1)}, f32[3,32,128]{2,1,0:T(8,128)S(1)}, u32[]{:S(2)}, u32[]{:S(2)}) collective-permute-start(f32[3,32,128]{2,1,0:T(8,128)S(1)} %shard_map.86.edges_ref), channel_id=1, source_target_pairs={{0,1},{1,0},{2,3},{3,2},{4,5},{5,4},{6,7},{7,6},{8,9},{9,8},{10,11... | collective-permute-start | bytes 147464 | tf_op jit(solution)/shard_map/ppermute | solution.py:61
  17.8 1.2 %collective-permute-start.4 = (bf16[4,16,128]{2,1,0:T(8,128)(2,1)S(1)}, bf16[4,16,128]{2,1,0:T(8,128)(2,1)S(1)}, u32[]{:S(2)}, u32[]{:S(2)}) collective-permute-start(bf16[4,16,128]{2,1,0:T(8,128)(2,1)S(1)} %get-tuple-element.37), channel_id=1, source_target_pairs={{0,4},{4,0},{8,12},{12,8},{16,20},{20,16},{24,28},{28,24},{1,5},{5... | collective-permute-start | bytes 49160 | tf_op jit(solution)/shard_map/ppermute | solution.py:65
  21.6 1.2 %collective-permute-start.8 = (bf16[2,64,128]{2,1,0:T(8,128)(2,1)S(1)}, bf16[2,64,128]{2,1,0:T(8,128)(2,1)S(1)}, u32[]{:S(2)}, u32[]{:S(2)}) collective-permute-start(bf16[2,64,128]{2,1,0:T(8,128)(2,1)S(1)} %shard_map.89.after_ref), channel_id=1, source_target_pairs={{0,4},{4,0},{8,12},{12,8},{16,20},{20,16},{24,28},{28,24},{1,5},{5... | collective-permute-start | bytes 98312 | tf_op jit(solution)/shard_map/ppermute | solution.py:65
  23.1 4.9 %collective-permute-start.9 = (bf16[3,32,128]{2,1,0:T(8,128)(2,1)S(1)}, bf16[3,32,128]{2,1,0:T(8,128)(2,1)S(1)}, u32[]{:S(2)}, u32[]{:S(2)}) collective-permute-start(bf16[3,32,128]{2,1,0:T(8,128)(2,1)S(1)} %get-tuple-element.53), channel_id=1, source_target_pairs={{0,4},{1,5},{2,6},{3,7},{4,0},{5,1},{6,2},{7,3},{8,12},{9,13},{10,... | collective-permute-start | bytes 73736 | tf_op jit(solution)/shard_map/ppermute | solution.py:61
  23.3 4.7 %collective-permute-start.10 = (bf16[3,32,128]{2,1,0:T(8,128)(2,1)S(1)}, bf16[3,32,128]{2,1,0:T(8,128)(2,1)S(1)}, u32[]{:S(2)}, u32[]{:S(2)}) collective-permute-start(bf16[3,32,128]{2,1,0:T(8,128)(2,1)S(1)} %get-tuple-element.45.after_ref), channel_id=1, source_target_pairs={{0,1},{1,0},{2,3},{3,2},{4,8},{5,9},{6,10},{7,11},{8,4},{9,5},{10,... | collective-permute-start | bytes 73736 | tf_op jit(solution)/shard_map/ppermute | solution.py:61
  28.2 7.7 %collective-permute-start.13 = (f32[56,128]{1,0:T(8,128)S(1)}, f32[56,128]{1,0:T(8,128)S(1)}, u32[]{:S(2)}, u32[]{:S(2)}) collective-permute-start(f32[56,128]{1,0:T(8,128)S(1)} %get-tuple-element.60), channel_id=1, source_target_pairs={{0,3},{1,2},{2,1},{3,0},{4,7},{5,6},{6,5},{7,4},{8,11},{9,10},{10,... | collective-permute-start | bytes 86024 | tf_op jit(solution)/shard_map/ppermute | solution.py:65
  31.2 4.7 %collective-permute-start.12 = (f32[48,128]{1,0:T(8,128)S(1)}, f32[48,128]{1,0:T(8,128)S(1)}, u32[]{:S(2)}, u32[]{:S(2)}) collective-permute-start(f32[48,128]{1,0:T(8,128)S(1)} %get-tuple-element.59), channel_id=1, source_target_pairs={{0,2},{1,3},{2,0},{3,1},{4,6},{5,7},{6,4},{7,5},{8,10},{9,11},{10,... | collective-permute-start | bytes 73736 | tf_op jit(solution)/shard_map/ppermute | solution.py:65
  31.2 3.8 %collective-permute-start.11 = (f32[40,128]{1,0:T(8,128)S(1)}, f32[40,128]{1,0:T(8,128)S(1)}, u32[]{:S(2)}, u32[]{:S(2)}) collective-permute-start(f32[40,128]{1,0:T(8,128)S(1)} %get-tuple-element.58), channel_id=1, source_target_pairs={{0,1},{1,0},{2,3},{3,2},{4,5},{5,4},{6,7},{7,6},{8,9},{9,8},{10,11... | collective-permute-start | bytes 61448 | tf_op jit(solution)/shard_map/ppermute | solution.py:65

commit v8 on v7

--- a/solution.py
+++ b/solution.py
@@ -369,14 +369,16 @@
         pick_ref[c] = (hit & (part == c)).astype(jnp.float32).astype(jnp.bfloat16)
 
 
-def product_kernel(cap, block, values_ref, after_ref, *refs):
+def product_kernel(cap, block, masks, values_ref, before_ref, *refs):
     chips, extra, width = values_ref.shape
-    recvs, out_ref = refs[:chips], refs[chips]
+    recvs, out_ref = refs[:-1], refs[-1]
     depth = cap * width
     row, lane = iotas(extra, depth)
     own = row // 3 == lane // width
     here = lax.axis_index("fluid") // 2
-    for m, recv_ref in enumerate(recvs):
+    if before_ref.shape == out_ref.shape:
+        out_ref[...] = before_ref[...]
+    for m, recv_ref in zip(masks, recvs):
         source = here ^ m
         at = pl.ds(pl.multiple_of(source * extra, extra), extra)
         weights = recv_ref[block, pl.ds(0, depth), :]
@@ -391,31 +393,31 @@
         out_ref[1, at, :] = (contrib - high.astype(jnp.float32)).astype(jnp.bfloat16)
 
 
-def forcing_rows(c, part, mine_ref, other_ref, pick_ref):
-    half = mine_ref.shape[1]
-    total = None
-    for i, share_ref in enumerate((mine_ref, other_ref)):
-        pick = pick_ref[c, part, i * half : (i + 1) * half]
-        for share in range(2):
-            product = jnp.dot(pick, share_ref[share], preferred_element_type=jnp.float32)
-            total = product if total is None else total + product
-    return total
+def shares(mine_ref, other_ref):
+    return jnp.concatenate([ref[part] for part in range(2) for ref in (mine_ref, other_ref)], axis=0)
+
+
+def forcing_rows(c, part, pick_ref, rows):
+    pick = pick_ref[c, part, :]
+    return jnp.dot(jnp.concatenate([pick, pick], axis=1), rows, preferred_element_type=jnp.float32)
 
 
 def ends_kernel(mine_ref, other_ref, pick_ref, first_ref, second_ref):
     _, rows, _ = first_ref.shape
     lines = pick_ref.shape[1]
     even = lax.axis_index("fluid") % 2 == 0
+    both = shares(mine_ref, other_ref)
     for c in range(3):
-        low = forcing_rows(c, slice(0, rows), mine_ref, other_ref, pick_ref)
-        high = forcing_rows(c, slice(lines - rows, lines), mine_ref, other_ref, pick_ref)
+        low = forcing_rows(c, slice(0, rows), pick_ref, both)
+        high = forcing_rows(c, slice(lines - rows, lines), pick_ref, both)
         first_ref[c] = jnp.where(even, high, low).astype(jnp.bfloat16)
         second_ref[c] = jnp.where(even, low, high).astype(jnp.bfloat16)
 
 
 def forcing_kernel(mine_ref, other_ref, pick_ref, after_ref, forcing_ref):
+    both = shares(mine_ref, other_ref)
     for c in range(3):
-        forcing_ref[c] = forcing_rows(c, slice(None), mine_ref, other_ref, pick_ref).reshape(forcing_ref.shape[1:])
+        forcing_ref[c] = forcing_rows(c, slice(None), pick_ref, both).reshape(forcing_ref.shape[1:])
 
 
 FOLD = 16
@@ -660,17 +662,19 @@
         (cells_of, z0, z1, zs, rim),
     )
 
-    def products(block, values, after):
+    def products(block, masks, values, before):
+        whole = (2, chips * extra, width)
         return call(
-            functools.partial(product_kernel, cap, block),
-            bf16(2, chips * extra, width),
-            [VMEM, ANY] + [VMEM] * chips,
-            (values, after, *recvs),
+            functools.partial(product_kernel, cap, block, masks),
+            bf16(*whole),
+            [VMEM, VMEM if before.shape == whole else ANY] + [VMEM] * len(masks),
+            (values, before, *(recvs[m] for m in masks)),
         )
 
-    given = products(1, borrowed, pick)
+    given = products(1, tuple(range(chips // 2)), borrowed, pick)
+    given = products(1, tuple(range(chips // 2, chips)), borrowed, given)
     other = cross(given, "fluid", 1)
-    held = products(0, mine, given)
+    held = products(0, tuple(range(chips)), mine, outside)
     fs0, fs1 = call(ends_kernel, (bf16(3, rows, width),) * 2, [VMEM] * 3, (held, other, pick))
     f0, f1 = swap(fs0, "fluid", 0), swap(fs1, "fluid", 1)
     forcing = call(forcing_kernel, f32(3, planes, rows, width), [VMEM] * 3 + [ANY], (held, other, pick, fs1))

time: 37.2 us -> 36.8 us (0.989)
    pallas_call x11 -> x12, Pallas kernels: 11.6 us -> 11.4 us  [call(): pl.pallas_call(kernel, out_shape=outs, in_specs=ins, out_specs=out_specs...]
  transfers between devices with their start and end apart: 14 -> 14, of which waited for: 7 -> 7; matrix products, arithmetic and copies ran while one was open for 0% -> 0% of each run, Pallas kernels for 20% -> 21%
where the time goes in v8:
time: 36.8 us; the launch traced here: 36.7 us
  starting transfers between devices  16.4 us (45%)
  Pallas kernels  11.4 us (31%)
  waiting for transfers between devices  8.17 us (22%)
  between operations  0.76 us (2%)
    pallas_call x12, Pallas kernels, call(): pl.pallas_call(kernel, out_shape=outs, in_specs=ins, out_specs=out_specs...  11.4 us
    ppermute x6, starting transfers between devices, swap(): return lax.ppermute(block, ('fluid', 'wall'), pairs)  8.34 us
    ppermute x8, starting transfers between devices, cross(): lax.ppermute(block, axis, [(i, i ^ mask) for i in range(lax.axis_size(axi...  8.01 us
    ppermute x8, waiting for transfers between devices, cross(): lax.ppermute(block, axis, [(i, i ^ mask) for i in range(lax.axis_size(axi...  6.1 us
    ppermute x6, waiting for transfers between devices, swap(): return lax.ppermute(block, ('fluid', 'wall'), pairs)  2.08 us
  transfers between devices with their start and end apart: 14, of which 7 were waited for; matrix products, arithmetic and copies ran while one was open for 0% of the time, Pallas kernels for 21%

profile of v8, /device:TPU:0, one launch (start us, length us, event | category | flops | bytes accessed | tf_op | source)
XLA Modules:
  0.0 36.7 jit_solution(15346182468155050740)
XLA Ops:
  0.7 1.8 %shard_map.85 = (bf16[2,528,128]{2,1,0:T(8,128)(2,1)S(1)}, bf16[2,528,128]{2,1,0:T(8,128)(2,1)S(1)}, bf16[2,528,128]{2,1,0:T(8,128)(2,1)S(1)}, bf16[2,528,128]{2...) custom-call(s32[32]{0:T(128)} %bitcast.12, bf16[32,128,128]{2,1,0:T(8,128)(2,1)} %bitcast.10, ...), custom_call_target="tpu_custom_call" | custom-call | flops 1 | bytes 1 | tf_op jit(solution)/shard_map/pallas_call | solution.py:27
  2.4 0.5 %collective-permute-start = (f32[4,32,128]{2,1,0:T(8,128)S(1)}, f32[4,32,128]{2,1,0:T(8,128)S(1)}, u32[]{:S(2)}, u32[]{:S(2)}) collective-permute-start(f32[4,32,128]{2,1,0:T(8,128)S(1)} %get-tuple-element.33), channel_id=1, source_target_pairs={{0,4},{1,5},{2,6},{3,7},{4,0},{5,1},{6,2},{7,3},{8,12},{9,13},{10,... | collective-permute-start | bytes 196616 | tf_op jit(solution)/shard_map/ppermute | solution.py:61
  2.9 2.6 %collective-permute-start.1 = (f32[4,32,128]{2,1,0:T(8,128)S(1)}, f32[4,32,128]{2,1,0:T(8,128)S(1)}, u32[]{:S(2)}, u32[]{:S(2)}) collective-permute-start(f32[4,32,128]{2,1,0:T(8,128)S(1)} %get-tuple-element.34), channel_id=1, source_target_pairs={{0,1},{1,0},{2,3},{3,2},{4,8},{5,9},{6,10},{7,11},{8,4},{9,5},{10,... | collective-permute-start | bytes 196616 | tf_op jit(solution)/shard_map/ppermute | solution.py:61
  5.6 2.0 %collective-permute-start.5 = (bf16[2,528,128]{2,1,0:T(8,128)(2,1)S(1)}, bf16[2,528,128]{2,1,0:T(8,128)(2,1)S(1)}, u32[]{:S(2)}, u32[]{:S(2)}) collective-permute-start(bf16[2,528,128]{2,1,0:T(8,128)(2,1)S(1)} %get-tuple-element.42), channel_id=1, source_target_pairs={{0,16},{4,20},{8,24},{12,28},{16,0},{20,4},{24,8},{28,12},{1,17},{... | collective-permute-start | bytes 811016 | tf_op jit(solution)/shard_map/ppermute | solution.py:65
  7.6 1.5 %collective-permute-start.6 = (bf16[2,528,128]{2,1,0:T(8,128)(2,1)S(1)}, bf16[2,528,128]{2,1,0:T(8,128)(2,1)S(1)}, u32[]{:S(2)}, u32[]{:S(2)}) collective-permute-start(bf16[2,528,128]{2,1,0:T(8,128)(2,1)S(1)} %get-tuple-element.43), channel_id=1, source_target_pairs={{0,24},{4,28},{8,16},{12,20},{16,8},{20,12},{24,0},{28,4},{1,25},{... | collective-permute-start | bytes 811016 | tf_op jit(solution)/shard_map/ppermute | solution.py:65
  9.1 0.7 %shard_map.86.edges_ref = f32[3,32,128]{2,1,0:T(8,128)S(1)} custom-call(f32[4,16,32,128]{3,2,1,0:T(8,128)S(1)} %copy-done, s32[16,32,128]{2,1,0:T(8,128)S(1)} %copy-done.1, f32[4,32,128]{2,1,0:T(8,128)S(1)} %collective-permute-done.x0_ref, f32[4,32,128]{2,1,0:T(8,128)S(1)} %collective-permute-done.1.x1_ref), custom_call_target="tpu_custom_call" | custom-call | flops 99999997952 | bytes 1 | tf_op jit(solution)/shard_map/pallas_call | solution.py:27
  9.9 3.1 %collective-permute-start.2 = (f32[3,32,128]{2,1,0:T(8,128)S(1)}, f32[3,32,128]{2,1,0:T(8,128)S(1)}, u32[]{:S(2)}, u32[]{:S(2)}) collective-permute-start(f32[3,32,128]{2,1,0:T(8,128)S(1)} %shard_map.86.edges_ref), channel_id=1, source_target_pairs={{0,1},{1,0},{2,3},{3,2},{4,5},{5,4},{6,7},{7,6},{8,9},{9,8},{10,11... | collective-permute-start | bytes 147464 | tf_op jit(solution)/shard_map/ppermute | solution.py:61
  13.1 2.1 %collective-permute-done.2.z0_ref = f32[3,32,128]{2,1,0:T(8,128)S(1)} collective-permute-done((f32[3,32,128]{2,1,0:T(8,128)S(1)}, f32[3,32,128]{2,1,0:T(8,128)S(1)}, u32[]{:S(2)}, u32[]{:S(2)}) %collective-permute-start.2) | collective-permute-done | bytes 49184 | tf_op jit(solution)/shard_map/ppermute | solution.py:61
  15.1 2.6 %shard_map.87 = (f32[3,16,32,128]{3,2,1,0:T(8,128)}, f32[3,16,32,128]{3,2,1,0:T(8,128)S(1)}, f32[17,32,128]{2,1,0:T(8,128)S(1)}, f32[16,32,128]{2,1,0:T(8,128)S(...) custom-call(s32[4,8]{1,0:T(4,128)S(1)} %bitcast.9, ...), custom_call_target="tpu_custom_call" | custom-call | flops 1 | bytes 1 | tf_op jit(solution)/shard_map/pallas_call | solution.py:27
  17.9 0.4 %shard_map.88 = (f32[32,128]{1,0:T(8,128)S(1)}, f32[32,128]{1,0:T(8,128)S(1)}, bf16[3,512,128]{2,1,0:T(8,128)(2,1)S(1)}) custom-call(s32[8,128]{1,0:T(8,128)S(1)} %get-tuple-element.37.cells_of_ref, f32[3,32,128]{2,1,0:T(8,128)S(1)} %collective-permute-done.2.z0_ref, f32[3,32,128]{2,1,0:T(8,128)S(1)} %collective-permute-done.3.z1_ref, ...), custom_call_target="tpu_custom_call" | custom-call | flops 1 | bytes 1 | tf_op jit(solution)/shard_map/pallas_call | solution.py:27
  18.3 0.7 %collective-permute-done.7.values_ref = bf16[4,16,128]{2,1,0:T(8,128)(2,1)S(1)} collective-permute-done((bf16[4,16,128]{2,1,0:T(8,128)(2,1)S(1)}, bf16[4,16,128]{2,1,0:T(8,128)(2,1)S(1)}, u32[]{:S(2)}, u32[]{:S(2)}) %collective-permute-start.7) | collective-permute-done | bytes 16416 | tf_op jit(solution)/shard_map/ppermute | solution.py:65
  19.0 0.4 %shard_map.90.before_ref = bf16[2,64,128]{2,1,0:T(8,128)(2,1)S(1)} custom-call(bf16[4,16,128]{2,1,0:T(8,128)(2,1)S(1)} %collective-permute-done.7.values_ref, bf16[3,512,128]{2,1,0:T(8,128)(2,1)S(1)} %get-tuple-element.45.before_ref.pick_ref, bf16[2,528,128]{2,1,0:T(8,128)(2,1)S(1)} %get-tuple-element.40.refs_0_, ...), custom_call_target="tpu_custom_call" | custom-call | flops 1 | bytes 1 | tf_op jit(solution)/shard_map/pallas_call | solution.py:27
  19.4 0.7 %collective-permute-done.5.refs_2_.refs_0_ = bf16[2,528,128]{2,1,0:T(8,128)(2,1)S(1)} collective-permute-done((bf16[2,528,128]{2,1,0:T(8,128)(2,1)S(1)}, bf16[2,528,128]{2,1,0:T(8,128)(2,1)S(1)}, u32[]{:S(2)}, u32[]{:S(2)}) %collective-permute-start.5) | collective-permute-done | bytes 270368 | tf_op jit(solution)/shard_map/ppermute | solution.py:65
  20.2 0.7 %collective-permute-done.6.refs_3_.refs_1_ = bf16[2,528,128]{2,1,0:T(8,128)(2,1)S(1)} collective-permute-done((bf16[2,528,128]{2,1,0:T(8,128)(2,1)S(1)}, bf16[2,528,128]{2,1,0:T(8,128)(2,1)S(1)}, u32[]{:S(2)}, u32[]{:S(2)}) %collective-permute-start.6) | collective-permute-done | bytes 270368 | tf_op jit(solution)/shard_map/ppermute | solution.py:65
  20.9 0.4 %shard_map.91 = bf16[2,64,128]{2,1,0:T(8,128)(2,1)S(1)} custom-call(bf16[4,16,128]{2,1,0:T(8,128)(2,1)S(1)} %collective-permute-done.7.values_ref, bf16[2,64,128]{2,1,0:T(8,128)(2,1)S(1)} %shard_map.90.before_ref, bf16[2,528,128]{2,1,0:T(8,128)(2,1)S(1)} %collective-permute-done.5.refs_2_.refs_0_, bf16[2,528,128]{2,1,0:T(8,128)(2,1)S(1)} %collective-permute-done.6.refs_3_.refs_1_), custom_call_target="tpu_custom_call" | custom-call | flops 1 | bytes 1 | tf_op jit(solution)/shard_map/pallas_call | solution.py:27
  21.3 0.7 %shard_map.89.mine_ref = bf16[2,64,128]{2,1,0:T(8,128)(2,1)S(1)} custom-call(bf16[4,16,128]{2,1,0:T(8,128)(2,1)S(1)} %get-tuple-element.36.values_ref, f32[32,128]{1,0:T(8,128)S(1)} %get-tuple-element.39.before_ref.outside_ref, bf16[2,528,128]{2,1,0:T(8,128)(2,1)S(1)} %get-tuple-element.40.refs_0_, bf16[2,528,128]{2,1,0:T(8,128)(2,1)S(1)} %collective-permute-done.4.refs_1_, ...), custom_call_target="tpu_custom_call" | custom-call | flops 1 | bytes 1 | tf_op jit(solution)/shard_map/pallas_call | solution.py:27
  22.0 0.5 %collective-permute-done.8.other_ref = bf16[2,64,128]{2,1,0:T(8,128)(2,1)S(1)} collective-permute-done((bf16[2,64,128]{2,1,0:T(8,128)(2,1)S(1)}, bf16[2,64,128]{2,1,0:T(8,128)(2,1)S(1)}, u32[]{:S(2)}, u32[]{:S(2)}) %collective-permute-start.8) | collective-permute-done | bytes 32800 | tf_op jit(solution)/shard_map/ppermute | solution.py:65
  22.9 1.7 %collective-permute-start.10 = (bf16[3,32,128]{2,1,0:T(8,128)(2,1)S(1)}, bf16[3,32,128]{2,1,0:T(8,128)(2,1)S(1)}, u32[]{:S(2)}, u32[]{:S(2)}) collective-permute-start(bf16[3,32,128]{2,1,0:T(8,128)(2,1)S(1)} %get-tuple-element.46.after_ref), channel_id=1, source_target_pairs={{0,1},{1,0},{2,3},{3,2},{4,8},{5,9},{6,10},{7,11},{8,4},{9,5},{10,... | collective-permute-start | bytes 73736 | tf_op jit(solution)/shard_map/ppermute | solution.py:61
  25.0 2.3 %shard_map.94 = (f32[3,16,32,128]{3,2,1,0:T(8,128)S(1)}, f32[32,128]{1,0:T(8,128)S(1)}, f32[8,128]{1,0:T(8,128)S(1)}) custom-call(f32[3,16,32,128]{3,2,1,0:T(8,128)S(1)} %shard_map.93.forcing_ref, f32[3,16,32,128]{3,2,1,0:T(8,128)S(1)} %get-tuple-element.47.next_ref, f32[17,32,128]{2,1,0:T(8,128)S(1)} %get-tuple-element.48.nux_ref, ...), custom_call_target="tpu_custom_call" | custom-call | flops 1 | bytes 1 | tf_op jit(solution)/shard_map/pallas_call | solution.py:27
  27.6 3.2 %collective-permute-start.13 = (f32[56,128]{1,0:T(8,128)S(1)}, f32[56,128]{1,0:T(8,128)S(1)}, u32[]{:S(2)}, u32[]{:S(2)}) collective-permute-start(f32[56,128]{1,0:T(8,128)S(1)} %get-tuple-element.60), channel_id=1, source_target_pairs={{0,3},{1,2},{2,1},{3,0},{4,7},{5,6},{6,5},{7,4},{8,11},{9,10},{10,... | collective-permute-start | bytes 86024 | tf_op jit(solution)/shard_map/ppermute | solution.py:65
  30.8 1.2 %collective-permute-start.11 = (f32[40,128]{1,0:T(8,128)S(1)}, f32[40,128]{1,0:T(8,128)S(1)}, u32[]{:S(2)}, u32[]{:S(2)}) collective-permute-start(f32[40,128]{1,0:T(8,128)S(1)} %get-tuple-element.58), channel_id=1, source_target_pairs={{0,1},{1,0},{2,3},{3,2},{4,5},{5,4},{6,7},{7,6},{8,9},{9,8},{10,11... | collective-permute-start | bytes 61448 | tf_op jit(solution)/shard_map/ppermute | solution.py:65
  32.1 2.8 %collective-permute-done.11.refs_0_ = f32[40,128]{1,0:T(8,128)S(1)} collective-permute-done((f32[40,128]{1,0:T(8,128)S(1)}, f32[40,128]{1,0:T(8,128)S(1)}, u32[]{:S(2)}, u32[]{:S(2)}) %collective-permute-start.11) | collective-permute-done | bytes 20512 | tf_op jit(solution)/shard_map/ppermute | solution.py:65
  34.9 0.7 %collective-permute-done.12.refs_1_ = f32[48,128]{1,0:T(8,128)S(1)} collective-permute-done((f32[48,128]{1,0:T(8,128)S(1)}, f32[48,128]{1,0:T(8,128)S(1)}, u32[]{:S(2)}, u32[]{:S(2)}) %collective-permute-start.12) | collective-permute-done | bytes 24608 | tf_op jit(solution)/shard_map/ppermute | solution.py:65
  35.5 1.1 %shard_map.96 = (f32[3,16,32,128]{3,2,1,0:T(8,128)}, f32[1,16]{1,0:T(1,128)}) custom-call(f32[3,16,32,128]{3,2,1,0:T(8,128)S(1)} %get-tuple-element.52.inner_ref, bf16[3,32,128]{2,1,0:T(8,128)(2,1)S(1)} %collective-permute-done.9.x0_ref, bf16[3,32,128]{2,1,0:T(8,128)(2,1)S(1)} %collective-permute-done.10.x1_ref, ...), custom_call_target="tpu_custom_call" | custom-call | flops 655360 | bytes 1572864 | tf_op jit(solution)/shard_map/pallas_call | solution.py:27
  (22 shorter events, 1.2 us)
Async XLA Ops:
  0.6 8.5 %copy-start = (f32[4,16,32,128]{3,2,1,0:T(8,128)S(1)}, f32[4,16,32,128]{3,2,1,0:T(8,128)}, u32[]{:S(2)}) copy-start(f32[4,16,32,128]{3,2,1,0:T(8,128)} %flow_ref.5) | copy-start | bytes 3145732
  0.6 8.5 %copy-start.1 = (s32[16,32,128]{2,1,0:T(8,128)S(1)}, s32[16,32,128]{2,1,0:T(8,128)}, u32[]{:S(2)}) copy-start(s32[16,32,128]{2,1,0:T(8,128)} %regions_ref.5) | copy-start | bytes 786436
  2.4 6.7 %collective-permute-start = (f32[4,32,128]{2,1,0:T(8,128)S(1)}, f32[4,32,128]{2,1,0:T(8,128)S(1)}, u32[]{:S(2)}, u32[]{:S(2)}) collective-permute-start(f32[4,32,128]{2,1,0:T(8,128)S(1)} %get-tuple-element.33), channel_id=1, source_target_pairs={{0,4},{1,5},{2,6},{3,7},{4,0},{5,1},{6,2},{7,3},{8,12},{9,13},{10,... | collective-permute-start | bytes 196616 | tf_op jit(solution)/shard_map/ppermute | solution.py:61
  2.9 6.1 %collective-permute-start.1 = (f32[4,32,128]{2,1,0:T(8,128)S(1)}, f32[4,32,128]{2,1,0:T(8,128)S(1)}, u32[]{:S(2)}, u32[]{:S(2)}) collective-permute-start(f32[4,32,128]{2,1,0:T(8,128)S(1)} %get-tuple-element.34), channel_id=1, source_target_pairs={{0,1},{1,0},{2,3},{3,2},{4,8},{5,9},{6,10},{7,11},{8,4},{9,5},{10,... | collective-permute-start | bytes 196616 | tf_op jit(solution)/shard_map/ppermute | solution.py:61
  5.6 13.4 %collective-permute-start.4 = (bf16[2,528,128]{2,1,0:T(8,128)(2,1)S(1)}, bf16[2,528,128]{2,1,0:T(8,128)(2,1)S(1)}, u32[]{:S(2)}, u32[]{:S(2)}) collective-permute-start(bf16[2,528,128]{2,1,0:T(8,128)(2,1)S(1)} %get-tuple-element.41), channel_id=1, source_target_pairs={{0,8},{4,12},{8,0},{12,4},{16,24},{20,28},{24,16},{28,20},{1,9},{5... | collective-permute-start | bytes 811016 | tf_op jit(solution)/shard_map/ppermute | solution.py:65
  5.6 14.6 %collective-permute-start.5 = (bf16[2,528,128]{2,1,0:T(8,128)(2,1)S(1)}, bf16[2,528,128]{2,1,0:T(8,128)(2,1)S(1)}, u32[]{:S(2)}, u32[]{:S(2)}) collective-permute-start(bf16[2,528,128]{2,1,0:T(8,128)(2,1)S(1)} %get-tuple-element.42), channel_id=1, source_target_pairs={{0,16},{4,20},{8,24},{12,28},{16,0},{20,4},{24,8},{28,12},{1,17},{... | collective-permute-start | bytes 811016 | tf_op jit(solution)/shard_map/ppermute | solution.py:65
  7.6 13.3 %collective-permute-start.6 = (bf16[2,528,128]{2,1,0:T(8,128)(2,1)S(1)}, bf16[2,528,128]{2,1,0:T(8,128)(2,1)S(1)}, u32[]{:S(2)}, u32[]{:S(2)}) collective-permute-start(bf16[2,528,128]{2,1,0:T(8,128)(2,1)S(1)} %get-tuple-element.43), channel_id=1, source_target_pairs={{0,24},{4,28},{8,16},{12,20},{16,8},{20,12},{24,0},{28,4},{1,25},{... | collective-permute-start | bytes 811016 | tf_op jit(solution)/shard_map/ppermute | solution.py:65
  9.1 6.0 %copy-start.2 = (s32[1,1,8,4]{2,3,1,0:T(4,128)S(1)}, s32[1,1,8,4]{2,3,1,0:T(4,128)}, u32[]{:S(2)}) copy-start(s32[1,1,8,4]{2,3,1,0:T(4,128)} %param.11) | copy-start | bytes 388
  9.9 3.2 %collective-permute-start.3 = (f32[3,32,128]{2,1,0:T(8,128)S(1)}, f32[3,32,128]{2,1,0:T(8,128)S(1)}, u32[]{:S(2)}, u32[]{:S(2)}) collective-permute-start(f32[3,32,128]{2,1,0:T(8,128)S(1)} %shard_map.86.edges_ref), channel_id=1, source_target_pairs={{0,4},{1,2},{2,1},{3,7},{4,0},{5,6},{6,5},{7,3},{8,12},{9,10},{10,... | collective-permute-start | bytes 147464 | tf_op jit(solution)/shard_map/ppermute | solution.py:61
  9.9 5.2 %collective-permute-start.2 = (f32[3,32,128]{2,1,0:T(8,128)S(1)}, f32[3,32,128]{2,1,0:T(8,128)S(1)}, u32[]{:S(2)}, u32[]{:S(2)}) collective-permute-start(f32[3,32,128]{2,1,0:T(8,128)S(1)} %shard_map.86.edges_ref), channel_id=1, source_target_pairs={{0,1},{1,0},{2,3},{3,2},{4,5},{5,4},{6,7},{7,6},{8,9},{9,8},{10,11... | collective-permute-start | bytes 147464 | tf_op jit(solution)/shard_map/ppermute | solution.py:61
  17.8 1.2 %collective-permute-start.7 = (bf16[4,16,128]{2,1,0:T(8,128)(2,1)S(1)}, bf16[4,16,128]{2,1,0:T(8,128)(2,1)S(1)}, u32[]{:S(2)}, u32[]{:S(2)}) collective-permute-start(bf16[4,16,128]{2,1,0:T(8,128)(2,1)S(1)} %get-tuple-element.44), channel_id=1, source_target_pairs={{0,4},{4,0},{8,12},{12,8},{16,20},{20,16},{24,28},{28,24},{1,5},{5... | collective-permute-start | bytes 49160 | tf_op jit(solution)/shard_map/ppermute | solution.py:65
  21.3 1.2 %collective-permute-start.8 = (bf16[2,64,128]{2,1,0:T(8,128)(2,1)S(1)}, bf16[2,64,128]{2,1,0:T(8,128)(2,1)S(1)}, u32[]{:S(2)}, u32[]{:S(2)}) collective-permute-start(bf16[2,64,128]{2,1,0:T(8,128)(2,1)S(1)} %shard_map.91), channel_id=1, source_target_pairs={{0,4},{4,0},{8,12},{12,8},{16,20},{20,16},{24,28},{28,24},{1,5},{5... | collective-permute-start | bytes 98312 | tf_op jit(solution)/shard_map/ppermute | solution.py:65
  22.7 4.6 %collective-permute-start.9 = (bf16[3,32,128]{2,1,0:T(8,128)(2,1)S(1)}, bf16[3,32,128]{2,1,0:T(8,128)(2,1)S(1)}, u32[]{:S(2)}, u32[]{:S(2)}) collective-permute-start(bf16[3,32,128]{2,1,0:T(8,128)(2,1)S(1)} %get-tuple-element.53), channel_id=1, source_target_pairs={{0,4},{1,5},{2,6},{3,7},{4,0},{5,1},{6,2},{7,3},{8,12},{9,13},{10,... | collective-permute-start | bytes 73736 | tf_op jit(solution)/shard_map/ppermute | solution.py:61
  22.9 4.4 %collective-permute-start.10 = (bf16[3,32,128]{2,1,0:T(8,128)(2,1)S(1)}, bf16[3,32,128]{2,1,0:T(8,128)(2,1)S(1)}, u32[]{:S(2)}, u32[]{:S(2)}) collective-permute-start(bf16[3,32,128]{2,1,0:T(8,128)(2,1)S(1)} %get-tuple-element.46.after_ref), channel_id=1, source_target_pairs={{0,1},{1,0},{2,3},{3,2},{4,8},{5,9},{6,10},{7,11},{8,4},{9,5},{10,... | collective-permute-start | bytes 73736 | tf_op jit(solution)/shard_map/ppermute | solution.py:61
  27.6 7.9 %collective-permute-start.13 = (f32[56,128]{1,0:T(8,128)S(1)}, f32[56,128]{1,0:T(8,128)S(1)}, u32[]{:S(2)}, u32[]{:S(2)}) collective-permute-start(f32[56,128]{1,0:T(8,128)S(1)} %get-tuple-element.60), channel_id=1, source_target_pairs={{0,3},{1,2},{2,1},{3,0},{4,7},{5,6},{6,5},{7,4},{8,11},{9,10},{10,... | collective-permute-start | bytes 86024 | tf_op jit(solution)/shard_map/ppermute | solution.py:65
  30.8 4.7 %collective-permute-start.12 = (f32[48,128]{1,0:T(8,128)S(1)}, f32[48,128]{1,0:T(8,128)S(1)}, u32[]{:S(2)}, u32[]{:S(2)}) collective-permute-start(f32[48,128]{1,0:T(8,128)S(1)} %get-tuple-element.59), channel_id=1, source_target_pairs={{0,2},{1,3},{2,0},{3,1},{4,6},{5,7},{6,4},{7,5},{8,10},{9,11},{10,... | collective-permute-start | bytes 73736 | tf_op jit(solution)/shard_map/ppermute | solution.py:65
  30.8 4.0 %collective-permute-start.11 = (f32[40,128]{1,0:T(8,128)S(1)}, f32[40,128]{1,0:T(8,128)S(1)}, u32[]{:S(2)}, u32[]{:S(2)}) collective-permute-start(f32[40,128]{1,0:T(8,128)S(1)} %get-tuple-element.58), channel_id=1, source_target_pairs={{0,1},{1,0},{2,3},{3,2},{4,5},{5,4},{6,7},{7,6},{8,9},{9,8},{10,11... | collective-permute-start | bytes 61448 | tf_op jit(solution)/shard_map/ppermute | solution.py:65

commit v9 on v8

--- a/solution.py
+++ b/solution.py
@@ -220,19 +220,6 @@
     slot_of = lax.fori_loop(
         0, count_tiles, place, jnp.full((8, count_tiles), -1, jnp.int32), unroll=True
     )
-    for p in range(in_sems.shape[0]):
-        load(p).wait()
-
-    for m in list(range(1, chips)) + [0]:
-        for j in range(2):
-            b = me ^ (2 * m + j)
-            for k in range(cap):
-                t = slot_ref[b * cap + k]
-                at = (j, slice(k * width, (k + 1) * width))
-                if slots > count_tiles:
-                    sends[m][at] = jnp.where(t >= 0, held_ref[jnp.maximum(t, 0)], jnp.zeros((width, width), jnp.bfloat16))
-                else:
-                    sends[m][at] = held_ref[t]
     seen.wait()
     row = lax.broadcasted_iota(jnp.int32, (groups * extra, count_tiles), 0)
     within = row % extra
@@ -246,6 +233,19 @@
         )
     rows_ref[...] = total.astype(jnp.bfloat16)
 
+    for p in range(in_sems.shape[0]):
+        load(p).wait()
+
+    for m in list(range(1, chips)) + [0]:
+        for j in range(2):
+            b = me ^ (2 * m + j)
+            for k in range(cap):
+                t = slot_ref[b * cap + k]
+                at = (j, slice(k * width, (k + 1) * width))
+                if slots > count_tiles:
+                    sends[m][at] = jnp.where(t >= 0, held_ref[jnp.maximum(t, 0)], jnp.zeros((width, width), jnp.bfloat16))
+                else:
+                    sends[m][at] = held_ref[t]
     for m in range(chips):
         for j in range(2):
             b = me ^ (2 * m + j)
@@ -346,7 +346,8 @@
 
 
 def pick_kernel(
-    sizes, cells_of_ref, z0_ref, z1_ref, edges_ref, rim_ref, outside_ref, rims_ref, pick_ref
+    sizes, cells_of_ref, z0_ref, z1_ref, edges_ref, rim_ref, nuy_ref, nuz_ref, nuy0_ref,
+    outside_ref, rims_ref, pick_ref, nuyd_ref, nuzd_ref,
 ):
     _, rows, width = edges_ref.shape
     groups, walls = sizes
@@ -367,6 +368,10 @@
     part = (slot_lane % extra) % 3
     for c in range(3):
         pick_ref[c] = (hit & (part == c)).astype(jnp.float32).astype(jnp.bfloat16)
+    row, _ = iotas(rows, width)
+    for x in range(planes):
+        nuyd_ref[x] = jnp.where(row == 0, nuy0_ref[x : x + 1, :], pltpu.roll(nuy_ref[x], 1, 0))
+        nuzd_ref[x] = jnp.where(lane == 0, edge_of(rim_nu, x), pltpu.roll(nuz_ref[x], 1, 1))
 
 
 def product_kernel(cap, block, masks, values_ref, before_ref, *refs):
@@ -451,7 +456,7 @@
 
 
 def inner_kernel(
-    forcing_ref, next_ref, nux_ref, nuy_ref, nuz_ref, nuy0_ref, rim_ref, regions_ref, outside_ref,
+    forcing_ref, next_ref, nux_ref, nuy_ref, nuyd_ref, nuz_ref, nuzd_ref, rim_ref, regions_ref, outside_ref,
     adjoint_ref, fpack_ref, sums_ref, main_ref, rest_ref, ones_ref,
 ):
     _, planes, rows, width = forcing_ref.shape
@@ -466,10 +471,7 @@
             part_ref[:, at] = part
 
     def plane(x, fpack):
-        nuy, nuz = nuy_ref[x], nuz_ref[x]
-        nuy_down = jnp.where(row == 0, nuy0_ref[pl.ds(x, 1), :], pltpu.roll(nuy, 1, 0))
-        nuz_down = jnp.where(lane == 0, edge_of(rim_nu, x), pltpu.roll(nuz, 1, 1))
-        nus = (nux_ref[x + 1], nux_ref[x], nuy, nuy_down, nuz, nuz_down)
+        nus = (nux_ref[x + 1], nux_ref[x], nuy_ref[x], nuyd_ref[x], nuz_ref[x], nuzd_ref[x])
         next_up, next_down = jnp.minimum(x + 1, planes - 1), jnp.maximum(x - 1, 0)
         at_top, at_bottom = x == planes - 1, x == 0
         product = None
@@ -655,11 +657,11 @@
         out_specs=(HBM,) + (VMEM,) * 9,
     )
     borrowed = cross(lent, "fluid", 1)
-    outside, rims, pick = call(
+    outside, rims, pick, nuyd, nuzd = call(
         functools.partial(pick_kernel, sizes),
-        (f32(rows, width), f32(rows, width), bf16(3, planes * rows, slot_rows)),
-        [VMEM] * 5,
-        (cells_of, z0, z1, zs, rim),
+        (f32(rows, width), f32(rows, width), bf16(3, planes * rows, slot_rows)) + (f32(planes, rows, width),) * 2,
+        [VMEM] * 8,
+        (cells_of, z0, z1, zs, rim, nuy, nuz, nuy0),
     )
 
     def products(block, masks, values, before):
@@ -685,8 +687,8 @@
     inner, fpack, sums = call(
         inner_kernel,
         (f32(3, planes, rows, width), f32(rows, width), f32(tops, columns)),
-        [VMEM] * 9,
-        (forcing, velocity, nux, nuy, nuz, nuy0, rim, regions, outside),
+        [VMEM] * 10,
+        (forcing, velocity, nux, nuy, nuyd, nuz, nuzd, rim, regions, outside),
         (
             pltpu.VMEM((tops * FOLD, span), jnp.bfloat16),
             pltpu.VMEM((tops * FOLD, span), jnp.bfloat16),

time: 36.8 us -> 36.7 us (level)
  no operation moved by 1% of the time
where the time goes in v9:
time: 36.7 us; the launch traced here: 36.5 us
  starting transfers between devices  16.4 us (45%)
  Pallas kernels  11.2 us (31%)
  waiting for transfers between devices  8.25 us (22%)
  between operations  0.76 us (2%)
    pallas_call x12, Pallas kernels, call(): pl.pallas_call(kernel, out_shape=outs, in_specs=ins, out_specs=out_specs...  11.2 us
    ppermute x6, starting transfers between devices, swap(): return lax.ppermute(block, ('fluid', 'wall'), pairs)  8.34 us
    ppermute x8, starting transfers between devices, cross(): lax.ppermute(block, axis, [(i, i ^ mask) for i in range(lax.axis_size(axi...  8.01 us
    ppermute x8, waiting for transfers between devices, cross(): lax.ppermute(block, axis, [(i, i ^ mask) for i in range(lax.axis_size(axi...  6.17 us
    ppermute x6, waiting for transfers between devices, swap(): return lax.ppermute(block, ('fluid', 'wall'), pairs)  2.08 us
  transfers between devices with their start and end apart: 14, of which 7 were waited for; matrix products, arithmetic and copies ran while one was open for 0% of the time, Pallas kernels for 21%

profile of v9, /device:TPU:0, one launch (start us, length us, event | category | flops | bytes accessed | tf_op | source)
XLA Modules:
  0.0 36.5 jit_solution(14598158983681050549)
XLA Ops:
  0.7 1.6 %shard_map.85 = (bf16[2,528,128]{2,1,0:T(8,128)(2,1)S(1)}, bf16[2,528,128]{2,1,0:T(8,128)(2,1)S(1)}, bf16[2,528,128]{2,1,0:T(8,128)(2,1)S(1)}, bf16[2,528,128]{2...) custom-call(s32[32]{0:T(128)} %bitcast.12, bf16[32,128,128]{2,1,0:T(8,128)(2,1)} %bitcast.10, ...), custom_call_target="tpu_custom_call" | custom-call | flops 1 | bytes 1 | tf_op jit(solution)/shard_map/pallas_call | solution.py:27
  2.3 0.5 %collective-permute-start = (f32[4,32,128]{2,1,0:T(8,128)S(1)}, f32[4,32,128]{2,1,0:T(8,128)S(1)}, u32[]{:S(2)}, u32[]{:S(2)}) collective-permute-start(f32[4,32,128]{2,1,0:T(8,128)S(1)} %get-tuple-element.35), channel_id=1, source_target_pairs={{0,4},{1,5},{2,6},{3,7},{4,0},{5,1},{6,2},{7,3},{8,12},{9,13},{10,... | collective-permute-start | bytes 196616 | tf_op jit(solution)/shard_map/ppermute | solution.py:61
  2.8 2.6 %collective-permute-start.1 = (f32[4,32,128]{2,1,0:T(8,128)S(1)}, f32[4,32,128]{2,1,0:T(8,128)S(1)}, u32[]{:S(2)}, u32[]{:S(2)}) collective-permute-start(f32[4,32,128]{2,1,0:T(8,128)S(1)} %get-tuple-element.36), channel_id=1, source_target_pairs={{0,1},{1,0},{2,3},{3,2},{4,8},{5,9},{6,10},{7,11},{8,4},{9,5},{10,... | collective-permute-start | bytes 196616 | tf_op jit(solution)/shard_map/ppermute | solution.py:61
  5.5 2.0 %collective-permute-start.5 = (bf16[2,528,128]{2,1,0:T(8,128)(2,1)S(1)}, bf16[2,528,128]{2,1,0:T(8,128)(2,1)S(1)}, u32[]{:S(2)}, u32[]{:S(2)}) collective-permute-start(bf16[2,528,128]{2,1,0:T(8,128)(2,1)S(1)} %get-tuple-element.47), channel_id=1, source_target_pairs={{0,16},{4,20},{8,24},{12,28},{16,0},{20,4},{24,8},{28,12},{1,17},{... | collective-permute-start | bytes 811016 | tf_op jit(solution)/shard_map/ppermute | solution.py:65
  7.5 1.5 %collective-permute-start.6 = (bf16[2,528,128]{2,1,0:T(8,128)(2,1)S(1)}, bf16[2,528,128]{2,1,0:T(8,128)(2,1)S(1)}, u32[]{:S(2)}, u32[]{:S(2)}) collective-permute-start(bf16[2,528,128]{2,1,0:T(8,128)(2,1)S(1)} %get-tuple-element.48), channel_id=1, source_target_pairs={{0,24},{4,28},{8,16},{12,20},{16,8},{20,12},{24,0},{28,4},{1,25},{... | collective-permute-start | bytes 811016 | tf_op jit(solution)/shard_map/ppermute | solution.py:65
  9.0 0.8 %shard_map.86.edges_ref = f32[3,32,128]{2,1,0:T(8,128)S(1)} custom-call(f32[4,16,32,128]{3,2,1,0:T(8,128)S(1)} %copy-done, s32[16,32,128]{2,1,0:T(8,128)S(1)} %copy-done.1, f32[4,32,128]{2,1,0:T(8,128)S(1)} %collective-permute-done.x0_ref, f32[4,32,128]{2,1,0:T(8,128)S(1)} %collective-permute-done.1.x1_ref), custom_call_target="tpu_custom_call" | custom-call | flops 99999997952 | bytes 1 | tf_op jit(solution)/shard_map/pallas_call | solution.py:27
  9.8 3.1 %collective-permute-start.2 = (f32[3,32,128]{2,1,0:T(8,128)S(1)}, f32[3,32,128]{2,1,0:T(8,128)S(1)}, u32[]{:S(2)}, u32[]{:S(2)}) collective-permute-start(f32[3,32,128]{2,1,0:T(8,128)S(1)} %shard_map.86.edges_ref), channel_id=1, source_target_pairs={{0,1},{1,0},{2,3},{3,2},{4,5},{5,4},{6,7},{7,6},{8,9},{9,8},{10,11... | collective-permute-start | bytes 147464 | tf_op jit(solution)/shard_map/ppermute | solution.py:61
  13.0 2.1 %collective-permute-done.2.z0_ref = f32[3,32,128]{2,1,0:T(8,128)S(1)} collective-permute-done((f32[3,32,128]{2,1,0:T(8,128)S(1)}, f32[3,32,128]{2,1,0:T(8,128)S(1)}, u32[]{:S(2)}, u32[]{:S(2)}) %collective-permute-start.2) | collective-permute-done | bytes 49184 | tf_op jit(solution)/shard_map/ppermute | solution.py:61
  15.0 2.6 %shard_map.87 = (f32[3,16,32,128]{3,2,1,0:T(8,128)}, f32[3,16,32,128]{3,2,1,0:T(8,128)S(1)}, f32[17,32,128]{2,1,0:T(8,128)S(1)}, f32[16,32,128]{2,1,0:T(8,128)S(...) custom-call(s32[4,8]{1,0:T(4,128)S(1)} %bitcast.9, ...), custom_call_target="tpu_custom_call" | custom-call | flops 1 | bytes 1 | tf_op jit(solution)/shard_map/pallas_call | solution.py:27
  17.8 0.5 %shard_map.88 = (f32[32,128]{1,0:T(8,128)S(1)}, f32[32,128]{1,0:T(8,128)S(1)}, bf16[3,512,128]{2,1,0:T(8,128)(2,1)S(1)}, f32[16,32,128]{2,1,0:T(8,128)S(1)}, f32[16,32,128]{2,1,0:T(8,128)S(1)}) custom-call(s32[8,128]{1,0:T(8,128)S(1)} %get-tuple-element.39.cells_of_ref, f32[3,32,128]{2,1,0:T(8,128)S(1)} %collective-permute-done.2.z0_ref, ...), custom_call_target="tpu_custom_call" | custom-call | flops 1 | bytes 1 | tf_op jit(solution)/shard_map/pallas_call | solution.py:27
  18.2 0.7 %collective-permute-done.7.values_ref = bf16[4,16,128]{2,1,0:T(8,128)(2,1)S(1)} collective-permute-done((bf16[4,16,128]{2,1,0:T(8,128)(2,1)S(1)}, bf16[4,16,128]{2,1,0:T(8,128)(2,1)S(1)}, u32[]{:S(2)}, u32[]{:S(2)}) %collective-permute-start.7) | collective-permute-done | bytes 16416 | tf_op jit(solution)/shard_map/ppermute | solution.py:65
  18.9 0.4 %shard_map.90.before_ref = bf16[2,64,128]{2,1,0:T(8,128)(2,1)S(1)} custom-call(bf16[4,16,128]{2,1,0:T(8,128)(2,1)S(1)} %collective-permute-done.7.values_ref, bf16[3,512,128]{2,1,0:T(8,128)(2,1)S(1)} %get-tuple-element.50.before_ref.pick_ref, bf16[2,528,128]{2,1,0:T(8,128)(2,1)S(1)} %get-tuple-element.45.refs_0_, ...), custom_call_target="tpu_custom_call" | custom-call | flops 1 | bytes 1 | tf_op jit(solution)/shard_map/pallas_call | solution.py:27
  19.3 0.7 %collective-permute-done.5.refs_2_.refs_0_ = bf16[2,528,128]{2,1,0:T(8,128)(2,1)S(1)} collective-permute-done((bf16[2,528,128]{2,1,0:T(8,128)(2,1)S(1)}, bf16[2,528,128]{2,1,0:T(8,128)(2,1)S(1)}, u32[]{:S(2)}, u32[]{:S(2)}) %collective-permute-start.5) | collective-permute-done | bytes 270368 | tf_op jit(solution)/shard_map/ppermute | solution.py:65
  20.0 0.7 %collective-permute-done.6.refs_3_.refs_1_ = bf16[2,528,128]{2,1,0:T(8,128)(2,1)S(1)} collective-permute-done((bf16[2,528,128]{2,1,0:T(8,128)(2,1)S(1)}, bf16[2,528,128]{2,1,0:T(8,128)(2,1)S(1)}, u32[]{:S(2)}, u32[]{:S(2)}) %collective-permute-start.6) | collective-permute-done | bytes 270368 | tf_op jit(solution)/shard_map/ppermute | solution.py:65
  20.7 0.4 %shard_map.91 = bf16[2,64,128]{2,1,0:T(8,128)(2,1)S(1)} custom-call(bf16[4,16,128]{2,1,0:T(8,128)(2,1)S(1)} %collective-permute-done.7.values_ref, bf16[2,64,128]{2,1,0:T(8,128)(2,1)S(1)} %shard_map.90.before_ref, bf16[2,528,128]{2,1,0:T(8,128)(2,1)S(1)} %collective-permute-done.5.refs_2_.refs_0_, bf16[2,528,128]{2,1,0:T(8,128)(2,1)S(1)} %collective-permute-done.6.refs_3_.refs_1_), custom_call_target="tpu_custom_call" | custom-call | flops 1 | bytes 1 | tf_op jit(solution)/shard_map/pallas_call | solution.py:27
  21.2 0.7 %shard_map.89.mine_ref = bf16[2,64,128]{2,1,0:T(8,128)(2,1)S(1)} custom-call(bf16[4,16,128]{2,1,0:T(8,128)(2,1)S(1)} %get-tuple-element.38.values_ref, f32[32,128]{1,0:T(8,128)S(1)} %get-tuple-element.44.before_ref.outside_ref, bf16[2,528,128]{2,1,0:T(8,128)(2,1)S(1)} %get-tuple-element.45.refs_0_, bf16[2,528,128]{2,1,0:T(8,128)(2,1)S(1)} %collective-permute-done.4.refs_1_, ...), custom_call_target="tpu_custom_call" | custom-call | flops 1 | bytes 1 | tf_op jit(solution)/shard_map/pallas_call | solution.py:27
  21.9 0.5 %collective-permute-done.8.other_ref = bf16[2,64,128]{2,1,0:T(8,128)(2,1)S(1)} collective-permute-done((bf16[2,64,128]{2,1,0:T(8,128)(2,1)S(1)}, bf16[2,64,128]{2,1,0:T(8,128)(2,1)S(1)}, u32[]{:S(2)}, u32[]{:S(2)}) %collective-permute-start.8) | collective-permute-done | bytes 32800 | tf_op jit(solution)/shard_map/ppermute | solution.py:65
  22.8 1.7 %collective-permute-start.10 = (bf16[3,32,128]{2,1,0:T(8,128)(2,1)S(1)}, bf16[3,32,128]{2,1,0:T(8,128)(2,1)S(1)}, u32[]{:S(2)}, u32[]{:S(2)}) collective-permute-start(bf16[3,32,128]{2,1,0:T(8,128)(2,1)S(1)} %get-tuple-element.51.after_ref), channel_id=1, source_target_pairs={{0,1},{1,0},{2,3},{3,2},{4,8},{5,9},{6,10},{7,11},{8,4},{9,5},{10,... | collective-permute-start | bytes 73736 | tf_op jit(solution)/shard_map/ppermute | solution.py:61
  24.9 2.2 %shard_map.94 = (f32[3,16,32,128]{3,2,1,0:T(8,128)S(1)}, f32[32,128]{1,0:T(8,128)S(1)}, f32[8,128]{1,0:T(8,128)S(1)}) custom-call(f32[3,16,32,128]{3,2,1,0:T(8,128)S(1)} %shard_map.93.forcing_ref, f32[3,16,32,128]{3,2,1,0:T(8,128)S(1)} %get-tuple-element.52.next_ref, f32[17,32,128]{2,1,0:T(8,128)S(1)} %get-tuple-element.53.nux_ref, ...), custom_call_target="tpu_custom_call" | custom-call | flops 1 | bytes 1 | tf_op jit(solution)/shard_map/pallas_call | solution.py:27
  27.3 3.3 %collective-permute-start.13 = (f32[56,128]{1,0:T(8,128)S(1)}, f32[56,128]{1,0:T(8,128)S(1)}, u32[]{:S(2)}, u32[]{:S(2)}) collective-permute-start(f32[56,128]{1,0:T(8,128)S(1)} %get-tuple-element.64), channel_id=1, source_target_pairs={{0,3},{1,2},{2,1},{3,0},{4,7},{5,6},{6,5},{7,4},{8,11},{9,10},{10,... | collective-permute-start | bytes 86024 | tf_op jit(solution)/shard_map/ppermute | solution.py:65
  30.7 1.1 %collective-permute-start.11 = (f32[40,128]{1,0:T(8,128)S(1)}, f32[40,128]{1,0:T(8,128)S(1)}, u32[]{:S(2)}, u32[]{:S(2)}) collective-permute-start(f32[40,128]{1,0:T(8,128)S(1)} %get-tuple-element.62), channel_id=1, source_target_pairs={{0,1},{1,0},{2,3},{3,2},{4,5},{5,4},{6,7},{7,6},{8,9},{9,8},{10,11... | collective-permute-start | bytes 61448 | tf_op jit(solution)/shard_map/ppermute | solution.py:65
  31.8 2.9 %collective-permute-done.11.refs_0_ = f32[40,128]{1,0:T(8,128)S(1)} collective-permute-done((f32[40,128]{1,0:T(8,128)S(1)}, f32[40,128]{1,0:T(8,128)S(1)}, u32[]{:S(2)}, u32[]{:S(2)}) %collective-permute-start.11) | collective-permute-done | bytes 20512 | tf_op jit(solution)/shard_map/ppermute | solution.py:65
  34.7 0.8 %collective-permute-done.12.refs_1_ = f32[48,128]{1,0:T(8,128)S(1)} collective-permute-done((f32[48,128]{1,0:T(8,128)S(1)}, f32[48,128]{1,0:T(8,128)S(1)}, u32[]{:S(2)}, u32[]{:S(2)}) %collective-permute-start.12) | collective-permute-done | bytes 24608 | tf_op jit(solution)/shard_map/ppermute | solution.py:65
  35.4 1.1 %shard_map.96 = (f32[3,16,32,128]{3,2,1,0:T(8,128)}, f32[1,16]{1,0:T(1,128)}) custom-call(f32[3,16,32,128]{3,2,1,0:T(8,128)S(1)} %get-tuple-element.56.inner_ref, bf16[3,32,128]{2,1,0:T(8,128)(2,1)S(1)} %collective-permute-done.9.x0_ref, bf16[3,32,128]{2,1,0:T(8,128)(2,1)S(1)} %collective-permute-done.10.x1_ref, ...), custom_call_target="tpu_custom_call" | custom-call | flops 655360 | bytes 1572864 | tf_op jit(solution)/shard_map/pallas_call | solution.py:27
  (22 shorter events, 1.2 us)
Async XLA Ops:
  0.6 8.3 %copy-start = (f32[4,16,32,128]{3,2,1,0:T(8,128)S(1)}, f32[4,16,32,128]{3,2,1,0:T(8,128)}, u32[]{:S(2)}) copy-start(f32[4,16,32,128]{3,2,1,0:T(8,128)} %flow_ref.5) | copy-start | bytes 3145732
  0.6 8.3 %copy-start.1 = (s32[16,32,128]{2,1,0:T(8,128)S(1)}, s32[16,32,128]{2,1,0:T(8,128)}, u32[]{:S(2)}) copy-start(s32[16,32,128]{2,1,0:T(8,128)} %regions_ref.5) | copy-start | bytes 786436
  2.3 6.7 %collective-permute-start = (f32[4,32,128]{2,1,0:T(8,128)S(1)}, f32[4,32,128]{2,1,0:T(8,128)S(1)}, u32[]{:S(2)}, u32[]{:S(2)}) collective-permute-start(f32[4,32,128]{2,1,0:T(8,128)S(1)} %get-tuple-element.35), channel_id=1, source_target_pairs={{0,4},{1,5},{2,6},{3,7},{4,0},{5,1},{6,2},{7,3},{8,12},{9,13},{10,... | collective-permute-start | bytes 196616 | tf_op jit(solution)/shard_map/ppermute | solution.py:61
  2.8 6.1 %collective-permute-start.1 = (f32[4,32,128]{2,1,0:T(8,128)S(1)}, f32[4,32,128]{2,1,0:T(8,128)S(1)}, u32[]{:S(2)}, u32[]{:S(2)}) collective-permute-start(f32[4,32,128]{2,1,0:T(8,128)S(1)} %get-tuple-element.36), channel_id=1, source_target_pairs={{0,1},{1,0},{2,3},{3,2},{4,8},{5,9},{6,10},{7,11},{8,4},{9,5},{10,... | collective-permute-start | bytes 196616 | tf_op jit(solution)/shard_map/ppermute | solution.py:61
  5.5 13.5 %collective-permute-start.4 = (bf16[2,528,128]{2,1,0:T(8,128)(2,1)S(1)}, bf16[2,528,128]{2,1,0:T(8,128)(2,1)S(1)}, u32[]{:S(2)}, u32[]{:S(2)}) collective-permute-start(bf16[2,528,128]{2,1,0:T(8,128)(2,1)S(1)} %get-tuple-element.46), channel_id=1, source_target_pairs={{0,8},{4,12},{8,0},{12,4},{16,24},{20,28},{24,16},{28,20},{1,9},{5... | collective-permute-start | bytes 811016 | tf_op jit(solution)/shard_map/ppermute | solution.py:65
  5.5 14.6 %collective-permute-start.5 = (bf16[2,528,128]{2,1,0:T(8,128)(2,1)S(1)}, bf16[2,528,128]{2,1,0:T(8,128)(2,1)S(1)}, u32[]{:S(2)}, u32[]{:S(2)}) collective-permute-start(bf16[2,528,128]{2,1,0:T(8,128)(2,1)S(1)} %get-tuple-element.47), channel_id=1, source_target_pairs={{0,16},{4,20},{8,24},{12,28},{16,0},{20,4},{24,8},{28,12},{1,17},{... | collective-permute-start | bytes 811016 | tf_op jit(solution)/shard_map/ppermute | solution.py:65
  7.5 13.3 %collective-permute-start.6 = (bf16[2,528,128]{2,1,0:T(8,128)(2,1)S(1)}, bf16[2,528,128]{2,1,0:T(8,128)(2,1)S(1)}, u32[]{:S(2)}, u32[]{:S(2)}) collective-permute-start(bf16[2,528,128]{2,1,0:T(8,128)(2,1)S(1)} %get-tuple-element.48), channel_id=1, source_target_pairs={{0,24},{4,28},{8,16},{12,20},{16,8},{20,12},{24,0},{28,4},{1,25},{... | collective-permute-start | bytes 811016 | tf_op jit(solution)/shard_map/ppermute | solution.py:65
  9.0 6.1 %copy-start.2 = (s32[1,1,8,4]{2,3,1,0:T(4,128)S(1)}, s32[1,1,8,4]{2,3,1,0:T(4,128)}, u32[]{:S(2)}) copy-start(s32[1,1,8,4]{2,3,1,0:T(4,128)} %param.11) | copy-start | bytes 388
  9.7 3.2 %collective-permute-start.3 = (f32[3,32,128]{2,1,0:T(8,128)S(1)}, f32[3,32,128]{2,1,0:T(8,128)S(1)}, u32[]{:S(2)}, u32[]{:S(2)}) collective-permute-start(f32[3,32,128]{2,1,0:T(8,128)S(1)} %shard_map.86.edges_ref), channel_id=1, source_target_pairs={{0,4},{1,2},{2,1},{3,7},{4,0},{5,6},{6,5},{7,3},{8,12},{9,10},{10,... | collective-permute-start | bytes 147464 | tf_op jit(solution)/shard_map/ppermute | solution.py:61
  9.8 5.2 %collective-permute-start.2 = (f32[3,32,128]{2,1,0:T(8,128)S(1)}, f32[3,32,128]{2,1,0:T(8,128)S(1)}, u32[]{:S(2)}, u32[]{:S(2)}) collective-permute-start(f32[3,32,128]{2,1,0:T(8,128)S(1)} %shard_map.86.edges_ref), channel_id=1, source_target_pairs={{0,1},{1,0},{2,3},{3,2},{4,5},{5,4},{6,7},{7,6},{8,9},{9,8},{10,11... | collective-permute-start | bytes 147464 | tf_op jit(solution)/shard_map/ppermute | solution.py:61
  17.7 1.2 %collective-permute-start.7 = (bf16[4,16,128]{2,1,0:T(8,128)(2,1)S(1)}, bf16[4,16,128]{2,1,0:T(8,128)(2,1)S(1)}, u32[]{:S(2)}, u32[]{:S(2)}) collective-permute-start(bf16[4,16,128]{2,1,0:T(8,128)(2,1)S(1)} %get-tuple-element.49), channel_id=1, source_target_pairs={{0,4},{4,0},{8,12},{12,8},{16,20},{20,16},{24,28},{28,24},{1,5},{5... | collective-permute-start | bytes 49160 | tf_op jit(solution)/shard_map/ppermute | solution.py:65
  21.2 1.2 %collective-permute-start.8 = (bf16[2,64,128]{2,1,0:T(8,128)(2,1)S(1)}, bf16[2,64,128]{2,1,0:T(8,128)(2,1)S(1)}, u32[]{:S(2)}, u32[]{:S(2)}) collective-permute-start(bf16[2,64,128]{2,1,0:T(8,128)(2,1)S(1)} %shard_map.91), channel_id=1, source_target_pairs={{0,4},{4,0},{8,12},{12,8},{16,20},{20,16},{24,28},{28,24},{1,5},{5... | collective-permute-start | bytes 98312 | tf_op jit(solution)/shard_map/ppermute | solution.py:65
  22.5 4.5 %collective-permute-start.9 = (bf16[3,32,128]{2,1,0:T(8,128)(2,1)S(1)}, bf16[3,32,128]{2,1,0:T(8,128)(2,1)S(1)}, u32[]{:S(2)}, u32[]{:S(2)}) collective-permute-start(bf16[3,32,128]{2,1,0:T(8,128)(2,1)S(1)} %get-tuple-element.57), channel_id=1, source_target_pairs={{0,4},{1,5},{2,6},{3,7},{4,0},{5,1},{6,2},{7,3},{8,12},{9,13},{10,... | collective-permute-start | bytes 73736 | tf_op jit(solution)/shard_map/ppermute | solution.py:61
  22.8 4.3 %collective-permute-start.10 = (bf16[3,32,128]{2,1,0:T(8,128)(2,1)S(1)}, bf16[3,32,128]{2,1,0:T(8,128)(2,1)S(1)}, u32[]{:S(2)}, u32[]{:S(2)}) collective-permute-start(bf16[3,32,128]{2,1,0:T(8,128)(2,1)S(1)} %get-tuple-element.51.after_ref), channel_id=1, source_target_pairs={{0,1},{1,0},{2,3},{3,2},{4,8},{5,9},{6,10},{7,11},{8,4},{9,5},{10,... | collective-permute-start | bytes 73736 | tf_op jit(solution)/shard_map/ppermute | solution.py:61
  27.3 8.1 %collective-permute-start.13 = (f32[56,128]{1,0:T(8,128)S(1)}, f32[56,128]{1,0:T(8,128)S(1)}, u32[]{:S(2)}, u32[]{:S(2)}) collective-permute-start(f32[56,128]{1,0:T(8,128)S(1)} %get-tuple-element.64), channel_id=1, source_target_pairs={{0,3},{1,2},{2,1},{3,0},{4,7},{5,6},{6,5},{7,4},{8,11},{9,10},{10,... | collective-permute-start | bytes 86024 | tf_op jit(solution)/shard_map/ppermute | solution.py:65
  30.7 4.7 %collective-permute-start.12 = (f32[48,128]{1,0:T(8,128)S(1)}, f32[48,128]{1,0:T(8,128)S(1)}, u32[]{:S(2)}, u32[]{:S(2)}) collective-permute-start(f32[48,128]{1,0:T(8,128)S(1)} %get-tuple-element.63), channel_id=1, source_target_pairs={{0,2},{1,3},{2,0},{3,1},{4,6},{5,7},{6,4},{7,5},{8,10},{9,11},{10,... | collective-permute-start | bytes 73736 | tf_op jit(solution)/shard_map/ppermute | solution.py:65
  30.7 4.0 %collective-permute-start.11 = (f32[40,128]{1,0:T(8,128)S(1)}, f32[40,128]{1,0:T(8,128)S(1)}, u32[]{:S(2)}, u32[]{:S(2)}) collective-permute-start(f32[40,128]{1,0:T(8,128)S(1)} %get-tuple-element.62), channel_id=1, source_target_pairs={{0,1},{1,0},{2,3},{3,2},{4,5},{5,4},{6,7},{7,6},{8,9},{9,8},{10,11... | collective-permute-start | bytes 61448 | tf_op jit(solution)/shard_map/ppermute | solution.py:65

commit v10 on v9

--- a/solution.py
+++ b/solution.py
@@ -374,14 +374,14 @@
         nuzd_ref[x] = jnp.where(lane == 0, edge_of(rim_nu, x), pltpu.roll(nuz_ref[x], 1, 1))
 
 
-def product_kernel(cap, block, masks, values_ref, before_ref, *refs):
+def product_kernel(cap, block, masks, more, values_ref, before_ref, *refs):
     chips, extra, width = values_ref.shape
     recvs, out_ref = refs[:-1], refs[-1]
     depth = cap * width
     row, lane = iotas(extra, depth)
     own = row // 3 == lane // width
     here = lax.axis_index("fluid") // 2
-    if before_ref.shape == out_ref.shape:
+    if more:
         out_ref[...] = before_ref[...]
     for m, recv_ref in zip(masks, recvs):
         source = here ^ m
@@ -664,19 +664,20 @@
         (cells_of, z0, z1, zs, rim, nuy, nuz, nuy0),
     )
 
-    def products(block, masks, values, before):
+    def products(block, masks, values, before, more=False):
         whole = (2, chips * extra, width)
         return call(
-            functools.partial(product_kernel, cap, block, masks),
+            functools.partial(product_kernel, cap, block, masks, more),
             bf16(*whole),
-            [VMEM, VMEM if before.shape == whole else ANY] + [VMEM] * len(masks),
+            [VMEM, VMEM if more else ANY] + [VMEM] * len(masks),
             (values, before, *(recvs[m] for m in masks)),
         )
 
-    given = products(1, tuple(range(chips // 2)), borrowed, pick)
-    given = products(1, tuple(range(chips // 2, chips)), borrowed, given)
+    held = products(0, tuple(range(chips // 2)), mine, pick)
+    given = products(1, tuple(range(chips // 2)), borrowed, held)
+    given = products(1, tuple(range(chips // 2, chips)), borrowed, given, True)
     other = cross(given, "fluid", 1)
-    held = products(0, tuple(range(chips)), mine, outside)
+    held = products(0, tuple(range(chips // 2, chips)), mine, held, True)
     fs0, fs1 = call(ends_kernel, (bf16(3, rows, width),) * 2, [VMEM] * 3, (held, other, pick))
     f0, f1 = swap(fs0, "fluid", 0), swap(fs1, "fluid", 1)
     forcing = call(forcing_kernel, f32(3, planes, rows, width), [VMEM] * 3 + [ANY], (held, other, pick, fs1))

time: 36.7 us -> 36.7 us (level)
    pallas_call x12 -> x13, Pallas kernels: 11.2 us -> 11.3 us  [call(): pl.pallas_call(kernel, out_shape=outs, in_specs=ins, out_specs=out_specs...]
where the time goes in v10:
time: 36.7 us; the launch traced here: 36.5 us
  starting transfers between devices  16.4 us (45%)
  Pallas kernels  11.3 us (31%)
  waiting for transfers between devices  8.13 us (22%)
  between operations  0.77 us (2%)
    pallas_call x13, Pallas kernels, call(): pl.pallas_call(kernel, out_shape=outs, in_specs=ins, out_specs=out_specs...  11.3 us
    ppermute x6, starting transfers between devices, swap(): return lax.ppermute(block, ('fluid', 'wall'), pairs)  8.34 us
    ppermute x8, starting transfers between devices, cross(): lax.ppermute(block, axis, [(i, i ^ mask) for i in range(lax.axis_size(axi...  8.01 us
    ppermute x8, waiting for transfers between devices, cross(): lax.ppermute(block, axis, [(i, i ^ mask) for i in range(lax.axis_size(axi...  6.05 us
    ppermute x6, waiting for transfers between devices, swap(): return lax.ppermute(block, ('fluid', 'wall'), pairs)  2.08 us
  transfers between devices with their start and end apart: 14, of which 7 were waited for; matrix products, arithmetic and copies ran while one was open for 0% of the time, Pallas kernels for 21%

profile of v10, /device:TPU:0, one launch (start us, length us, event | category | flops | bytes accessed | tf_op | source)
XLA Modules:
  0.0 36.5 jit_solution(15199831667480075279)
XLA Ops:
  0.7 1.6 %shard_map.85 = (bf16[2,528,128]{2,1,0:T(8,128)(2,1)S(1)}, bf16[2,528,128]{2,1,0:T(8,128)(2,1)S(1)}, bf16[2,528,128]{2,1,0:T(8,128)(2,1)S(1)}, bf16[2,528,128]{2...) custom-call(s32[32]{0:T(128)} %bitcast.12, bf16[32,128,128]{2,1,0:T(8,128)(2,1)} %bitcast.10, ...), custom_call_target="tpu_custom_call" | custom-call | flops 1 | bytes 1 | tf_op jit(solution)/shard_map/pallas_call | solution.py:27
  2.3 0.5 %collective-permute-start = (f32[4,32,128]{2,1,0:T(8,128)S(1)}, f32[4,32,128]{2,1,0:T(8,128)S(1)}, u32[]{:S(2)}, u32[]{:S(2)}) collective-permute-start(f32[4,32,128]{2,1,0:T(8,128)S(1)} %get-tuple-element.35), channel_id=1, source_target_pairs={{0,4},{1,5},{2,6},{3,7},{4,0},{5,1},{6,2},{7,3},{8,12},{9,13},{10,... | collective-permute-start | bytes 196616 | tf_op jit(solution)/shard_map/ppermute | solution.py:61
  2.8 2.6 %collective-permute-start.1 = (f32[4,32,128]{2,1,0:T(8,128)S(1)}, f32[4,32,128]{2,1,0:T(8,128)S(1)}, u32[]{:S(2)}, u32[]{:S(2)}) collective-permute-start(f32[4,32,128]{2,1,0:T(8,128)S(1)} %get-tuple-element.36), channel_id=1, source_target_pairs={{0,1},{1,0},{2,3},{3,2},{4,8},{5,9},{6,10},{7,11},{8,4},{9,5},{10,... | collective-permute-start | bytes 196616 | tf_op jit(solution)/shard_map/ppermute | solution.py:61
  5.5 2.0 %collective-permute-start.5 = (bf16[2,528,128]{2,1,0:T(8,128)(2,1)S(1)}, bf16[2,528,128]{2,1,0:T(8,128)(2,1)S(1)}, u32[]{:S(2)}, u32[]{:S(2)}) collective-permute-start(bf16[2,528,128]{2,1,0:T(8,128)(2,1)S(1)} %get-tuple-element.47), channel_id=1, source_target_pairs={{0,16},{4,20},{8,24},{12,28},{16,0},{20,4},{24,8},{28,12},{1,17},{... | collective-permute-start | bytes 811016 | tf_op jit(solution)/shard_map/ppermute | solution.py:65
  7.5 1.5 %collective-permute-start.6 = (bf16[2,528,128]{2,1,0:T(8,128)(2,1)S(1)}, bf16[2,528,128]{2,1,0:T(8,128)(2,1)S(1)}, u32[]{:S(2)}, u32[]{:S(2)}) collective-permute-start(bf16[2,528,128]{2,1,0:T(8,128)(2,1)S(1)} %get-tuple-element.48), channel_id=1, source_target_pairs={{0,24},{4,28},{8,16},{12,20},{16,8},{20,12},{24,0},{28,4},{1,25},{... | collective-permute-start | bytes 811016 | tf_op jit(solution)/shard_map/ppermute | solution.py:65
  9.0 0.8 %shard_map.86.edges_ref = f32[3,32,128]{2,1,0:T(8,128)S(1)} custom-call(f32[4,16,32,128]{3,2,1,0:T(8,128)S(1)} %copy-done, s32[16,32,128]{2,1,0:T(8,128)S(1)} %copy-done.1, f32[4,32,128]{2,1,0:T(8,128)S(1)} %collective-permute-done.x0_ref, f32[4,32,128]{2,1,0:T(8,128)S(1)} %collective-permute-done.1.x1_ref), custom_call_target="tpu_custom_call" | custom-call | flops 99999997952 | bytes 1 | tf_op jit(solution)/shard_map/pallas_call | solution.py:27
  9.8 3.1 %collective-permute-start.2 = (f32[3,32,128]{2,1,0:T(8,128)S(1)}, f32[3,32,128]{2,1,0:T(8,128)S(1)}, u32[]{:S(2)}, u32[]{:S(2)}) collective-permute-start(f32[3,32,128]{2,1,0:T(8,128)S(1)} %shard_map.86.edges_ref), channel_id=1, source_target_pairs={{0,1},{1,0},{2,3},{3,2},{4,5},{5,4},{6,7},{7,6},{8,9},{9,8},{10,11... | collective-permute-start | bytes 147464 | tf_op jit(solution)/shard_map/ppermute | solution.py:61
  13.0 2.1 %collective-permute-done.2.z0_ref = f32[3,32,128]{2,1,0:T(8,128)S(1)} collective-permute-done((f32[3,32,128]{2,1,0:T(8,128)S(1)}, f32[3,32,128]{2,1,0:T(8,128)S(1)}, u32[]{:S(2)}, u32[]{:S(2)}) %collective-permute-start.2) | collective-permute-done | bytes 49184 | tf_op jit(solution)/shard_map/ppermute | solution.py:61
  15.0 2.6 %shard_map.87 = (f32[3,16,32,128]{3,2,1,0:T(8,128)}, f32[3,16,32,128]{3,2,1,0:T(8,128)S(1)}, f32[17,32,128]{2,1,0:T(8,128)S(1)}, f32[16,32,128]{2,1,0:T(8,128)S(...) custom-call(s32[4,8]{1,0:T(4,128)S(1)} %bitcast.9, ...), custom_call_target="tpu_custom_call" | custom-call | flops 1 | bytes 1 | tf_op jit(solution)/shard_map/pallas_call | solution.py:27
  17.8 0.5 %shard_map.88 = (f32[32,128]{1,0:T(8,128)S(1)}, f32[32,128]{1,0:T(8,128)S(1)}, bf16[3,512,128]{2,1,0:T(8,128)(2,1)S(1)}, f32[16,32,128]{2,1,0:T(8,128)S(1)}, f32[16,32,128]{2,1,0:T(8,128)S(1)}) custom-call(s32[8,128]{1,0:T(8,128)S(1)} %get-tuple-element.39.cells_of_ref, f32[3,32,128]{2,1,0:T(8,128)S(1)} %collective-permute-done.2.z0_ref, ...), custom_call_target="tpu_custom_call" | custom-call | flops 1 | bytes 1 | tf_op jit(solution)/shard_map/pallas_call | solution.py:27
  18.3 0.4 %shard_map.89.before_ref = bf16[2,64,128]{2,1,0:T(8,128)(2,1)S(1)} custom-call(bf16[4,16,128]{2,1,0:T(8,128)(2,1)S(1)} %get-tuple-element.38.values_ref, bf16[3,512,128]{2,1,0:T(8,128)(2,1)S(1)} %get-tuple-element.44.before_ref.pick_ref, bf16[2,528,128]{2,1,0:T(8,128)(2,1)S(1)} %get-tuple-element.45.refs_0_, ...), custom_call_target="tpu_custom_call" | custom-call | flops 1 | bytes 1 | tf_op jit(solution)/shard_map/pallas_call | solution.py:27
  18.9 0.4 %shard_map.91.before_ref = bf16[2,64,128]{2,1,0:T(8,128)(2,1)S(1)} custom-call(bf16[4,16,128]{2,1,0:T(8,128)(2,1)S(1)} %collective-permute-done.7.values_ref, bf16[2,64,128]{2,1,0:T(8,128)(2,1)S(1)} %shard_map.89.before_ref, bf16[2,528,128]{2,1,0:T(8,128)(2,1)S(1)} %get-tuple-element.45.refs_0_, bf16[2,528,128]{2,1,0:T(8,128)(2,1)S(1)} %collective-permute-done.4.refs_1_), custom_call_target="tpu_custom_call" | custom-call | flops 1 | bytes 1 | tf_op jit(solution)/shard_map/pallas_call | solution.py:27
  19.3 0.7 %collective-permute-done.5.refs_0_ = bf16[2,528,128]{2,1,0:T(8,128)(2,1)S(1)} collective-permute-done((bf16[2,528,128]{2,1,0:T(8,128)(2,1)S(1)}, bf16[2,528,128]{2,1,0:T(8,128)(2,1)S(1)}, u32[]{:S(2)}, u32[]{:S(2)}) %collective-permute-start.5) | collective-permute-done | bytes 270368 | tf_op jit(solution)/shard_map/ppermute | solution.py:65
  20.0 0.7 %collective-permute-done.6.refs_1_ = bf16[2,528,128]{2,1,0:T(8,128)(2,1)S(1)} collective-permute-done((bf16[2,528,128]{2,1,0:T(8,128)(2,1)S(1)}, bf16[2,528,128]{2,1,0:T(8,128)(2,1)S(1)}, u32[]{:S(2)}, u32[]{:S(2)}) %collective-permute-start.6) | collective-permute-done | bytes 270368 | tf_op jit(solution)/shard_map/ppermute | solution.py:65
  20.7 0.4 %shard_map.92 = bf16[2,64,128]{2,1,0:T(8,128)(2,1)S(1)} custom-call(bf16[4,16,128]{2,1,0:T(8,128)(2,1)S(1)} %collective-permute-done.7.values_ref, bf16[2,64,128]{2,1,0:T(8,128)(2,1)S(1)} %shard_map.91.before_ref, bf16[2,528,128]{2,1,0:T(8,128)(2,1)S(1)} %collective-permute-done.5.refs_0_, bf16[2,528,128]{2,1,0:T(8,128)(2,1)S(1)} %collective-permute-done.6.refs_1_), custom_call_target="tpu_custom_call" | custom-call | flops 1 | bytes 1 | tf_op jit(solution)/shard_map/pallas_call | solution.py:27
  21.2 0.4 %shard_map.90.mine_ref = bf16[2,64,128]{2,1,0:T(8,128)(2,1)S(1)} custom-call(bf16[4,16,128]{2,1,0:T(8,128)(2,1)S(1)} %get-tuple-element.38.values_ref, bf16[2,64,128]{2,1,0:T(8,128)(2,1)S(1)} %shard_map.89.before_ref, bf16[2,528,128]{2,1,0:T(8,128)(2,1)S(1)} %collective-permute-done.5.refs_0_, bf16[2,528,128]{2,1,0:T(8,128)(2,1)S(1)} %collective-permute-done.6.refs_1_), custom_call_target="tpu_custom_call" | custom-call | flops 1 | bytes 1 | tf_op jit(solution)/shard_map/pallas_call | solution.py:27
  21.6 0.8 %collective-permute-done.8.other_ref = bf16[2,64,128]{2,1,0:T(8,128)(2,1)S(1)} collective-permute-done((bf16[2,64,128]{2,1,0:T(8,128)(2,1)S(1)}, bf16[2,64,128]{2,1,0:T(8,128)(2,1)S(1)}, u32[]{:S(2)}, u32[]{:S(2)}) %collective-permute-start.8) | collective-permute-done | bytes 32800 | tf_op jit(solution)/shard_map/ppermute | solution.py:65
  22.8 1.7 %collective-permute-start.10 = (bf16[3,32,128]{2,1,0:T(8,128)(2,1)S(1)}, bf16[3,32,128]{2,1,0:T(8,128)(2,1)S(1)}, u32[]{:S(2)}, u32[]{:S(2)}) collective-permute-start(bf16[3,32,128]{2,1,0:T(8,128)(2,1)S(1)} %get-tuple-element.50.after_ref), channel_id=1, source_target_pairs={{0,1},{1,0},{2,3},{3,2},{4,8},{5,9},{6,10},{7,11},{8,4},{9,5},{10,... | collective-permute-start | bytes 73736 | tf_op jit(solution)/shard_map/ppermute | solution.py:61
  24.9 2.2 %shard_map.95 = (f32[3,16,32,128]{3,2,1,0:T(8,128)S(1)}, f32[32,128]{1,0:T(8,128)S(1)}, f32[8,128]{1,0:T(8,128)S(1)}) custom-call(f32[3,16,32,128]{3,2,1,0:T(8,128)S(1)} %shard_map.94.forcing_ref, f32[3,16,32,128]{3,2,1,0:T(8,128)S(1)} %get-tuple-element.51.next_ref, f32[17,32,128]{2,1,0:T(8,128)S(1)} %get-tuple-element.52.nux_ref, ...), custom_call_target="tpu_custom_call" | custom-call | flops 1 | bytes 1 | tf_op jit(solution)/shard_map/pallas_call | solution.py:27
  27.3 3.3 %collective-permute-start.13 = (f32[56,128]{1,0:T(8,128)S(1)}, f32[56,128]{1,0:T(8,128)S(1)}, u32[]{:S(2)}, u32[]{:S(2)}) collective-permute-start(f32[56,128]{1,0:T(8,128)S(1)} %get-tuple-element.64), channel_id=1, source_target_pairs={{0,3},{1,2},{2,1},{3,0},{4,7},{5,6},{6,5},{7,4},{8,11},{9,10},{10,... | collective-permute-start | bytes 86024 | tf_op jit(solution)/shard_map/ppermute | solution.py:65
  30.7 1.1 %collective-permute-start.11 = (f32[40,128]{1,0:T(8,128)S(1)}, f32[40,128]{1,0:T(8,128)S(1)}, u32[]{:S(2)}, u32[]{:S(2)}) collective-permute-start(f32[40,128]{1,0:T(8,128)S(1)} %get-tuple-element.62), channel_id=1, source_target_pairs={{0,1},{1,0},{2,3},{3,2},{4,5},{5,4},{6,7},{7,6},{8,9},{9,8},{10,11... | collective-permute-start | bytes 61448 | tf_op jit(solution)/shard_map/ppermute | solution.py:65
  31.8 2.9 %collective-permute-done.11.refs_0_ = f32[40,128]{1,0:T(8,128)S(1)} collective-permute-done((f32[40,128]{1,0:T(8,128)S(1)}, f32[40,128]{1,0:T(8,128)S(1)}, u32[]{:S(2)}, u32[]{:S(2)}) %collective-permute-start.11) | collective-permute-done | bytes 20512 | tf_op jit(solution)/shard_map/ppermute | solution.py:65
  34.7 0.8 %collective-permute-done.12.refs_1_ = f32[48,128]{1,0:T(8,128)S(1)} collective-permute-done((f32[48,128]{1,0:T(8,128)S(1)}, f32[48,128]{1,0:T(8,128)S(1)}, u32[]{:S(2)}, u32[]{:S(2)}) %collective-permute-start.12) | collective-permute-done | bytes 24608 | tf_op jit(solution)/shard_map/ppermute | solution.py:65
  35.4 1.1 %shard_map.97 = (f32[3,16,32,128]{3,2,1,0:T(8,128)}, f32[1,16]{1,0:T(1,128)}) custom-call(f32[3,16,32,128]{3,2,1,0:T(8,128)S(1)} %get-tuple-element.56.inner_ref, bf16[3,32,128]{2,1,0:T(8,128)(2,1)S(1)} %collective-permute-done.9.x0_ref, bf16[3,32,128]{2,1,0:T(8,128)(2,1)S(1)} %collective-permute-done.10.x1_ref, ...), custom_call_target="tpu_custom_call" | custom-call | flops 655360 | bytes 1572864 | tf_op jit(solution)/shard_map/pallas_call | solution.py:27
  (23 shorter events, 1.4 us)
Async XLA Ops:
  0.6 8.3 %copy-start = (f32[4,16,32,128]{3,2,1,0:T(8,128)S(1)}, f32[4,16,32,128]{3,2,1,0:T(8,128)}, u32[]{:S(2)}) copy-start(f32[4,16,32,128]{3,2,1,0:T(8,128)} %flow_ref.5) | copy-start | bytes 3145732
  0.6 8.3 %copy-start.1 = (s32[16,32,128]{2,1,0:T(8,128)S(1)}, s32[16,32,128]{2,1,0:T(8,128)}, u32[]{:S(2)}) copy-start(s32[16,32,128]{2,1,0:T(8,128)} %regions_ref.5) | copy-start | bytes 786436
  2.3 6.7 %collective-permute-start = (f32[4,32,128]{2,1,0:T(8,128)S(1)}, f32[4,32,128]{2,1,0:T(8,128)S(1)}, u32[]{:S(2)}, u32[]{:S(2)}) collective-permute-start(f32[4,32,128]{2,1,0:T(8,128)S(1)} %get-tuple-element.35), channel_id=1, source_target_pairs={{0,4},{1,5},{2,6},{3,7},{4,0},{5,1},{6,2},{7,3},{8,12},{9,13},{10,... | collective-permute-start | bytes 196616 | tf_op jit(solution)/shard_map/ppermute | solution.py:61
  2.8 6.1 %collective-permute-start.1 = (f32[4,32,128]{2,1,0:T(8,128)S(1)}, f32[4,32,128]{2,1,0:T(8,128)S(1)}, u32[]{:S(2)}, u32[]{:S(2)}) collective-permute-start(f32[4,32,128]{2,1,0:T(8,128)S(1)} %get-tuple-element.36), channel_id=1, source_target_pairs={{0,1},{1,0},{2,3},{3,2},{4,8},{5,9},{6,10},{7,11},{8,4},{9,5},{10,... | collective-permute-start | bytes 196616 | tf_op jit(solution)/shard_map/ppermute | solution.py:61
  5.5 12.8 %collective-permute-start.4 = (bf16[2,528,128]{2,1,0:T(8,128)(2,1)S(1)}, bf16[2,528,128]{2,1,0:T(8,128)(2,1)S(1)}, u32[]{:S(2)}, u32[]{:S(2)}) collective-permute-start(bf16[2,528,128]{2,1,0:T(8,128)(2,1)S(1)} %get-tuple-element.46), channel_id=1, source_target_pairs={{0,8},{4,12},{8,0},{12,4},{16,24},{20,28},{24,16},{28,20},{1,9},{5... | collective-permute-start | bytes 811016 | tf_op jit(solution)/shard_map/ppermute | solution.py:65
  5.5 14.6 %collective-permute-start.5 = (bf16[2,528,128]{2,1,0:T(8,128)(2,1)S(1)}, bf16[2,528,128]{2,1,0:T(8,128)(2,1)S(1)}, u32[]{:S(2)}, u32[]{:S(2)}) collective-permute-start(bf16[2,528,128]{2,1,0:T(8,128)(2,1)S(1)} %get-tuple-element.47), channel_id=1, source_target_pairs={{0,16},{4,20},{8,24},{12,28},{16,0},{20,4},{24,8},{28,12},{1,17},{... | collective-permute-start | bytes 811016 | tf_op jit(solution)/shard_map/ppermute | solution.py:65
  7.5 13.3 %collective-permute-start.6 = (bf16[2,528,128]{2,1,0:T(8,128)(2,1)S(1)}, bf16[2,528,128]{2,1,0:T(8,128)(2,1)S(1)}, u32[]{:S(2)}, u32[]{:S(2)}) collective-permute-start(bf16[2,528,128]{2,1,0:T(8,128)(2,1)S(1)} %get-tuple-element.48), channel_id=1, source_target_pairs={{0,24},{4,28},{8,16},{12,20},{16,8},{20,12},{24,0},{28,4},{1,25},{... | collective-permute-start | bytes 811016 | tf_op jit(solution)/shard_map/ppermute | solution.py:65
  9.0 6.1 %copy-start.2 = (s32[1,1,8,4]{2,3,1,0:T(4,128)S(1)}, s32[1,1,8,4]{2,3,1,0:T(4,128)}, u32[]{:S(2)}) copy-start(s32[1,1,8,4]{2,3,1,0:T(4,128)} %param.11) | copy-start | bytes 388
  9.7 3.2 %collective-permute-start.3 = (f32[3,32,128]{2,1,0:T(8,128)S(1)}, f32[3,32,128]{2,1,0:T(8,128)S(1)}, u32[]{:S(2)}, u32[]{:S(2)}) collective-permute-start(f32[3,32,128]{2,1,0:T(8,128)S(1)} %shard_map.86.edges_ref), channel_id=1, source_target_pairs={{0,4},{1,2},{2,1},{3,7},{4,0},{5,6},{6,5},{7,3},{8,12},{9,10},{10,... | collective-permute-start | bytes 147464 | tf_op jit(solution)/shard_map/ppermute | solution.py:61
  9.8 5.2 %collective-permute-start.2 = (f32[3,32,128]{2,1,0:T(8,128)S(1)}, f32[3,32,128]{2,1,0:T(8,128)S(1)}, u32[]{:S(2)}, u32[]{:S(2)}) collective-permute-start(f32[3,32,128]{2,1,0:T(8,128)S(1)} %shard_map.86.edges_ref), channel_id=1, source_target_pairs={{0,1},{1,0},{2,3},{3,2},{4,5},{5,4},{6,7},{7,6},{8,9},{9,8},{10,11... | collective-permute-start | bytes 147464 | tf_op jit(solution)/shard_map/ppermute | solution.py:61
  17.7 1.2 %collective-permute-start.7 = (bf16[4,16,128]{2,1,0:T(8,128)(2,1)S(1)}, bf16[4,16,128]{2,1,0:T(8,128)(2,1)S(1)}, u32[]{:S(2)}, u32[]{:S(2)}) collective-permute-start(bf16[4,16,128]{2,1,0:T(8,128)(2,1)S(1)} %get-tuple-element.49), channel_id=1, source_target_pairs={{0,4},{4,0},{8,12},{12,8},{16,20},{20,16},{24,28},{28,24},{1,5},{5... | collective-permute-start | bytes 49160 | tf_op jit(solution)/shard_map/ppermute | solution.py:65
  21.2 1.2 %collective-permute-start.8 = (bf16[2,64,128]{2,1,0:T(8,128)(2,1)S(1)}, bf16[2,64,128]{2,1,0:T(8,128)(2,1)S(1)}, u32[]{:S(2)}, u32[]{:S(2)}) collective-permute-start(bf16[2,64,128]{2,1,0:T(8,128)(2,1)S(1)} %shard_map.92), channel_id=1, source_target_pairs={{0,4},{4,0},{8,12},{12,8},{16,20},{20,16},{24,28},{28,24},{1,5},{5... | collective-permute-start | bytes 98312 | tf_op jit(solution)/shard_map/ppermute | solution.py:65
  22.5 4.5 %collective-permute-start.9 = (bf16[3,32,128]{2,1,0:T(8,128)(2,1)S(1)}, bf16[3,32,128]{2,1,0:T(8,128)(2,1)S(1)}, u32[]{:S(2)}, u32[]{:S(2)}) collective-permute-start(bf16[3,32,128]{2,1,0:T(8,128)(2,1)S(1)} %get-tuple-element.57), channel_id=1, source_target_pairs={{0,4},{1,5},{2,6},{3,7},{4,0},{5,1},{6,2},{7,3},{8,12},{9,13},{10,... | collective-permute-start | bytes 73736 | tf_op jit(solution)/shard_map/ppermute | solution.py:61
  22.8 4.3 %collective-permute-start.10 = (bf16[3,32,128]{2,1,0:T(8,128)(2,1)S(1)}, bf16[3,32,128]{2,1,0:T(8,128)(2,1)S(1)}, u32[]{:S(2)}, u32[]{:S(2)}) collective-permute-start(bf16[3,32,128]{2,1,0:T(8,128)(2,1)S(1)} %get-tuple-element.50.after_ref), channel_id=1, source_target_pairs={{0,1},{1,0},{2,3},{3,2},{4,8},{5,9},{6,10},{7,11},{8,4},{9,5},{10,... | collective-permute-start | bytes 73736 | tf_op jit(solution)/shard_map/ppermute | solution.py:61
  27.3 8.1 %collective-permute-start.13 = (f32[56,128]{1,0:T(8,128)S(1)}, f32[56,128]{1,0:T(8,128)S(1)}, u32[]{:S(2)}, u32[]{:S(2)}) collective-permute-start(f32[56,128]{1,0:T(8,128)S(1)} %get-tuple-element.64), channel_id=1, source_target_pairs={{0,3},{1,2},{2,1},{3,0},{4,7},{5,6},{6,5},{7,4},{8,11},{9,10},{10,... | collective-permute-start | bytes 86024 | tf_op jit(solution)/shard_map/ppermute | solution.py:65
  30.7 4.7 %collective-permute-start.12 = (f32[48,128]{1,0:T(8,128)S(1)}, f32[48,128]{1,0:T(8,128)S(1)}, u32[]{:S(2)}, u32[]{:S(2)}) collective-permute-start(f32[48,128]{1,0:T(8,128)S(1)} %get-tuple-element.63), channel_id=1, source_target_pairs={{0,2},{1,3},{2,0},{3,1},{4,6},{5,7},{6,4},{7,5},{8,10},{9,11},{10,... | collective-permute-start | bytes 73736 | tf_op jit(solution)/shard_map/ppermute | solution.py:65
  30.7 4.0 %collective-permute-start.11 = (f32[40,128]{1,0:T(8,128)S(1)}, f32[40,128]{1,0:T(8,128)S(1)}, u32[]{:S(2)}, u32[]{:S(2)}) collective-permute-start(f32[40,128]{1,0:T(8,128)S(1)} %get-tuple-element.62), channel_id=1, source_target_pairs={{0,1},{1,0},{2,3},{3,2},{4,5},{5,4},{6,7},{7,6},{8,9},{9,8},{10,11... | collective-permute-start | bytes 61448 | tf_op jit(solution)/shard_map/ppermute | solution.py:65

commit v11 on v9

--- a/solution.py
+++ b/solution.py
@@ -517,14 +517,16 @@
         region_rows(time_step * nux_ref[planes] * high, regions_ref[planes - 1], tops),
     ]
     total = sums_ref[...] + region_sums(*(jnp.concatenate(both, axis=1) for both in zip(*ends)))
-    height = tops * (columns // width)
+    total = jnp.concatenate([total[:, at : at + width] for at in range(0, columns, width)], axis=0)
+    high = total.astype(jnp.bfloat16)
+    total = jnp.concatenate([high, (total - high.astype(jnp.float32)).astype(jnp.bfloat16)], axis=0)
+    height = total.shape[0]
     for mask, out_ref in zip((0,) + masks, outs):
-        for i in range(columns // width):
-            out_ref[i * tops : (i + 1) * tops, :] = total[:, i * width : (i + 1) * width]
+        out_ref[:height, :] = total
         if mask:
-            out_ref[height : height + rows, :] = fpack_ref[...]
+            out_ref[height : height + rows, :] = fpack_ref[...].astype(jnp.bfloat16)
             if out_ref.shape[0] > height + rows:
-                out_ref[height + rows :, :] = jnp.zeros((out_ref.shape[0] - height - rows, width), jnp.float32)
+                out_ref[height + rows :, :] = jnp.zeros((out_ref.shape[0] - height - rows, width), jnp.bfloat16)
 
 
 def beside_of(c, groups, x0_ref, x1_ref):
@@ -540,13 +542,18 @@
     per = own_ref.shape[0]
     _, lane = iotas(rows, width)
     me = lax.axis_index("wall")
-    total = own_ref[...]
+
+    def sums_of(ref):
+        parts = ref[:per, :].astype(jnp.float32)
+        return parts[: per // 2] + parts[per // 2 :]
+
+    total = sums_of(own_ref)
     below = jnp.zeros((rows, width), jnp.float32)
     above = jnp.zeros((rows, width), jnp.float32)
     for mask, ref in zip(range(1, walls), arrived):
-        total = total + ref[:per, :]
+        total = total + sums_of(ref)
         if mask & (mask + 1) == 0:
-            edges = ref[per : per + rows, :]
+            edges = ref[per : per + rows, :].astype(jnp.float32)
             above = jnp.where((me ^ mask) == me + 1, edges, above)
             below = jnp.where((me ^ mask) == me - 1, edges, below)
     mixed = mix_edges(below, above, lane)
@@ -683,7 +690,7 @@
     tops = reg_count // 8
     columns = 8 * FOLD
     span = (planes + 1) * rows // FOLD * width
-    sum_rows = tops * (columns // width)
+    sum_rows = 2 * tops * (columns // width)
     inner, fpack, sums = call(
         inner_kernel,
         (f32(3, planes, rows, width), f32(rows, width), f32(tops, columns)),
@@ -696,10 +703,10 @@
         ),
     )
     masks = tuple(range(1, walls))
-    heights = [sum_rows] + [sum_rows + rows + 8 * (mask - 1) for mask in masks]
+    heights = [sum_rows] + [sum_rows + rows + 16 * (mask - 1) for mask in masks]
     own, *parts = call(
         functools.partial(edge_kernel, groups, masks),
-        tuple(f32(height, width) for height in heights),
+        tuple(bf16(height, width) for height in heights),
         [VMEM] * 7,
         (f0, f1, nux, velocity, regions, sums, fpack),
     )

time: 36.7 us -> 36.6 us (level)
  no operation moved by 1% of the time
where the time goes in v11:
time: 36.6 us; the launch traced here: 36.5 us
  starting transfers between devices  16.4 us (45%)
  Pallas kernels  11.2 us (31%)
  waiting for transfers between devices  8.16 us (22%)
  between operations  0.76 us (2%)
    pallas_call x12, Pallas kernels, call(): pl.pallas_call(kernel, out_shape=outs, in_specs=ins, out_specs=out_specs...  11.2 us
    ppermute x6, starting transfers between devices, swap(): return lax.ppermute(block, ('fluid', 'wall'), pairs)  8.34 us
    ppermute x8, starting transfers between devices, cross(): lax.ppermute(block, axis, [(i, i ^ mask) for i in range(lax.axis_size(axi...  8.01 us
    ppermute x8, waiting for transfers between devices, cross(): lax.ppermute(block, axis, [(i, i ^ mask) for i in range(lax.axis_size(axi...  6.09 us
    ppermute x6, waiting for transfers between devices, swap(): return lax.ppermute(block, ('fluid', 'wall'), pairs)  2.08 us
  transfers between devices with their start and end apart: 14, of which 7 were waited for; matrix products, arithmetic and copies ran while one was open for 0% of the time, Pallas kernels for 21%

profile of v11, /device:TPU:0, one launch (start us, length us, event | category | flops | bytes accessed | tf_op | source)
XLA Modules:
  0.0 36.5 jit_solution(7300042386154908313)
XLA Ops:
  0.7 1.6 %shard_map.85 = (bf16[2,528,128]{2,1,0:T(8,128)(2,1)S(1)}, bf16[2,528,128]{2,1,0:T(8,128)(2,1)S(1)}, bf16[2,528,128]{2,1,0:T(8,128)(2,1)S(1)}, bf16[2,528,128]{2...) custom-call(s32[32]{0:T(128)} %bitcast.12, bf16[32,128,128]{2,1,0:T(8,128)(2,1)} %bitcast.10, ...), custom_call_target="tpu_custom_call" | custom-call | flops 1 | bytes 1 | tf_op jit(solution)/shard_map/pallas_call | solution.py:27
  2.3 0.5 %collective-permute-start = (f32[4,32,128]{2,1,0:T(8,128)S(1)}, f32[4,32,128]{2,1,0:T(8,128)S(1)}, u32[]{:S(2)}, u32[]{:S(2)}) collective-permute-start(f32[4,32,128]{2,1,0:T(8,128)S(1)} %get-tuple-element.35), channel_id=1, source_target_pairs={{0,4},{1,5},{2,6},{3,7},{4,0},{5,1},{6,2},{7,3},{8,12},{9,13},{10,... | collective-permute-start | bytes 196616 | tf_op jit(solution)/shard_map/ppermute | solution.py:61
  2.8 2.6 %collective-permute-start.1 = (f32[4,32,128]{2,1,0:T(8,128)S(1)}, f32[4,32,128]{2,1,0:T(8,128)S(1)}, u32[]{:S(2)}, u32[]{:S(2)}) collective-permute-start(f32[4,32,128]{2,1,0:T(8,128)S(1)} %get-tuple-element.36), channel_id=1, source_target_pairs={{0,1},{1,0},{2,3},{3,2},{4,8},{5,9},{6,10},{7,11},{8,4},{9,5},{10,... | collective-permute-start | bytes 196616 | tf_op jit(solution)/shard_map/ppermute | solution.py:61
  5.5 2.0 %collective-permute-start.5 = (bf16[2,528,128]{2,1,0:T(8,128)(2,1)S(1)}, bf16[2,528,128]{2,1,0:T(8,128)(2,1)S(1)}, u32[]{:S(2)}, u32[]{:S(2)}) collective-permute-start(bf16[2,528,128]{2,1,0:T(8,128)(2,1)S(1)} %get-tuple-element.47), channel_id=1, source_target_pairs={{0,16},{4,20},{8,24},{12,28},{16,0},{20,4},{24,8},{28,12},{1,17},{... | collective-permute-start | bytes 811016 | tf_op jit(solution)/shard_map/ppermute | solution.py:65
  7.5 1.5 %collective-permute-start.6 = (bf16[2,528,128]{2,1,0:T(8,128)(2,1)S(1)}, bf16[2,528,128]{2,1,0:T(8,128)(2,1)S(1)}, u32[]{:S(2)}, u32[]{:S(2)}) collective-permute-start(bf16[2,528,128]{2,1,0:T(8,128)(2,1)S(1)} %get-tuple-element.48), channel_id=1, source_target_pairs={{0,24},{4,28},{8,16},{12,20},{16,8},{20,12},{24,0},{28,4},{1,25},{... | collective-permute-start | bytes 811016 | tf_op jit(solution)/shard_map/ppermute | solution.py:65
  9.0 0.8 %shard_map.86.edges_ref = f32[3,32,128]{2,1,0:T(8,128)S(1)} custom-call(f32[4,16,32,128]{3,2,1,0:T(8,128)S(1)} %copy-done, s32[16,32,128]{2,1,0:T(8,128)S(1)} %copy-done.1, f32[4,32,128]{2,1,0:T(8,128)S(1)} %collective-permute-done.x0_ref, f32[4,32,128]{2,1,0:T(8,128)S(1)} %collective-permute-done.1.x1_ref), custom_call_target="tpu_custom_call" | custom-call | flops 99999997952 | bytes 1 | tf_op jit(solution)/shard_map/pallas_call | solution.py:27
  9.8 3.1 %collective-permute-start.2 = (f32[3,32,128]{2,1,0:T(8,128)S(1)}, f32[3,32,128]{2,1,0:T(8,128)S(1)}, u32[]{:S(2)}, u32[]{:S(2)}) collective-permute-start(f32[3,32,128]{2,1,0:T(8,128)S(1)} %shard_map.86.edges_ref), channel_id=1, source_target_pairs={{0,1},{1,0},{2,3},{3,2},{4,5},{5,4},{6,7},{7,6},{8,9},{9,8},{10,11... | collective-permute-start | bytes 147464 | tf_op jit(solution)/shard_map/ppermute | solution.py:61
  13.0 2.1 %collective-permute-done.2.z0_ref = f32[3,32,128]{2,1,0:T(8,128)S(1)} collective-permute-done((f32[3,32,128]{2,1,0:T(8,128)S(1)}, f32[3,32,128]{2,1,0:T(8,128)S(1)}, u32[]{:S(2)}, u32[]{:S(2)}) %collective-permute-start.2) | collective-permute-done | bytes 49184 | tf_op jit(solution)/shard_map/ppermute | solution.py:61
  15.0 2.6 %shard_map.87 = (f32[3,16,32,128]{3,2,1,0:T(8,128)}, f32[3,16,32,128]{3,2,1,0:T(8,128)S(1)}, f32[17,32,128]{2,1,0:T(8,128)S(1)}, f32[16,32,128]{2,1,0:T(8,128)S(...) custom-call(s32[4,8]{1,0:T(4,128)S(1)} %bitcast.9, ...), custom_call_target="tpu_custom_call" | custom-call | flops 1 | bytes 1 | tf_op jit(solution)/shard_map/pallas_call | solution.py:27
  17.8 0.5 %shard_map.88 = (f32[32,128]{1,0:T(8,128)S(1)}, f32[32,128]{1,0:T(8,128)S(1)}, bf16[3,512,128]{2,1,0:T(8,128)(2,1)S(1)}, f32[16,32,128]{2,1,0:T(8,128)S(1)}, f32[16,32,128]{2,1,0:T(8,128)S(1)}) custom-call(s32[8,128]{1,0:T(8,128)S(1)} %get-tuple-element.39.cells_of_ref, f32[3,32,128]{2,1,0:T(8,128)S(1)} %collective-permute-done.2.z0_ref, ...), custom_call_target="tpu_custom_call" | custom-call | flops 1 | bytes 1 | tf_op jit(solution)/shard_map/pallas_call | solution.py:27
  18.2 0.7 %collective-permute-done.7.values_ref = bf16[4,16,128]{2,1,0:T(8,128)(2,1)S(1)} collective-permute-done((bf16[4,16,128]{2,1,0:T(8,128)(2,1)S(1)}, bf16[4,16,128]{2,1,0:T(8,128)(2,1)S(1)}, u32[]{:S(2)}, u32[]{:S(2)}) %collective-permute-start.7) | collective-permute-done | bytes 16416 | tf_op jit(solution)/shard_map/ppermute | solution.py:65
  18.9 0.4 %shard_map.90.before_ref = bf16[2,64,128]{2,1,0:T(8,128)(2,1)S(1)} custom-call(bf16[4,16,128]{2,1,0:T(8,128)(2,1)S(1)} %collective-permute-done.7.values_ref, bf16[3,512,128]{2,1,0:T(8,128)(2,1)S(1)} %get-tuple-element.50.before_ref.pick_ref, bf16[2,528,128]{2,1,0:T(8,128)(2,1)S(1)} %get-tuple-element.45.refs_0_, ...), custom_call_target="tpu_custom_call" | custom-call | flops 1 | bytes 1 | tf_op jit(solution)/shard_map/pallas_call | solution.py:27
  19.3 0.7 %collective-permute-done.5.refs_2_.refs_0_ = bf16[2,528,128]{2,1,0:T(8,128)(2,1)S(1)} collective-permute-done((bf16[2,528,128]{2,1,0:T(8,128)(2,1)S(1)}, bf16[2,528,128]{2,1,0:T(8,128)(2,1)S(1)}, u32[]{:S(2)}, u32[]{:S(2)}) %collective-permute-start.5) | collective-permute-done | bytes 270368 | tf_op jit(solution)/shard_map/ppermute | solution.py:65
  20.0 0.7 %collective-permute-done.6.refs_3_.refs_1_ = bf16[2,528,128]{2,1,0:T(8,128)(2,1)S(1)} collective-permute-done((bf16[2,528,128]{2,1,0:T(8,128)(2,1)S(1)}, bf16[2,528,128]{2,1,0:T(8,128)(2,1)S(1)}, u32[]{:S(2)}, u32[]{:S(2)}) %collective-permute-start.6) | collective-permute-done | bytes 270368 | tf_op jit(solution)/shard_map/ppermute | solution.py:65
  20.7 0.4 %shard_map.91 = bf16[2,64,128]{2,1,0:T(8,128)(2,1)S(1)} custom-call(bf16[4,16,128]{2,1,0:T(8,128)(2,1)S(1)} %collective-permute-done.7.values_ref, bf16[2,64,128]{2,1,0:T(8,128)(2,1)S(1)} %shard_map.90.before_ref, bf16[2,528,128]{2,1,0:T(8,128)(2,1)S(1)} %collective-permute-done.5.refs_2_.refs_0_, bf16[2,528,128]{2,1,0:T(8,128)(2,1)S(1)} %collective-permute-done.6.refs_3_.refs_1_), custom_call_target="tpu_custom_call" | custom-call | flops 1 | bytes 1 | tf_op jit(solution)/shard_map/pallas_call | solution.py:27
  21.2 0.7 %shard_map.89.mine_ref = bf16[2,64,128]{2,1,0:T(8,128)(2,1)S(1)} custom-call(bf16[4,16,128]{2,1,0:T(8,128)(2,1)S(1)} %get-tuple-element.38.values_ref, f32[32,128]{1,0:T(8,128)S(1)} %get-tuple-element.44.before_ref.outside_ref, bf16[2,528,128]{2,1,0:T(8,128)(2,1)S(1)} %get-tuple-element.45.refs_0_, bf16[2,528,128]{2,1,0:T(8,128)(2,1)S(1)} %collective-permute-done.4.refs_1_, ...), custom_call_target="tpu_custom_call" | custom-call | flops 1 | bytes 1 | tf_op jit(solution)/shard_map/pallas_call | solution.py:27
  21.9 0.5 %collective-permute-done.8.other_ref = bf16[2,64,128]{2,1,0:T(8,128)(2,1)S(1)} collective-permute-done((bf16[2,64,128]{2,1,0:T(8,128)(2,1)S(1)}, bf16[2,64,128]{2,1,0:T(8,128)(2,1)S(1)}, u32[]{:S(2)}, u32[]{:S(2)}) %collective-permute-start.8) | collective-permute-done | bytes 32800 | tf_op jit(solution)/shard_map/ppermute | solution.py:65
  22.8 1.7 %collective-permute-start.10 = (bf16[3,32,128]{2,1,0:T(8,128)(2,1)S(1)}, bf16[3,32,128]{2,1,0:T(8,128)(2,1)S(1)}, u32[]{:S(2)}, u32[]{:S(2)}) collective-permute-start(bf16[3,32,128]{2,1,0:T(8,128)(2,1)S(1)} %get-tuple-element.51.after_ref), channel_id=1, source_target_pairs={{0,1},{1,0},{2,3},{3,2},{4,8},{5,9},{6,10},{7,11},{8,4},{9,5},{10,... | collective-permute-start | bytes 73736 | tf_op jit(solution)/shard_map/ppermute | solution.py:61
  24.9 2.2 %shard_map.94 = (f32[3,16,32,128]{3,2,1,0:T(8,128)S(1)}, f32[32,128]{1,0:T(8,128)S(1)}, f32[8,128]{1,0:T(8,128)S(1)}) custom-call(f32[3,16,32,128]{3,2,1,0:T(8,128)S(1)} %shard_map.93.forcing_ref, f32[3,16,32,128]{3,2,1,0:T(8,128)S(1)} %get-tuple-element.52.next_ref, f32[17,32,128]{2,1,0:T(8,128)S(1)} %get-tuple-element.53.nux_ref, ...), custom_call_target="tpu_custom_call" | custom-call | flops 1 | bytes 1 | tf_op jit(solution)/shard_map/pallas_call | solution.py:27
  27.3 3.3 %collective-permute-start.13 = (bf16[80,128]{1,0:T(8,128)(2,1)S(1)}, bf16[80,128]{1,0:T(8,128)(2,1)S(1)}, u32[]{:S(2)}, u32[]{:S(2)}) collective-permute-start(bf16[80,128]{1,0:T(8,128)(2,1)S(1)} %get-tuple-element.64), channel_id=1, source_target_pairs={{0,3},{1,2},{2,1},{3,0},{4,7},{5,6},{6,5},{7,4},{8,11},{9,10},{10,... | collective-permute-start | bytes 61448 | tf_op jit(solution)/shard_map/ppermute | solution.py:65
  30.7 1.1 %collective-permute-start.11 = (bf16[48,128]{1,0:T(8,128)(2,1)S(1)}, bf16[48,128]{1,0:T(8,128)(2,1)S(1)}, u32[]{:S(2)}, u32[]{:S(2)}) collective-permute-start(bf16[48,128]{1,0:T(8,128)(2,1)S(1)} %get-tuple-element.62), channel_id=1, source_target_pairs={{0,1},{1,0},{2,3},{3,2},{4,5},{5,4},{6,7},{7,6},{8,9},{9,8},{10,11... | collective-permute-start | bytes 36872 | tf_op jit(solution)/shard_map/ppermute | solution.py:65
  31.8 2.7 %collective-permute-done.11.refs_0_ = bf16[48,128]{1,0:T(8,128)(2,1)S(1)} collective-permute-done((bf16[48,128]{1,0:T(8,128)(2,1)S(1)}, bf16[48,128]{1,0:T(8,128)(2,1)S(1)}, u32[]{:S(2)}, u32[]{:S(2)}) %collective-permute-start.11) | collective-permute-done | bytes 12320 | tf_op jit(solution)/shard_map/ppermute | solution.py:65
  34.5 0.8 %collective-permute-done.12.refs_1_ = bf16[64,128]{1,0:T(8,128)(2,1)S(1)} collective-permute-done((bf16[64,128]{1,0:T(8,128)(2,1)S(1)}, bf16[64,128]{1,0:T(8,128)(2,1)S(1)}, u32[]{:S(2)}, u32[]{:S(2)}) %collective-permute-start.12) | collective-permute-done | bytes 16416 | tf_op jit(solution)/shard_map/ppermute | solution.py:65
  35.3 1.1 %shard_map.96 = (f32[3,16,32,128]{3,2,1,0:T(8,128)}, f32[1,16]{1,0:T(1,128)}) custom-call(f32[3,16,32,128]{3,2,1,0:T(8,128)S(1)} %get-tuple-element.56.inner_ref, bf16[3,32,128]{2,1,0:T(8,128)(2,1)S(1)} %collective-permute-done.9.x0_ref, bf16[3,32,128]{2,1,0:T(8,128)(2,1)S(1)} %collective-permute-done.10.x1_ref, ...), custom_call_target="tpu_custom_call" | custom-call | flops 655360 | bytes 1572864 | tf_op jit(solution)/shard_map/pallas_call | solution.py:27
  (22 shorter events, 1.2 us)
Async XLA Ops:
  0.6 8.3 %copy-start = (f32[4,16,32,128]{3,2,1,0:T(8,128)S(1)}, f32[4,16,32,128]{3,2,1,0:T(8,128)}, u32[]{:S(2)}) copy-start(f32[4,16,32,128]{3,2,1,0:T(8,128)} %flow_ref.5) | copy-start | bytes 3145732
  0.6 8.3 %copy-start.1 = (s32[16,32,128]{2,1,0:T(8,128)S(1)}, s32[16,32,128]{2,1,0:T(8,128)}, u32[]{:S(2)}) copy-start(s32[16,32,128]{2,1,0:T(8,128)} %regions_ref.5) | copy-start | bytes 786436
  2.3 6.7 %collective-permute-start = (f32[4,32,128]{2,1,0:T(8,128)S(1)}, f32[4,32,128]{2,1,0:T(8,128)S(1)}, u32[]{:S(2)}, u32[]{:S(2)}) collective-permute-start(f32[4,32,128]{2,1,0:T(8,128)S(1)} %get-tuple-element.35), channel_id=1, source_target_pairs={{0,4},{1,5},{2,6},{3,7},{4,0},{5,1},{6,2},{7,3},{8,12},{9,13},{10,... | collective-permute-start | bytes 196616 | tf_op jit(solution)/shard_map/ppermute | solution.py:61
  2.8 6.1 %collective-permute-start.1 = (f32[4,32,128]{2,1,0:T(8,128)S(1)}, f32[4,32,128]{2,1,0:T(8,128)S(1)}, u32[]{:S(2)}, u32[]{:S(2)}) collective-permute-start(f32[4,32,128]{2,1,0:T(8,128)S(1)} %get-tuple-element.36), channel_id=1, source_target_pairs={{0,1},{1,0},{2,3},{3,2},{4,8},{5,9},{6,10},{7,11},{8,4},{9,5},{10,... | collective-permute-start | bytes 196616 | tf_op jit(solution)/shard_map/ppermute | solution.py:61
  5.5 13.5 %collective-permute-start.4 = (bf16[2,528,128]{2,1,0:T(8,128)(2,1)S(1)}, bf16[2,528,128]{2,1,0:T(8,128)(2,1)S(1)}, u32[]{:S(2)}, u32[]{:S(2)}) collective-permute-start(bf16[2,528,128]{2,1,0:T(8,128)(2,1)S(1)} %get-tuple-element.46), channel_id=1, source_target_pairs={{0,8},{4,12},{8,0},{12,4},{16,24},{20,28},{24,16},{28,20},{1,9},{5... | collective-permute-start | bytes 811016 | tf_op jit(solution)/shard_map/ppermute | solution.py:65
  5.5 14.6 %collective-permute-start.5 = (bf16[2,528,128]{2,1,0:T(8,128)(2,1)S(1)}, bf16[2,528,128]{2,1,0:T(8,128)(2,1)S(1)}, u32[]{:S(2)}, u32[]{:S(2)}) collective-permute-start(bf16[2,528,128]{2,1,0:T(8,128)(2,1)S(1)} %get-tuple-element.47), channel_id=1, source_target_pairs={{0,16},{4,20},{8,24},{12,28},{16,0},{20,4},{24,8},{28,12},{1,17},{... | collective-permute-start | bytes 811016 | tf_op jit(solution)/shard_map/ppermute | solution.py:65
  7.5 13.3 %collective-permute-start.6 = (bf16[2,528,128]{2,1,0:T(8,128)(2,1)S(1)}, bf16[2,528,128]{2,1,0:T(8,128)(2,1)S(1)}, u32[]{:S(2)}, u32[]{:S(2)}) collective-permute-start(bf16[2,528,128]{2,1,0:T(8,128)(2,1)S(1)} %get-tuple-element.48), channel_id=1, source_target_pairs={{0,24},{4,28},{8,16},{12,20},{16,8},{20,12},{24,0},{28,4},{1,25},{... | collective-permute-start | bytes 811016 | tf_op jit(solution)/shard_map/ppermute | solution.py:65
  9.0 6.1 %copy-start.2 = (s32[1,1,8,4]{2,3,1,0:T(4,128)S(1)}, s32[1,1,8,4]{2,3,1,0:T(4,128)}, u32[]{:S(2)}) copy-start(s32[1,1,8,4]{2,3,1,0:T(4,128)} %param.11) | copy-start | bytes 388
  9.7 3.2 %collective-permute-start.3 = (f32[3,32,128]{2,1,0:T(8,128)S(1)}, f32[3,32,128]{2,1,0:T(8,128)S(1)}, u32[]{:S(2)}, u32[]{:S(2)}) collective-permute-start(f32[3,32,128]{2,1,0:T(8,128)S(1)} %shard_map.86.edges_ref), channel_id=1, source_target_pairs={{0,4},{1,2},{2,1},{3,7},{4,0},{5,6},{6,5},{7,3},{8,12},{9,10},{10,... | collective-permute-start | bytes 147464 | tf_op jit(solution)/shard_map/ppermute | solution.py:61
  9.8 5.2 %collective-permute-start.2 = (f32[3,32,128]{2,1,0:T(8,128)S(1)}, f32[3,32,128]{2,1,0:T(8,128)S(1)}, u32[]{:S(2)}, u32[]{:S(2)}) collective-permute-start(f32[3,32,128]{2,1,0:T(8,128)S(1)} %shard_map.86.edges_ref), channel_id=1, source_target_pairs={{0,1},{1,0},{2,3},{3,2},{4,5},{5,4},{6,7},{7,6},{8,9},{9,8},{10,11... | collective-permute-start | bytes 147464 | tf_op jit(solution)/shard_map/ppermute | solution.py:61
  17.7 1.2 %collective-permute-start.7 = (bf16[4,16,128]{2,1,0:T(8,128)(2,1)S(1)}, bf16[4,16,128]{2,1,0:T(8,128)(2,1)S(1)}, u32[]{:S(2)}, u32[]{:S(2)}) collective-permute-start(bf16[4,16,128]{2,1,0:T(8,128)(2,1)S(1)} %get-tuple-element.49), channel_id=1, source_target_pairs={{0,4},{4,0},{8,12},{12,8},{16,20},{20,16},{24,28},{28,24},{1,5},{5... | collective-permute-start | bytes 49160 | tf_op jit(solution)/shard_map/ppermute | solution.py:65
  21.2 1.2 %collective-permute-start.8 = (bf16[2,64,128]{2,1,0:T(8,128)(2,1)S(1)}, bf16[2,64,128]{2,1,0:T(8,128)(2,1)S(1)}, u32[]{:S(2)}, u32[]{:S(2)}) collective-permute-start(bf16[2,64,128]{2,1,0:T(8,128)(2,1)S(1)} %shard_map.91), channel_id=1, source_target_pairs={{0,4},{4,0},{8,12},{12,8},{16,20},{20,16},{24,28},{28,24},{1,5},{5... | collective-permute-start | bytes 98312 | tf_op jit(solution)/shard_map/ppermute | solution.py:65
  22.5 4.5 %collective-permute-start.9 = (bf16[3,32,128]{2,1,0:T(8,128)(2,1)S(1)}, bf16[3,32,128]{2,1,0:T(8,128)(2,1)S(1)}, u32[]{:S(2)}, u32[]{:S(2)}) collective-permute-start(bf16[3,32,128]{2,1,0:T(8,128)(2,1)S(1)} %get-tuple-element.57), channel_id=1, source_target_pairs={{0,4},{1,5},{2,6},{3,7},{4,0},{5,1},{6,2},{7,3},{8,12},{9,13},{10,... | collective-permute-start | bytes 73736 | tf_op jit(solution)/shard_map/ppermute | solution.py:61
  22.8 4.3 %collective-permute-start.10 = (bf16[3,32,128]{2,1,0:T(8,128)(2,1)S(1)}, bf16[3,32,128]{2,1,0:T(8,128)(2,1)S(1)}, u32[]{:S(2)}, u32[]{:S(2)}) collective-permute-start(bf16[3,32,128]{2,1,0:T(8,128)(2,1)S(1)} %get-tuple-element.51.after_ref), channel_id=1, source_target_pairs={{0,1},{1,0},{2,3},{3,2},{4,8},{5,9},{6,10},{7,11},{8,4},{9,5},{10,... | collective-permute-start | bytes 73736 | tf_op jit(solution)/shard_map/ppermute | solution.py:61
  27.3 8.0 %collective-permute-start.13 = (bf16[80,128]{1,0:T(8,128)(2,1)S(1)}, bf16[80,128]{1,0:T(8,128)(2,1)S(1)}, u32[]{:S(2)}, u32[]{:S(2)}) collective-permute-start(bf16[80,128]{1,0:T(8,128)(2,1)S(1)} %get-tuple-element.64), channel_id=1, source_target_pairs={{0,3},{1,2},{2,1},{3,0},{4,7},{5,6},{6,5},{7,4},{8,11},{9,10},{10,... | collective-permute-start | bytes 61448 | tf_op jit(solution)/shard_map/ppermute | solution.py:65
  30.7 4.6 %collective-permute-start.12 = (bf16[64,128]{1,0:T(8,128)(2,1)S(1)}, bf16[64,128]{1,0:T(8,128)(2,1)S(1)}, u32[]{:S(2)}, u32[]{:S(2)}) collective-permute-start(bf16[64,128]{1,0:T(8,128)(2,1)S(1)} %get-tuple-element.63), channel_id=1, source_target_pairs={{0,2},{1,3},{2,0},{3,1},{4,6},{5,7},{6,4},{7,5},{8,10},{9,11},{10,... | collective-permute-start | bytes 49160 | tf_op jit(solution)/shard_map/ppermute | solution.py:65
  30.7 3.8 %collective-permute-start.11 = (bf16[48,128]{1,0:T(8,128)(2,1)S(1)}, bf16[48,128]{1,0:T(8,128)(2,1)S(1)}, u32[]{:S(2)}, u32[]{:S(2)}) collective-permute-start(bf16[48,128]{1,0:T(8,128)(2,1)S(1)} %get-tuple-element.62), channel_id=1, source_target_pairs={{0,1},{1,0},{2,3},{3,2},{4,5},{5,4},{6,7},{7,6},{8,9},{9,8},{10,11... | collective-permute-start | bytes 36872 | tf_op jit(solution)/shard_map/ppermute | solution.py:65

commit v12 on v11

--- a/solution.py
+++ b/solution.py
@@ -374,14 +374,14 @@
         nuzd_ref[x] = jnp.where(lane == 0, edge_of(rim_nu, x), pltpu.roll(nuz_ref[x], 1, 1))
 
 
-def product_kernel(cap, block, masks, values_ref, before_ref, *refs):
+def product_kernel(cap, block, masks, more, values_ref, before_ref, *refs):
     chips, extra, width = values_ref.shape
     recvs, out_ref = refs[:-1], refs[-1]
     depth = cap * width
     row, lane = iotas(extra, depth)
     own = row // 3 == lane // width
     here = lax.axis_index("fluid") // 2
-    if before_ref.shape == out_ref.shape:
+    if more:
         out_ref[...] = before_ref[...]
     for m, recv_ref in zip(masks, recvs):
         source = here ^ m
@@ -671,19 +671,20 @@
         (cells_of, z0, z1, zs, rim, nuy, nuz, nuy0),
     )
 
-    def products(block, masks, values, before):
+    def products(block, masks, values, before, more=False):
         whole = (2, chips * extra, width)
         return call(
-            functools.partial(product_kernel, cap, block, masks),
+            functools.partial(product_kernel, cap, block, masks, more),
             bf16(*whole),
-            [VMEM, VMEM if before.shape == whole else ANY] + [VMEM] * len(masks),
+            [VMEM, VMEM if more else ANY] + [VMEM] * len(masks),
             (values, before, *(recvs[m] for m in masks)),
         )
 
-    given = products(1, tuple(range(chips // 2)), borrowed, pick)
-    given = products(1, tuple(range(chips // 2, chips)), borrowed, given)
+    held = products(0, tuple(range(chips // 2)), mine, pick)
+    given = products(1, tuple(range(chips // 2)), borrowed, held)
+    given = products(1, tuple(range(chips // 2, chips)), borrowed, given, True)
     other = cross(given, "fluid", 1)
-    held = products(0, tuple(range(chips)), mine, outside)
+    held = products(0, tuple(range(chips // 2, chips)), mine, held, True)
     fs0, fs1 = call(ends_kernel, (bf16(3, rows, width),) * 2, [VMEM] * 3, (held, other, pick))
     f0, f1 = swap(fs0, "fluid", 0), swap(fs1, "fluid", 1)
     forcing = call(forcing_kernel, f32(3, planes, rows, width), [VMEM] * 3 + [ANY], (held, other, pick, fs1))

time: 36.6 us -> 36.6 us (level)
    pallas_call x12 -> x13, Pallas kernels: 11.2 us -> 11.3 us  [call(): pl.pallas_call(kernel, out_shape=outs, in_specs=ins, out_specs=out_specs...]
where the time goes in v12:
time: 36.6 us; the launch traced here: 36.5 us
  starting transfers between devices  16.4 us (45%)
  Pallas kernels  11.3 us (31%)
  waiting for transfers between devices  8.04 us (22%)
  between operations  0.77 us (2%)
    pallas_call x13, Pallas kernels, call(): pl.pallas_call(kernel, out_shape=outs, in_specs=ins, out_specs=out_specs...  11.3 us
    ppermute x6, starting transfers between devices, swap(): return lax.ppermute(block, ('fluid', 'wall'), pairs)  8.34 us
    ppermute x8, starting transfers between devices, cross(): lax.ppermute(block, axis, [(i, i ^ mask) for i in range(lax.axis_size(axi...  8.01 us
    ppermute x8, waiting for transfers between devices, cross(): lax.ppermute(block, axis, [(i, i ^ mask) for i in range(lax.axis_size(axi...  5.96 us
    ppermute x6, waiting for transfers between devices, swap(): return lax.ppermute(block, ('fluid', 'wall'), pairs)  2.08 us
  transfers between devices with their start and end apart: 14, of which 7 were waited for; matrix products, arithmetic and copies ran while one was open for 0% of the time, Pallas kernels for 21%

profile of v12, /device:TPU:0, one launch (start us, length us, event | category | flops | bytes accessed | tf_op | source)
XLA Modules:
  0.0 36.5 jit_solution(14732138544935831690)
XLA Ops:
  0.7 1.6 %shard_map.85 = (bf16[2,528,128]{2,1,0:T(8,128)(2,1)S(1)}, bf16[2,528,128]{2,1,0:T(8,128)(2,1)S(1)}, bf16[2,528,128]{2,1,0:T(8,128)(2,1)S(1)}, bf16[2,528,128]{2...) custom-call(s32[32]{0:T(128)} %bitcast.12, bf16[32,128,128]{2,1,0:T(8,128)(2,1)} %bitcast.10, ...), custom_call_target="tpu_custom_call" | custom-call | flops 1 | bytes 1 | tf_op jit(solution)/shard_map/pallas_call | solution.py:27
  2.3 0.5 %collective-permute-start = (f32[4,32,128]{2,1,0:T(8,128)S(1)}, f32[4,32,128]{2,1,0:T(8,128)S(1)}, u32[]{:S(2)}, u32[]{:S(2)}) collective-permute-start(f32[4,32,128]{2,1,0:T(8,128)S(1)} %get-tuple-element.35), channel_id=1, source_target_pairs={{0,4},{1,5},{2,6},{3,7},{4,0},{5,1},{6,2},{7,3},{8,12},{9,13},{10,... | collective-permute-start | bytes 196616 | tf_op jit(solution)/shard_map/ppermute | solution.py:61
  2.8 2.6 %collective-permute-start.1 = (f32[4,32,128]{2,1,0:T(8,128)S(1)}, f32[4,32,128]{2,1,0:T(8,128)S(1)}, u32[]{:S(2)}, u32[]{:S(2)}) collective-permute-start(f32[4,32,128]{2,1,0:T(8,128)S(1)} %get-tuple-element.36), channel_id=1, source_target_pairs={{0,1},{1,0},{2,3},{3,2},{4,8},{5,9},{6,10},{7,11},{8,4},{9,5},{10,... | collective-permute-start | bytes 196616 | tf_op jit(solution)/shard_map/ppermute | solution.py:61
  5.5 2.0 %collective-permute-start.5 = (bf16[2,528,128]{2,1,0:T(8,128)(2,1)S(1)}, bf16[2,528,128]{2,1,0:T(8,128)(2,1)S(1)}, u32[]{:S(2)}, u32[]{:S(2)}) collective-permute-start(bf16[2,528,128]{2,1,0:T(8,128)(2,1)S(1)} %get-tuple-element.47), channel_id=1, source_target_pairs={{0,16},{4,20},{8,24},{12,28},{16,0},{20,4},{24,8},{28,12},{1,17},{... | collective-permute-start | bytes 811016 | tf_op jit(solution)/shard_map/ppermute | solution.py:65
  7.5 1.5 %collective-permute-start.6 = (bf16[2,528,128]{2,1,0:T(8,128)(2,1)S(1)}, bf16[2,528,128]{2,1,0:T(8,128)(2,1)S(1)}, u32[]{:S(2)}, u32[]{:S(2)}) collective-permute-start(bf16[2,528,128]{2,1,0:T(8,128)(2,1)S(1)} %get-tuple-element.48), channel_id=1, source_target_pairs={{0,24},{4,28},{8,16},{12,20},{16,8},{20,12},{24,0},{28,4},{1,25},{... | collective-permute-start | bytes 811016 | tf_op jit(solution)/shard_map/ppermute | solution.py:65
  9.0 0.8 %shard_map.86.edges_ref = f32[3,32,128]{2,1,0:T(8,128)S(1)} custom-call(f32[4,16,32,128]{3,2,1,0:T(8,128)S(1)} %copy-done, s32[16,32,128]{2,1,0:T(8,128)S(1)} %copy-done.1, f32[4,32,128]{2,1,0:T(8,128)S(1)} %collective-permute-done.x0_ref, f32[4,32,128]{2,1,0:T(8,128)S(1)} %collective-permute-done.1.x1_ref), custom_call_target="tpu_custom_call" | custom-call | flops 99999997952 | bytes 1 | tf_op jit(solution)/shard_map/pallas_call | solution.py:27
  9.8 3.1 %collective-permute-start.2 = (f32[3,32,128]{2,1,0:T(8,128)S(1)}, f32[3,32,128]{2,1,0:T(8,128)S(1)}, u32[]{:S(2)}, u32[]{:S(2)}) collective-permute-start(f32[3,32,128]{2,1,0:T(8,128)S(1)} %shard_map.86.edges_ref), channel_id=1, source_target_pairs={{0,1},{1,0},{2,3},{3,2},{4,5},{5,4},{6,7},{7,6},{8,9},{9,8},{10,11... | collective-permute-start | bytes 147464 | tf_op jit(solution)/shard_map/ppermute | solution.py:61
  13.0 2.1 %collective-permute-done.2.z0_ref = f32[3,32,128]{2,1,0:T(8,128)S(1)} collective-permute-done((f32[3,32,128]{2,1,0:T(8,128)S(1)}, f32[3,32,128]{2,1,0:T(8,128)S(1)}, u32[]{:S(2)}, u32[]{:S(2)}) %collective-permute-start.2) | collective-permute-done | bytes 49184 | tf_op jit(solution)/shard_map/ppermute | solution.py:61
  15.0 2.6 %shard_map.87 = (f32[3,16,32,128]{3,2,1,0:T(8,128)}, f32[3,16,32,128]{3,2,1,0:T(8,128)S(1)}, f32[17,32,128]{2,1,0:T(8,128)S(1)}, f32[16,32,128]{2,1,0:T(8,128)S(...) custom-call(s32[4,8]{1,0:T(4,128)S(1)} %bitcast.9, ...), custom_call_target="tpu_custom_call" | custom-call | flops 1 | bytes 1 | tf_op jit(solution)/shard_map/pallas_call | solution.py:27
  17.8 0.5 %shard_map.88 = (f32[32,128]{1,0:T(8,128)S(1)}, f32[32,128]{1,0:T(8,128)S(1)}, bf16[3,512,128]{2,1,0:T(8,128)(2,1)S(1)}, f32[16,32,128]{2,1,0:T(8,128)S(1)}, f32[16,32,128]{2,1,0:T(8,128)S(1)}) custom-call(s32[8,128]{1,0:T(8,128)S(1)} %get-tuple-element.39.cells_of_ref, f32[3,32,128]{2,1,0:T(8,128)S(1)} %collective-permute-done.2.z0_ref, ...), custom_call_target="tpu_custom_call" | custom-call | flops 1 | bytes 1 | tf_op jit(solution)/shard_map/pallas_call | solution.py:27
  18.3 0.4 %shard_map.89.before_ref = bf16[2,64,128]{2,1,0:T(8,128)(2,1)S(1)} custom-call(bf16[4,16,128]{2,1,0:T(8,128)(2,1)S(1)} %get-tuple-element.38.values_ref, bf16[3,512,128]{2,1,0:T(8,128)(2,1)S(1)} %get-tuple-element.44.before_ref.pick_ref, bf16[2,528,128]{2,1,0:T(8,128)(2,1)S(1)} %get-tuple-element.45.refs_0_, ...), custom_call_target="tpu_custom_call" | custom-call | flops 1 | bytes 1 | tf_op jit(solution)/shard_map/pallas_call | solution.py:27
  18.9 0.4 %shard_map.91.before_ref = bf16[2,64,128]{2,1,0:T(8,128)(2,1)S(1)} custom-call(bf16[4,16,128]{2,1,0:T(8,128)(2,1)S(1)} %collective-permute-done.7.values_ref, bf16[2,64,128]{2,1,0:T(8,128)(2,1)S(1)} %shard_map.89.before_ref, bf16[2,528,128]{2,1,0:T(8,128)(2,1)S(1)} %get-tuple-element.45.refs_0_, bf16[2,528,128]{2,1,0:T(8,128)(2,1)S(1)} %collective-permute-done.4.refs_1_), custom_call_target="tpu_custom_call" | custom-call | flops 1 | bytes 1 | tf_op jit(solution)/shard_map/pallas_call | solution.py:27
  19.3 0.7 %collective-permute-done.5.refs_0_ = bf16[2,528,128]{2,1,0:T(8,128)(2,1)S(1)} collective-permute-done((bf16[2,528,128]{2,1,0:T(8,128)(2,1)S(1)}, bf16[2,528,128]{2,1,0:T(8,128)(2,1)S(1)}, u32[]{:S(2)}, u32[]{:S(2)}) %collective-permute-start.5) | collective-permute-done | bytes 270368 | tf_op jit(solution)/shard_map/ppermute | solution.py:65
  20.0 0.7 %collective-permute-done.6.refs_1_ = bf16[2,528,128]{2,1,0:T(8,128)(2,1)S(1)} collective-permute-done((bf16[2,528,128]{2,1,0:T(8,128)(2,1)S(1)}, bf16[2,528,128]{2,1,0:T(8,128)(2,1)S(1)}, u32[]{:S(2)}, u32[]{:S(2)}) %collective-permute-start.6) | collective-permute-done | bytes 270368 | tf_op jit(solution)/shard_map/ppermute | solution.py:65
  20.7 0.4 %shard_map.92 = bf16[2,64,128]{2,1,0:T(8,128)(2,1)S(1)} custom-call(bf16[4,16,128]{2,1,0:T(8,128)(2,1)S(1)} %collective-permute-done.7.values_ref, bf16[2,64,128]{2,1,0:T(8,128)(2,1)S(1)} %shard_map.91.before_ref, bf16[2,528,128]{2,1,0:T(8,128)(2,1)S(1)} %collective-permute-done.5.refs_0_, bf16[2,528,128]{2,1,0:T(8,128)(2,1)S(1)} %collective-permute-done.6.refs_1_), custom_call_target="tpu_custom_call" | custom-call | flops 1 | bytes 1 | tf_op jit(solution)/shard_map/pallas_call | solution.py:27
  21.2 0.4 %shard_map.90.mine_ref = bf16[2,64,128]{2,1,0:T(8,128)(2,1)S(1)} custom-call(bf16[4,16,128]{2,1,0:T(8,128)(2,1)S(1)} %get-tuple-element.38.values_ref, bf16[2,64,128]{2,1,0:T(8,128)(2,1)S(1)} %shard_map.89.before_ref, bf16[2,528,128]{2,1,0:T(8,128)(2,1)S(1)} %collective-permute-done.5.refs_0_, bf16[2,528,128]{2,1,0:T(8,128)(2,1)S(1)} %collective-permute-done.6.refs_1_), custom_call_target="tpu_custom_call" | custom-call | flops 1 | bytes 1 | tf_op jit(solution)/shard_map/pallas_call | solution.py:27
  21.6 0.8 %collective-permute-done.8.other_ref = bf16[2,64,128]{2,1,0:T(8,128)(2,1)S(1)} collective-permute-done((bf16[2,64,128]{2,1,0:T(8,128)(2,1)S(1)}, bf16[2,64,128]{2,1,0:T(8,128)(2,1)S(1)}, u32[]{:S(2)}, u32[]{:S(2)}) %collective-permute-start.8) | collective-permute-done | bytes 32800 | tf_op jit(solution)/shard_map/ppermute | solution.py:65
  22.8 1.7 %collective-permute-start.10 = (bf16[3,32,128]{2,1,0:T(8,128)(2,1)S(1)}, bf16[3,32,128]{2,1,0:T(8,128)(2,1)S(1)}, u32[]{:S(2)}, u32[]{:S(2)}) collective-permute-start(bf16[3,32,128]{2,1,0:T(8,128)(2,1)S(1)} %get-tuple-element.50.after_ref), channel_id=1, source_target_pairs={{0,1},{1,0},{2,3},{3,2},{4,8},{5,9},{6,10},{7,11},{8,4},{9,5},{10,... | collective-permute-start | bytes 73736 | tf_op jit(solution)/shard_map/ppermute | solution.py:61
  24.9 2.2 %shard_map.95 = (f32[3,16,32,128]{3,2,1,0:T(8,128)S(1)}, f32[32,128]{1,0:T(8,128)S(1)}, f32[8,128]{1,0:T(8,128)S(1)}) custom-call(f32[3,16,32,128]{3,2,1,0:T(8,128)S(1)} %shard_map.94.forcing_ref, f32[3,16,32,128]{3,2,1,0:T(8,128)S(1)} %get-tuple-element.51.next_ref, f32[17,32,128]{2,1,0:T(8,128)S(1)} %get-tuple-element.52.nux_ref, ...), custom_call_target="tpu_custom_call" | custom-call | flops 1 | bytes 1 | tf_op jit(solution)/shard_map/pallas_call | solution.py:27
  27.3 3.3 %collective-permute-start.13 = (bf16[80,128]{1,0:T(8,128)(2,1)S(1)}, bf16[80,128]{1,0:T(8,128)(2,1)S(1)}, u32[]{:S(2)}, u32[]{:S(2)}) collective-permute-start(bf16[80,128]{1,0:T(8,128)(2,1)S(1)} %get-tuple-element.64), channel_id=1, source_target_pairs={{0,3},{1,2},{2,1},{3,0},{4,7},{5,6},{6,5},{7,4},{8,11},{9,10},{10,... | collective-permute-start | bytes 61448 | tf_op jit(solution)/shard_map/ppermute | solution.py:65
  30.7 1.1 %collective-permute-start.11 = (bf16[48,128]{1,0:T(8,128)(2,1)S(1)}, bf16[48,128]{1,0:T(8,128)(2,1)S(1)}, u32[]{:S(2)}, u32[]{:S(2)}) collective-permute-start(bf16[48,128]{1,0:T(8,128)(2,1)S(1)} %get-tuple-element.62), channel_id=1, source_target_pairs={{0,1},{1,0},{2,3},{3,2},{4,5},{5,4},{6,7},{7,6},{8,9},{9,8},{10,11... | collective-permute-start | bytes 36872 | tf_op jit(solution)/shard_map/ppermute | solution.py:65
  31.8 2.7 %collective-permute-done.11.refs_0_ = bf16[48,128]{1,0:T(8,128)(2,1)S(1)} collective-permute-done((bf16[48,128]{1,0:T(8,128)(2,1)S(1)}, bf16[48,128]{1,0:T(8,128)(2,1)S(1)}, u32[]{:S(2)}, u32[]{:S(2)}) %collective-permute-start.11) | collective-permute-done | bytes 12320 | tf_op jit(solution)/shard_map/ppermute | solution.py:65
  34.5 0.8 %collective-permute-done.12.refs_1_ = bf16[64,128]{1,0:T(8,128)(2,1)S(1)} collective-permute-done((bf16[64,128]{1,0:T(8,128)(2,1)S(1)}, bf16[64,128]{1,0:T(8,128)(2,1)S(1)}, u32[]{:S(2)}, u32[]{:S(2)}) %collective-permute-start.12) | collective-permute-done | bytes 16416 | tf_op jit(solution)/shard_map/ppermute | solution.py:65
  35.3 1.1 %shard_map.97 = (f32[3,16,32,128]{3,2,1,0:T(8,128)}, f32[1,16]{1,0:T(1,128)}) custom-call(f32[3,16,32,128]{3,2,1,0:T(8,128)S(1)} %get-tuple-element.56.inner_ref, bf16[3,32,128]{2,1,0:T(8,128)(2,1)S(1)} %collective-permute-done.9.x0_ref, bf16[3,32,128]{2,1,0:T(8,128)(2,1)S(1)} %collective-permute-done.10.x1_ref, ...), custom_call_target="tpu_custom_call" | custom-call | flops 655360 | bytes 1572864 | tf_op jit(solution)/shard_map/pallas_call | solution.py:27
  (23 shorter events, 1.5 us)
Async XLA Ops:
  0.6 8.3 %copy-start = (f32[4,16,32,128]{3,2,1,0:T(8,128)S(1)}, f32[4,16,32,128]{3,2,1,0:T(8,128)}, u32[]{:S(2)}) copy-start(f32[4,16,32,128]{3,2,1,0:T(8,128)} %flow_ref.5) | copy-start | bytes 3145732
  0.6 8.3 %copy-start.1 = (s32[16,32,128]{2,1,0:T(8,128)S(1)}, s32[16,32,128]{2,1,0:T(8,128)}, u32[]{:S(2)}) copy-start(s32[16,32,128]{2,1,0:T(8,128)} %regions_ref.5) | copy-start | bytes 786436
  2.3 6.7 %collective-permute-start = (f32[4,32,128]{2,1,0:T(8,128)S(1)}, f32[4,32,128]{2,1,0:T(8,128)S(1)}, u32[]{:S(2)}, u32[]{:S(2)}) collective-permute-start(f32[4,32,128]{2,1,0:T(8,128)S(1)} %get-tuple-element.35), channel_id=1, source_target_pairs={{0,4},{1,5},{2,6},{3,7},{4,0},{5,1},{6,2},{7,3},{8,12},{9,13},{10,... | collective-permute-start | bytes 196616 | tf_op jit(solution)/shard_map/ppermute | solution.py:61
  2.8 6.1 %collective-permute-start.1 = (f32[4,32,128]{2,1,0:T(8,128)S(1)}, f32[4,32,128]{2,1,0:T(8,128)S(1)}, u32[]{:S(2)}, u32[]{:S(2)}) collective-permute-start(f32[4,32,128]{2,1,0:T(8,128)S(1)} %get-tuple-element.36), channel_id=1, source_target_pairs={{0,1},{1,0},{2,3},{3,2},{4,8},{5,9},{6,10},{7,11},{8,4},{9,5},{10,... | collective-permute-start | bytes 196616 | tf_op jit(solution)/shard_map/ppermute | solution.py:61
  5.5 12.8 %collective-permute-start.4 = (bf16[2,528,128]{2,1,0:T(8,128)(2,1)S(1)}, bf16[2,528,128]{2,1,0:T(8,128)(2,1)S(1)}, u32[]{:S(2)}, u32[]{:S(2)}) collective-permute-start(bf16[2,528,128]{2,1,0:T(8,128)(2,1)S(1)} %get-tuple-element.46), channel_id=1, source_target_pairs={{0,8},{4,12},{8,0},{12,4},{16,24},{20,28},{24,16},{28,20},{1,9},{5... | collective-permute-start | bytes 811016 | tf_op jit(solution)/shard_map/ppermute | solution.py:65
  5.5 14.6 %collective-permute-start.5 = (bf16[2,528,128]{2,1,0:T(8,128)(2,1)S(1)}, bf16[2,528,128]{2,1,0:T(8,128)(2,1)S(1)}, u32[]{:S(2)}, u32[]{:S(2)}) collective-permute-start(bf16[2,528,128]{2,1,0:T(8,128)(2,1)S(1)} %get-tuple-element.47), channel_id=1, source_target_pairs={{0,16},{4,20},{8,24},{12,28},{16,0},{20,4},{24,8},{28,12},{1,17},{... | collective-permute-start | bytes 811016 | tf_op jit(solution)/shard_map/ppermute | solution.py:65
  7.5 13.3 %collective-permute-start.6 = (bf16[2,528,128]{2,1,0:T(8,128)(2,1)S(1)}, bf16[2,528,128]{2,1,0:T(8,128)(2,1)S(1)}, u32[]{:S(2)}, u32[]{:S(2)}) collective-permute-start(bf16[2,528,128]{2,1,0:T(8,128)(2,1)S(1)} %get-tuple-element.48), channel_id=1, source_target_pairs={{0,24},{4,28},{8,16},{12,20},{16,8},{20,12},{24,0},{28,4},{1,25},{... | collective-permute-start | bytes 811016 | tf_op jit(solution)/shard_map/ppermute | solution.py:65
  9.0 6.1 %copy-start.2 = (s32[1,1,8,4]{2,3,1,0:T(4,128)S(1)}, s32[1,1,8,4]{2,3,1,0:T(4,128)}, u32[]{:S(2)}) copy-start(s32[1,1,8,4]{2,3,1,0:T(4,128)} %param.11) | copy-start | bytes 388
  9.7 3.2 %collective-permute-start.3 = (f32[3,32,128]{2,1,0:T(8,128)S(1)}, f32[3,32,128]{2,1,0:T(8,128)S(1)}, u32[]{:S(2)}, u32[]{:S(2)}) collective-permute-start(f32[3,32,128]{2,1,0:T(8,128)S(1)} %shard_map.86.edges_ref), channel_id=1, source_target_pairs={{0,4},{1,2},{2,1},{3,7},{4,0},{5,6},{6,5},{7,3},{8,12},{9,10},{10,... | collective-permute-start | bytes 147464 | tf_op jit(solution)/shard_map/ppermute | solution.py:61
  9.8 5.2 %collective-permute-start.2 = (f32[3,32,128]{2,1,0:T(8,128)S(1)}, f32[3,32,128]{2,1,0:T(8,128)S(1)}, u32[]{:S(2)}, u32[]{:S(2)}) collective-permute-start(f32[3,32,128]{2,1,0:T(8,128)S(1)} %shard_map.86.edges_ref), channel_id=1, source_target_pairs={{0,1},{1,0},{2,3},{3,2},{4,5},{5,4},{6,7},{7,6},{8,9},{9,8},{10,11... | collective-permute-start | bytes 147464 | tf_op jit(solution)/shard_map/ppermute | solution.py:61
  17.7 1.2 %collective-permute-start.7 = (bf16[4,16,128]{2,1,0:T(8,128)(2,1)S(1)}, bf16[4,16,128]{2,1,0:T(8,128)(2,1)S(1)}, u32[]{:S(2)}, u32[]{:S(2)}) collective-permute-start(bf16[4,16,128]{2,1,0:T(8,128)(2,1)S(1)} %get-tuple-element.49), channel_id=1, source_target_pairs={{0,4},{4,0},{8,12},{12,8},{16,20},{20,16},{24,28},{28,24},{1,5},{5... | collective-permute-start | bytes 49160 | tf_op jit(solution)/shard_map/ppermute | solution.py:65
  21.2 1.2 %collective-permute-start.8 = (bf16[2,64,128]{2,1,0:T(8,128)(2,1)S(1)}, bf16[2,64,128]{2,1,0:T(8,128)(2,1)S(1)}, u32[]{:S(2)}, u32[]{:S(2)}) collective-permute-start(bf16[2,64,128]{2,1,0:T(8,128)(2,1)S(1)} %shard_map.92), channel_id=1, source_target_pairs={{0,4},{4,0},{8,12},{12,8},{16,20},{20,16},{24,28},{28,24},{1,5},{5... | collective-permute-start | bytes 98312 | tf_op jit(solution)/shard_map/ppermute | solution.py:65
  22.5 4.5 %collective-permute-start.9 = (bf16[3,32,128]{2,1,0:T(8,128)(2,1)S(1)}, bf16[3,32,128]{2,1,0:T(8,128)(2,1)S(1)}, u32[]{:S(2)}, u32[]{:S(2)}) collective-permute-start(bf16[3,32,128]{2,1,0:T(8,128)(2,1)S(1)} %get-tuple-element.57), channel_id=1, source_target_pairs={{0,4},{1,5},{2,6},{3,7},{4,0},{5,1},{6,2},{7,3},{8,12},{9,13},{10,... | collective-permute-start | bytes 73736 | tf_op jit(solution)/shard_map/ppermute | solution.py:61
  22.8 4.3 %collective-permute-start.10 = (bf16[3,32,128]{2,1,0:T(8,128)(2,1)S(1)}, bf16[3,32,128]{2,1,0:T(8,128)(2,1)S(1)}, u32[]{:S(2)}, u32[]{:S(2)}) collective-permute-start(bf16[3,32,128]{2,1,0:T(8,128)(2,1)S(1)} %get-tuple-element.50.after_ref), channel_id=1, source_target_pairs={{0,1},{1,0},{2,3},{3,2},{4,8},{5,9},{6,10},{7,11},{8,4},{9,5},{10,... | collective-permute-start | bytes 73736 | tf_op jit(solution)/shard_map/ppermute | solution.py:61
  27.3 8.0 %collective-permute-start.13 = (bf16[80,128]{1,0:T(8,128)(2,1)S(1)}, bf16[80,128]{1,0:T(8,128)(2,1)S(1)}, u32[]{:S(2)}, u32[]{:S(2)}) collective-permute-start(bf16[80,128]{1,0:T(8,128)(2,1)S(1)} %get-tuple-element.64), channel_id=1, source_target_pairs={{0,3},{1,2},{2,1},{3,0},{4,7},{5,6},{6,5},{7,4},{8,11},{9,10},{10,... | collective-permute-start | bytes 61448 | tf_op jit(solution)/shard_map/ppermute | solution.py:65
  30.7 4.6 %collective-permute-start.12 = (bf16[64,128]{1,0:T(8,128)(2,1)S(1)}, bf16[64,128]{1,0:T(8,128)(2,1)S(1)}, u32[]{:S(2)}, u32[]{:S(2)}) collective-permute-start(bf16[64,128]{1,0:T(8,128)(2,1)S(1)} %get-tuple-element.63), channel_id=1, source_target_pairs={{0,2},{1,3},{2,0},{3,1},{4,6},{5,7},{6,4},{7,5},{8,10},{9,11},{10,... | collective-permute-start | bytes 49160 | tf_op jit(solution)/shard_map/ppermute | solution.py:65
  30.7 3.8 %collective-permute-start.11 = (bf16[48,128]{1,0:T(8,128)(2,1)S(1)}, bf16[48,128]{1,0:T(8,128)(2,1)S(1)}, u32[]{:S(2)}, u32[]{:S(2)}) collective-permute-start(bf16[48,128]{1,0:T(8,128)(2,1)S(1)} %get-tuple-element.62), channel_id=1, source_target_pairs={{0,1},{1,0},{2,3},{3,2},{4,5},{5,4},{6,7},{7,6},{8,9},{9,8},{10,11... | collective-permute-start | bytes 36872 | tf_op jit(solution)/shard_map/ppermute | solution.py:65
